TPU v7x, 32 devices: a whole 2x2x4 slice. The times are simulated.
32 devices in a mesh: blk: 16 (over z, y, core), rep: 2 (over x).
Axes of the slice: x: 2, y: 2, z: 4, core: 2. Of those that a mesh axis runs over, the one named last changes fastest.
Arguments:
- features: bfloat16 [8192, 100], P(('blk', 'rep')), may hold values from -6 to 6
- node_order: int32 [16, 512], P('blk'), may hold values from 0 to 511, each once within a row
- tile_values: bfloat16 [32, 16, 256, 256], P(('blk', 'rep')), may hold values from 0 to 2, as said below
- tile_rows: int32 [32, 16], P(('blk', 'rep')), may hold values from 0 to 31, as said below
- tile_columns: int32 [32, 16], P(('blk', 'rep')), may hold values from 0 to 31, as said below
- tile_live: int32 [32], P(('blk', 'rep')), may hold values from 4 to 16, as said below
- first_weight: bfloat16 [100, 128], replicated, may hold values from -0.625 to 0.625
- first_bias: float32 [128], replicated, may hold values from -3 to 3
- second_weight: bfloat16 [128, 47], replicated, may hold values from -0.5 to 0.5
- second_bias: float32 [47], replicated, may hold values from -3 to 3
Outputs:
- logits: float32 [8192, 47], P(('blk', 'rep'))
Inputs may be any that keep to these rules, and one draw needn't show every extreme that they name: `node_order`: each row is a permutation of 0 to 511. `tile_rows`: the slots of the device at blk index b name row blocks b * 2 to b * 2 + 1. `tile_columns`: the slots of the device at rep index r name column blocks p * 2 + r. `tile_live`: 16 on some devices in every draw. `tile_values`: nonnegative.
All inputs are finite; a program needn't handle non-finite values.
Results may differ from a plain program's by a relative error of at most 0.0015.
Values may be sent and summed in bfloat16 or wider, within the bound.
No kernel may reach another device: no remote copies, remote signals or barrier semaphores. Data moves between devices by JAX's collectives and lax.ppermute only.
A program may use at most 64 MiB of HBM per device.

v0:
```python
import jax
import jax.numpy as jnp
from jax import lax
from jax.sharding import PartitionSpec as P


def add_slots(running, portion, slot_data):
    tile_blocks, local_rows, panel_index, in_use = slot_data
    tile_size = tile_blocks.shape[1]
    length = portion.shape[0]
    padded = jnp.pad(portion, ((tile_size, tile_size), (0, 0)))

    def slot_step(slot_index, current):
        shifted = panel_index[slot_index] * tile_size
        intersection = in_use[slot_index] & (shifted > -tile_size) & (shifted < length)

        def add_tile(existing):
            offset = jnp.clip(shifted + tile_size, 0, length + tile_size)
            window = lax.dynamic_slice_in_dim(padded, offset, tile_size, 0)
            product = jnp.dot(tile_blocks[slot_index], window, preferred_element_type=jnp.float32)
            row_start = local_rows[slot_index] * tile_size
            earlier = lax.dynamic_slice_in_dim(existing, row_start, tile_size, 0)
            return lax.dynamic_update_slice_in_dim(existing, earlier + product, row_start, 0)

        return lax.cond(intersection, add_tile, lambda existing: existing, current)

    return lax.fori_loop(0, tile_blocks.shape[0], slot_step, running)


def body(
    features,
    node_order,
    tile_values,
    tile_rows,
    tile_columns,
    tile_live,
    first_weight,
    first_bias,
    second_weight,
    second_bias,
):
    tile_size = features.shape[0]
    replicas = lax.axis_size("rep")
    member = lax.axis_index("rep")
    group_index = lax.axis_index("blk")
    group_rows = replicas * tile_size
    gathered = lax.all_gather(features, "rep", axis=0, tiled=True)
    row_order = lax.dynamic_slice_in_dim(node_order[0], member * tile_size, tile_size, 0)
    ordered = jnp.take(gathered, row_order, axis=0)
    hidden_in = jnp.dot(ordered, first_weight, preferred_element_type=jnp.float32).astype(
        jnp.bfloat16
    )
    tile_blocks = tile_values[0]
    local_rows = tile_rows[0] - group_index * replicas
    panel_index = tile_columns[0] // replicas
    in_use = jnp.arange(tile_blocks.shape[0], dtype=jnp.int32) < tile_live[0]
    slot_data = (tile_blocks, local_rows, panel_index, in_use)
    row_sums = jnp.sum(tile_blocks, axis=2, dtype=jnp.float32)
    placement = (
        (local_rows[:, None] == jnp.arange(replicas, dtype=jnp.int32)[None, :]) & in_use[:, None]
    ).astype(jnp.float32)
    degree_part = jnp.einsum(
        "kr,ki->ri", placement, row_sums, precision=lax.Precision.HIGHEST
    ).reshape(group_rows)
    zero_sums = jnp.zeros((group_rows, first_weight.shape[1]), jnp.float32)
    summed = add_slots(zero_sums, lax.all_gather(hidden_in, "blk", axis=0, tiled=True), slot_data)
    own_sums, degree = (
        lax.psum_scatter(summed, "rep", scatter_dimension=0, tiled=True),
        lax.psum_scatter(degree_part, "rep", scatter_dimension=0, tiled=True),
    )
    scaling = lax.rsqrt(1.0 + degree)[:, None]
    hidden_out = jax.nn.relu(
        scaling * (own_sums + hidden_in.astype(jnp.float32)) + first_bias
    ).astype(jnp.bfloat16)
    classes_in = jnp.dot(hidden_out, second_weight, preferred_element_type=jnp.float32).astype(
        jnp.bfloat16
    )
    zero_classes = jnp.zeros((group_rows, second_weight.shape[1]), jnp.float32)
    summed_second = add_slots(
        zero_classes, lax.all_gather(classes_in, "blk", axis=0, tiled=True), slot_data
    )
    own_second = lax.psum_scatter(summed_second, "rep", scatter_dimension=0, tiled=True)
    return scaling * (own_second + classes_in.astype(jnp.float32)) + second_bias


def solution(mesh):
    placed = (
        P(("blk", "rep"), None),
        P("blk", None),
        P(("blk", "rep"), None, None, None),
        P(("blk", "rep"), None),
        P(("blk", "rep"), None),
        P(("blk", "rep")),
        P(),
        P(),
        P(),
        P(),
    )
    return jax.shard_map(
        body, mesh=mesh, in_specs=placed, out_specs=P(("blk", "rep"), None), check_vma=False
    )
```

profile of v0, /device:TPU:0, one launch (start us, length us, event | category | flops | bytes accessed | tf_op | source)
XLA Modules:
  0.0 262.3 jit_solution(4189078046475533003)
XLA Ops:
  6.5 0.8 compare_select_fusion
  7.4 0.9 copy.15
  8.3 5.8 %all_gather.9 = bf16[512,100]{1,0:T(8,128)(2,1)S(1)} all-gather(bf16[256,100]{1,0:T(8,128)(2,1)S(1)} %copy.15), channel_id=1, replica_groups=mesh['blk'=16,'rep'=2] {'rep'}, dimensions={0}, use_global_device_ids=true | all-gather | bytes 153600 | tf_op jit(solution)/shard_map/all_gather | solution.py:47
  14.2 0.9 gather_fusion
  15.0 0.8 convolution_convert_fusion
  16.6 0.7 and_select_fusion
  17.3 0.7 subtract_bitcast_fusion
  17.9 37.9 %all-gather.2.cloned.1.call-done = bf16[4096,128]{1,0:T(8,128)(2,1)} async-done(((bf16[256,128]{1,0:T(8,128)(2,1)}), bf16[4096,128]{1,0:T(8,128)(2,1)}) %all-gather.2.cloned.1.call-update) | async-done | bytes 1048592 | tf_op jit(solution)/shard_map/all_gather | solution.py:66
  55.8 2.3 pad.8
  58.2 48.1 %while.32 = (s32[]{:T(128)}, f32[512,128]{1,0:T(8,128)S(1)}, pred[16]{0:T(512)(128)(4,1)S(1)}, s32[16]{0:T(128)S(1)}, s32[16]{0:T(128)S(1)}, /*index=5*/bf16[16,...) while((s32[]{:T(128)}, f32[512,128]{1,0:T(8,128)S(1)}, ...), condition=%wide.region_5.6_spmd, body=%wide.region_2.5_spmd.sunk | while | flops 16810000 | bytes 459116 | solution.py:27
  58.2 0.6 dynamic_slice.83
  60.6 2.4 conditional.4
  60.6 0.7 dynamic_slice.44
  61.9 1.1 fusion
  65.4 2.4 conditional.4
  65.4 0.7 dynamic_slice.44
  66.8 1.1 fusion
  70.2 2.4 conditional.4
  70.3 0.7 dynamic_slice.44
  71.6 1.1 fusion
  75.1 2.4 conditional.4
  75.1 0.7 dynamic_slice.44
  76.4 1.1 fusion
  106.4 0.7 copy-done.2
  107.1 0.6 convert_reduce_fusion
  108.0 0.7 dynamic-slice.1
  109.4 9.2 %all-reduce.2 = f32[512]{0:T(512)S(1)} all-reduce(f32[512]{0:T(512)S(1)} %bitcast.47), channel_id=2, replica_groups=mesh['blk'=16,'rep'=2] {'rep'}, use_global_device_ids=true, to_apply=%region_1.2.clone | all-reduce | flops 512 | bytes 4096
  118.6 25.9 %reduce-scatter.3.cloned.1.call-done = f32[256,128]{1,0:T(8,128)} async-done(((f32[512,128]{1,0:T(8,128)}), f32[256,128]{1,0:T(8,128)}) %reduce-scatter.3.cloned.1.call-update) | async-done | bytes 131088 | tf_op jit(solution)/shard_map/reduce_scatter | solution.py:68
  144.6 1.1 convolution_convert_fusion.1
  145.7 24.0 %all_gather.11 = bf16[4096,47]{0,1:T(8,128)(2,1)} all-gather(bf16[256,47]{0,1:T(8,128)(2,1)S(1)} %convolution_convert_fusion.1), channel_id=1, replica_groups=mesh['blk'=16,'rep'=2] {'blk'}, dimensions={0}, use_global_device_ids=true | all-gather | bytes 409088 | tf_op jit(solution)/shard_map/all_gather | solution.py:80
  169.7 1.5 copy.17
  171.2 1.2 pad.9.clone
  172.4 48.2 %while.33 = (s32[]{:T(128)}, f32[512,47]{0,1:T(8,128)S(1)}, pred[16]{0:T(512)(128)(4,1)S(1)}, s32[16]{0:T(128)S(1)}, s32[16]{0:T(128)S(1)}, /*index=5*/bf16[16,2...) while((s32[]{:T(128)}, f32[512,47]{0,1:T(8,128)S(1)}, ...), condition=%wide.region_10.11_spmd, body=%wide.region_7.10_spmd.sunk | while | flops 6172434 | bytes 295276 | solution.py:27
  174.8 2.5 conditional.5
  174.8 0.7 dynamic_slice.50
  176.2 1.1 fusion.5
  179.7 2.5 conditional.5
  179.7 0.7 dynamic_slice.50
  181.0 1.1 fusion.5
  184.5 2.5 conditional.5
  184.5 0.7 dynamic_slice.50
  185.9 1.1 fusion.5
  189.4 2.5 conditional.5
  189.4 0.7 dynamic_slice.50
  190.7 1.1 fusion.5
  220.7 0.6 copy-done.3
  221.3 32.9 %reduce-scatter.5.cloned.1.call-done = f32[256,47]{0,1:T(8,128)} async-done(((f32[512,47]{0,1:T(8,128)}), f32[256,47]{0,1:T(8,128)}) %reduce-scatter.5.cloned.1.call-update) | async-done | bytes 48144 | tf_op jit(solution)/shard_map/reduce_scatter | solution.py:82
  254.2 1.5 multiply_add_fusion
  (117 shorter events, 37.5 us)
Async XLA Ops:
  6.5 8.5 %copy-start = (bf16[100,128]{1,0:T(8,128)(2,1)S(1)}, bf16[100,128]{1,0:T(8,128)(2,1)}, u32[]{:S(2)}) copy-start(bf16[100,128]{1,0:T(8,128)(2,1)} %param.24) | copy-start | bytes 76804
  6.5 51.6 %copy-start.1 = (bf16[1,16,256,256]{3,2,1,0:T(8,128)(2,1)S(1)}, bf16[1,16,256,256]{3,2,1,0:T(8,128)(2,1)}, u32[]{:S(2)}) copy-start(bf16[1,16,256,256]{3,2,1,0:T(8,128)(2,1)} %param.20) | copy-start | bytes 6291460
  6.5 49.2 %all-gather.2.cloned.1.call-start = ((), (), s32[]{:S(2)}) async-start(), calls=%async_computation.2 | async-start | bytes 1114112 | tf_op jit(solution)/shard_map/all_gather | solution.py:66
  15.9 128.7 %reduce-scatter.3.cloned.1.call-start = ((), (), s32[]{:S(2)}) async-start(), calls=%async_computation.3 | async-start | bytes 393216 | tf_op jit(solution)/shard_map/reduce_scatter | solution.py:68
  58.1 49.9 %copy-start.8 = (u32[32]{0:T(128)S(1)}, u32[32]{0:T(128)}, u32[]{:S(2)}) copy-start(u32[32]{0:T(128)} %constant.172) | copy-start | bytes 388
  58.2 86.4 %copy-start.4 = (bf16[256,128]{1,0:T(8,128)(2,1)S(1)}, bf16[256,128]{1,0:T(8,128)(2,1)}, u32[]{:S(2)}) copy-start(bf16[256,128]{1,0:T(8,128)(2,1)} %convolution_convert_fusion) | copy-start | bytes 196612
  58.2 86.4 %copy-start.5 = (bf16[128,47]{0,1:T(8,128)(2,1)S(1)}, bf16[128,47]{0,1:T(8,128)(2,1)}, u32[]{:S(2)}) copy-start(bf16[128,47]{0,1:T(8,128)(2,1)} %param.26) | copy-start | bytes 36100
  58.2 86.4 %copy-start.6 = (f32[128]{0:T(128)S(1)}, f32[128]{0:T(128)}, u32[]{:S(2)}) copy-start(f32[128]{0:T(128)} %param.25) | copy-start | bytes 1540
  106.4 0.7 copy-start.2
  107.1 147.2 %reduce-scatter.5.cloned.1.call-start = ((), (), s32[]{:S(2)}) async-start(), calls=%async_computation.4 | async-start | bytes 147456 | tf_op jit(solution)/shard_map/reduce_scatter | solution.py:82
  171.2 83.1 %copy-start.7 = (f32[47]{0:T(128)S(1)}, f32[47]{0:T(128)}, u32[]{:S(2)}) copy-start(f32[47]{0:T(128)} %param.27) | copy-start | bytes 568
  220.7 0.6 copy-start.3
Sparse Core Ops, SparseCore 0:
  16.0 39.7 all-gather.1
  107.2 37.3 reduce-scatter.2
  221.5 32.7 reduce-scatter.4
where the time goes:
time: 266 us; the launch traced here: 262 us
  waiting for transfers between devices  96.7 us (36%)
  local copies, waits for them, and re-layouts  51.4 us (19%)
  loops' own time  45.2 us (17%)
  blocking collectives  39 us (15%)
  between operations  14.6 us (5%)
  matrix products  10.9 us (4%)
  other arithmetic  4.36 us (2%)
    another operation x2, loops' own time, add_slots(): return lax.fori_loop(0, tile_blocks.shape[0], slot_step, running)  39.2 us
    all_gather x1, waiting for transfers between devices, body(): lax.all_gather(hidden_in, 'blk', axis=0, tiled=True)  37.9 us
    reduce_scatter x1, waiting for transfers between devices, body(): lax.psum_scatter(summed_second, 'rep', scatter_dimension=0, tiled=True)  32.9 us
    reduce_scatter x1, waiting for transfers between devices, body(): lax.psum_scatter(summed, 'rep', scatter_dimension=0, tiled=True)  25.9 us
    all_gather x1, blocking collectives, body(): lax.all_gather(classes_in, 'blk', axis=0, tiled=True)  24 us
    dynamic_slice x32, local copies, waits for them, and re-layouts, slot_step(): shifted = panel_index[slot_index] * tile_size  19.4 us
    dynamic_slice x32, local copies, waits for them, and re-layouts, slot_step(): in_use[slot_index] & (shifted > -tile_size) & (shifted < length)  18 us
    unnamed x1, blocking collectives  9.21 us
  transfers between devices with their start and end apart: 3, of which 3 were waited for; matrix products, arithmetic and copies ran while one was open for 1% of the time, Pallas kernels for 0%

commit v1 on v0

v1 whole, which is shorter than its diff:
```python
import functools

import jax
import jax.numpy as jnp
from jax import lax
from jax.experimental import pallas as pl
from jax.experimental.pallas import tpu as pltpu
from jax.sharding import PartitionSpec as P

BF16 = jnp.bfloat16
F32 = jnp.float32
ONES_ROWS = 16
VMEM_LIMIT = 32 * 1024 * 1024


def nn(a, b):
    return lax.dot_general(a, b, (((1,), (0,)), ((), ())), preferred_element_type=F32)


def nt(a, b):
    return lax.dot_general(a, b, (((1,), (1,)), ((), ())), preferred_element_type=F32)


def call(kernel, outs, n_smem, n_vmem):
    return pl.pallas_call(
        kernel,
        out_shape=outs,
        in_specs=[pl.BlockSpec(memory_space=pltpu.SMEM)] * n_smem
        + [pl.BlockSpec(memory_space=pltpu.VMEM)] * n_vmem,
        compiler_params=pltpu.CompilerParams(vmem_limit_bytes=VMEM_LIMIT),
    )


def order_project(ids, order, weight_t, *rest):
    *features, out = rest
    reps = len(features)
    tile = features[0].shape[1]
    member = ids[1]
    wanted = order[:, pl.ds(pl.multiple_of(member * tile, tile), tile)]
    total = jnp.zeros(out.shape, F32)
    for step in range(reps):
        owner = lax.rem(member + step, reps)
        hidden = nn(weight_t[...], features[step][...]).astype(BF16)
        source = lax.broadcasted_iota(jnp.int32, (tile, tile), 0) + owner * tile
        pick = jnp.where(source == wanted, 1.0, 0.0).astype(BF16)
        total = total + nn(hidden, pick)
    out[...] = total.astype(BF16)


def aggregate(reps, count_rows, ids, live, rows, columns, tiles, near, far, *outs):
    slots, tile = tiles.shape[0], tiles.shape[1]
    height = near.shape[1]
    half = near.shape[0]
    outer = half // 2
    block, member = ids[0], ids[1]
    my_outer, my_inner, my_core = block // 4, (block // 2) % 2, block % 2
    extra = ONES_ROWS if count_rows else 0
    total = jnp.zeros((reps * (height + extra), tile), F32)
    for slot in range(slots):
        panel = lax.clamp(0, columns[0, slot] // reps, 2 * half - 1)
        d_outer = lax.rem(panel // 4 - my_outer + outer, outer)
        d_inner = lax.rem((panel // 2) % 2 + my_inner, 2)
        d_core = lax.rem(panel % 2 + my_core, 2)
        place = d_inner * outer + d_outer
        values = jnp.where(d_core == 0, near[place], far[place])
        local = rows[0, slot] - block * reps
        pieces = []
        for step in range(reps):
            wanted = lax.rem(member + step, reps)
            used = ((local == wanted) & (slot < live[0])).astype(F32)
            pieces.append(values * used.astype(BF16))
            if extra:
                pieces.append(jnp.full((extra, tile), used, F32).astype(BF16))
        total = total + nt(jnp.concatenate(pieces, axis=0), tiles[slot])
    for step in range(reps):
        start = step * (height + extra)
        outs[step][...] = total[start : start + outs[step].shape[0]]


def combine(reps, hidden_in, bias, weight_t, own, *rest):
    arrived, (out, scale_out) = rest[: reps - 1], rest[reps - 1 :]
    height = hidden_in.shape[0]
    total = own[...]
    for part in arrived:
        total = total + part[...]
    scaling = lax.rsqrt(1.0 + total[height : height + 1])
    hidden = scaling * (total[:height] + hidden_in[...].astype(F32)) + bias[...]
    hidden = jnp.maximum(hidden, 0.0).astype(BF16)
    classes = nn(weight_t[...], hidden).astype(BF16)
    out[: classes.shape[0]] = classes
    scale_out[...] = scaling


def finish(reps, classes_in, scaling, bias, own, *rest):
    arrived, out = rest[: reps - 1], rest[reps - 1]
    total = own[...]
    for part in arrived:
        total = total + part[...]
    classes = out.shape[0]
    whole = total + classes_in[...].astype(F32)
    out[...] = scaling[...] * whole[:classes] + bias[...]


def shifted(value, axis, step):
    size = lax.axis_size(axis)
    return lax.ppermute(value, axis, [((d + step) % size, d) for d in range(size)])


def gather_blocks(value):
    size = lax.axis_size("blk")
    outer = size // 4
    along = [value]
    for step in range(1, outer):
        along.append(lax.ppermute(value, "blk", [((d + 4 * step) % size, d) for d in range(size)]))
    column = jnp.stack(along)
    across = lax.ppermute(column, "blk", [(d ^ 2, d) for d in range(size)])
    near = jnp.concatenate([column, across])
    far = lax.ppermute(near, "blk", [(d ^ 1, d) for d in range(size)])
    return near, far


def body(
    features,
    node_order,
    tile_values,
    tile_rows,
    tile_columns,
    tile_live,
    first_weight,
    first_bias,
    second_weight,
    second_bias,
):
    tile = features.shape[0]
    reps = lax.axis_size("rep")
    hidden, classes = second_weight.shape
    padded = -(-classes // 16) * 16
    ids = jnp.stack([lax.axis_index("blk"), lax.axis_index("rep")]).astype(jnp.int32)
    tiles = tile_values[0]

    own_t = features.T
    parts = [own_t] + [shifted(own_t, "rep", step) for step in range(1, reps)]
    hidden_in = call(
        order_project, jax.ShapeDtypeStruct((hidden, tile), BF16), 1, 2 + reps
    )(ids, node_order, first_weight.T, *parts)

    near, far = gather_blocks(hidden_in)
    sums = call(
        functools.partial(aggregate, reps, True),
        [jax.ShapeDtypeStruct((hidden + 8, tile), F32)] * reps,
        4,
        3,
    )(ids, tile_live, tile_rows, tile_columns, tiles, near, far)
    arrived = [shifted(sums[reps - step], "rep", step) for step in range(1, reps)]
    classes_in, scaling = call(
        functools.partial(combine, reps),
        [jax.ShapeDtypeStruct((padded, tile), BF16), jax.ShapeDtypeStruct((1, tile), F32)],
        0,
        4 + reps - 1,
    )(
        hidden_in,
        first_bias[:, None],
        jnp.pad(second_weight.T, ((0, padded - classes), (0, 0))),
        sums[0],
        *arrived,
    )

    near, far = gather_blocks(classes_in)
    sums = call(
        functools.partial(aggregate, reps, False),
        [jax.ShapeDtypeStruct((padded, tile), F32)] * reps,
        4,
        3,
    )(ids, tile_live, tile_rows, tile_columns, tiles, near, far)
    arrived = [shifted(sums[reps - step], "rep", step) for step in range(1, reps)]
    logits = call(
        functools.partial(finish, reps),
        jax.ShapeDtypeStruct((classes, tile), F32),
        0,
        4 + reps - 1,
    )(classes_in, scaling, second_bias[:, None], sums[0], *arrived)
    return logits.T


def solution(mesh):
    placed = (
        P(("blk", "rep"), None),
        P("blk", None),
        P(("blk", "rep"), None, None, None),
        P(("blk", "rep"), None),
        P(("blk", "rep"), None),
        P(("blk", "rep")),
        P(),
        P(),
        P(),
        P(),
    )
    return jax.shard_map(
        body, mesh=mesh, in_specs=placed, out_specs=P(("blk", "rep"), None), check_vma=False
    )
```

time: 266 us -> 56.8 us (0.21); the launches traced: 262 us -> 56.5 us
  waiting for transfers between devices: 96.7 us -> 27.3 us
  local copies, waits for them, and re-layouts: 51.4 us -> 5.55 us
  loops' own time: 45.2 us -> 0 us
  blocking collectives: 39 us -> 0 us
  starting transfers between devices: 0.09 us -> 18.4 us
  between operations: 14.6 us -> 0.78 us
  matrix products: 10.9 us -> 0 us
  Pallas kernels: 0 us -> 4.41 us
  other arithmetic: 4.36 us -> 0.12 us
    reduce_scatter x2 -> x0, waiting for transfers between devices: 58.8 us -> none  [the longest x1 32.9 us: body(): lax.psum_scatter(summed_second, 'rep', scatter_dimension=0, tiled=True)]
    another operation x34 -> x0, loops' own time: 45.2 us -> none  [the longest x2 39.2 us: add_slots(): return lax.fori_loop(0, tile_blocks.shape[0], slot_step, running)]
    dynamic_slice x72 -> x0, local copies, waits for them, and re-layouts: 42.6 us -> none  [the longest x32 19.4 us: slot_step(): shifted = panel_index[slot_index] * tile_size]
    all_gather x1 -> x0, waiting for transfers between devices: 37.9 us -> none  [body(): lax.all_gather(hidden_in, 'blk', axis=0, tiled=True)]
    all_gather x2 -> x0, blocking collectives: 29.8 us -> none  [the longest x1 24 us: body(): lax.all_gather(classes_in, 'blk', axis=0, tiled=True)]
    ppermute x0 -> x13, waiting for transfers between devices: none -> 27.3 us  [the longest x6 8.71 us: gather_blocks(): lax.ppermute(value, 'blk', [((d + 4 * step) % size, d) for d in range(siz...]
    ppermute x0 -> x13, starting transfers between devices: none -> 18.4 us  [the longest x6 9.03 us: gather_blocks(): lax.ppermute(value, 'blk', [((d + 4 * step) % size, d) for d in range(siz...]
    dot_general x11 -> x0, matrix products: 10.9 us -> none  [the longest x8 8.64 us: add_tile(): jnp.dot(tile_blocks[slot_index], window, preferred_element_type=jnp.float32)]
  transfers between devices with their start and end apart: 3 -> 13, of which waited for: 3 -> 12; matrix products, arithmetic and copies ran while one was open for 1% -> 2% of each run, Pallas kernels for 0% -> 0%
where the time goes in v1:
time: 56.8 us; the launch traced here: 56.5 us
  waiting for transfers between devices  27.3 us (48%)
  starting transfers between devices  18.4 us (32%)
  local copies, waits for them, and re-layouts  5.55 us (10%)
  Pallas kernels  4.41 us (8%)
  between operations  0.78 us (1%)
    ppermute x6, starting transfers between devices, gather_blocks(): lax.ppermute(value, 'blk', [((d + 4 * step) % size, d) for d in range(siz...  9.03 us
    ppermute x6, waiting for transfers between devices, gather_blocks(): lax.ppermute(value, 'blk', [((d + 4 * step) % size, d) for d in range(siz...  8.71 us
    ppermute x3, waiting for transfers between devices, shifted(): lax.ppermute(value, axis, [((d + step) % size, d) for d in range(size)])  7.98 us
    ppermute x2, waiting for transfers between devices, gather_blocks(): across = lax.ppermute(column, 'blk', [(d ^ 2, d) for d in range(size)])  7.91 us
    ppermute x3, starting transfers between devices, shifted(): lax.ppermute(value, axis, [((d + step) % size, d) for d in range(size)])  6.05 us
    unnamed x31, local copies, waits for them, and re-layouts  5.3 us
    ppermute x2, starting transfers between devices, gather_blocks(): across = lax.ppermute(column, 'blk', [(d ^ 2, d) for d in range(size)])  3.17 us
    ppermute x2, waiting for transfers between devices, gather_blocks(): far = lax.ppermute(near, 'blk', [(d ^ 1, d) for d in range(size)])  2.68 us
  transfers between devices with their start and end apart: 13, of which 12 were waited for; matrix products, arithmetic and copies ran while one was open for 2% of the time, Pallas kernels for 0%

profile of v1, /device:TPU:0, one launch (start us, length us, event | category | flops | bytes accessed | tf_op | source)
XLA Modules:
  0.0 56.5 jit_solution(706191678061451216)
XLA Ops:
  0.0 2.9 %collective-permute-start = (bf16[100,256]{1,0:T(8,128)(2,1)}, bf16[100,256]{1,0:T(8,128)(2,1)S(1)}, u32[]{:S(2)}, u32[]{:S(2)}) collective-permute-start(bf16[100,256]{1,0:T(8,128)(2,1)} %bitcast.30), channel_id=1, source_target_pairs={{1,0},{0,1},{3,2},{2,3},{5,4},{4,5},{7,6},{6,7},{9,8},{8,9},{11,10... | collective-permute-start | bytes 153608 | tf_op jit(solution)/shard_map/ppermute | solution.py:106
  2.9 0.1 pad_add_fusion.ids
  3.0 0.9 %copy.11 = bf16[100,128]{0,1:T(8,128)(2,1)S(1)} copy(bf16[100,128]{1,0:T(8,128)(2,1)} %param.16) | data formatting | bytes 51200 | tf_op args[6]
  3.9 1.4 %collective-permute-done.rest_1_ = bf16[100,256]{1,0:T(8,128)(2,1)S(1)} collective-permute-done((bf16[100,256]{1,0:T(8,128)(2,1)}, bf16[100,256]{1,0:T(8,128)(2,1)S(1)}, u32[]{:S(2)}, u32[]{:S(2)}) %collective-permute-start) | collective-permute-done | bytes 51232 | tf_op jit(solution)/shard_map/ppermute | solution.py:106
  5.3 0.8 %copy-done.2 = bf16[256,100]{0,1:T(8,128)(2,1)S(1)} copy-done((bf16[256,100]{0,1:T(8,128)(2,1)S(1)}, bf16[256,100]{0,1:T(8,128)(2,1)}, u32[]{:S(2)}) %copy-start.2) | copy-done | bytes 51224
  6.1 0.7 %copy-done.3 = s32[1,512]{1,0:T(1,128)S(1)} copy-done((s32[1,512]{1,0:T(1,128)S(1)}, s32[1,512]{1,0:T(1,128)}, u32[]{:S(2)}) %copy-start.3) | copy-done | bytes 2072
  6.8 0.8 %shard_map.100.hidden_in = bf16[128,256]{1,0:T(8,128)(2,1)S(1)} custom-call(s32[2]{0:T(128)S(1)} %pad_add_fusion.ids, s32[1,512]{1,0:T(1,128)S(1)} %copy-done.3, bf16[128,100]{1,0:T(8,128)(2,1)S(1)} %bitcast.29, bf16[100,256]{1,0:T(8,128)(2,1)S(1)} %bitcast.31, bf16[100,256]{1,0:T(8,128)(2,1)S(1)} %collective-permute-done.rest_1_), custom_call_target="tpu_custom_call" | custom-call | tf_op jit(solution)/shard_map/pallas_call | solution.py:143
  7.6 4.2 %collective-permute-start.1 = (bf16[128,256]{1,0:T(8,128)(2,1)S(1)}, bf16[128,256]{1,0:T(8,128)(2,1)S(1)}, u32[]{:S(2)}, u32[]{:S(2)}) collective-permute-start(bf16[128,256]{1,0:T(8,128)(2,1)S(1)} %shard_map.100.hidden_in), channel_id=1, source_target_pairs={{8,0},{10,2},{12,4},{14,6},{16,8},{18,10},{20,12},{22,14},{24,16},... | collective-permute-start | bytes 196616 | tf_op jit(solution)/shard_map/ppermute | solution.py:114
  11.8 0.0 collective-permute-start.2
  11.8 1.0 %collective-permute-start.3 = (bf16[128,256]{1,0:T(8,128)(2,1)S(1)}, bf16[128,256]{1,0:T(8,128)(2,1)S(1)}, u32[]{:S(2)}, u32[]{:S(2)}) collective-permute-start(bf16[128,256]{1,0:T(8,128)(2,1)S(1)} %shard_map.100.hidden_in), channel_id=1, source_target_pairs={{24,0},{26,2},{28,4},{30,6},{0,8},{2,10},{4,12},{6,14},{8,16},{10,... | collective-permute-start | bytes 196616 | tf_op jit(solution)/shard_map/ppermute | solution.py:114
  12.8 0.9 %collective-permute-done.1 = bf16[128,256]{1,0:T(8,128)(2,1)S(1)} collective-permute-done((bf16[128,256]{1,0:T(8,128)(2,1)S(1)}, bf16[128,256]{1,0:T(8,128)(2,1)S(1)}, u32[]{:S(2)}, u32[]{:S(2)}) %collective-permute-start.1) | collective-permute-done | bytes 65568 | tf_op jit(solution)/shard_map/ppermute | solution.py:114
  13.7 3.3 %collective-permute-done.2 = bf16[128,256]{1,0:T(8,128)(2,1)S(1)} collective-permute-done((bf16[128,256]{1,0:T(8,128)(2,1)S(1)}, bf16[128,256]{1,0:T(8,128)(2,1)S(1)}, u32[]{:S(2)}, u32[]{:S(2)}) %collective-permute-start.2) | collective-permute-done | bytes 65568 | tf_op jit(solution)/shard_map/ppermute | solution.py:114
  16.9 0.9 %collective-permute-done.3 = bf16[128,256]{1,0:T(8,128)(2,1)S(1)} collective-permute-done((bf16[128,256]{1,0:T(8,128)(2,1)S(1)}, bf16[128,256]{1,0:T(8,128)(2,1)S(1)}, u32[]{:S(2)}, u32[]{:S(2)}) %collective-permute-start.3) | collective-permute-done | bytes 65568 | tf_op jit(solution)/shard_map/ppermute | solution.py:114
  17.9 0.0 copy-start.9
  17.9 0.0 copy-start.8
  17.9 1.6 %collective-permute-start.4 = (bf16[4,128,256]{2,1,0:T(8,128)(2,1)S(1)}, bf16[4,128,256]{2,1,0:T(8,128)(2,1)S(1)}, u32[]{:S(2)}, u32[]{:S(2)}) collective-permute-start(bf16[4,128,256]{2,1,0:T(8,128)(2,1)S(1)} %pad_maximum_fusion), channel_id=1, source_target_pairs={{4,0},{6,2},{0,4},{2,6},{12,8},{14,10},{8,12},{10,14},{20,16},{22,... | collective-permute-start | bytes 786440 | tf_op jit(solution)/shard_map/ppermute | solution.py:116
  19.5 4.8 %collective-permute-done.4 = bf16[4,128,256]{2,1,0:T(8,128)(2,1)S(1)} collective-permute-done((bf16[4,128,256]{2,1,0:T(8,128)(2,1)S(1)}, bf16[4,128,256]{2,1,0:T(8,128)(2,1)S(1)}, u32[]{:S(2)}, u32[]{:S(2)}) %collective-permute-start.4) | collective-permute-done | bytes 262176 | tf_op jit(solution)/shard_map/ppermute | solution.py:116
  24.4 0.1 collective-permute-start.5
  25.1 1.2 %collective-permute-done.5.far = bf16[8,128,256]{2,1,0:T(8,128)(2,1)S(1)} collective-permute-done((bf16[8,128,256]{2,1,0:T(8,128)(2,1)S(1)}, bf16[8,128,256]{2,1,0:T(8,128)(2,1)S(1)}, u32[]{:S(2)}, u32[]{:S(2)}) %collective-permute-start.5) | collective-permute-done | bytes 524320 | tf_op jit(solution)/shard_map/ppermute | solution.py:118
  26.3 1.6 %copy-done = bf16[1,16,256,256]{3,2,1,0:T(8,128)(2,1)S(1)} copy-done((bf16[1,16,256,256]{3,2,1,0:T(8,128)(2,1)S(1)}, bf16[1,16,256,256]{3,2,1,0:T(8,128)(2,1)}, u32[]{:S(2)}) %copy-start) | copy-done | bytes 2097176
  27.9 0.7 %copy-done.4 = s32[1,16]{1,0:T(1,128)S(1)} copy-done((s32[1,16]{1,0:T(1,128)S(1)}, s32[1,16]{1,0:T(1,128)}, u32[]{:S(2)}) %copy-start.4) | copy-done | bytes 88
  28.6 0.7 %copy-done.6 = s32[1,16]{1,0:T(1,128)S(1)} copy-done((s32[1,16]{1,0:T(1,128)S(1)}, s32[1,16]{1,0:T(1,128)}, u32[]{:S(2)}) %copy-start.6) | copy-done | bytes 88
  29.3 1.4 %shard_map.101 = (f32[136,256]{1,0:T(8,128)S(1)}, f32[136,256]{1,0:T(8,128)S(1)}) custom-call(s32[2]{0:T(128)S(1)} %pad_add_fusion.ids, s32[1]{0:T(128)S(6)} %copy.22.live, s32[1,16]{1,0:T(1,128)S(1)} %copy-done.4, s32[1,16]{1,0:T(1,128)S(1)} %copy-done.6, bf16[16,256,256]{2,1,0:T(8,128)(2,1)S(1)} %bitcast.25, ...), custom_call_target="tpu_custom_call" | custom-call | tf_op jit(solution)/shard_map/pallas_call | solution.py:148
  30.6 0.0 copy-start.10
  30.6 1.6 %collective-permute-start.6 = (f32[136,256]{1,0:T(8,128)S(1)}, f32[136,256]{1,0:T(8,128)S(1)}, u32[]{:S(2)}, u32[]{:S(2)}) collective-permute-start(f32[136,256]{1,0:T(8,128)S(1)} %get-tuple-element.12), channel_id=1, source_target_pairs={{1,0},{0,1},{3,2},{2,3},{5,4},{4,5},{7,6},{6,7},{9,8},{8,9},{11,10... | collective-permute-start | bytes 417800 | tf_op jit(solution)/shard_map/ppermute | solution.py:106
  32.2 0.0 copy-done.9
  32.2 0.1 copy.12.bias
  32.3 0.0 copy-done.8
  32.3 4.1 %collective-permute-done.6.rest_0_ = f32[136,256]{1,0:T(8,128)S(1)} collective-permute-done((f32[136,256]{1,0:T(8,128)S(1)}, f32[136,256]{1,0:T(8,128)S(1)}, u32[]{:S(2)}, u32[]{:S(2)}) %collective-permute-start.6) | collective-permute-done | bytes 139296 | tf_op jit(solution)/shard_map/ppermute | solution.py:106
  36.4 0.2 shard_map.102
  36.6 1.3 %collective-permute-start.7 = (bf16[48,256]{1,0:T(8,128)(2,1)S(1)}, bf16[48,256]{1,0:T(8,128)(2,1)S(1)}, u32[]{:S(2)}, u32[]{:S(2)}) collective-permute-start(bf16[48,256]{1,0:T(8,128)(2,1)S(1)} %get-tuple-element.13.classes_in), channel_id=1, source_target_pairs={{8,0},{10,2},{12,4},{14,6},{16,8},{18,10},{20,12},{22,14},{24,16},... | collective-permute-start | bytes 73736 | tf_op jit(solution)/shard_map/ppermute | solution.py:114
  37.9 0.6 %collective-permute-start.8 = (bf16[48,256]{1,0:T(8,128)(2,1)S(1)}, bf16[48,256]{1,0:T(8,128)(2,1)S(1)}, u32[]{:S(2)}, u32[]{:S(2)}) collective-permute-start(bf16[48,256]{1,0:T(8,128)(2,1)S(1)} %get-tuple-element.13.classes_in), channel_id=1, source_target_pairs={{16,0},{18,2},{20,4},{22,6},{24,8},{26,10},{28,12},{30,14},{0,16},... | collective-permute-start | bytes 73736 | tf_op jit(solution)/shard_map/ppermute | solution.py:114
  38.5 2.0 %collective-permute-start.9 = (bf16[48,256]{1,0:T(8,128)(2,1)S(1)}, bf16[48,256]{1,0:T(8,128)(2,1)S(1)}, u32[]{:S(2)}, u32[]{:S(2)}) collective-permute-start(bf16[48,256]{1,0:T(8,128)(2,1)S(1)} %get-tuple-element.13.classes_in), channel_id=1, source_target_pairs={{24,0},{26,2},{28,4},{30,6},{0,8},{2,10},{4,12},{6,14},{8,16},{10,... | collective-permute-start | bytes 73736 | tf_op jit(solution)/shard_map/ppermute | solution.py:114
  40.5 0.0 collective-permute-done.7
  40.5 2.2 %collective-permute-done.8 = bf16[48,256]{1,0:T(8,128)(2,1)S(1)} collective-permute-done((bf16[48,256]{1,0:T(8,128)(2,1)S(1)}, bf16[48,256]{1,0:T(8,128)(2,1)S(1)}, u32[]{:S(2)}, u32[]{:S(2)}) %collective-permute-start.8) | collective-permute-done | bytes 24608 | tf_op jit(solution)/shard_map/ppermute | solution.py:114
  42.7 1.5 %collective-permute-done.9 = bf16[48,256]{1,0:T(8,128)(2,1)S(1)} collective-permute-done((bf16[48,256]{1,0:T(8,128)(2,1)S(1)}, bf16[48,256]{1,0:T(8,128)(2,1)S(1)}, u32[]{:S(2)}, u32[]{:S(2)}) %collective-permute-start.9) | collective-permute-done | bytes 24608 | tf_op jit(solution)/shard_map/ppermute | solution.py:114
  44.2 1.6 %collective-permute-start.10 = (bf16[4,48,256]{2,1,0:T(8,128)(2,1)S(1)}, bf16[4,48,256]{2,1,0:T(8,128)(2,1)S(1)}, u32[]{:S(2)}, u32[]{:S(2)}) collective-permute-start(bf16[4,48,256]{2,1,0:T(8,128)(2,1)S(1)} %pad_maximum_fusion.1), channel_id=1, source_target_pairs={{4,0},{6,2},{0,4},{2,6},{12,8},{14,10},{8,12},{10,14},{20,16},{22,... | collective-permute-start | bytes 294920 | tf_op jit(solution)/shard_map/ppermute | solution.py:116
  45.8 3.1 %collective-permute-done.10 = bf16[4,48,256]{2,1,0:T(8,128)(2,1)S(1)} collective-permute-done((bf16[4,48,256]{2,1,0:T(8,128)(2,1)S(1)}, bf16[4,48,256]{2,1,0:T(8,128)(2,1)S(1)}, u32[]{:S(2)}, u32[]{:S(2)}) %collective-permute-start.10) | collective-permute-done | bytes 98336 | tf_op jit(solution)/shard_map/ppermute | solution.py:116
  48.8 0.1 collective-permute-start.11
  48.9 1.4 %collective-permute-done.11.far = bf16[8,48,256]{2,1,0:T(8,128)(2,1)S(1)} collective-permute-done((bf16[8,48,256]{2,1,0:T(8,128)(2,1)S(1)}, bf16[8,48,256]{2,1,0:T(8,128)(2,1)S(1)}, u32[]{:S(2)}, u32[]{:S(2)}) %collective-permute-start.11) | collective-permute-done | bytes 196640 | tf_op jit(solution)/shard_map/ppermute | solution.py:118
  50.4 0.0 copy-done.1
  50.4 0.0 copy-done.5
  50.4 0.0 copy-done.7
  50.4 1.3 %shard_map.103 = (f32[48,256]{1,0:T(8,128)S(1)}, f32[48,256]{1,0:T(8,128)S(1)}) custom-call(s32[2]{0:T(128)S(1)} %pad_add_fusion.ids, s32[1]{0:T(128)S(6)} %copy.22.live, s32[1,16]{1,0:T(1,128)S(1)} %copy-done.5, s32[1,16]{1,0:T(1,128)S(1)} %copy-done.7, bf16[16,256,256]{2,1,0:T(8,128)(2,1)S(1)} %bitcast.26, ...), custom_call_target="tpu_custom_call" | custom-call | tf_op jit(solution)/shard_map/pallas_call | solution.py:169
  51.7 1.6 %collective-permute-start.12 = (f32[48,256]{1,0:T(8,128)S(1)}, f32[48,256]{1,0:T(8,128)S(1)}, u32[]{:S(2)}, u32[]{:S(2)}) collective-permute-start(f32[48,256]{1,0:T(8,128)S(1)} %get-tuple-element.16), channel_id=1, source_target_pairs={{1,0},{0,1},{3,2},{2,3},{5,4},{4,5},{7,6},{6,7},{9,8},{8,9},{11,10... | collective-permute-start | bytes 147464 | tf_op jit(solution)/shard_map/ppermute | solution.py:106
  53.2 0.1 copy.13.bias
  53.3 2.5 %collective-permute-done.12.rest_0_ = f32[48,256]{1,0:T(8,128)S(1)} collective-permute-done((f32[48,256]{1,0:T(8,128)S(1)}, f32[48,256]{1,0:T(8,128)S(1)}, u32[]{:S(2)}, u32[]{:S(2)}) %collective-permute-start.12) | collective-permute-done | bytes 49184 | tf_op jit(solution)/shard_map/ppermute | solution.py:106
  55.8 0.7 %shard_map.104 = f32[47,256]{1,0:T(8,128)} custom-call(bf16[48,256]{1,0:T(8,128)(2,1)S(1)} %get-tuple-element.13.classes_in, f32[1,256]{1,0:T(1,128)S(1)} %get-tuple-element.14.scaling, f32[47,1]{1,0:T(8,128)S(1)} %copy.13.bias, f32[48,256]{1,0:T(8,128)S(1)} %get-tuple-element.15.own, f32[48,256]{1,0:T(8,128)S(1)} %collective-permute-done.12.rest_0_), custom_call_target="tpu_custom_call" | custom-call | tf_op jit(solution)/shard_map/pallas_call | solution.py:176
  (22 shorter events, 0.1 us)
Async XLA Ops:
  0.0 5.3 %collective-permute-start = (bf16[100,256]{1,0:T(8,128)(2,1)}, bf16[100,256]{1,0:T(8,128)(2,1)S(1)}, u32[]{:S(2)}, u32[]{:S(2)}) collective-permute-start(bf16[100,256]{1,0:T(8,128)(2,1)} %bitcast.30), channel_id=1, source_target_pairs={{1,0},{0,1},{3,2},{2,3},{5,4},{4,5},{7,6},{6,7},{9,8},{8,9},{11,10... | collective-permute-start | bytes 153608 | tf_op jit(solution)/shard_map/ppermute | solution.py:106
  5.3 0.8 %copy-start.2 = (bf16[256,100]{0,1:T(8,128)(2,1)S(1)}, bf16[256,100]{0,1:T(8,128)(2,1)}, u32[]{:S(2)}) copy-start(bf16[256,100]{0,1:T(8,128)(2,1)} %param.10) | copy-start | bytes 153604
  6.1 0.7 %copy-start.3 = (s32[1,512]{1,0:T(1,128)S(1)}, s32[1,512]{1,0:T(1,128)}, u32[]{:S(2)}) copy-start(s32[1,512]{1,0:T(1,128)} %order.1) | copy-start | bytes 6148
  7.6 6.1 %collective-permute-start.1 = (bf16[128,256]{1,0:T(8,128)(2,1)S(1)}, bf16[128,256]{1,0:T(8,128)(2,1)S(1)}, u32[]{:S(2)}, u32[]{:S(2)}) collective-permute-start(bf16[128,256]{1,0:T(8,128)(2,1)S(1)} %shard_map.100.hidden_in), channel_id=1, source_target_pairs={{8,0},{10,2},{12,4},{14,6},{16,8},{18,10},{20,12},{22,14},{24,16},... | collective-permute-start | bytes 196616 | tf_op jit(solution)/shard_map/ppermute | solution.py:114
  11.8 5.2 %collective-permute-start.2 = (bf16[128,256]{1,0:T(8,128)(2,1)S(1)}, bf16[128,256]{1,0:T(8,128)(2,1)S(1)}, u32[]{:S(2)}, u32[]{:S(2)}) collective-permute-start(bf16[128,256]{1,0:T(8,128)(2,1)S(1)} %shard_map.100.hidden_in), channel_id=1, source_target_pairs={{16,0},{18,2},{20,4},{22,6},{24,8},{26,10},{28,12},{30,14},{0,16},... | collective-permute-start | bytes 196616 | tf_op jit(solution)/shard_map/ppermute | solution.py:114
  11.8 6.1 %collective-permute-start.3 = (bf16[128,256]{1,0:T(8,128)(2,1)S(1)}, bf16[128,256]{1,0:T(8,128)(2,1)S(1)}, u32[]{:S(2)}, u32[]{:S(2)}) collective-permute-start(bf16[128,256]{1,0:T(8,128)(2,1)S(1)} %shard_map.100.hidden_in), channel_id=1, source_target_pairs={{24,0},{26,2},{28,4},{30,6},{0,8},{2,10},{4,12},{6,14},{8,16},{10,... | collective-permute-start | bytes 196616 | tf_op jit(solution)/shard_map/ppermute | solution.py:114
  17.9 14.3 %copy-start.9 = (f32[128]{0:T(128)S(1)}, f32[128]{0:T(128)}, u32[]{:S(2)}) copy-start(f32[128]{0:T(128)} %param.17) | copy-start | bytes 1540
  17.9 14.4 %copy-start.8 = (bf16[128,47]{0,1:T(8,128)(2,1)S(1)}, bf16[128,47]{0,1:T(8,128)(2,1)}, u32[]{:S(2)}) copy-start(bf16[128,47]{0,1:T(8,128)(2,1)} %param.18) | copy-start | bytes 36100
  17.9 6.4 %collective-permute-start.4 = (bf16[4,128,256]{2,1,0:T(8,128)(2,1)S(1)}, bf16[4,128,256]{2,1,0:T(8,128)(2,1)S(1)}, u32[]{:S(2)}, u32[]{:S(2)}) collective-permute-start(bf16[4,128,256]{2,1,0:T(8,128)(2,1)S(1)} %pad_maximum_fusion), channel_id=1, source_target_pairs={{4,0},{6,2},{0,4},{2,6},{12,8},{14,10},{8,12},{10,14},{20,16},{22,... | collective-permute-start | bytes 786440 | tf_op jit(solution)/shard_map/ppermute | solution.py:116
  24.4 2.0 %collective-permute-start.5 = (bf16[8,128,256]{2,1,0:T(8,128)(2,1)S(1)}, bf16[8,128,256]{2,1,0:T(8,128)(2,1)S(1)}, u32[]{:S(2)}, u32[]{:S(2)}) collective-permute-start(bf16[8,128,256]{2,1,0:T(8,128)(2,1)S(1)} %constant_dynamic-update-slice_fusion.near), channel_id=1, source_target_pairs={{2,0},{0,2},{6,4},{4,6},{10,8},{8,10},{14,12},{12,14},{18,16},{16,... | collective-permute-start | bytes 1572872 | tf_op jit(solution)/shard_map/ppermute | solution.py:118
  26.3 1.6 %copy-start = (bf16[1,16,256,256]{3,2,1,0:T(8,128)(2,1)S(1)}, bf16[1,16,256,256]{3,2,1,0:T(8,128)(2,1)}, u32[]{:S(2)}) copy-start(bf16[1,16,256,256]{3,2,1,0:T(8,128)(2,1)} %param.12) | copy-start | bytes 6291460
  27.9 0.7 %copy-start.4 = (s32[1,16]{1,0:T(1,128)S(1)}, s32[1,16]{1,0:T(1,128)}, u32[]{:S(2)}) copy-start(s32[1,16]{1,0:T(1,128)} %rows.3) | copy-start | bytes 196
  28.6 0.7 %copy-start.6 = (s32[1,16]{1,0:T(1,128)S(1)}, s32[1,16]{1,0:T(1,128)}, u32[]{:S(2)}) copy-start(s32[1,16]{1,0:T(1,128)} %columns.3) | copy-start | bytes 196
  29.2 21.1 %copy-start.1 = (bf16[1,16,256,256]{3,2,1,0:T(8,128)(2,1)S(1)}, bf16[1,16,256,256]{3,2,1,0:T(8,128)(2,1)}, u32[]{:S(2)}) copy-start(bf16[1,16,256,256]{3,2,1,0:T(8,128)(2,1)} %param.12) | copy-start | bytes 6291460
  29.2 21.1 %copy-start.5 = (s32[1,16]{1,0:T(1,128)S(1)}, s32[1,16]{1,0:T(1,128)}, u32[]{:S(2)}) copy-start(s32[1,16]{1,0:T(1,128)} %rows.3) | copy-start | bytes 196
  29.2 21.1 %copy-start.7 = (s32[1,16]{1,0:T(1,128)S(1)}, s32[1,16]{1,0:T(1,128)}, u32[]{:S(2)}) copy-start(s32[1,16]{1,0:T(1,128)} %columns.3) | copy-start | bytes 196
  30.6 22.6 %copy-start.10 = (f32[47]{0:T(128)S(1)}, f32[47]{0:T(128)}, u32[]{:S(2)}) copy-start(f32[47]{0:T(128)} %param.19) | copy-start | bytes 568
  30.6 5.8 %collective-permute-start.6 = (f32[136,256]{1,0:T(8,128)S(1)}, f32[136,256]{1,0:T(8,128)S(1)}, u32[]{:S(2)}, u32[]{:S(2)}) collective-permute-start(f32[136,256]{1,0:T(8,128)S(1)} %get-tuple-element.12), channel_id=1, source_target_pairs={{1,0},{0,1},{3,2},{2,3},{5,4},{4,5},{7,6},{6,7},{9,8},{8,9},{11,10... | collective-permute-start | bytes 417800 | tf_op jit(solution)/shard_map/ppermute | solution.py:106
  36.6 3.8 %collective-permute-start.7 = (bf16[48,256]{1,0:T(8,128)(2,1)S(1)}, bf16[48,256]{1,0:T(8,128)(2,1)S(1)}, u32[]{:S(2)}, u32[]{:S(2)}) collective-permute-start(bf16[48,256]{1,0:T(8,128)(2,1)S(1)} %get-tuple-element.13.classes_in), channel_id=1, source_target_pairs={{8,0},{10,2},{12,4},{14,6},{16,8},{18,10},{20,12},{22,14},{24,16},... | collective-permute-start | bytes 73736 | tf_op jit(solution)/shard_map/ppermute | solution.py:114
  37.9 4.7 %collective-permute-start.8 = (bf16[48,256]{1,0:T(8,128)(2,1)S(1)}, bf16[48,256]{1,0:T(8,128)(2,1)S(1)}, u32[]{:S(2)}, u32[]{:S(2)}) collective-permute-start(bf16[48,256]{1,0:T(8,128)(2,1)S(1)} %get-tuple-element.13.classes_in), channel_id=1, source_target_pairs={{16,0},{18,2},{20,4},{22,6},{24,8},{26,10},{28,12},{30,14},{0,16},... | collective-permute-start | bytes 73736 | tf_op jit(solution)/shard_map/ppermute | solution.py:114
  38.5 5.6 %collective-permute-start.9 = (bf16[48,256]{1,0:T(8,128)(2,1)S(1)}, bf16[48,256]{1,0:T(8,128)(2,1)S(1)}, u32[]{:S(2)}, u32[]{:S(2)}) collective-permute-start(bf16[48,256]{1,0:T(8,128)(2,1)S(1)} %get-tuple-element.13.classes_in), channel_id=1, source_target_pairs={{24,0},{26,2},{28,4},{30,6},{0,8},{2,10},{4,12},{6,14},{8,16},{10,... | collective-permute-start | bytes 73736 | tf_op jit(solution)/shard_map/ppermute | solution.py:114
  44.2 4.7 %collective-permute-start.10 = (bf16[4,48,256]{2,1,0:T(8,128)(2,1)S(1)}, bf16[4,48,256]{2,1,0:T(8,128)(2,1)S(1)}, u32[]{:S(2)}, u32[]{:S(2)}) collective-permute-start(bf16[4,48,256]{2,1,0:T(8,128)(2,1)S(1)} %pad_maximum_fusion.1), channel_id=1, source_target_pairs={{4,0},{6,2},{0,4},{2,6},{12,8},{14,10},{8,12},{10,14},{20,16},{22,... | collective-permute-start | bytes 294920 | tf_op jit(solution)/shard_map/ppermute | solution.py:116
  48.8 1.5 %collective-permute-start.11 = (bf16[8,48,256]{2,1,0:T(8,128)(2,1)S(1)}, bf16[8,48,256]{2,1,0:T(8,128)(2,1)S(1)}, u32[]{:S(2)}, u32[]{:S(2)}) collective-permute-start(bf16[8,48,256]{2,1,0:T(8,128)(2,1)S(1)} %constant_dynamic-update-slice_fusion.5.near), channel_id=1, source_target_pairs={{2,0},{0,2},{6,4},{4,6},{10,8},{8,10},{14,12},{12,14},{18,16},{16,... | collective-permute-start | bytes 589832 | tf_op jit(solution)/shard_map/ppermute | solution.py:118
  51.7 4.2 %collective-permute-start.12 = (f32[48,256]{1,0:T(8,128)S(1)}, f32[48,256]{1,0:T(8,128)S(1)}, u32[]{:S(2)}, u32[]{:S(2)}) collective-permute-start(f32[48,256]{1,0:T(8,128)S(1)} %get-tuple-element.16), channel_id=1, source_target_pairs={{1,0},{0,1},{3,2},{2,3},{5,4},{4,5},{7,6},{6,7},{9,8},{8,9},{11,10... | collective-permute-start | bytes 147464 | tf_op jit(solution)/shard_map/ppermute | solution.py:106

commit v2 on v1

v2 whole, which is shorter than its diff:
```python
import functools

import jax
import jax.numpy as jnp
from jax import lax
from jax.experimental import pallas as pl
from jax.experimental.pallas import tpu as pltpu
from jax.sharding import PartitionSpec as P

BF16 = jnp.bfloat16
F32 = jnp.float32
ONES_ROWS = 16
VMEM_LIMIT = 32 * 1024 * 1024


def nn(a, b):
    return lax.dot_general(a, b, (((1,), (0,)), ((), ())), preferred_element_type=F32)


def nt(a, b):
    return lax.dot_general(a, b, (((1,), (1,)), ((), ())), preferred_element_type=F32)


def call(kernel, outs, n_smem, n_vmem, n_hbm=0, scratch=(), flops=0):
    return pl.pallas_call(
        kernel,
        out_shape=outs,
        in_specs=[pl.BlockSpec(memory_space=pltpu.SMEM)] * n_smem
        + [pl.BlockSpec(memory_space=pltpu.VMEM)] * n_vmem
        + [pl.BlockSpec(memory_space=pltpu.HBM)] * n_hbm,
        scratch_shapes=scratch,
        compiler_params=pltpu.CompilerParams(vmem_limit_bytes=VMEM_LIMIT),
        cost_estimate=pl.CostEstimate(flops=flops, bytes_accessed=1 << 20, transcendentals=0),
    )


def in_hbm(value):
    return pltpu.with_memory_space_constraint(value, pltpu.HBM)


def picked(weight_t, features, wanted, owner):
    tile = features.shape[1]
    hidden = nn(weight_t[...], features[...]).astype(BF16)
    source = lax.broadcasted_iota(jnp.int32, (tile, tile), 0) + owner * tile
    return nn(hidden, jnp.where(source == wanted, 1.0, 0.0).astype(BF16))


def prepare(plan, weight_t, order, features, tiles, *rest):
    part, wanted_out, weight_out, tiles_out, order_in, features_in, sems = rest
    fetches = [
        pltpu.make_async_copy(order, order_in, sems.at[0]),
        pltpu.make_async_copy(features, features_in, sems.at[1]),
        pltpu.make_async_copy(tiles, tiles_out, sems.at[2]),
    ]
    for fetch in fetches:
        fetch.start()
    weight_out[...] = weight_t[...]
    fetches[0].wait()
    fetches[1].wait()
    tile = features.shape[1]
    member = plan[1]
    wanted = order_in[:, pl.ds(pl.multiple_of(member * tile, tile), tile)]
    wanted_out[...] = wanted
    part[...] = picked(weight_t, features_in, wanted, member).astype(BF16)
    fetches[2].wait()


def order_project(plan, part, wanted, weight_t, *rest):
    *features, out = rest
    reps = len(features) + 1
    total = part[...].astype(F32)
    for step in range(1, reps):
        owner = lax.rem(plan[1] + step, reps)
        total = total + picked(weight_t, features[step - 1], wanted[...], owner)
    out[...] = total.astype(BF16)


def aggregate(reps, count_rows, plan, tiles, near, far, *outs):
    slots, tile = tiles.shape[0], tiles.shape[1]
    height = near.shape[1]
    half = near.shape[0]
    block, member, live = plan[0], plan[1], plan[2]
    extra = ONES_ROWS if count_rows else 0
    total = jnp.zeros((reps * (height + extra), tile), F32)
    for slot in range(slots):
        panel = lax.clamp(0, plan[3 + slots + slot] // reps, 2 * half - 1)
        place = panel // 2
        values = jnp.where(panel % 2 == block % 2, near[place], far[place])
        local = plan[3 + slot] - block * reps
        pieces = []
        for step in range(reps):
            wanted = lax.rem(member + step, reps)
            used = ((local == wanted) & (slot < live)).astype(F32)
            pieces.append(values * used.astype(BF16))
            if extra:
                pieces.append(jnp.full((extra, tile), used, F32).astype(BF16))
        total = total + nt(jnp.concatenate(pieces, axis=0), tiles[slot])
    for step in range(reps):
        start = step * (height + extra)
        outs[step][...] = total[start : start + outs[step].shape[0]]


def combine(reps, hidden_in, bias, weight_t, own, *rest):
    arrived, (out, scale_out) = rest[: reps - 1], rest[reps - 1 :]
    height = hidden_in.shape[0]
    total = own[...]
    for part in arrived:
        total = total + part[...]
    scaling = lax.rsqrt(1.0 + total[height : height + 1])
    hidden = scaling * (total[:height] + hidden_in[...].astype(F32)) + bias[...]
    hidden = jnp.maximum(hidden, 0.0).astype(BF16)
    classes = nn(weight_t[...], hidden).astype(BF16)
    out[: classes.shape[0]] = classes
    scale_out[...] = scaling


def finish(reps, classes_in, scaling, bias, own, *rest):
    arrived, out = rest[: reps - 1], rest[reps - 1]
    total = own[...]
    for part in arrived:
        total = total + part[...]
    classes = out.shape[0]
    whole = total + classes_in[...].astype(F32)
    out[...] = scaling[...] * whole[:classes] + bias[...]


def shifted(value, axis, step):
    size = lax.axis_size(axis)
    return lax.ppermute(value, axis, [((d + step) % size, d) for d in range(size)])


def gather_blocks(value):
    size = lax.axis_size("blk")
    groups = [list(range(core, size, 2)) for core in range(2)]
    copies = jnp.broadcast_to(value[None], (size // 2, *value.shape))
    near = lax.all_to_all(copies, "blk", 0, 0, axis_index_groups=groups)
    far = lax.ppermute(near, "blk", [(d ^ 1, d) for d in range(size)])
    return near, far


def body(
    features,
    node_order,
    tile_values,
    tile_rows,
    tile_columns,
    tile_live,
    first_weight,
    first_bias,
    second_weight,
    second_bias,
):
    tile = features.shape[0]
    reps = lax.axis_size("rep")
    hidden, classes = second_weight.shape
    padded = -(-classes // 16) * 16
    ids = [lax.axis_index("blk"), lax.axis_index("rep")]
    plan = jnp.concatenate(
        [jnp.stack(ids).astype(jnp.int32), tile_live, tile_rows[0], tile_columns[0]]
    )
    shape = jax.ShapeDtypeStruct

    own_t = features.T
    others = [shifted(own_t, "rep", step) for step in range(1, reps)]
    part, wanted, weight_t, tiles = call(
        prepare,
        [
            shape((hidden, tile), BF16),
            shape((1, tile), jnp.int32),
            shape(first_weight.shape[::-1], BF16),
            shape(tile_values.shape[1:], BF16),
        ],
        1,
        1,
        3,
        [
            pltpu.VMEM(node_order.shape, jnp.int32),
            pltpu.VMEM(own_t.shape, BF16),
            pltpu.SemaphoreType.DMA((3,)),
        ],
        1 << 28,
    )(plan, first_weight.T, *map(in_hbm, (node_order, own_t, tile_values[0])))
    hidden_in = call(order_project, shape((hidden, tile), BF16), 1, 3 + reps - 1)(
        plan, part, wanted, weight_t, *others
    )

    near, far = gather_blocks(hidden_in)
    sums = call(
        functools.partial(aggregate, reps, True),
        [shape((hidden + 8, tile), F32)] * reps,
        1,
        3,
    )(plan, tiles, near, far)
    arrived = [shifted(sums[reps - step], "rep", step) for step in range(1, reps)]
    classes_in, scaling = call(
        functools.partial(combine, reps),
        [shape((padded, tile), BF16), shape((1, tile), F32)],
        0,
        4 + reps - 1,
    )(
        hidden_in,
        first_bias[:, None],
        jnp.pad(second_weight.T, ((0, padded - classes), (0, 0))),
        sums[0],
        *arrived,
    )

    near, far = gather_blocks(classes_in)
    sums = call(
        functools.partial(aggregate, reps, False),
        [shape((padded, tile), F32)] * reps,
        1,
        3,
    )(plan, tiles, near, far)
    arrived = [shifted(sums[reps - step], "rep", step) for step in range(1, reps)]
    logits = call(
        functools.partial(finish, reps),
        shape((classes, tile), F32),
        0,
        4 + reps - 1,
    )(classes_in, scaling, second_bias[:, None], sums[0], *arrived)
    return logits.T


def solution(mesh):
    placed = (
        P(("blk", "rep"), None),
        P("blk", None),
        P(("blk", "rep"), None, None, None),
        P(("blk", "rep"), None),
        P(("blk", "rep"), None),
        P(("blk", "rep")),
        P(),
        P(),
        P(),
        P(),
    )
    return jax.shard_map(
        body, mesh=mesh, in_specs=placed, out_specs=P(("blk", "rep"), None), check_vma=False
    )
```

time: 56.8 us -> 56.6 us (level)
  blocking collectives: 0 us -> 31.1 us
  waiting for transfers between devices: 27.3 us -> 11.8 us
  starting transfers between devices: 18.4 us -> 4.14 us
  local copies, waits for them, and re-layouts: 5.55 us -> 1.9 us
  Pallas kernels: 4.41 us -> 6.62 us
    all_to_all x0 -> x2, blocking collectives: none -> 31.1 us  [gather_blocks(): near = lax.all_to_all(copies, 'blk', 0, 0, axis_index_groups=groups)]
    ppermute x8 -> x0, waiting for transfers between devices: 16.6 us -> none  [the longest x6 8.71 us: gather_blocks(): lax.ppermute(value, 'blk', [((d + 4 * step) % size, d) for d in range(siz...]
    ppermute x8 -> x0, starting transfers between devices: 12.2 us -> none  [the longest x6 9.03 us: gather_blocks(): lax.ppermute(value, 'blk', [((d + 4 * step) % size, d) for d in range(siz...]
    unnamed x31 -> x7, local copies, waits for them, and re-layouts: 5.3 us -> 0.87 us
    pallas_call x5 -> x6, Pallas kernels: 4.41 us -> 6.62 us  [the longest x1 2.21 us: body(): call(prepare, [shape((hidden, tile), BF16), shape((1, tile), jnp.int32),...]
    ppermute x3, starting transfers between devices: 6.05 us -> 4.13 us  [shifted(): lax.ppermute(value, axis, [((d + step) % size, d) for d in range(size)])]
    concatenate x2 -> x1, local copies, waits for them, and re-layouts: 0.03 us -> 0.76 us  [body(): jnp.concatenate([jnp.stack(ids).astype(jnp.int32), tile_live, tile_rows[0...]
    ppermute x2, waiting for transfers between devices: 2.68 us -> 3.35 us  [gather_blocks(): far = lax.ppermute(near, 'blk', [(d ^ 1, d) for d in range(size)])]
  transfers between devices with their start and end apart: 13 -> 5, of which waited for: 12 -> 4; matrix products, arithmetic and copies ran while one was open for 2% -> 3% of each run, Pallas kernels for 0% -> 4%
where the time goes in v2:
time: 56.6 us; the launch traced here: 56.3 us
  blocking collectives  31.1 us (55%)
  waiting for transfers between devices  11.8 us (21%)
  Pallas kernels  6.62 us (12%)
  starting transfers between devices  4.14 us (7%)
  local copies, waits for them, and re-layouts  1.9 us (3%)
  between operations  0.75 us (1%)
    all_to_all x2, blocking collectives, gather_blocks(): near = lax.all_to_all(copies, 'blk', 0, 0, axis_index_groups=groups)  31.1 us
    ppermute x3, waiting for transfers between devices, shifted(): lax.ppermute(value, axis, [((d + step) % size, d) for d in range(size)])  8.5 us
    ppermute x3, starting transfers between devices, shifted(): lax.ppermute(value, axis, [((d + step) % size, d) for d in range(size)])  4.13 us
    ppermute x2, waiting for transfers between devices, gather_blocks(): far = lax.ppermute(near, 'blk', [(d ^ 1, d) for d in range(size)])  3.35 us
    pallas_call x1, Pallas kernels, body(): call(prepare, [shape((hidden, tile), BF16), shape((1, tile), jnp.int32),...  2.21 us
    pallas_call x1, Pallas kernels, body(): call(functools.partial(aggregate, reps, True), [shape((hidden + 8, tile),...  1.36 us
    pallas_call x1, Pallas kernels, body(): call(functools.partial(aggregate, reps, False), [shape((padded, tile), F3...  1.32 us
  transfers between devices with their start and end apart: 5, of which 4 were waited for; matrix products, arithmetic and copies ran while one was open for 3% of the time, Pallas kernels for 4%

profile of v2, /device:TPU:0, one launch (start us, length us, event | category | flops | bytes accessed | tf_op | source)
XLA Modules:
  0.0 56.3 jit_solution(11313533912973084078)
XLA Ops:
  0.0 2.9 %collective-permute-start = (bf16[100,256]{1,0:T(8,128)(2,1)}, bf16[100,256]{1,0:T(8,128)(2,1)S(1)}, u32[]{:S(2)}, u32[]{:S(2)}) collective-permute-start(bf16[100,256]{1,0:T(8,128)(2,1)} %bitcast.13), channel_id=1, source_target_pairs={{1,0},{0,1},{3,2},{2,3},{5,4},{4,5},{7,6},{6,7},{9,8},{8,9},{11,10... | collective-permute-start | bytes 153608 | tf_op jit(solution)/shard_map/ppermute | solution.py:129
  3.6 0.9 %copy.11 = bf16[100,128]{0,1:T(8,128)(2,1)S(1)} copy(bf16[100,128]{1,0:T(8,128)(2,1)} %param.16) | data formatting | bytes 51200 | tf_op args[6]
  4.4 0.8 %concatenate.3.plan = s32[35]{0:T(128)S(1)} concatenate(s32[1]{0:T(128)} %bitcast, s32[1]{0:T(128)} %bitcast.1, s32[1]{0:T(128)S(6)} %copy.14, s32[16]{0:T(128)} %bitcast.18, s32[16]{0:T(128)} %bitcast.19), dimensions={0} | concatenate | bytes 280 | tf_op jit(solution)/shard_map/concatenate | solution.py:158
  5.2 2.2 %shard_map.100 = (bf16[128,256]{1,0:T(8,128)(2,1)S(1)}, s32[1,256]{1,0:T(1,128)S(1)}, bf16[128,100]{1,0:T(8,128)(2,1)S(1)}, bf16[16,256,256]{2,1,0:T(8,128)(2,1)S(1)}) custom-call(s32[35]{0:T(128)S(1)} %concatenate.3.plan, bf16[128,100]{1,0:T(8,128)(2,1)S(1)} %bitcast.11, s32[1,512]{1,0:T(1,128)} %order.1, bf16[100,256]{1,0:T(8,128)(2,1)} %bitcast.14, ...), custom_call_target="tpu_custom_call" | custom-call | flops 268435456 | bytes 1048576 | tf_op jit(solution)/shard_map/pallas_call | solution.py:165
  7.4 0.0 collective-permute-done.rest_0_
  7.4 0.8 %shard_map.101.hidden_in = bf16[128,256]{1,0:T(8,128)(2,1)S(1)} custom-call(s32[35]{0:T(128)S(1)} %concatenate.3.plan, bf16[128,256]{1,0:T(8,128)(2,1)S(1)} %get-tuple-element.15.part, s32[1,256]{1,0:T(1,128)S(1)} %get-tuple-element.16.wanted, bf16[128,100]{1,0:T(8,128)(2,1)S(1)} %get-tuple-element.17.weight_t, bf16[100,256]{1,0:T(8,128)(2,1)S(1)} %collective-permute-done.rest_0_), custom_call_target="tpu_custom_call" | custom-call | bytes 1048576 | tf_op jit(solution)/shard_map/pallas_call | solution.py:183
  8.3 0.0 copy-start.1
  8.3 0.0 copy-start
  8.3 19.8 %all_to_all.10.near = bf16[8,128,256]{2,1,0:T(8,128)(2,1)S(1)} all-to-all(bf16[8,128,256]{2,1,0:T(8,128)(2,1)S(1)} %broadcast_in_dim.9), channel_id=1, replica_groups={{0,4,8,12,16,20,24,28},{2,6,10,14,18,22,26,30},{1,5,9,13,17,21,25,29},{..., dimensions={0} | all-to-all | bytes 1048576 | tf_op jit(solution)/shard_map/all_to_all | solution.py:136
  28.2 0.0 collective-permute-start.1
  28.2 1.9 %collective-permute-done.1.far = bf16[8,128,256]{2,1,0:T(8,128)(2,1)S(1)} collective-permute-done((bf16[8,128,256]{2,1,0:T(8,128)(2,1)S(1)}, bf16[8,128,256]{2,1,0:T(8,128)(2,1)S(1)}, u32[]{:S(2)}, u32[]{:S(2)}) %collective-permute-start.1) | collective-permute-done | bytes 524320 | tf_op jit(solution)/shard_map/ppermute | solution.py:137
  30.1 1.4 %shard_map.102 = (f32[136,256]{1,0:T(8,128)S(1)}, f32[136,256]{1,0:T(8,128)S(1)}) custom-call(s32[35]{0:T(128)S(1)} %concatenate.3.plan, bf16[16,256,256]{2,1,0:T(8,128)(2,1)S(1)} %get-tuple-element.18.tiles, bf16[8,128,256]{2,1,0:T(8,128)(2,1)S(1)} %all_to_all.10.near, bf16[8,128,256]{2,1,0:T(8,128)(2,1)S(1)} %collective-permute-done.1.far), custom_call_target="tpu_custom_call" | custom-call | bytes 1048576 | tf_op jit(solution)/shard_map/pallas_call | solution.py:188
  31.4 0.0 copy-start.2
  31.5 0.6 %collective-permute-start.2 = (f32[136,256]{1,0:T(8,128)S(1)}, f32[136,256]{1,0:T(8,128)S(1)}, u32[]{:S(2)}, u32[]{:S(2)}) collective-permute-start(f32[136,256]{1,0:T(8,128)S(1)} %get-tuple-element.20), channel_id=1, source_target_pairs={{1,0},{0,1},{3,2},{2,3},{5,4},{4,5},{7,6},{6,7},{9,8},{8,9},{11,10... | collective-permute-start | bytes 417800 | tf_op jit(solution)/shard_map/ppermute | solution.py:129
  32.0 0.0 copy-done.1
  32.1 0.1 copy.12.bias
  32.2 0.0 copy-done
  32.2 5.0 %collective-permute-done.2.rest_0_ = f32[136,256]{1,0:T(8,128)S(1)} collective-permute-done((f32[136,256]{1,0:T(8,128)S(1)}, f32[136,256]{1,0:T(8,128)S(1)}, u32[]{:S(2)}, u32[]{:S(2)}) %collective-permute-start.2) | collective-permute-done | bytes 139296 | tf_op jit(solution)/shard_map/ppermute | solution.py:129
  37.2 0.2 shard_map.103
  37.5 11.2 %all_to_all.11.near = bf16[8,48,256]{2,1,0:T(8,128)(2,1)S(1)} all-to-all(bf16[8,48,256]{2,1,0:T(8,128)(2,1)S(1)} %broadcast_in_dim.21), channel_id=1, replica_groups={{0,4,8,12,16,20,24,28},{2,6,10,14,18,22,26,30},{1,5,9,13,17,21,25,29},{..., dimensions={0} | all-to-all | bytes 393216 | tf_op jit(solution)/shard_map/all_to_all | solution.py:136
  48.7 0.0 collective-permute-start.3
  48.7 1.4 %collective-permute-done.3.far = bf16[8,48,256]{2,1,0:T(8,128)(2,1)S(1)} collective-permute-done((bf16[8,48,256]{2,1,0:T(8,128)(2,1)S(1)}, bf16[8,48,256]{2,1,0:T(8,128)(2,1)S(1)}, u32[]{:S(2)}, u32[]{:S(2)}) %collective-permute-start.3) | collective-permute-done | bytes 196640 | tf_op jit(solution)/shard_map/ppermute | solution.py:137
  50.1 1.3 %shard_map.104 = (f32[48,256]{1,0:T(8,128)S(1)}, f32[48,256]{1,0:T(8,128)S(1)}) custom-call(s32[35]{0:T(128)S(1)} %concatenate.3.plan, bf16[16,256,256]{2,1,0:T(8,128)(2,1)S(1)} %get-tuple-element.18.tiles, bf16[8,48,256]{2,1,0:T(8,128)(2,1)S(1)} %all_to_all.11.near, bf16[8,48,256]{2,1,0:T(8,128)(2,1)S(1)} %collective-permute-done.3.far), custom_call_target="tpu_custom_call" | custom-call | bytes 1048576 | tf_op jit(solution)/shard_map/pallas_call | solution.py:209
  51.5 0.6 %collective-permute-start.4 = (f32[48,256]{1,0:T(8,128)S(1)}, f32[48,256]{1,0:T(8,128)S(1)}, u32[]{:S(2)}, u32[]{:S(2)}) collective-permute-start(f32[48,256]{1,0:T(8,128)S(1)} %get-tuple-element.24), channel_id=1, source_target_pairs={{1,0},{0,1},{3,2},{2,3},{5,4},{4,5},{7,6},{6,7},{9,8},{8,9},{11,10... | collective-permute-start | bytes 147464 | tf_op jit(solution)/shard_map/ppermute | solution.py:129
  52.1 0.0 copy-done.2
  52.1 0.1 copy.13.bias
  52.2 3.5 %collective-permute-done.4.rest_0_ = f32[48,256]{1,0:T(8,128)S(1)} collective-permute-done((f32[48,256]{1,0:T(8,128)S(1)}, f32[48,256]{1,0:T(8,128)S(1)}, u32[]{:S(2)}, u32[]{:S(2)}) %collective-permute-start.4) | collective-permute-done | bytes 49184 | tf_op jit(solution)/shard_map/ppermute | solution.py:129
  55.6 0.7 %shard_map.105 = f32[47,256]{1,0:T(8,128)} custom-call(bf16[48,256]{1,0:T(8,128)(2,1)S(1)} %get-tuple-element.21.classes_in, f32[1,256]{1,0:T(1,128)S(1)} %get-tuple-element.22.scaling, f32[47,1]{1,0:T(8,128)S(1)} %copy.13.bias, f32[48,256]{1,0:T(8,128)S(1)} %get-tuple-element.23.own, f32[48,256]{1,0:T(8,128)S(1)} %collective-permute-done.4.rest_0_), custom_call_target="tpu_custom_call" | custom-call | bytes 1048576 | tf_op jit(solution)/shard_map/pallas_call | solution.py:216
  (3 shorter events, 0.1 us)
Async XLA Ops:
  0.0 7.4 %collective-permute-start = (bf16[100,256]{1,0:T(8,128)(2,1)}, bf16[100,256]{1,0:T(8,128)(2,1)S(1)}, u32[]{:S(2)}, u32[]{:S(2)}) collective-permute-start(bf16[100,256]{1,0:T(8,128)(2,1)} %bitcast.13), channel_id=1, source_target_pairs={{1,0},{0,1},{3,2},{2,3},{5,4},{4,5},{7,6},{6,7},{9,8},{8,9},{11,10... | collective-permute-start | bytes 153608 | tf_op jit(solution)/shard_map/ppermute | solution.py:129
  8.3 23.8 %copy-start.1 = (f32[128]{0:T(128)S(1)}, f32[128]{0:T(128)}, u32[]{:S(2)}) copy-start(f32[128]{0:T(128)} %param.17) | copy-start | bytes 1540
  8.3 23.9 %copy-start = (bf16[128,47]{0,1:T(8,128)(2,1)S(1)}, bf16[128,47]{0,1:T(8,128)(2,1)}, u32[]{:S(2)}) copy-start(bf16[128,47]{0,1:T(8,128)(2,1)} %param.18) | copy-start | bytes 36100
  28.2 1.9 %collective-permute-start.1 = (bf16[8,128,256]{2,1,0:T(8,128)(2,1)S(1)}, bf16[8,128,256]{2,1,0:T(8,128)(2,1)S(1)}, u32[]{:S(2)}, u32[]{:S(2)}) collective-permute-start(bf16[8,128,256]{2,1,0:T(8,128)(2,1)S(1)} %all_to_all.10.near), channel_id=1, source_target_pairs={{2,0},{0,2},{6,4},{4,6},{10,8},{8,10},{14,12},{12,14},{18,16},{16,... | collective-permute-start | bytes 1572872 | tf_op jit(solution)/shard_map/ppermute | solution.py:137
  31.4 20.6 %copy-start.2 = (f32[47]{0:T(128)S(1)}, f32[47]{0:T(128)}, u32[]{:S(2)}) copy-start(f32[47]{0:T(128)} %param.19) | copy-start | bytes 568
  31.5 5.8 %collective-permute-start.2 = (f32[136,256]{1,0:T(8,128)S(1)}, f32[136,256]{1,0:T(8,128)S(1)}, u32[]{:S(2)}, u32[]{:S(2)}) collective-permute-start(f32[136,256]{1,0:T(8,128)S(1)} %get-tuple-element.20), channel_id=1, source_target_pairs={{1,0},{0,1},{3,2},{2,3},{5,4},{4,5},{7,6},{6,7},{9,8},{8,9},{11,10... | collective-permute-start | bytes 417800 | tf_op jit(solution)/shard_map/ppermute | solution.py:129
  48.7 1.4 %collective-permute-start.3 = (bf16[8,48,256]{2,1,0:T(8,128)(2,1)S(1)}, bf16[8,48,256]{2,1,0:T(8,128)(2,1)S(1)}, u32[]{:S(2)}, u32[]{:S(2)}) collective-permute-start(bf16[8,48,256]{2,1,0:T(8,128)(2,1)S(1)} %all_to_all.11.near), channel_id=1, source_target_pairs={{2,0},{0,2},{6,4},{4,6},{10,8},{8,10},{14,12},{12,14},{18,16},{16,... | collective-permute-start | bytes 589832 | tf_op jit(solution)/shard_map/ppermute | solution.py:137
  51.5 4.2 %collective-permute-start.4 = (f32[48,256]{1,0:T(8,128)S(1)}, f32[48,256]{1,0:T(8,128)S(1)}, u32[]{:S(2)}, u32[]{:S(2)}) collective-permute-start(f32[48,256]{1,0:T(8,128)S(1)} %get-tuple-element.24), channel_id=1, source_target_pairs={{1,0},{0,1},{3,2},{2,3},{5,4},{4,5},{7,6},{6,7},{9,8},{8,9},{11,10... | collective-permute-start | bytes 147464 | tf_op jit(solution)/shard_map/ppermute | solution.py:129

commit v3 on v2

v3 whole, which is shorter than its diff:
```python
import functools

import jax
import jax.numpy as jnp
from jax import lax
from jax.experimental import pallas as pl
from jax.experimental.pallas import tpu as pltpu
from jax.sharding import PartitionSpec as P

BF16 = jnp.bfloat16
F32 = jnp.float32
ONES_ROWS = 16
VMEM_LIMIT = 32 * 1024 * 1024


def nn(a, b):
    return lax.dot_general(a, b, (((1,), (0,)), ((), ())), preferred_element_type=F32)


def nt(a, b):
    return lax.dot_general(a, b, (((1,), (1,)), ((), ())), preferred_element_type=F32)


def tn(a, b):
    return lax.dot_general(a, b, (((0,), (0,)), ((), ())), preferred_element_type=F32)


def call(kernel, outs, n_smem, n_vmem, n_hbm=0, scratch=(), cost=1 << 20):
    return pl.pallas_call(
        kernel,
        out_shape=outs,
        in_specs=[pl.BlockSpec(memory_space=pltpu.SMEM)] * n_smem
        + [pl.BlockSpec(memory_space=pltpu.VMEM)] * n_vmem
        + [pl.BlockSpec(memory_space=pltpu.HBM)] * n_hbm,
        scratch_shapes=scratch,
        compiler_params=pltpu.CompilerParams(vmem_limit_bytes=VMEM_LIMIT),
        cost_estimate=pl.CostEstimate(flops=cost, bytes_accessed=cost, transcendentals=0),
    )


def in_hbm(value):
    return pltpu.with_memory_space_constraint(value, pltpu.HBM)


def picked(weight_t, features, wanted, owner):
    tile = features.shape[1]
    hidden = nn(weight_t, features[...]).astype(BF16)
    source = lax.broadcasted_iota(jnp.int32, (tile, tile), 0) + owner * tile
    return nn(hidden, jnp.where(source == wanted, 1.0, 0.0).astype(BF16))


def prepare(order, features, weight, part, wanted_out, weight_out, *rest):
    order_in, features_in, weight_in, sems = rest
    fetches = [
        pltpu.make_async_copy(order, order_in, sems.at[0]),
        pltpu.make_async_copy(weight, weight_in, sems.at[1]),
        pltpu.make_async_copy(features, features_in, sems.at[2]),
    ]
    for fetch in fetches:
        fetch.start()
    for fetch in fetches:
        fetch.wait()
    tile = features.shape[1]
    member = lax.axis_index("rep")
    wanted = order_in[:, pl.ds(pl.multiple_of(member * tile, tile), tile)]
    wanted_out[...] = wanted
    weight_t = weight_in[...].astype(F32).T.astype(BF16)
    weight_out[...] = weight_t
    part[...] = picked(weight_t, features_in, wanted, member).astype(BF16)


def fetch_tiles(tiles, out, sem):
    fetch = pltpu.make_async_copy(tiles, out, sem)
    fetch.start()
    fetch.wait()


def order_project(part, wanted, weight_t, *rest):
    *features, out = rest
    reps = len(features) + 1
    member = lax.axis_index("rep")
    total = part[...].astype(F32)
    for step in range(1, reps):
        owner = lax.rem(member + step, reps)
        total = total + picked(weight_t[...], features[step - 1], wanted[...], owner)
    out[...] = total.astype(BF16)


def aggregate(reps, first, count_rows, plan, tiles, near, far, *outs):
    slots, tile = tiles.shape[0], tiles.shape[1]
    height = near.shape[1]
    half = near.shape[0]
    block, member, live = plan[0], plan[1], plan[2]
    extra = ONES_ROWS if count_rows else 0
    total = jnp.zeros((len(outs) * (height + extra), tile), F32)
    for slot in range(slots):
        panel = lax.clamp(0, plan[3 + slots + slot] // reps, 2 * half - 1)
        place = (panel // 2) ^ (block // 2)
        values = jnp.where(panel % 2 == block % 2, near[place], far[place])
        local = plan[3 + slot] - block * reps
        pieces = []
        for step in range(len(outs)):
            wanted = lax.rem(member + first + step, reps)
            used = ((local == wanted) & (slot < live)).astype(F32)
            pieces.append(values * used.astype(BF16))
            if extra:
                pieces.append(jnp.full((extra, tile), used, F32).astype(BF16))
        total = total + nt(jnp.concatenate(pieces, axis=0), tiles[slot])
    for step, out in enumerate(outs):
        start = step * (height + extra)
        out[...] = total[start : start + out.shape[0]]


def combine(reps, hidden_in, bias, weight_t, own, *rest):
    arrived, (out, scale_out) = rest[: reps - 1], rest[reps - 1 :]
    height = hidden_in.shape[0]
    total = own[...]
    for part in arrived:
        total = total + part[...]
    scaling = lax.rsqrt(1.0 + total[height : height + 1])
    hidden = scaling * (total[:height] + hidden_in[...].astype(F32)) + bias[...]
    hidden = jnp.maximum(hidden, 0.0).astype(BF16)
    out[...] = nn(weight_t[...], hidden).astype(BF16)
    scale_out[...] = scaling


def finish(reps, classes_in, scaling, bias, own, *rest):
    arrived, out = rest[: reps - 1], rest[reps - 1]
    total = own[...]
    for part in arrived:
        total = total + part[...]
    classes = out.shape[0]
    whole = total + classes_in[...].astype(F32)
    out[...] = scaling[...] * whole[:classes] + bias[...]


def shifted(value, axis, step):
    size = lax.axis_size(axis)
    return lax.ppermute(value, axis, [((d + step) % size, d) for d in range(size)])


def swapped(value, mask):
    return lax.ppermute(value, "blk", [(d ^ mask, d) for d in range(lax.axis_size("blk"))])


def gather_blocks(value):
    chips = lax.axis_size("blk") // 2
    parts = {0: value}
    for step in range(2, chips, 2):
        parts[step] = swapped(value, 2 * step)
    for step in range(0, chips, 2):
        parts[step + 1] = swapped(parts[step], 2)
    near = jnp.stack([parts[step] for step in range(chips)])
    return near, swapped(near, 1)


def body(
    features,
    node_order,
    tile_values,
    tile_rows,
    tile_columns,
    tile_live,
    first_weight,
    first_bias,
    second_weight,
    second_bias,
):
    tile = features.shape[0]
    reps = lax.axis_size("rep")
    hidden, classes = second_weight.shape
    padded = -(-classes // 16) * 16
    shape = jax.ShapeDtypeStruct
    ids = [lax.axis_index("blk"), lax.axis_index("rep")]
    plan = jnp.concatenate(
        [jnp.stack(ids).astype(jnp.int32), tile_live, tile_rows[0], tile_columns[0]]
    )

    def aggregated(near, far, tiles, rows, count_rows):
        others = call(
            functools.partial(aggregate, reps, 1, count_rows),
            [shape((rows, tile), F32)] * (reps - 1),
            1,
            3,
        )(plan, tiles, near, far)
        arrived = [shifted(others[reps - 1 - step], "rep", step) for step in range(1, reps)]
        own = call(
            functools.partial(aggregate, reps, 0, count_rows), [shape((rows, tile), F32)], 1, 3
        )(plan, tiles, near, far)
        return [*own, *arrived]

    own_t = features.T
    others = [shifted(own_t, "rep", step) for step in range(1, reps)]
    part, wanted, weight_t = call(
        prepare,
        [
            shape((hidden, tile), BF16),
            shape((1, tile), jnp.int32),
            shape(first_weight.shape[::-1], BF16),
        ],
        0,
        0,
        3,
        [
            pltpu.VMEM(node_order.shape, jnp.int32),
            pltpu.VMEM(own_t.shape, BF16),
            pltpu.VMEM(first_weight.shape, BF16),
            pltpu.SemaphoreType.DMA((3,)),
        ],
    )(*map(in_hbm, (node_order, own_t, first_weight)))
    hidden_in = call(order_project, shape((hidden, tile), BF16), 0, 3 + reps - 1)(
        part, wanted, weight_t, *others
    )

    tiles = call(
        fetch_tiles,
        shape(tile_values.shape[1:], BF16),
        0,
        0,
        1,
        [pltpu.SemaphoreType.DMA],
    )(in_hbm(tile_values[0]))
    sums = aggregated(*gather_blocks(hidden_in), tiles, hidden + 8, True)
    classes_in, scaling = call(
        functools.partial(combine, reps),
        [shape((padded, tile), BF16), shape((1, tile), F32)],
        0,
        3 + reps,
    )(
        hidden_in,
        first_bias[:, None],
        jnp.pad(second_weight.T, ((0, padded - classes), (0, 0))),
        *sums,
    )

    sums = aggregated(*gather_blocks(classes_in), tiles, padded, False)
    logits = call(functools.partial(finish, reps), shape((classes, tile), F32), 0, 3 + reps)(
        classes_in, scaling, second_bias[:, None], *sums
    )
    return logits.T


def solution(mesh):
    placed = (
        P(("blk", "rep"), None),
        P("blk", None),
        P(("blk", "rep"), None, None, None),
        P(("blk", "rep"), None),
        P(("blk", "rep"), None),
        P(("blk", "rep")),
        P(),
        P(),
        P(),
        P(),
    )
    return jax.shard_map(
        body, mesh=mesh, in_specs=placed, out_specs=P(("blk", "rep"), None), check_vma=False
    )
```

time: 56.6 us -> 52.2 us (0.922)
  blocking collectives: 31.1 us -> 0 us
  starting transfers between devices: 4.14 us -> 22.5 us
  waiting for transfers between devices: 11.8 us -> 16.2 us
  Pallas kernels: 6.62 us -> 9.28 us
  local copies, waits for them, and re-layouts: 1.9 us -> 3.06 us
    all_to_all x2 -> x0, blocking collectives: 31.1 us -> none  [gather_blocks(): near = lax.all_to_all(copies, 'blk', 0, 0, axis_index_groups=groups)]
    ppermute x2 -> x16, starting transfers between devices: 0.01 us -> 16.5 us  [swapped(): lax.ppermute(value, 'blk', [(d ^ mask, d) for d in range(lax.axis_size('b...]
    ppermute x2 -> x16, waiting for transfers between devices: 3.35 us -> 12.8 us  [swapped(): lax.ppermute(value, 'blk', [(d ^ mask, d) for d in range(lax.axis_size('b...]
    ppermute x3, waiting for transfers between devices: 8.5 us -> 3.38 us  [shifted(): lax.ppermute(value, axis, [((d + step) % size, d) for d in range(size)])]
    pallas_call x4 -> x7, Pallas kernels: 4.19 us -> 7.85 us  [the longest x2 2.64 us: aggregated(): call(functools.partial(aggregate, reps, 1, count_rows), [shape((rows, til...]
    ppermute x3, starting transfers between devices: 4.13 us -> 6.05 us  [shifted(): lax.ppermute(value, axis, [((d + step) % size, d) for d in range(size)])]
    pallas_call x1, Pallas kernels: 2.21 us -> 1.21 us  [body(): call(prepare, [shape((hidden, tile), BF16), shape((1, tile), jnp.int32),...]
    pad x1, local copies, waits for them, and re-layouts: 0.01 us -> 0.71 us  [body(): jnp.pad(second_weight.T, ((0, padded - classes), (0, 0)))]
  transfers between devices with their start and end apart: 5 -> 19, of which waited for: 4 -> 12; matrix products, arithmetic and copies ran while one was open for 3% -> 5% of each run, Pallas kernels for 4% -> 10%
where the time goes in v3:
time: 52.2 us; the launch traced here: 51.9 us
  starting transfers between devices  22.5 us (43%)
  waiting for transfers between devices  16.2 us (31%)
  Pallas kernels  9.28 us (18%)
  local copies, waits for them, and re-layouts  3.06 us (6%)
  between operations  0.8 us (2%)
    ppermute x16, starting transfers between devices, swapped(): lax.ppermute(value, 'blk', [(d ^ mask, d) for d in range(lax.axis_size('b...  16.5 us
    ppermute x16, waiting for transfers between devices, swapped(): lax.ppermute(value, 'blk', [(d ^ mask, d) for d in range(lax.axis_size('b...  12.8 us
    ppermute x3, starting transfers between devices, shifted(): lax.ppermute(value, axis, [((d + step) % size, d) for d in range(size)])  6.05 us
    ppermute x3, waiting for transfers between devices, shifted(): lax.ppermute(value, axis, [((d + step) % size, d) for d in range(size)])  3.38 us
    pallas_call x2, Pallas kernels, aggregated(): call(functools.partial(aggregate, reps, 1, count_rows), [shape((rows, til...  2.64 us
    pallas_call x2, Pallas kernels, aggregated(): call(functools.partial(aggregate, reps, 0, count_rows), [shape((rows, til...  2.63 us
    pallas_call x1, Pallas kernels, body(): call(fetch_tiles, shape(tile_values.shape[1:], BF16), 0, 0, 1, [pltpu.Sem...  1.6 us
    pallas_call x1, Pallas kernels, body(): call(prepare, [shape((hidden, tile), BF16), shape((1, tile), jnp.int32),...  1.21 us
  transfers between devices with their start and end apart: 19, of which 12 were waited for; matrix products, arithmetic and copies ran while one was open for 5% of the time, Pallas kernels for 10%

profile of v3, /device:TPU:0, one launch (start us, length us, event | category | flops | bytes accessed | tf_op | source)
XLA Modules:
  0.0 51.9 jit_solution(1511345672494471681)
XLA Ops:
  0.0 2.9 %collective-permute-start = (bf16[100,256]{1,0:T(8,128)(2,1)}, bf16[100,256]{1,0:T(8,128)(2,1)S(1)}, u32[]{:S(2)}, u32[]{:S(2)}) collective-permute-start(bf16[100,256]{1,0:T(8,128)(2,1)} %bitcast.43), channel_id=1, source_target_pairs={{1,0},{0,1},{3,2},{2,3},{5,4},{4,5},{7,6},{6,7},{9,8},{8,9},{11,10... | collective-permute-start | bytes 153608 | tf_op jit(solution)/shard_map/ppermute | solution.py:139
  2.9 1.2 %shard_map.100 = (bf16[128,256]{1,0:T(8,128)(2,1)S(1)}, s32[1,256]{1,0:T(1,128)S(1)}, bf16[128,100]{1,0:T(8,128)(2,1)S(1)}) custom-call(s32[1,512]{1,0:T(1,128)} %order.1, bf16[100,256]{1,0:T(8,128)(2,1)} %bitcast.44, bf16[100,128]{1,0:T(8,128)(2,1)} %weight.1), custom_call_target="tpu_custom_call" | custom-call | flops 1048576 | bytes 1048576 | tf_op jit(solution)/shard_map/pallas_call | solution.py:194
  4.2 1.1 %collective-permute-done.rest_0_ = bf16[100,256]{1,0:T(8,128)(2,1)S(1)} collective-permute-done((bf16[100,256]{1,0:T(8,128)(2,1)}, bf16[100,256]{1,0:T(8,128)(2,1)S(1)}, u32[]{:S(2)}, u32[]{:S(2)}) %collective-permute-start) | collective-permute-done | bytes 51232 | tf_op jit(solution)/shard_map/ppermute | solution.py:139
  5.3 0.3 shard_map.101.hidden_in
  5.5 2.1 %collective-permute-start.1 = (bf16[128,256]{1,0:T(8,128)(2,1)S(1)}, bf16[128,256]{1,0:T(8,128)(2,1)S(1)}, u32[]{:S(2)}, u32[]{:S(2)}) collective-permute-start(bf16[128,256]{1,0:T(8,128)(2,1)S(1)} %shard_map.101.hidden_in), channel_id=1, source_target_pairs={{4,0},{6,2},{0,4},{2,6},{12,8},{14,10},{8,12},{10,14},{20,16},{22,... | collective-permute-start | bytes 196616 | tf_op jit(solution)/shard_map/ppermute | solution.py:143
  7.7 1.6 %collective-permute-start.2 = (bf16[128,256]{1,0:T(8,128)(2,1)S(1)}, bf16[128,256]{1,0:T(8,128)(2,1)S(1)}, u32[]{:S(2)}, u32[]{:S(2)}) collective-permute-start(bf16[128,256]{1,0:T(8,128)(2,1)S(1)} %shard_map.101.hidden_in), channel_id=1, source_target_pairs={{8,0},{10,2},{12,4},{14,6},{0,8},{2,10},{4,12},{6,14},{24,16},{26,... | collective-permute-start | bytes 196616 | tf_op jit(solution)/shard_map/ppermute | solution.py:143
  9.2 2.6 %collective-permute-start.4 = (bf16[128,256]{1,0:T(8,128)(2,1)S(1)}, bf16[128,256]{1,0:T(8,128)(2,1)S(1)}, u32[]{:S(2)}, u32[]{:S(2)}) collective-permute-start(bf16[128,256]{1,0:T(8,128)(2,1)S(1)} %shard_map.101.hidden_in), channel_id=1, source_target_pairs={{16,0},{18,2},{20,4},{22,6},{24,8},{26,10},{28,12},{30,14},{0,16},... | collective-permute-start | bytes 196616 | tf_op jit(solution)/shard_map/ppermute | solution.py:143
  11.8 0.2 collective-permute-start.6
  12.1 0.1 collective-permute-done.2
  12.2 0.4 collective-permute-start.3
  12.7 3.2 %collective-permute-done.4 = bf16[128,256]{1,0:T(8,128)(2,1)S(1)} collective-permute-done((bf16[128,256]{1,0:T(8,128)(2,1)S(1)}, bf16[128,256]{1,0:T(8,128)(2,1)S(1)}, u32[]{:S(2)}, u32[]{:S(2)}) %collective-permute-start.4) | collective-permute-done | bytes 65568 | tf_op jit(solution)/shard_map/ppermute | solution.py:143
  15.8 0.5 collective-permute-start.5
  16.3 1.6 %collective-permute-done.6 = bf16[128,256]{1,0:T(8,128)(2,1)S(1)} collective-permute-done((bf16[128,256]{1,0:T(8,128)(2,1)S(1)}, bf16[128,256]{1,0:T(8,128)(2,1)S(1)}, u32[]{:S(2)}, u32[]{:S(2)}) %collective-permute-start.6) | collective-permute-done | bytes 65568 | tf_op jit(solution)/shard_map/ppermute | solution.py:143
  17.9 0.5 collective-permute-start.7
  18.4 1.6 %collective-permute-done.5 = bf16[128,256]{1,0:T(8,128)(2,1)S(1)} collective-permute-done((bf16[128,256]{1,0:T(8,128)(2,1)S(1)}, bf16[128,256]{1,0:T(8,128)(2,1)S(1)}, u32[]{:S(2)}, u32[]{:S(2)}) %collective-permute-start.5) | collective-permute-done | bytes 65568 | tf_op jit(solution)/shard_map/ppermute | solution.py:143
  20.1 2.1 %collective-permute-done.7 = bf16[128,256]{1,0:T(8,128)(2,1)S(1)} collective-permute-done((bf16[128,256]{1,0:T(8,128)(2,1)S(1)}, bf16[128,256]{1,0:T(8,128)(2,1)S(1)}, u32[]{:S(2)}, u32[]{:S(2)}) %collective-permute-start.7) | collective-permute-done | bytes 65568 | tf_op jit(solution)/shard_map/ppermute | solution.py:143
  22.8 0.7 %concatenate.3.plan = s32[35]{0:T(128)S(1)} concatenate(s32[1]{0:T(128)} %bitcast.3, s32[1]{0:T(128)} %bitcast.4, s32[1]{0:T(128)S(6)} %copy.27, s32[16]{0:T(128)} %bitcast.48, s32[16]{0:T(128)} %bitcast.49), dimensions={0} | concatenate | bytes 280 | tf_op jit(solution)/shard_map/concatenate | solution.py:175
  23.6 1.6 %shard_map.102.tiles = bf16[16,256,256]{2,1,0:T(8,128)(2,1)S(1)} custom-call(bf16[16,256,256]{2,1,0:T(8,128)(2,1)} %bitcast.42), custom_call_target="tpu_custom_call" | custom-call | flops 1048576 | bytes 1048576 | tf_op jit(solution)/shard_map/pallas_call | solution.py:215
  25.2 0.0 collective-permute-done.8.far
  25.2 1.4 %shard_map.104 = f32[136,256]{1,0:T(8,128)S(1)} custom-call(s32[35]{0:T(128)S(1)} %concatenate.3.plan, bf16[16,256,256]{2,1,0:T(8,128)(2,1)S(1)} %shard_map.102.tiles, bf16[8,128,256]{2,1,0:T(8,128)(2,1)S(1)} %bitcast_dynamic-update-slice_fusion.near, bf16[8,128,256]{2,1,0:T(8,128)(2,1)S(1)} %collective-permute-done.8.far), custom_call_target="tpu_custom_call" | custom-call | flops 1048576 | bytes 1048576 | tf_op jit(solution)/shard_map/pallas_call | solution.py:180
  26.6 1.6 %collective-permute-start.9 = (f32[136,256]{1,0:T(8,128)S(1)}, f32[136,256]{1,0:T(8,128)S(1)}, u32[]{:S(2)}, u32[]{:S(2)}) collective-permute-start(f32[136,256]{1,0:T(8,128)S(1)} %shard_map.104), channel_id=1, source_target_pairs={{1,0},{0,1},{3,2},{2,3},{5,4},{4,5},{7,6},{6,7},{9,8},{8,9},{11,10... | collective-permute-start | bytes 417800 | tf_op jit(solution)/shard_map/ppermute | solution.py:139
  28.1 0.8 %copy.11.bias = f32[128,1]{1,0:T(8,128)S(1)} copy(f32[128,1]{0,1:T(1,128)} %bitcast.46) | data formatting | bytes 1024 | tf_op jit(solution)/shard_map/broadcast_in_dim | solution.py:231
  28.9 0.7 %pad.4.weight_t = bf16[48,128]{1,0:T(8,128)(2,1)S(1)} pad(bf16[47,128]{1,0:T(8,128)(2,1)} %bitcast.45, bf16[]{:T(256)} %constant.8.clone.1), padding=0_1x0_0 | pad | bytes 24322 | tf_op jit(solution)/shard_map/jit(_pad)/pad | solution.py:232
  29.6 0.7 %copy-done.1 = s32[35]{0:T(128)S(1)} copy-done((s32[35]{0:T(128)S(1)}, s32[35]{0:T(128)}, u32[]{:S(2)}) %copy-start.1) | copy-done | bytes 164
  30.3 1.4 %shard_map.103.own = f32[136,256]{1,0:T(8,128)S(1)} custom-call(s32[35]{0:T(128)S(1)} %copy-done.1, bf16[16,256,256]{2,1,0:T(8,128)(2,1)S(1)} %shard_map.102.tiles, bf16[8,128,256]{2,1,0:T(8,128)(2,1)S(1)} %bitcast_dynamic-update-slice_fusion.near, bf16[8,128,256]{2,1,0:T(8,128)(2,1)S(1)} %collective-permute-done.8.far), custom_call_target="tpu_custom_call" | custom-call | flops 1048576 | bytes 1048576 | tf_op jit(solution)/shard_map/pallas_call | solution.py:187
  31.6 0.0 copy-start.3
  31.7 0.0 copy-start.2
  31.7 1.1 %collective-permute-done.9.rest_0_ = f32[136,256]{1,0:T(8,128)S(1)} collective-permute-done((f32[136,256]{1,0:T(8,128)S(1)}, f32[136,256]{1,0:T(8,128)S(1)}, u32[]{:S(2)}, u32[]{:S(2)}) %collective-permute-start.9) | collective-permute-done | bytes 139296 | tf_op jit(solution)/shard_map/ppermute | solution.py:139
  32.7 0.2 shard_map.105
  33.0 0.5 collective-permute-start.10
  33.5 1.4 %collective-permute-start.13 = (bf16[48,256]{1,0:T(8,128)(2,1)S(1)}, bf16[48,256]{1,0:T(8,128)(2,1)S(1)}, u32[]{:S(2)}, u32[]{:S(2)}) collective-permute-start(bf16[48,256]{1,0:T(8,128)(2,1)S(1)} %get-tuple-element.13.classes_in), channel_id=1, source_target_pairs={{16,0},{18,2},{20,4},{22,6},{24,8},{26,10},{28,12},{30,14},{0,16},... | collective-permute-start | bytes 73736 | tf_op jit(solution)/shard_map/ppermute | solution.py:143
  34.8 3.0 %collective-permute-start.15 = (bf16[48,256]{1,0:T(8,128)(2,1)S(1)}, bf16[48,256]{1,0:T(8,128)(2,1)S(1)}, u32[]{:S(2)}, u32[]{:S(2)}) collective-permute-start(bf16[48,256]{1,0:T(8,128)(2,1)S(1)} %get-tuple-element.13.classes_in), channel_id=1, source_target_pairs={{24,0},{26,2},{28,4},{30,6},{16,8},{18,10},{20,12},{22,14},{8,16},... | collective-permute-start | bytes 73736 | tf_op jit(solution)/shard_map/ppermute | solution.py:143
  37.8 0.0 collective-permute-done.11
  37.9 1.5 %collective-permute-start.12 = (bf16[48,256]{1,0:T(8,128)(2,1)S(1)}, bf16[48,256]{1,0:T(8,128)(2,1)S(1)}, u32[]{:S(2)}, u32[]{:S(2)}) collective-permute-start(bf16[48,256]{1,0:T(8,128)(2,1)S(1)} %collective-permute-done.11), channel_id=1, source_target_pairs={{4,0},{6,2},{0,4},{2,6},{12,8},{14,10},{8,12},{10,14},{20,16},{22,... | collective-permute-start | bytes 73736 | tf_op jit(solution)/shard_map/ppermute | solution.py:143
  39.4 0.0 collective-permute-done.13
  39.4 0.6 %collective-permute-start.14 = (bf16[48,256]{1,0:T(8,128)(2,1)S(1)}, bf16[48,256]{1,0:T(8,128)(2,1)S(1)}, u32[]{:S(2)}, u32[]{:S(2)}) collective-permute-start(bf16[48,256]{1,0:T(8,128)(2,1)S(1)} %collective-permute-done.13), channel_id=1, source_target_pairs={{4,0},{6,2},{0,4},{2,6},{12,8},{14,10},{8,12},{10,14},{20,16},{22,... | collective-permute-start | bytes 73736 | tf_op jit(solution)/shard_map/ppermute | solution.py:143
  40.0 0.5 collective-permute-done.15
  40.5 1.5 %collective-permute-start.16 = (bf16[48,256]{1,0:T(8,128)(2,1)S(1)}, bf16[48,256]{1,0:T(8,128)(2,1)S(1)}, u32[]{:S(2)}, u32[]{:S(2)}) collective-permute-start(bf16[48,256]{1,0:T(8,128)(2,1)S(1)} %collective-permute-done.15), channel_id=1, source_target_pairs={{4,0},{6,2},{0,4},{2,6},{12,8},{14,10},{8,12},{10,14},{20,16},{22,... | collective-permute-start | bytes 73736 | tf_op jit(solution)/shard_map/ppermute | solution.py:143
  42.0 1.3 %collective-permute-done.14 = bf16[48,256]{1,0:T(8,128)(2,1)S(1)} collective-permute-done((bf16[48,256]{1,0:T(8,128)(2,1)S(1)}, bf16[48,256]{1,0:T(8,128)(2,1)S(1)}, u32[]{:S(2)}, u32[]{:S(2)}) %collective-permute-start.14) | collective-permute-done | bytes 24608 | tf_op jit(solution)/shard_map/ppermute | solution.py:143
  43.3 1.0 %collective-permute-done.16 = bf16[48,256]{1,0:T(8,128)(2,1)S(1)} collective-permute-done((bf16[48,256]{1,0:T(8,128)(2,1)S(1)}, bf16[48,256]{1,0:T(8,128)(2,1)S(1)}, u32[]{:S(2)}, u32[]{:S(2)}) %collective-permute-start.16) | collective-permute-done | bytes 24608 | tf_op jit(solution)/shard_map/ppermute | solution.py:143
  44.3 0.0 collective-permute-start.17
  44.3 1.4 %collective-permute-done.17.far = bf16[8,48,256]{2,1,0:T(8,128)(2,1)S(1)} collective-permute-done((bf16[8,48,256]{2,1,0:T(8,128)(2,1)S(1)}, bf16[8,48,256]{2,1,0:T(8,128)(2,1)S(1)}, u32[]{:S(2)}, u32[]{:S(2)}) %collective-permute-start.17) | collective-permute-done | bytes 196640 | tf_op jit(solution)/shard_map/ppermute | solution.py:143
  45.7 1.3 %shard_map.107 = f32[48,256]{1,0:T(8,128)S(1)} custom-call(s32[35]{0:T(128)S(1)} %copy-done.1, bf16[16,256,256]{2,1,0:T(8,128)(2,1)S(1)} %shard_map.102.tiles, bf16[8,48,256]{2,1,0:T(8,128)(2,1)S(1)} %constant_dynamic-update-slice_fusion.near, bf16[8,48,256]{2,1,0:T(8,128)(2,1)S(1)} %collective-permute-done.17.far), custom_call_target="tpu_custom_call" | custom-call | flops 1048576 | bytes 1048576 | tf_op jit(solution)/shard_map/pallas_call | solution.py:180
  47.0 1.6 %collective-permute-start.18 = (f32[48,256]{1,0:T(8,128)S(1)}, f32[48,256]{1,0:T(8,128)S(1)}, u32[]{:S(2)}, u32[]{:S(2)}) collective-permute-start(f32[48,256]{1,0:T(8,128)S(1)} %shard_map.107), channel_id=1, source_target_pairs={{1,0},{0,1},{3,2},{2,3},{5,4},{4,5},{7,6},{6,7},{9,8},{8,9},{11,10... | collective-permute-start | bytes 147464 | tf_op jit(solution)/shard_map/ppermute | solution.py:139
  48.6 0.1 copy.12.bias
  48.7 1.3 %shard_map.106.own = f32[48,256]{1,0:T(8,128)S(1)} custom-call(s32[35]{0:T(128)S(1)} %copy-done.2, bf16[16,256,256]{2,1,0:T(8,128)(2,1)S(1)} %shard_map.102.tiles, bf16[8,48,256]{2,1,0:T(8,128)(2,1)S(1)} %constant_dynamic-update-slice_fusion.near, bf16[8,48,256]{2,1,0:T(8,128)(2,1)S(1)} %collective-permute-done.17.far), custom_call_target="tpu_custom_call" | custom-call | flops 1048576 | bytes 1048576 | tf_op jit(solution)/shard_map/pallas_call | solution.py:187
  50.0 1.2 %collective-permute-done.18.rest_0_ = f32[48,256]{1,0:T(8,128)S(1)} collective-permute-done((f32[48,256]{1,0:T(8,128)S(1)}, f32[48,256]{1,0:T(8,128)S(1)}, u32[]{:S(2)}, u32[]{:S(2)}) %collective-permute-start.18) | collective-permute-done | bytes 49184 | tf_op jit(solution)/shard_map/ppermute | solution.py:139
  51.2 0.7 %shard_map.108 = f32[47,256]{1,0:T(8,128)} custom-call(bf16[48,256]{1,0:T(8,128)(2,1)S(1)} %get-tuple-element.13.classes_in, f32[1,256]{1,0:T(1,128)S(1)} %get-tuple-element.14.scaling, f32[47,1]{1,0:T(8,128)S(1)} %copy.12.bias, f32[48,256]{1,0:T(8,128)S(1)} %shard_map.106.own, f32[48,256]{1,0:T(8,128)S(1)} %collective-permute-done.18.rest_0_), custom_call_target="tpu_custom_call" | custom-call | flops 1048576 | bytes 1048576 | tf_op jit(solution)/shard_map/pallas_call | solution.py:237
  (27 shorter events, 0.1 us)
Async XLA Ops:
  0.0 5.3 %collective-permute-start = (bf16[100,256]{1,0:T(8,128)(2,1)}, bf16[100,256]{1,0:T(8,128)(2,1)S(1)}, u32[]{:S(2)}, u32[]{:S(2)}) collective-permute-start(bf16[100,256]{1,0:T(8,128)(2,1)} %bitcast.43), channel_id=1, source_target_pairs={{1,0},{0,1},{3,2},{2,3},{5,4},{4,5},{7,6},{6,7},{9,8},{8,9},{11,10... | collective-permute-start | bytes 153608 | tf_op jit(solution)/shard_map/ppermute | solution.py:139
  5.5 7.1 %collective-permute-start.1 = (bf16[128,256]{1,0:T(8,128)(2,1)S(1)}, bf16[128,256]{1,0:T(8,128)(2,1)S(1)}, u32[]{:S(2)}, u32[]{:S(2)}) collective-permute-start(bf16[128,256]{1,0:T(8,128)(2,1)S(1)} %shard_map.101.hidden_in), channel_id=1, source_target_pairs={{4,0},{6,2},{0,4},{2,6},{12,8},{14,10},{8,12},{10,14},{20,16},{22,... | collective-permute-start | bytes 196616 | tf_op jit(solution)/shard_map/ppermute | solution.py:143
  7.7 4.5 %collective-permute-start.2 = (bf16[128,256]{1,0:T(8,128)(2,1)S(1)}, bf16[128,256]{1,0:T(8,128)(2,1)S(1)}, u32[]{:S(2)}, u32[]{:S(2)}) collective-permute-start(bf16[128,256]{1,0:T(8,128)(2,1)S(1)} %shard_map.101.hidden_in), channel_id=1, source_target_pairs={{8,0},{10,2},{12,4},{14,6},{0,8},{2,10},{4,12},{6,14},{24,16},{26,... | collective-permute-start | bytes 196616 | tf_op jit(solution)/shard_map/ppermute | solution.py:143
  9.2 6.6 %collective-permute-start.4 = (bf16[128,256]{1,0:T(8,128)(2,1)S(1)}, bf16[128,256]{1,0:T(8,128)(2,1)S(1)}, u32[]{:S(2)}, u32[]{:S(2)}) collective-permute-start(bf16[128,256]{1,0:T(8,128)(2,1)S(1)} %shard_map.101.hidden_in), channel_id=1, source_target_pairs={{16,0},{18,2},{20,4},{22,6},{24,8},{26,10},{28,12},{30,14},{0,16},... | collective-permute-start | bytes 196616 | tf_op jit(solution)/shard_map/ppermute | solution.py:143
  11.8 6.1 %collective-permute-start.6 = (bf16[128,256]{1,0:T(8,128)(2,1)S(1)}, bf16[128,256]{1,0:T(8,128)(2,1)S(1)}, u32[]{:S(2)}, u32[]{:S(2)}) collective-permute-start(bf16[128,256]{1,0:T(8,128)(2,1)S(1)} %shard_map.101.hidden_in), channel_id=1, source_target_pairs={{24,0},{26,2},{28,4},{30,6},{16,8},{18,10},{20,12},{22,14},{8,16},... | collective-permute-start | bytes 196616 | tf_op jit(solution)/shard_map/ppermute | solution.py:143
  12.2 6.2 %collective-permute-start.3 = (bf16[128,256]{1,0:T(8,128)(2,1)S(1)}, bf16[128,256]{1,0:T(8,128)(2,1)S(1)}, u32[]{:S(2)}, u32[]{:S(2)}) collective-permute-start(bf16[128,256]{1,0:T(8,128)(2,1)S(1)} %collective-permute-done.2), channel_id=1, source_target_pairs={{4,0},{6,2},{0,4},{2,6},{12,8},{14,10},{8,12},{10,14},{20,16},{22,... | collective-permute-start | bytes 196616 | tf_op jit(solution)/shard_map/ppermute | solution.py:143
  15.8 4.3 %collective-permute-start.5 = (bf16[128,256]{1,0:T(8,128)(2,1)S(1)}, bf16[128,256]{1,0:T(8,128)(2,1)S(1)}, u32[]{:S(2)}, u32[]{:S(2)}) collective-permute-start(bf16[128,256]{1,0:T(8,128)(2,1)S(1)} %collective-permute-done.4), channel_id=1, source_target_pairs={{4,0},{6,2},{0,4},{2,6},{12,8},{14,10},{8,12},{10,14},{20,16},{22,... | collective-permute-start | bytes 196616 | tf_op jit(solution)/shard_map/ppermute | solution.py:143
  17.9 4.3 %collective-permute-start.7 = (bf16[128,256]{1,0:T(8,128)(2,1)S(1)}, bf16[128,256]{1,0:T(8,128)(2,1)S(1)}, u32[]{:S(2)}, u32[]{:S(2)}) collective-permute-start(bf16[128,256]{1,0:T(8,128)(2,1)S(1)} %collective-permute-done.6), channel_id=1, source_target_pairs={{4,0},{6,2},{0,4},{2,6},{12,8},{14,10},{8,12},{10,14},{20,16},{22,... | collective-permute-start | bytes 196616 | tf_op jit(solution)/shard_map/ppermute | solution.py:143
  22.2 3.0 %collective-permute-start.8 = (bf16[8,128,256]{2,1,0:T(8,128)(2,1)S(1)}, bf16[8,128,256]{2,1,0:T(8,128)(2,1)S(1)}, u32[]{:S(2)}, u32[]{:S(2)}) collective-permute-start(bf16[8,128,256]{2,1,0:T(8,128)(2,1)S(1)} %bitcast_dynamic-update-slice_fusion.near), channel_id=1, source_target_pairs={{2,0},{0,2},{6,4},{4,6},{10,8},{8,10},{14,12},{12,14},{18,16},{16,... | collective-permute-start | bytes 1572872 | tf_op jit(solution)/shard_map/ppermute | solution.py:143
  23.6 1.6 %copy-start = (s32[35]{0:T(128)}, s32[35]{0:T(128)S(1)}, u32[]{:S(2)}) copy-start(s32[35]{0:T(128)S(1)} %concatenate.3.plan) | copy-start | bytes 424
  26.6 6.1 %collective-permute-start.9 = (f32[136,256]{1,0:T(8,128)S(1)}, f32[136,256]{1,0:T(8,128)S(1)}, u32[]{:S(2)}, u32[]{:S(2)}) collective-permute-start(f32[136,256]{1,0:T(8,128)S(1)} %shard_map.104), channel_id=1, source_target_pairs={{1,0},{0,1},{3,2},{2,3},{5,4},{4,5},{7,6},{6,7},{9,8},{8,9},{11,10... | collective-permute-start | bytes 417800 | tf_op jit(solution)/shard_map/ppermute | solution.py:139
  29.6 0.7 %copy-start.1 = (s32[35]{0:T(128)S(1)}, s32[35]{0:T(128)}, u32[]{:S(2)}) copy-start(s32[35]{0:T(128)} %copy-done) | copy-start | bytes 424
  31.6 16.9 %copy-start.3 = (f32[47]{0:T(128)S(1)}, f32[47]{0:T(128)}, u32[]{:S(2)}) copy-start(f32[47]{0:T(128)} %param.19) | copy-start | bytes 568
  31.7 17.0 %copy-start.2 = (s32[35]{0:T(128)S(1)}, s32[35]{0:T(128)}, u32[]{:S(2)}) copy-start(s32[35]{0:T(128)} %copy-done) | copy-start | bytes 424
  33.0 6.4 %collective-permute-start.10 = (bf16[48,256]{1,0:T(8,128)(2,1)S(1)}, bf16[48,256]{1,0:T(8,128)(2,1)S(1)}, u32[]{:S(2)}, u32[]{:S(2)}) collective-permute-start(bf16[48,256]{1,0:T(8,128)(2,1)S(1)} %get-tuple-element.13.classes_in), channel_id=1, source_target_pairs={{4,0},{6,2},{0,4},{2,6},{12,8},{14,10},{8,12},{10,14},{20,16},{22,... | collective-permute-start | bytes 73736 | tf_op jit(solution)/shard_map/ppermute | solution.py:143
  33.5 4.4 %collective-permute-start.11 = (bf16[48,256]{1,0:T(8,128)(2,1)S(1)}, bf16[48,256]{1,0:T(8,128)(2,1)S(1)}, u32[]{:S(2)}, u32[]{:S(2)}) collective-permute-start(bf16[48,256]{1,0:T(8,128)(2,1)S(1)} %get-tuple-element.13.classes_in), channel_id=1, source_target_pairs={{8,0},{10,2},{12,4},{14,6},{0,8},{2,10},{4,12},{6,14},{24,16},{26,... | collective-permute-start | bytes 73736 | tf_op jit(solution)/shard_map/ppermute | solution.py:143
  33.5 5.9 %collective-permute-start.13 = (bf16[48,256]{1,0:T(8,128)(2,1)S(1)}, bf16[48,256]{1,0:T(8,128)(2,1)S(1)}, u32[]{:S(2)}, u32[]{:S(2)}) collective-permute-start(bf16[48,256]{1,0:T(8,128)(2,1)S(1)} %get-tuple-element.13.classes_in), channel_id=1, source_target_pairs={{16,0},{18,2},{20,4},{22,6},{24,8},{26,10},{28,12},{30,14},{0,16},... | collective-permute-start | bytes 73736 | tf_op jit(solution)/shard_map/ppermute | solution.py:143
  34.8 5.6 %collective-permute-start.15 = (bf16[48,256]{1,0:T(8,128)(2,1)S(1)}, bf16[48,256]{1,0:T(8,128)(2,1)S(1)}, u32[]{:S(2)}, u32[]{:S(2)}) collective-permute-start(bf16[48,256]{1,0:T(8,128)(2,1)S(1)} %get-tuple-element.13.classes_in), channel_id=1, source_target_pairs={{24,0},{26,2},{28,4},{30,6},{16,8},{18,10},{20,12},{22,14},{8,16},... | collective-permute-start | bytes 73736 | tf_op jit(solution)/shard_map/ppermute | solution.py:143
  37.9 4.1 %collective-permute-start.12 = (bf16[48,256]{1,0:T(8,128)(2,1)S(1)}, bf16[48,256]{1,0:T(8,128)(2,1)S(1)}, u32[]{:S(2)}, u32[]{:S(2)}) collective-permute-start(bf16[48,256]{1,0:T(8,128)(2,1)S(1)} %collective-permute-done.11), channel_id=1, source_target_pairs={{4,0},{6,2},{0,4},{2,6},{12,8},{14,10},{8,12},{10,14},{20,16},{22,... | collective-permute-start | bytes 73736 | tf_op jit(solution)/shard_map/ppermute | solution.py:143
  39.4 3.9 %collective-permute-start.14 = (bf16[48,256]{1,0:T(8,128)(2,1)S(1)}, bf16[48,256]{1,0:T(8,128)(2,1)S(1)}, u32[]{:S(2)}, u32[]{:S(2)}) collective-permute-start(bf16[48,256]{1,0:T(8,128)(2,1)S(1)} %collective-permute-done.13), channel_id=1, source_target_pairs={{4,0},{6,2},{0,4},{2,6},{12,8},{14,10},{8,12},{10,14},{20,16},{22,... | collective-permute-start | bytes 73736 | tf_op jit(solution)/shard_map/ppermute | solution.py:143
  40.5 3.8 %collective-permute-start.16 = (bf16[48,256]{1,0:T(8,128)(2,1)S(1)}, bf16[48,256]{1,0:T(8,128)(2,1)S(1)}, u32[]{:S(2)}, u32[]{:S(2)}) collective-permute-start(bf16[48,256]{1,0:T(8,128)(2,1)S(1)} %collective-permute-done.15), channel_id=1, source_target_pairs={{4,0},{6,2},{0,4},{2,6},{12,8},{14,10},{8,12},{10,14},{20,16},{22,... | collective-permute-start | bytes 73736 | tf_op jit(solution)/shard_map/ppermute | solution.py:143
  44.3 1.4 %collective-permute-start.17 = (bf16[8,48,256]{2,1,0:T(8,128)(2,1)S(1)}, bf16[8,48,256]{2,1,0:T(8,128)(2,1)S(1)}, u32[]{:S(2)}, u32[]{:S(2)}) collective-permute-start(bf16[8,48,256]{2,1,0:T(8,128)(2,1)S(1)} %constant_dynamic-update-slice_fusion.near), channel_id=1, source_target_pairs={{2,0},{0,2},{6,4},{4,6},{10,8},{8,10},{14,12},{12,14},{18,16},{16,... | collective-permute-start | bytes 589832 | tf_op jit(solution)/shard_map/ppermute | solution.py:143
  47.0 4.2 %collective-permute-start.18 = (f32[48,256]{1,0:T(8,128)S(1)}, f32[48,256]{1,0:T(8,128)S(1)}, u32[]{:S(2)}, u32[]{:S(2)}) collective-permute-start(f32[48,256]{1,0:T(8,128)S(1)} %shard_map.107), channel_id=1, source_target_pairs={{1,0},{0,1},{3,2},{2,3},{5,4},{4,5},{7,6},{6,7},{9,8},{8,9},{11,10... | collective-permute-start | bytes 147464 | tf_op jit(solution)/shard_map/ppermute | solution.py:139

commit v4 on v3

--- a/solution.py
+++ b/solution.py
@@ -95,7 +95,7 @@
     total = jnp.zeros((len(outs) * (height + extra), tile), F32)
     for slot in range(slots):
         panel = lax.clamp(0, plan[3 + slots + slot] // reps, 2 * half - 1)
-        place = (panel // 2) ^ (block // 2)
+        place = panel // 2
         values = jnp.where(panel % 2 == block % 2, near[place], far[place])
         local = plan[3 + slot] - block * reps
         pieces = []
@@ -144,13 +144,9 @@
 
 
 def gather_blocks(value):
-    chips = lax.axis_size("blk") // 2
-    parts = {0: value}
-    for step in range(2, chips, 2):
-        parts[step] = swapped(value, 2 * step)
-    for step in range(0, chips, 2):
-        parts[step + 1] = swapped(parts[step], 2)
-    near = jnp.stack([parts[step] for step in range(chips)])
+    size = lax.axis_size("blk")
+    groups = [list(range(core, size, 2)) for core in range(2)]
+    near = lax.all_gather(value, "blk", axis_index_groups=groups)
     return near, swapped(near, 1)
 
 

time: 52.2 us -> 87.1 us (1.67)
  blocking collectives: 0 us -> 62.9 us
  starting transfers between devices: 22.5 us -> 6.06 us
  waiting for transfers between devices: 16.2 us -> 4.83 us
    all_gather x0 -> x2, blocking collectives: none -> 62.9 us  [gather_blocks(): near = lax.all_gather(value, 'blk', axis_index_groups=groups)]
    ppermute x16 -> x2, starting transfers between devices: 16.5 us -> 0.01 us  [swapped(): lax.ppermute(value, 'blk', [(d ^ mask, d) for d in range(lax.axis_size('b...]
    ppermute x16 -> x2, waiting for transfers between devices: 12.8 us -> 1.44 us  [swapped(): lax.ppermute(value, 'blk', [(d ^ mask, d) for d in range(lax.axis_size('b...]
  transfers between devices with their start and end apart: 19 -> 5, of which waited for: 12 -> 4; matrix products, arithmetic and copies ran while one was open for 5% -> 3% of each run, Pallas kernels for 10% -> 6%
where the time goes in v4:
time: 87.1 us; the launch traced here: 86.8 us
  blocking collectives  62.9 us (72%)
  Pallas kernels  9.28 us (11%)
  starting transfers between devices  6.06 us (7%)
  waiting for transfers between devices  4.83 us (6%)
  local copies, waits for them, and re-layouts  3 us (3%)
    all_gather x2, blocking collectives, gather_blocks(): near = lax.all_gather(value, 'blk', axis_index_groups=groups)  62.9 us
    ppermute x3, starting transfers between devices, shifted(): lax.ppermute(value, axis, [((d + step) % size, d) for d in range(size)])  6.05 us
    ppermute x3, waiting for transfers between devices, shifted(): lax.ppermute(value, axis, [((d + step) % size, d) for d in range(size)])  3.38 us
    pallas_call x2, Pallas kernels, aggregated(): call(functools.partial(aggregate, reps, 0, count_rows), [shape((rows, til...  2.64 us
    pallas_call x2, Pallas kernels, aggregated(): call(functools.partial(aggregate, reps, 1, count_rows), [shape((rows, til...  2.64 us
  transfers between devices with their start and end apart: 5, of which 4 were waited for; matrix products, arithmetic and copies ran while one was open for 3% of the time, Pallas kernels for 6%

profile of v4, /device:TPU:0, one launch (start us, length us, event | category | flops | bytes accessed | tf_op | source)
XLA Modules:
  0.0 86.8 jit_solution(17506637379680390101)
XLA Ops:
  0.0 2.9 %collective-permute-start = (bf16[100,256]{1,0:T(8,128)(2,1)}, bf16[100,256]{1,0:T(8,128)(2,1)S(1)}, u32[]{:S(2)}, u32[]{:S(2)}) collective-permute-start(bf16[100,256]{1,0:T(8,128)(2,1)} %bitcast.19), channel_id=1, source_target_pairs={{1,0},{0,1},{3,2},{2,3},{5,4},{4,5},{7,6},{6,7},{9,8},{8,9},{11,10... | collective-permute-start | bytes 153608 | tf_op jit(solution)/shard_map/ppermute | solution.py:139
  2.9 1.2 %shard_map.100 = (bf16[128,256]{1,0:T(8,128)(2,1)S(1)}, s32[1,256]{1,0:T(1,128)S(1)}, bf16[128,100]{1,0:T(8,128)(2,1)S(1)}) custom-call(s32[1,512]{1,0:T(1,128)} %order.1, bf16[100,256]{1,0:T(8,128)(2,1)} %bitcast.20, bf16[100,128]{1,0:T(8,128)(2,1)} %weight.1), custom_call_target="tpu_custom_call" | custom-call | flops 1048576 | bytes 1048576 | tf_op jit(solution)/shard_map/pallas_call | solution.py:190
  4.2 1.1 %collective-permute-done.rest_0_ = bf16[100,256]{1,0:T(8,128)(2,1)S(1)} collective-permute-done((bf16[100,256]{1,0:T(8,128)(2,1)}, bf16[100,256]{1,0:T(8,128)(2,1)S(1)}, u32[]{:S(2)}, u32[]{:S(2)}) %collective-permute-start) | collective-permute-done | bytes 51232 | tf_op jit(solution)/shard_map/ppermute | solution.py:139
  5.3 0.3 shard_map.101.hidden_in
  5.5 32.3 %all-gather = bf16[1024,256]{1,0:T(8,128)(2,1)S(1)} all-gather(bf16[128,256]{1,0:T(8,128)(2,1)S(1)} %shard_map.101.hidden_in), channel_id=2, replica_groups={{0,4,8,12,16,20,24,28},{2,6,10,14,18,22,26,30},{1,5,9,13,17,21,25,29},{..., dimensions={0}, use_global_device_ids=true | all-gather | bytes 589824 | tf_op jit(solution)/shard_map/all_gather | solution.py:149
  37.8 0.0 collective-permute-start.1
  38.5 0.7 concatenate.3.plan
  39.2 0.0 copy-start
  39.2 1.6 %shard_map.102.tiles = bf16[16,256,256]{2,1,0:T(8,128)(2,1)S(1)} custom-call(bf16[16,256,256]{2,1,0:T(8,128)(2,1)} %bitcast.18), custom_call_target="tpu_custom_call" | custom-call | flops 1048576 | bytes 1048576 | tf_op jit(solution)/shard_map/pallas_call | solution.py:211
  40.8 0.0 collective-permute-done.1.far
  40.8 0.0 copy-done
  40.8 1.4 %shard_map.104 = f32[136,256]{1,0:T(8,128)S(1)} custom-call(s32[35]{0:T(128)S(1)} %concatenate.3.plan, bf16[16,256,256]{2,1,0:T(8,128)(2,1)S(1)} %shard_map.102.tiles, bf16[8,128,256]{2,1,0:T(8,128)(2,1)S(1)} %bitcast.13, bf16[8,128,256]{2,1,0:T(8,128)(2,1)S(1)} %collective-permute-done.1.far), custom_call_target="tpu_custom_call" | custom-call | flops 1048576 | bytes 1048576 | tf_op jit(solution)/shard_map/pallas_call | solution.py:176
  42.2 1.6 %collective-permute-start.2 = (f32[136,256]{1,0:T(8,128)S(1)}, f32[136,256]{1,0:T(8,128)S(1)}, u32[]{:S(2)}, u32[]{:S(2)}) collective-permute-start(f32[136,256]{1,0:T(8,128)S(1)} %shard_map.104), channel_id=1, source_target_pairs={{1,0},{0,1},{3,2},{2,3},{5,4},{4,5},{7,6},{6,7},{9,8},{8,9},{11,10... | collective-permute-start | bytes 417800 | tf_op jit(solution)/shard_map/ppermute | solution.py:139
  43.8 0.8 copy.11.bias
  44.5 0.7 pad.4.weight_t
  45.3 0.0 copy-start.1
  45.3 0.7 copy-done.1
  45.9 1.4 %shard_map.103.own = f32[136,256]{1,0:T(8,128)S(1)} custom-call(s32[35]{0:T(128)S(1)} %copy-done.1, bf16[16,256,256]{2,1,0:T(8,128)(2,1)S(1)} %shard_map.102.tiles, bf16[8,128,256]{2,1,0:T(8,128)(2,1)S(1)} %bitcast.14, bf16[8,128,256]{2,1,0:T(8,128)(2,1)S(1)} %collective-permute-done.1.far), custom_call_target="tpu_custom_call" | custom-call | flops 1048576 | bytes 1048576 | tf_op jit(solution)/shard_map/pallas_call | solution.py:183
  47.3 0.0 copy-start.3
  47.3 0.0 copy-start.2
  47.3 1.1 %collective-permute-done.2.rest_0_ = f32[136,256]{1,0:T(8,128)S(1)} collective-permute-done((f32[136,256]{1,0:T(8,128)S(1)}, f32[136,256]{1,0:T(8,128)S(1)}, u32[]{:S(2)}, u32[]{:S(2)}) %collective-permute-start.2) | collective-permute-done | bytes 139296 | tf_op jit(solution)/shard_map/ppermute | solution.py:139
  48.4 0.2 shard_map.105
  48.6 30.7 %all-gather.1 = bf16[384,256]{1,0:T(8,128)(2,1)S(1)} all-gather(bf16[48,256]{1,0:T(8,128)(2,1)S(1)} %get-tuple-element.13.classes_in), channel_id=3, replica_groups={{0,4,8,12,16,20,24,28},{2,6,10,14,18,22,26,30},{1,5,9,13,17,21,25,29},{..., dimensions={0}, use_global_device_ids=true | all-gather | bytes 221184 | tf_op jit(solution)/shard_map/all_gather | solution.py:149
  79.2 0.0 collective-permute-start.3
  79.2 1.4 %collective-permute-done.3.far = bf16[8,48,256]{2,1,0:T(8,128)(2,1)S(1)} collective-permute-done((bf16[8,48,256]{2,1,0:T(8,128)(2,1)S(1)}, bf16[8,48,256]{2,1,0:T(8,128)(2,1)S(1)}, u32[]{:S(2)}, u32[]{:S(2)}) %collective-permute-start.3) | collective-permute-done | bytes 196640 | tf_op jit(solution)/shard_map/ppermute | solution.py:143
  80.7 1.3 %shard_map.107 = f32[48,256]{1,0:T(8,128)S(1)} custom-call(s32[35]{0:T(128)S(1)} %copy-done.1, bf16[16,256,256]{2,1,0:T(8,128)(2,1)S(1)} %shard_map.102.tiles, bf16[8,48,256]{2,1,0:T(8,128)(2,1)S(1)} %bitcast.16, bf16[8,48,256]{2,1,0:T(8,128)(2,1)S(1)} %collective-permute-done.3.far), custom_call_target="tpu_custom_call" | custom-call | flops 1048576 | bytes 1048576 | tf_op jit(solution)/shard_map/pallas_call | solution.py:176
  82.0 1.6 %collective-permute-start.4 = (f32[48,256]{1,0:T(8,128)S(1)}, f32[48,256]{1,0:T(8,128)S(1)}, u32[]{:S(2)}, u32[]{:S(2)}) collective-permute-start(f32[48,256]{1,0:T(8,128)S(1)} %shard_map.107), channel_id=1, source_target_pairs={{1,0},{0,1},{3,2},{2,3},{5,4},{4,5},{7,6},{6,7},{9,8},{8,9},{11,10... | collective-permute-start | bytes 147464 | tf_op jit(solution)/shard_map/ppermute | solution.py:139
  83.5 0.0 copy-done.3
  83.5 0.1 copy.12.bias
  83.6 0.0 copy-done.2
  83.6 1.3 %shard_map.106.own = f32[48,256]{1,0:T(8,128)S(1)} custom-call(s32[35]{0:T(128)S(1)} %copy-done.2, bf16[16,256,256]{2,1,0:T(8,128)(2,1)S(1)} %shard_map.102.tiles, bf16[8,48,256]{2,1,0:T(8,128)(2,1)S(1)} %bitcast.17, bf16[8,48,256]{2,1,0:T(8,128)(2,1)S(1)} %collective-permute-done.3.far), custom_call_target="tpu_custom_call" | custom-call | flops 1048576 | bytes 1048576 | tf_op jit(solution)/shard_map/pallas_call | solution.py:183
  84.9 1.2 %collective-permute-done.4.rest_0_ = f32[48,256]{1,0:T(8,128)S(1)} collective-permute-done((f32[48,256]{1,0:T(8,128)S(1)}, f32[48,256]{1,0:T(8,128)S(1)}, u32[]{:S(2)}, u32[]{:S(2)}) %collective-permute-start.4) | collective-permute-done | bytes 49184 | tf_op jit(solution)/shard_map/ppermute | solution.py:139
  86.1 0.7 shard_map.108
Async XLA Ops:
  0.0 5.3 %collective-permute-start = (bf16[100,256]{1,0:T(8,128)(2,1)}, bf16[100,256]{1,0:T(8,128)(2,1)S(1)}, u32[]{:S(2)}, u32[]{:S(2)}) collective-permute-start(bf16[100,256]{1,0:T(8,128)(2,1)} %bitcast.19), channel_id=1, source_target_pairs={{1,0},{0,1},{3,2},{2,3},{5,4},{4,5},{7,6},{6,7},{9,8},{8,9},{11,10... | collective-permute-start | bytes 153608 | tf_op jit(solution)/shard_map/ppermute | solution.py:139
  37.8 3.0 %collective-permute-start.1 = (bf16[8,128,256]{2,1,0:T(8,128)(2,1)S(1)}, bf16[8,128,256]{2,1,0:T(8,128)(2,1)S(1)}, u32[]{:S(2)}, u32[]{:S(2)}) collective-permute-start(bf16[8,128,256]{2,1,0:T(8,128)(2,1)S(1)} %bitcast.12), channel_id=1, source_target_pairs={{2,0},{0,2},{6,4},{4,6},{10,8},{8,10},{14,12},{12,14},{18,16},{16,... | collective-permute-start | bytes 1572872 | tf_op jit(solution)/shard_map/ppermute | solution.py:143
  39.2 1.6 %copy-start = (s32[35]{0:T(128)}, s32[35]{0:T(128)S(1)}, u32[]{:S(2)}) copy-start(s32[35]{0:T(128)S(1)} %concatenate.3.plan) | copy-start | bytes 424
  42.2 6.1 %collective-permute-start.2 = (f32[136,256]{1,0:T(8,128)S(1)}, f32[136,256]{1,0:T(8,128)S(1)}, u32[]{:S(2)}, u32[]{:S(2)}) collective-permute-start(f32[136,256]{1,0:T(8,128)S(1)} %shard_map.104), channel_id=1, source_target_pairs={{1,0},{0,1},{3,2},{2,3},{5,4},{4,5},{7,6},{6,7},{9,8},{8,9},{11,10... | collective-permute-start | bytes 417800 | tf_op jit(solution)/shard_map/ppermute | solution.py:139
  45.3 0.7 copy-start.1
  47.3 36.2 %copy-start.3 = (f32[47]{0:T(128)S(1)}, f32[47]{0:T(128)}, u32[]{:S(2)}) copy-start(f32[47]{0:T(128)} %param.19) | copy-start | bytes 568
  47.3 36.3 %copy-start.2 = (s32[35]{0:T(128)S(1)}, s32[35]{0:T(128)}, u32[]{:S(2)}) copy-start(s32[35]{0:T(128)} %copy-done) | copy-start | bytes 424
  79.2 1.4 %collective-permute-start.3 = (bf16[8,48,256]{2,1,0:T(8,128)(2,1)S(1)}, bf16[8,48,256]{2,1,0:T(8,128)(2,1)S(1)}, u32[]{:S(2)}, u32[]{:S(2)}) collective-permute-start(bf16[8,48,256]{2,1,0:T(8,128)(2,1)S(1)} %bitcast.15), channel_id=1, source_target_pairs={{2,0},{0,2},{6,4},{4,6},{10,8},{8,10},{14,12},{12,14},{18,16},{16,... | collective-permute-start | bytes 589832 | tf_op jit(solution)/shard_map/ppermute | solution.py:143
  82.0 4.2 %collective-permute-start.4 = (f32[48,256]{1,0:T(8,128)S(1)}, f32[48,256]{1,0:T(8,128)S(1)}, u32[]{:S(2)}, u32[]{:S(2)}) collective-permute-start(f32[48,256]{1,0:T(8,128)S(1)} %shard_map.107), channel_id=1, source_target_pairs={{1,0},{0,1},{3,2},{2,3},{5,4},{4,5},{7,6},{6,7},{9,8},{8,9},{11,10... | collective-permute-start | bytes 147464 | tf_op jit(solution)/shard_map/ppermute | solution.py:139

commit v5 on v4

v5 whole, which is shorter than its diff:
```python
import functools

import jax
import jax.numpy as jnp
from jax import lax
from jax.experimental import pallas as pl
from jax.experimental.pallas import tpu as pltpu
from jax.sharding import PartitionSpec as P

BF16 = jnp.bfloat16
F32 = jnp.float32
ONES_ROWS = 16
VMEM_LIMIT = 32 * 1024 * 1024


def nn(a, b):
    return lax.dot_general(a, b, (((1,), (0,)), ((), ())), preferred_element_type=F32)


def nt(a, b):
    return lax.dot_general(a, b, (((1,), (1,)), ((), ())), preferred_element_type=F32)


def call(kernel, outs, smem=(), vmem=(), hbm=(), scratch=(), smem_outs=0, cost=1 << 20):
    spaces = [pltpu.SMEM] * len(smem) + [pltpu.VMEM] * len(vmem) + [pltpu.HBM] * len(hbm)
    out_spaces = [pltpu.SMEM] * smem_outs + [pltpu.VMEM] * (len(outs) - smem_outs)
    return pl.pallas_call(
        kernel,
        out_shape=outs,
        in_specs=[pl.BlockSpec(memory_space=space) for space in spaces],
        out_specs=[pl.BlockSpec(memory_space=space) for space in out_spaces],
        scratch_shapes=scratch,
        compiler_params=pltpu.CompilerParams(vmem_limit_bytes=VMEM_LIMIT),
        cost_estimate=pl.CostEstimate(flops=cost, bytes_accessed=cost, transcendentals=0),
    )(*smem, *vmem, *[pltpu.with_memory_space_constraint(value, pltpu.HBM) for value in hbm])


def fetched(sources, targets, sems):
    copies = [
        pltpu.make_async_copy(source, target, sems.at[index])
        for index, (source, target) in enumerate(zip(sources, targets))
    ]
    for copy in copies:
        copy.start()
    return copies


def picked(weight_t, features, wanted, owner):
    tile = features.shape[1]
    hidden = nn(weight_t, features[...]).astype(BF16)
    source = lax.broadcasted_iota(jnp.int32, (tile, tile), 0) + owner * tile
    return nn(hidden, jnp.where(source == wanted, 1.0, 0.0).astype(BF16))


def prepare(order, features, weight, part, wanted_out, weight_out, *rest):
    order_in, features_in, weight_in, sems = rest
    for copy in fetched((order, weight, features), (order_in, weight_in, features_in), sems):
        copy.wait()
    tile = features.shape[1]
    member = lax.axis_index("rep")
    wanted = order_in[:, pl.ds(pl.multiple_of(member * tile, tile), tile)]
    wanted_out[...] = wanted
    weight_t = weight_in[...].astype(F32).T.astype(BF16)
    weight_out[...] = weight_t
    part[...] = picked(weight_t, features_in, wanted, member).astype(BF16)


def order_project(part, wanted, weight_t, *rest):
    *features, out = rest
    reps = len(features) + 1
    member = lax.axis_index("rep")
    total = part[...].astype(F32)
    for step in range(1, reps):
        owner = lax.rem(member + step, reps)
        total = total + picked(weight_t[...], features[step - 1], wanted[...], owner)
    out[...] = total.astype(BF16)


def stage(reps, places, live, _, *refs):
    sources, (plan, bias_1, bias_2, weight, tiles), scratch = refs[:6], refs[6:11], refs[11:]
    rows_in, columns_in, row_1, row_2, sems = scratch
    slots = tiles.shape[0]
    copies = fetched(sources, (rows_in, columns_in, row_1, row_2, weight, tiles), sems)
    for copy in copies[:4]:
        copy.wait()
    bias_1[...] = jnp.broadcast_to(row_1[...], (8, row_1.shape[1])).T[:, :1]
    bias_2[...] = jnp.broadcast_to(row_2[...], (8, row_2.shape[1])).T[:, :1]
    block, member = lax.axis_index("blk"), lax.axis_index("rep")
    for slot in range(slots):
        panel = lax.clamp(0, columns_in[0, slot] // reps, len(places[0]) - 1)
        apart = panel ^ block
        place = jnp.int32(0)
        for core in range(2):
            for index, value in enumerate(places[core]):
                place = jnp.where((apart == index) & (block % 2 == core), value, place)
        local = rows_in[0, slot] - block * reps
        step = lax.rem(local - member + reps, reps)
        plan[slot] = place
        plan[slots + slot] = jnp.where((slot < live[0]) & (local >= 0) & (local < reps), step, -1)
    for copy in copies[4:]:
        copy.wait()


def aggregate(count_rows, plan, tiles, *rest):
    parts, outs, panels = rest[:3], rest[3:-1], rest[-1]
    slots, tile = tiles.shape[0], tiles.shape[1]
    height = panels.shape[1]
    extra = ONES_ROWS if count_rows else 0
    start = 0
    for part in parts:
        panels[start : start + part.shape[0]] = part[...]
        start += part.shape[0]
    total = jnp.zeros((len(outs) * (height + extra), tile), F32)
    for slot in range(slots):
        values = panels[plan[slot]]
        pieces = []
        for step in range(len(outs)):
            used = (plan[slots + slot] == step).astype(F32)
            pieces.append(values * used.astype(BF16))
            if extra:
                pieces.append(jnp.full((extra, tile), used, F32).astype(BF16))
        total = total + nt(jnp.concatenate(pieces, axis=0), tiles[slot])
    for step, out in enumerate(outs):
        start = step * (height + extra)
        out[...] = total[start : start + out.shape[0]]


def combine(hidden_in, bias, weight_t, own, *rest):
    *arrived, out, scale_out = rest
    height = hidden_in.shape[0]
    total = own[...]
    for part in arrived:
        total = total + part[...]
    scaling = lax.rsqrt(1.0 + total[height : height + 1])
    hidden = scaling * (total[:height] + hidden_in[...].astype(F32)) + bias[...]
    hidden = jnp.maximum(hidden, 0.0).astype(BF16)
    classes = nn(weight_t[...], hidden)
    blank = jnp.zeros((out.shape[0] - classes.shape[0], classes.shape[1]), F32)
    out[...] = jnp.concatenate([classes, blank], axis=0).astype(BF16)
    scale_out[...] = scaling


def finish(classes_in, scaling, bias, own, *rest):
    *arrived, out = rest
    total = own[...]
    for part in arrived:
        total = total + part[...]
    classes = out.shape[0]
    whole = total + classes_in[...].astype(F32)
    out[...] = scaling[...] * whole[:classes] + bias[...]


def relay(arrived, out):
    out[...] = arrived[...]


def shifted(value, axis, step):
    size = lax.axis_size(axis)
    return lax.ppermute(value, axis, [((d + step) % size, d) for d in range(size)])


def swapped(value, masks):
    return lax.ppermute(value, "blk", [(d ^ masks[d % 2], d) for d in range(lax.axis_size("blk"))])


def chip_order(chips):
    far = [step for step in range(chips - 1, 0, -1) if step % 2 == 0]
    near = [step for step in range(chips - 1, 0, -1) if step % 2]
    order = sorted(far + near, key=lambda step: (step < chips // 2, step % 2, -step))
    return order[0], list(zip(order[1::2], order[2::2]))


def panel_places(chips):
    first, pairs = chip_order(chips)
    tables = []
    for core in range(2):
        near = [2 * first] + [2 * pair[core] + e for pair in pairs for e in range(2)]
        far = [2 * first + 1] + [2 * pair[1 - core] + 1 - e for pair in pairs for e in range(2)]
        stack = [0, 1, *near, *far]
        tables.append([stack.index(apart) for apart in range(2 * chips)])
    return tables


def gather_blocks(value, aside):
    chips = lax.axis_size("blk") // 2
    first, pairs = chip_order(chips)
    parts = [swapped(value, (2 * first, 2 * first))[None]]
    other = swapped(value, (1, 1))
    both = jnp.stack([value, other])
    for pair in pairs:
        parts.append(swapped(both, (2 * pair[0], 2 * pair[1])))
    parts[0], beside = lax.optimization_barrier(aside(parts[0]))
    near = jnp.concatenate(parts)
    return (both, near, swapped(near, (1, 1))), beside


def body(
    features,
    node_order,
    tile_values,
    tile_rows,
    tile_columns,
    tile_live,
    first_weight,
    first_bias,
    second_weight,
    second_bias,
):
    tile = features.shape[0]
    slots = tile_values.shape[1]
    reps = lax.axis_size("rep")
    blocks = lax.axis_size("blk")
    hidden, classes = second_weight.shape
    padded = -(-classes // 16) * 16
    shape = jax.ShapeDtypeStruct

    own_t = features.T
    others = [shifted(own_t, "rep", step) for step in range(1, reps)]
    prepared = call(
        prepare,
        [
            shape((hidden, tile), BF16),
            shape((1, tile), jnp.int32),
            shape(first_weight.shape[::-1], BF16),
        ],
        hbm=(node_order, own_t, first_weight),
        scratch=[
            pltpu.VMEM(node_order.shape, jnp.int32),
            pltpu.VMEM(own_t.shape, BF16),
            pltpu.VMEM(first_weight.shape, BF16),
            pltpu.SemaphoreType.DMA((3,)),
        ],
    )
    (hidden_in,) = call(order_project, [shape((hidden, tile), BF16)], vmem=(*prepared, *others))
    def staged(arrived):
        values = call(
            functools.partial(stage, reps, panel_places(blocks // 2)),
            [
                shape((2 * slots,), jnp.int32),
                shape((hidden, 1), F32),
                shape((classes, 1), F32),
                shape((classes, hidden), BF16),
                shape(tile_values.shape[1:], BF16),
            ],
            smem=(tile_live,),
            vmem=(arrived,),
            hbm=(
                tile_rows,
                tile_columns,
                first_bias[None],
                second_bias[None],
                second_weight.T,
                tile_values[0],
            ),
            scratch=[
                pltpu.SMEM((1, slots), jnp.int32),
                pltpu.SMEM((1, slots), jnp.int32),
                pltpu.VMEM((1, hidden), F32),
                pltpu.VMEM((1, classes), F32),
                pltpu.SemaphoreType.DMA((6,)),
            ],
            smem_outs=1,
        )
        return arrived, values

    def relayed(arrived):
        return call(relay, [shape(arrived.shape, BF16)], vmem=(arrived,), cost=1 << 28)[0], ()

    def aggregated(parts, rows, count_rows):
        sums = call(
            functools.partial(aggregate, count_rows),
            [shape((rows, tile), F32)] * reps,
            smem=(plan,),
            vmem=(tiles, *parts),
            scratch=[pltpu.VMEM((blocks, *parts[0].shape[1:]), BF16)],
        )
        return [sums[0]] + [shifted(sums[reps - step], "rep", step) for step in range(1, reps)]

    parts, (plan, bias_1, bias_2, weight_2, tiles) = gather_blocks(hidden_in, staged)
    sums = aggregated(parts, hidden + 8, True)
    classes_in, scaling = call(
        combine,
        [shape((padded, tile), BF16), shape((1, tile), F32)],
        vmem=(hidden_in, bias_1, weight_2, *sums),
    )
    parts, _ = gather_blocks(classes_in, relayed)
    sums = aggregated(parts, padded, False)
    (logits,) = call(
        finish, [shape((classes, tile), F32)], vmem=(classes_in, scaling, bias_2, *sums)
    )
    return logits.T


def solution(mesh):
    placed = (
        P(("blk", "rep"), None),
        P("blk", None),
        P(("blk", "rep"), None, None, None),
        P(("blk", "rep"), None),
        P(("blk", "rep"), None),
        P(("blk", "rep")),
        P(),
        P(),
        P(),
        P(),
    )
    return jax.shard_map(
        body, mesh=mesh, in_specs=placed, out_specs=P(("blk", "rep"), None), check_vma=False
    )
```

time: 87.1 us -> 50.6 us (0.58)
  blocking collectives: 62.9 us -> 0 us
  waiting for transfers between devices: 4.83 us -> 22 us
  starting transfers between devices: 6.06 us -> 20.2 us
  local copies, waits for them, and re-layouts: 3 us -> 0.03 us
  Pallas kernels: 9.28 us -> 7.36 us
    all_gather x2 -> x0, blocking collectives: 62.9 us -> none  [gather_blocks(): near = lax.all_gather(value, 'blk', axis_index_groups=groups)]
    ppermute x2 -> x12, starting transfers between devices: 0.01 us -> 14.1 us  [swapped(): lax.ppermute(value, 'blk', [(d ^ masks[d % 2], d) for d in range(lax.axis...]
    ppermute x2 -> x12, waiting for transfers between devices: 1.44 us -> 14.1 us  [swapped(): lax.ppermute(value, 'blk', [(d ^ masks[d % 2], d) for d in range(lax.axis...]
    ppermute x3, waiting for transfers between devices: 3.38 us -> 7.92 us  [shifted(): lax.ppermute(value, axis, [((d + step) % size, d) for d in range(size)])]
    pallas_call x9 -> x8, Pallas kernels: 9.28 us -> 7.36 us  [call(): pl.pallas_call(kernel, out_shape=outs, in_specs=[pl.BlockSpec(memory_spac...]
  transfers between devices with their start and end apart: 5 -> 15, of which waited for: 4 -> 11; matrix products, arithmetic and copies ran while one was open for 3% -> 0% of each run, Pallas kernels for 6% -> 7%
where the time goes in v5:
time: 50.6 us; the launch traced here: 50.4 us
  waiting for transfers between devices  22 us (43%)
  starting transfers between devices  20.2 us (40%)
  Pallas kernels  7.36 us (15%)
  between operations  0.77 us (2%)
    ppermute x12, starting transfers between devices, swapped(): lax.ppermute(value, 'blk', [(d ^ masks[d % 2], d) for d in range(lax.axis...  14.1 us
    ppermute x12, waiting for transfers between devices, swapped(): lax.ppermute(value, 'blk', [(d ^ masks[d % 2], d) for d in range(lax.axis...  14.1 us
    ppermute x3, waiting for transfers between devices, shifted(): lax.ppermute(value, axis, [((d + step) % size, d) for d in range(size)])  7.92 us
    pallas_call x8, Pallas kernels, call(): pl.pallas_call(kernel, out_shape=outs, in_specs=[pl.BlockSpec(memory_spac...  7.36 us
    ppermute x3, starting transfers between devices, shifted(): lax.ppermute(value, axis, [((d + step) % size, d) for d in range(size)])  6.05 us
  transfers between devices with their start and end apart: 15, of which 11 were waited for; matrix products, arithmetic and copies ran while one was open for 0% of the time, Pallas kernels for 7%

profile of v5, /device:TPU:0, one launch (start us, length us, event | category | flops | bytes accessed | tf_op | source)
XLA Modules:
  0.0 50.4 jit_solution(11632520177959044846)
XLA Ops:
  0.0 2.9 %collective-permute-start = (bf16[100,256]{1,0:T(8,128)(2,1)}, bf16[100,256]{1,0:T(8,128)(2,1)S(1)}, u32[]{:S(2)}, u32[]{:S(2)}) collective-permute-start(bf16[100,256]{1,0:T(8,128)(2,1)} %bitcast.19), channel_id=1, source_target_pairs={{1,0},{0,1},{3,2},{2,3},{5,4},{4,5},{7,6},{6,7},{9,8},{8,9},{11,10... | collective-permute-start | bytes 153608 | tf_op jit(solution)/shard_map/ppermute | solution.py:159
  2.9 1.2 %shard_map.100 = (bf16[128,256]{1,0:T(8,128)(2,1)S(1)}, s32[1,256]{1,0:T(1,128)S(1)}, bf16[128,100]{1,0:T(8,128)(2,1)S(1)}) custom-call(s32[1,512]{1,0:T(1,128)} %order.1, bf16[100,256]{1,0:T(8,128)(2,1)} %bitcast.20, bf16[100,128]{1,0:T(8,128)(2,1)} %weight.1), custom_call_target="tpu_custom_call" | custom-call | flops 1048576 | bytes 1048576 | tf_op jit(solution)/shard_map/pallas_call | solution.py:27
  4.2 1.1 %collective-permute-done.rest_0_ = bf16[100,256]{1,0:T(8,128)(2,1)S(1)} collective-permute-done((bf16[100,256]{1,0:T(8,128)(2,1)}, bf16[100,256]{1,0:T(8,128)(2,1)S(1)}, u32[]{:S(2)}, u32[]{:S(2)}) %collective-permute-start) | collective-permute-done | bytes 51232 | tf_op jit(solution)/shard_map/ppermute | solution.py:159
  5.3 0.3 shard_map.101.hidden_in
  5.5 0.1 collective-permute-start.2
  5.6 4.2 %collective-permute-start.1 = (bf16[128,256]{1,0:T(8,128)(2,1)S(1)}, bf16[128,256]{1,0:T(8,128)(2,1)S(1)}, u32[]{:S(2)}, u32[]{:S(2)}) collective-permute-start(bf16[128,256]{1,0:T(8,128)(2,1)S(1)} %shard_map.101.hidden_in), channel_id=1, source_target_pairs={{24,0},{26,2},{28,4},{30,6},{16,8},{18,10},{20,12},{22,14},{8,16},... | collective-permute-start | bytes 196616 | tf_op jit(solution)/shard_map/ppermute | solution.py:163
  9.8 0.0 collective-permute-done.2
  9.8 0.2 collective-permute-start.3
  10.7 3.8 %collective-permute-start.4 = (bf16[2,128,256]{2,1,0:T(8,128)(2,1)S(1)}, bf16[2,128,256]{2,1,0:T(8,128)(2,1)S(1)}, u32[]{:S(2)}, u32[]{:S(2)}) collective-permute-start(bf16[2,128,256]{2,1,0:T(8,128)(2,1)S(1)} %pad_maximum_fusion.1.rest_0_), channel_id=1, source_target_pairs={{20,0},{10,2},{16,4},{14,6},{28,8},{2,10},{24,12},{6,14},{4,16},{2... | collective-permute-start | bytes 393224 | tf_op jit(solution)/shard_map/ppermute | solution.py:163
  14.5 0.0 collective-permute-start.5
  14.5 0.0 collective-permute-done.1
  14.5 2.3 %shard_map.102 = (s32[32]{0:T(128)S(1)}, f32[128,1]{1,0:T(8,128)S(1)}, f32[47,1]{1,0:T(8,128)S(1)}, bf16[47,128]{1,0:T(8,128)(2,1)S(1)}, bf16[16,256,256]{2,1,0:T(8,128)(2,1)S(1)}) custom-call(s32[1]{0:T(128)S(6)} %copy.14.live, bf16[1,128,256]{2,1,0:T(8,128)(2,1)S(1)} %bitcast.13, s32[1,16]{1,0:T(1,128)} %refs_0_.1, s32[1,16]{1,0:T(1,128)} %refs_1_.1, ...), custom_call_target="tpu_custom_call" | custom-call | flops 1048576 | bytes 1048576 | tf_op jit(solution)/shard_map/pallas_call | solution.py:27
  16.8 3.3 %collective-permute-done.3 = bf16[2,128,256]{2,1,0:T(8,128)(2,1)S(1)} collective-permute-done((bf16[2,128,256]{2,1,0:T(8,128)(2,1)S(1)}, bf16[2,128,256]{2,1,0:T(8,128)(2,1)S(1)}, u32[]{:S(2)}, u32[]{:S(2)}) %collective-permute-start.3) | collective-permute-done | bytes 131104 | tf_op jit(solution)/shard_map/ppermute | solution.py:163
  20.1 2.3 %collective-permute-done.4 = bf16[2,128,256]{2,1,0:T(8,128)(2,1)S(1)} collective-permute-done((bf16[2,128,256]{2,1,0:T(8,128)(2,1)S(1)}, bf16[2,128,256]{2,1,0:T(8,128)(2,1)S(1)}, u32[]{:S(2)}, u32[]{:S(2)}) %collective-permute-start.4) | collective-permute-done | bytes 131104 | tf_op jit(solution)/shard_map/ppermute | solution.py:163
  22.5 0.3 collective-permute-done.5
  22.8 0.1 collective-permute-start.6
  22.9 1.8 %collective-permute-done.6.rest_2_ = bf16[7,128,256]{2,1,0:T(8,128)(2,1)S(1)} collective-permute-done((bf16[7,128,256]{2,1,0:T(8,128)(2,1)S(1)}, bf16[7,128,256]{2,1,0:T(8,128)(2,1)S(1)}, u32[]{:S(2)}, u32[]{:S(2)}) %collective-permute-start.6) | collective-permute-done | bytes 458784 | tf_op jit(solution)/shard_map/ppermute | solution.py:163
  24.7 1.4 %shard_map.103 = (f32[136,256]{1,0:T(8,128)S(1)}, f32[136,256]{1,0:T(8,128)S(1)}) custom-call(s32[32]{0:T(128)S(1)} %get-tuple-element.35.plan, bf16[16,256,256]{2,1,0:T(8,128)(2,1)S(1)} %get-tuple-element.36.tiles, bf16[2,128,256]{2,1,0:T(8,128)(2,1)S(1)} %pad_maximum_fusion.1.rest_0_, bf16[7,128,256]{2,1,0:T(8,128)(2,1)S(1)} %constant_dynamic-update-slice_fusion.rest_1_, ...), custom_call_target="tpu_custom_call" | custom-call | flops 1048576 | bytes 1048576 | tf_op jit(solution)/shard_map/pallas_call | solution.py:27
  26.0 1.6 %collective-permute-start.7 = (f32[136,256]{1,0:T(8,128)S(1)}, f32[136,256]{1,0:T(8,128)S(1)}, u32[]{:S(2)}, u32[]{:S(2)}) collective-permute-start(f32[136,256]{1,0:T(8,128)S(1)} %get-tuple-element.39), channel_id=1, source_target_pairs={{1,0},{0,1},{3,2},{2,3},{5,4},{4,5},{7,6},{6,7},{9,8},{8,9},{11,10... | collective-permute-start | bytes 417800 | tf_op jit(solution)/shard_map/ppermute | solution.py:159
  27.6 4.2 %collective-permute-done.7.rest_0_ = f32[136,256]{1,0:T(8,128)S(1)} collective-permute-done((f32[136,256]{1,0:T(8,128)S(1)}, f32[136,256]{1,0:T(8,128)S(1)}, u32[]{:S(2)}, u32[]{:S(2)}) %collective-permute-start.7) | collective-permute-done | bytes 139296 | tf_op jit(solution)/shard_map/ppermute | solution.py:159
  31.8 0.2 shard_map.104
  32.0 0.0 collective-permute-start.8
  32.1 2.3 %collective-permute-start.9 = (bf16[48,256]{1,0:T(8,128)(2,1)S(1)}, bf16[48,256]{1,0:T(8,128)(2,1)S(1)}, u32[]{:S(2)}, u32[]{:S(2)}) collective-permute-start(bf16[48,256]{1,0:T(8,128)(2,1)S(1)} %get-tuple-element.40.classes_in), channel_id=1, source_target_pairs={{24,0},{26,2},{28,4},{30,6},{16,8},{18,10},{20,12},{22,14},{8,16},... | collective-permute-start | bytes 73736 | tf_op jit(solution)/shard_map/ppermute | solution.py:163
  34.3 0.0 collective-permute-done.8
  34.3 0.1 collective-permute-start.10
  34.4 3.4 %collective-permute-start.11 = (bf16[2,48,256]{2,1,0:T(8,128)(2,1)S(1)}, bf16[2,48,256]{2,1,0:T(8,128)(2,1)S(1)}, u32[]{:S(2)}, u32[]{:S(2)}) collective-permute-start(bf16[2,48,256]{2,1,0:T(8,128)(2,1)S(1)} %pad_maximum_fusion.2.rest_0_), channel_id=1, source_target_pairs={{20,0},{10,2},{16,4},{14,6},{28,8},{2,10},{24,12},{6,14},{4,16},{2... | collective-permute-start | bytes 147464 | tf_op jit(solution)/shard_map/ppermute | solution.py:163
  37.8 0.0 collective-permute-start.12
  37.8 0.0 collective-permute-done.9
  37.8 1.7 %collective-permute-done.10 = bf16[2,48,256]{2,1,0:T(8,128)(2,1)S(1)} collective-permute-done((bf16[2,48,256]{2,1,0:T(8,128)(2,1)S(1)}, bf16[2,48,256]{2,1,0:T(8,128)(2,1)S(1)}, u32[]{:S(2)}, u32[]{:S(2)}) %collective-permute-start.10) | collective-permute-done | bytes 49184 | tf_op jit(solution)/shard_map/ppermute | solution.py:163
  39.5 1.5 %collective-permute-done.11 = bf16[2,48,256]{2,1,0:T(8,128)(2,1)S(1)} collective-permute-done((bf16[2,48,256]{2,1,0:T(8,128)(2,1)S(1)}, bf16[2,48,256]{2,1,0:T(8,128)(2,1)S(1)}, u32[]{:S(2)}, u32[]{:S(2)}) %collective-permute-start.11) | collective-permute-done | bytes 49184 | tf_op jit(solution)/shard_map/ppermute | solution.py:163
  41.0 1.8 %collective-permute-done.12 = bf16[2,48,256]{2,1,0:T(8,128)(2,1)S(1)} collective-permute-done((bf16[2,48,256]{2,1,0:T(8,128)(2,1)S(1)}, bf16[2,48,256]{2,1,0:T(8,128)(2,1)S(1)}, u32[]{:S(2)}, u32[]{:S(2)}) %collective-permute-start.12) | collective-permute-done | bytes 49184 | tf_op jit(solution)/shard_map/ppermute | solution.py:163
  42.8 0.1 collective-permute-start.13
  42.9 1.4 %collective-permute-done.13.rest_2_ = bf16[7,48,256]{2,1,0:T(8,128)(2,1)S(1)} collective-permute-done((bf16[7,48,256]{2,1,0:T(8,128)(2,1)S(1)}, bf16[7,48,256]{2,1,0:T(8,128)(2,1)S(1)}, u32[]{:S(2)}, u32[]{:S(2)}) %collective-permute-start.13) | collective-permute-done | bytes 172064 | tf_op jit(solution)/shard_map/ppermute | solution.py:163
  44.3 1.3 %shard_map.106 = (f32[48,256]{1,0:T(8,128)S(1)}, f32[48,256]{1,0:T(8,128)S(1)}) custom-call(s32[32]{0:T(128)S(1)} %get-tuple-element.35.plan, bf16[16,256,256]{2,1,0:T(8,128)(2,1)S(1)} %get-tuple-element.36.tiles, bf16[2,48,256]{2,1,0:T(8,128)(2,1)S(1)} %pad_maximum_fusion.2.rest_0_, bf16[7,48,256]{2,1,0:T(8,128)(2,1)S(1)} %pad_maximum_fusion.rest_1_, ...), custom_call_target="tpu_custom_call" | custom-call | flops 1048576 | bytes 1048576 | tf_op jit(solution)/shard_map/pallas_call | solution.py:27
  45.6 1.6 %collective-permute-start.14 = (f32[48,256]{1,0:T(8,128)S(1)}, f32[48,256]{1,0:T(8,128)S(1)}, u32[]{:S(2)}, u32[]{:S(2)}) collective-permute-start(f32[48,256]{1,0:T(8,128)S(1)} %get-tuple-element.44), channel_id=1, source_target_pairs={{1,0},{0,1},{3,2},{2,3},{5,4},{4,5},{7,6},{6,7},{9,8},{8,9},{11,10... | collective-permute-start | bytes 147464 | tf_op jit(solution)/shard_map/ppermute | solution.py:159
  47.1 2.6 %collective-permute-done.14.rest_0_ = f32[48,256]{1,0:T(8,128)S(1)} collective-permute-done((f32[48,256]{1,0:T(8,128)S(1)}, f32[48,256]{1,0:T(8,128)S(1)}, u32[]{:S(2)}, u32[]{:S(2)}) %collective-permute-start.14) | collective-permute-done | bytes 49184 | tf_op jit(solution)/shard_map/ppermute | solution.py:159
  49.7 0.7 %shard_map.107 = f32[47,256]{1,0:T(8,128)} custom-call(bf16[48,256]{1,0:T(8,128)(2,1)S(1)} %get-tuple-element.40.classes_in, f32[1,256]{1,0:T(1,128)S(1)} %get-tuple-element.41.scaling, f32[47,1]{1,0:T(8,128)S(1)} %get-tuple-element.42.bias, f32[48,256]{1,0:T(8,128)S(1)} %get-tuple-element.43.own, f32[48,256]{1,0:T(8,128)S(1)} %collective-permute-done.14.rest_0_), custom_call_target="tpu_custom_call" | custom-call | flops 1048576 | bytes 1048576 | tf_op jit(solution)/shard_map/pallas_call | solution.py:27
  (8 shorter events, 0.1 us)
Async XLA Ops:
  0.0 5.3 %collective-permute-start = (bf16[100,256]{1,0:T(8,128)(2,1)}, bf16[100,256]{1,0:T(8,128)(2,1)S(1)}, u32[]{:S(2)}, u32[]{:S(2)}) collective-permute-start(bf16[100,256]{1,0:T(8,128)(2,1)} %bitcast.19), channel_id=1, source_target_pairs={{1,0},{0,1},{3,2},{2,3},{5,4},{4,5},{7,6},{6,7},{9,8},{8,9},{11,10... | collective-permute-start | bytes 153608 | tf_op jit(solution)/shard_map/ppermute | solution.py:159
  5.5 4.3 %collective-permute-start.2 = (bf16[128,256]{1,0:T(8,128)(2,1)S(1)}, bf16[128,256]{1,0:T(8,128)(2,1)S(1)}, u32[]{:S(2)}, u32[]{:S(2)}) collective-permute-start(bf16[128,256]{1,0:T(8,128)(2,1)S(1)} %shard_map.101.hidden_in), channel_id=1, source_target_pairs={{2,0},{0,2},{6,4},{4,6},{10,8},{8,10},{14,12},{12,14},{18,16},{16,... | collective-permute-start | bytes 196616 | tf_op jit(solution)/shard_map/ppermute | solution.py:163
  5.6 8.9 %collective-permute-start.1 = (bf16[128,256]{1,0:T(8,128)(2,1)S(1)}, bf16[128,256]{1,0:T(8,128)(2,1)S(1)}, u32[]{:S(2)}, u32[]{:S(2)}) collective-permute-start(bf16[128,256]{1,0:T(8,128)(2,1)S(1)} %shard_map.101.hidden_in), channel_id=1, source_target_pairs={{24,0},{26,2},{28,4},{30,6},{16,8},{18,10},{20,12},{22,14},{8,16},... | collective-permute-start | bytes 196616 | tf_op jit(solution)/shard_map/ppermute | solution.py:163
  9.8 10.3 %collective-permute-start.3 = (bf16[2,128,256]{2,1,0:T(8,128)(2,1)S(1)}, bf16[2,128,256]{2,1,0:T(8,128)(2,1)S(1)}, u32[]{:S(2)}, u32[]{:S(2)}) collective-permute-start(bf16[2,128,256]{2,1,0:T(8,128)(2,1)S(1)} %pad_maximum_fusion.1.rest_0_), channel_id=1, source_target_pairs={{16,0},{30,2},{20,4},{26,6},{24,8},{22,10},{28,12},{18,14},{0,16},... | collective-permute-start | bytes 393224 | tf_op jit(solution)/shard_map/ppermute | solution.py:163
  10.7 11.7 %collective-permute-start.4 = (bf16[2,128,256]{2,1,0:T(8,128)(2,1)S(1)}, bf16[2,128,256]{2,1,0:T(8,128)(2,1)S(1)}, u32[]{:S(2)}, u32[]{:S(2)}) collective-permute-start(bf16[2,128,256]{2,1,0:T(8,128)(2,1)S(1)} %pad_maximum_fusion.1.rest_0_), channel_id=1, source_target_pairs={{20,0},{10,2},{16,4},{14,6},{28,8},{2,10},{24,12},{6,14},{4,16},{2... | collective-permute-start | bytes 393224 | tf_op jit(solution)/shard_map/ppermute | solution.py:163
  14.5 8.3 %collective-permute-start.5 = (bf16[2,128,256]{2,1,0:T(8,128)(2,1)S(1)}, bf16[2,128,256]{2,1,0:T(8,128)(2,1)S(1)}, u32[]{:S(2)}, u32[]{:S(2)}) collective-permute-start(bf16[2,128,256]{2,1,0:T(8,128)(2,1)S(1)} %pad_maximum_fusion.1.rest_0_), channel_id=1, source_target_pairs={{12,0},{6,2},{8,4},{2,6},{4,8},{14,10},{0,12},{10,14},{28,16},{22,... | collective-permute-start | bytes 393224 | tf_op jit(solution)/shard_map/ppermute | solution.py:163
  22.8 1.9 %collective-permute-start.6 = (bf16[7,128,256]{2,1,0:T(8,128)(2,1)S(1)}, bf16[7,128,256]{2,1,0:T(8,128)(2,1)S(1)}, u32[]{:S(2)}, u32[]{:S(2)}) collective-permute-start(bf16[7,128,256]{2,1,0:T(8,128)(2,1)S(1)} %constant_dynamic-update-slice_fusion.rest_1_), channel_id=1, source_target_pairs={{2,0},{0,2},{6,4},{4,6},{10,8},{8,10},{14,12},{12,14},{18,16},{16,... | collective-permute-start | bytes 1376264 | tf_op jit(solution)/shard_map/ppermute | solution.py:163
  26.0 5.8 %collective-permute-start.7 = (f32[136,256]{1,0:T(8,128)S(1)}, f32[136,256]{1,0:T(8,128)S(1)}, u32[]{:S(2)}, u32[]{:S(2)}) collective-permute-start(f32[136,256]{1,0:T(8,128)S(1)} %get-tuple-element.39), channel_id=1, source_target_pairs={{1,0},{0,1},{3,2},{2,3},{5,4},{4,5},{7,6},{6,7},{9,8},{8,9},{11,10... | collective-permute-start | bytes 417800 | tf_op jit(solution)/shard_map/ppermute | solution.py:159
  32.0 2.3 %collective-permute-start.8 = (bf16[48,256]{1,0:T(8,128)(2,1)S(1)}, bf16[48,256]{1,0:T(8,128)(2,1)S(1)}, u32[]{:S(2)}, u32[]{:S(2)}) collective-permute-start(bf16[48,256]{1,0:T(8,128)(2,1)S(1)} %get-tuple-element.40.classes_in), channel_id=1, source_target_pairs={{2,0},{0,2},{6,4},{4,6},{10,8},{8,10},{14,12},{12,14},{18,16},{16,... | collective-permute-start | bytes 73736 | tf_op jit(solution)/shard_map/ppermute | solution.py:163
  32.1 5.7 %collective-permute-start.9 = (bf16[48,256]{1,0:T(8,128)(2,1)S(1)}, bf16[48,256]{1,0:T(8,128)(2,1)S(1)}, u32[]{:S(2)}, u32[]{:S(2)}) collective-permute-start(bf16[48,256]{1,0:T(8,128)(2,1)S(1)} %get-tuple-element.40.classes_in), channel_id=1, source_target_pairs={{24,0},{26,2},{28,4},{30,6},{16,8},{18,10},{20,12},{22,14},{8,16},... | collective-permute-start | bytes 73736 | tf_op jit(solution)/shard_map/ppermute | solution.py:163
  34.3 5.2 %collective-permute-start.10 = (bf16[2,48,256]{2,1,0:T(8,128)(2,1)S(1)}, bf16[2,48,256]{2,1,0:T(8,128)(2,1)S(1)}, u32[]{:S(2)}, u32[]{:S(2)}) collective-permute-start(bf16[2,48,256]{2,1,0:T(8,128)(2,1)S(1)} %pad_maximum_fusion.2.rest_0_), channel_id=1, source_target_pairs={{16,0},{30,2},{20,4},{26,6},{24,8},{22,10},{28,12},{18,14},{0,16},... | collective-permute-start | bytes 147464 | tf_op jit(solution)/shard_map/ppermute | solution.py:163
  34.4 6.6 %collective-permute-start.11 = (bf16[2,48,256]{2,1,0:T(8,128)(2,1)S(1)}, bf16[2,48,256]{2,1,0:T(8,128)(2,1)S(1)}, u32[]{:S(2)}, u32[]{:S(2)}) collective-permute-start(bf16[2,48,256]{2,1,0:T(8,128)(2,1)S(1)} %pad_maximum_fusion.2.rest_0_), channel_id=1, source_target_pairs={{20,0},{10,2},{16,4},{14,6},{28,8},{2,10},{24,12},{6,14},{4,16},{2... | collective-permute-start | bytes 147464 | tf_op jit(solution)/shard_map/ppermute | solution.py:163
  37.8 5.0 %collective-permute-start.12 = (bf16[2,48,256]{2,1,0:T(8,128)(2,1)S(1)}, bf16[2,48,256]{2,1,0:T(8,128)(2,1)S(1)}, u32[]{:S(2)}, u32[]{:S(2)}) collective-permute-start(bf16[2,48,256]{2,1,0:T(8,128)(2,1)S(1)} %pad_maximum_fusion.2.rest_0_), channel_id=1, source_target_pairs={{12,0},{6,2},{8,4},{2,6},{4,8},{14,10},{0,12},{10,14},{28,16},{22,... | collective-permute-start | bytes 147464 | tf_op jit(solution)/shard_map/ppermute | solution.py:163
  42.8 1.5 %collective-permute-start.13 = (bf16[7,48,256]{2,1,0:T(8,128)(2,1)S(1)}, bf16[7,48,256]{2,1,0:T(8,128)(2,1)S(1)}, u32[]{:S(2)}, u32[]{:S(2)}) collective-permute-start(bf16[7,48,256]{2,1,0:T(8,128)(2,1)S(1)} %pad_maximum_fusion.rest_1_), channel_id=1, source_target_pairs={{2,0},{0,2},{6,4},{4,6},{10,8},{8,10},{14,12},{12,14},{18,16},{16,... | collective-permute-start | bytes 516104 | tf_op jit(solution)/shard_map/ppermute | solution.py:163
  45.6 4.2 %collective-permute-start.14 = (f32[48,256]{1,0:T(8,128)S(1)}, f32[48,256]{1,0:T(8,128)S(1)}, u32[]{:S(2)}, u32[]{:S(2)}) collective-permute-start(f32[48,256]{1,0:T(8,128)S(1)} %get-tuple-element.44), channel_id=1, source_target_pairs={{1,0},{0,1},{3,2},{2,3},{5,4},{4,5},{7,6},{6,7},{9,8},{8,9},{11,10... | collective-permute-start | bytes 147464 | tf_op jit(solution)/shard_map/ppermute | solution.py:159

commit v6 on v5

--- a/solution.py
+++ b/solution.py
@@ -22,7 +22,7 @@
 
 
 def call(kernel, outs, smem=(), vmem=(), hbm=(), scratch=(), smem_outs=0, cost=1 << 20):
-    spaces = [pltpu.SMEM] * len(smem) + [pltpu.VMEM] * len(vmem) + [pltpu.HBM] * len(hbm)
+    spaces = [pltpu.VMEM] * len(vmem) + [pltpu.SMEM] * len(smem) + [pltpu.HBM] * len(hbm)
     out_spaces = [pltpu.SMEM] * smem_outs + [pltpu.VMEM] * (len(outs) - smem_outs)
     return pl.pallas_call(
         kernel,
@@ -32,7 +32,7 @@
         scratch_shapes=scratch,
         compiler_params=pltpu.CompilerParams(vmem_limit_bytes=VMEM_LIMIT),
         cost_estimate=pl.CostEstimate(flops=cost, bytes_accessed=cost, transcendentals=0),
-    )(*smem, *vmem, *[pltpu.with_memory_space_constraint(value, pltpu.HBM) for value in hbm])
+    )(*vmem, *smem, *[pltpu.with_memory_space_constraint(value, pltpu.HBM) for value in hbm])
 
 
 def fetched(sources, targets, sems):
@@ -76,11 +76,12 @@
     out[...] = total.astype(BF16)
 
 
-def stage(reps, places, live, _, *refs):
-    sources, (plan, bias_1, bias_2, weight, tiles), scratch = refs[:6], refs[6:11], refs[11:]
+def stage(reps, places, arrived, live, *refs):
+    sources, (plan, bias_1, bias_2, weight, tiles), scratch = refs[:6], refs[6:11], refs[12:]
     rows_in, columns_in, row_1, row_2, sems = scratch
     slots = tiles.shape[0]
     copies = fetched(sources, (rows_in, columns_in, row_1, row_2, weight, tiles), sems)
+    refs[11][...] = arrived[...]
     for copy in copies[:4]:
         copy.wait()
     bias_1[...] = jnp.broadcast_to(row_1[...], (8, row_1.shape[1])).T[:, :1]
@@ -101,8 +102,8 @@
         copy.wait()
 
 
-def aggregate(count_rows, plan, tiles, *rest):
-    parts, outs, panels = rest[:3], rest[3:-1], rest[-1]
+def aggregate(count_rows, *refs):
+    parts, (tiles, plan), outs, panels = refs[:3], refs[3:5], refs[5:-1], refs[-1]
     slots, tile = tiles.shape[0], tiles.shape[1]
     height = panels.shape[1]
     extra = ONES_ROWS if count_rows else 0
@@ -163,34 +164,46 @@
     return lax.ppermute(value, "blk", [(d ^ masks[d % 2], d) for d in range(lax.axis_size("blk"))])
 
 
-def chip_order(chips):
-    far = [step for step in range(chips - 1, 0, -1) if step % 2 == 0]
-    near = [step for step in range(chips - 1, 0, -1) if step % 2]
-    order = sorted(far + near, key=lambda step: (step < chips // 2, step % 2, -step))
-    return order[0], list(zip(order[1::2], order[2::2]))
-
-
-def panel_places(chips):
-    first, pairs = chip_order(chips)
+def outer_order(outer):
+    first = outer // 2
+    rest = [step for step in range(outer - 1, 0, -1) if step != first]
+    return first, list(zip(rest[0::2], rest[1::2]))
+
+
+def panel_places(outer):
+    first, pairs = outer_order(outer)
+    lists = []
+    for core in range(2):
+        across = [4 * pair[core] + e for pair in pairs for e in range(2)]
+        over = [2, 4 * first + 2] + [apart + 2 for apart in across]
+        lists.append([4 * first, *across, *over])
     tables = []
     for core in range(2):
-        near = [2 * first] + [2 * pair[core] + e for pair in pairs for e in range(2)]
-        far = [2 * first + 1] + [2 * pair[1 - core] + 1 - e for pair in pairs for e in range(2)]
-        stack = [0, 1, *near, *far]
-        tables.append([stack.index(apart) for apart in range(2 * chips)])
+        stack = [0, 1, *lists[core], *[apart ^ 1 for apart in lists[1 - core]]]
+        tables.append([stack.index(apart) for apart in range(4 * outer)])
     return tables
 
 
+def packed(*parts):
+    def pack(*refs):
+        for index, ref in enumerate(refs[:-1]):
+            refs[-1][index] = ref[...]
+
+    return call(pack, [jax.ShapeDtypeStruct((len(parts), *parts[0].shape), BF16)], vmem=parts, cost=1 << 32)[0]
+
+
 def gather_blocks(value, aside):
-    chips = lax.axis_size("blk") // 2
-    first, pairs = chip_order(chips)
-    parts = [swapped(value, (2 * first, 2 * first))[None]]
+    outer = lax.axis_size("blk") // 4
+    first, pairs = outer_order(outer)
     other = swapped(value, (1, 1))
+    ahead = swapped(value, (4 * first, 4 * first))
     both = jnp.stack([value, other])
-    for pair in pairs:
-        parts.append(swapped(both, (2 * pair[0], 2 * pair[1])))
-    parts[0], beside = lax.optimization_barrier(aside(parts[0]))
-    near = jnp.concatenate(parts)
+    across = [swapped(both, (4 * pair[0], 4 * pair[1])) for pair in pairs]
+    across = across[0] if len(across) == 1 else jnp.concatenate(across)
+    over = swapped(packed(value, ahead), (2, 2))
+    beyond = swapped(across, (2, 2))
+    over, beside = aside(over)
+    near = jnp.concatenate([ahead[None], across, over, beyond])
     return (both, near, swapped(near, (1, 1))), beside
 
 
@@ -234,13 +247,14 @@
     (hidden_in,) = call(order_project, [shape((hidden, tile), BF16)], vmem=(*prepared, *others))
     def staged(arrived):
         values = call(
-            functools.partial(stage, reps, panel_places(blocks // 2)),
+            functools.partial(stage, reps, panel_places(blocks // 4)),
             [
                 shape((2 * slots,), jnp.int32),
                 shape((hidden, 1), F32),
                 shape((classes, 1), F32),
                 shape((classes, hidden), BF16),
                 shape(tile_values.shape[1:], BF16),
+                shape(arrived.shape, BF16),
             ],
             smem=(tile_live,),
             vmem=(arrived,),
@@ -260,8 +274,9 @@
                 pltpu.SemaphoreType.DMA((6,)),
             ],
             smem_outs=1,
+            cost=1 << 28,
         )
-        return arrived, values
+        return values[-1], values[:-1]
 
     def relayed(arrived):
         return call(relay, [shape(arrived.shape, BF16)], vmem=(arrived,), cost=1 << 28)[0], ()
@@ -271,7 +286,7 @@
             functools.partial(aggregate, count_rows),
             [shape((rows, tile), F32)] * reps,
             smem=(plan,),
-            vmem=(tiles, *parts),
+            vmem=(*parts, tiles),
             scratch=[pltpu.VMEM((blocks, *parts[0].shape[1:]), BF16)],
         )
         return [sums[0]] + [shifted(sums[reps - step], "rep", step) for step in range(1, reps)]

time: 50.6 us -> 50.7 us (level)
  starting transfers between devices: 20.2 us -> 23.8 us
  waiting for transfers between devices: 22 us -> 18.5 us
    ppermute x12, starting transfers between devices: 14.1 us -> 17.7 us  [swapped(): lax.ppermute(value, 'blk', [(d ^ masks[d % 2], d) for d in range(lax.axis...]
    ppermute x12, waiting for transfers between devices: 14.1 us -> 10.6 us  [swapped(): lax.ppermute(value, 'blk', [(d ^ masks[d % 2], d) for d in range(lax.axis...]
    pallas_call x8 -> x10, Pallas kernels: 7.36 us -> 7.37 us  [call(): pl.pallas_call(kernel, out_shape=outs, in_specs=[pl.BlockSpec(memory_spac...]
where the time goes in v6:
time: 50.7 us; the launch traced here: 50.5 us
  starting transfers between devices  23.8 us (47%)
  waiting for transfers between devices  18.5 us (36%)
  Pallas kernels  7.37 us (15%)
  between operations  0.76 us (1%)
    ppermute x12, starting transfers between devices, swapped(): lax.ppermute(value, 'blk', [(d ^ masks[d % 2], d) for d in range(lax.axis...  17.7 us
    ppermute x12, waiting for transfers between devices, swapped(): lax.ppermute(value, 'blk', [(d ^ masks[d % 2], d) for d in range(lax.axis...  10.6 us
    ppermute x3, waiting for transfers between devices, shifted(): lax.ppermute(value, axis, [((d + step) % size, d) for d in range(size)])  7.85 us
    pallas_call x10, Pallas kernels, call(): pl.pallas_call(kernel, out_shape=outs, in_specs=[pl.BlockSpec(memory_spac...  7.37 us
    ppermute x3, starting transfers between devices, shifted(): lax.ppermute(value, axis, [((d + step) % size, d) for d in range(size)])  6.13 us
  transfers between devices with their start and end apart: 15, of which 11 were waited for; matrix products, arithmetic and copies ran while one was open for 0% of the time, Pallas kernels for 7%

profile of v6, /device:TPU:0, one launch (start us, length us, event | category | flops | bytes accessed | tf_op | source)
XLA Modules:
  0.0 50.5 jit_solution(11984806353671260455)
XLA Ops:
  0.0 2.9 %collective-permute-start = (bf16[100,256]{1,0:T(8,128)(2,1)}, bf16[100,256]{1,0:T(8,128)(2,1)S(1)}, u32[]{:S(2)}, u32[]{:S(2)}) collective-permute-start(bf16[100,256]{1,0:T(8,128)(2,1)} %bitcast.18), channel_id=1, source_target_pairs={{1,0},{0,1},{3,2},{2,3},{5,4},{4,5},{7,6},{6,7},{9,8},{8,9},{11,10... | collective-permute-start | bytes 153608 | tf_op jit(solution)/shard_map/ppermute | solution.py:160
  2.9 1.2 %shard_map.100 = (bf16[128,256]{1,0:T(8,128)(2,1)S(1)}, s32[1,256]{1,0:T(1,128)S(1)}, bf16[128,100]{1,0:T(8,128)(2,1)S(1)}) custom-call(s32[1,512]{1,0:T(1,128)} %order.1, bf16[100,256]{1,0:T(8,128)(2,1)} %bitcast.19, bf16[100,128]{1,0:T(8,128)(2,1)} %weight.1), custom_call_target="tpu_custom_call" | custom-call | flops 1048576 | bytes 1048576 | tf_op jit(solution)/shard_map/pallas_call | solution.py:27
  4.2 1.1 %collective-permute-done.rest_0_ = bf16[100,256]{1,0:T(8,128)(2,1)S(1)} collective-permute-done((bf16[100,256]{1,0:T(8,128)(2,1)}, bf16[100,256]{1,0:T(8,128)(2,1)S(1)}, u32[]{:S(2)}, u32[]{:S(2)}) %collective-permute-start) | collective-permute-done | bytes 51232 | tf_op jit(solution)/shard_map/ppermute | solution.py:160
  5.3 0.3 shard_map.101.refs_0_.hidden_in
  5.5 0.1 collective-permute-start.3
  5.6 3.2 %collective-permute-start.1 = (bf16[128,256]{1,0:T(8,128)(2,1)S(1)}, bf16[128,256]{1,0:T(8,128)(2,1)S(1)}, u32[]{:S(2)}, u32[]{:S(2)}) collective-permute-start(bf16[128,256]{1,0:T(8,128)(2,1)S(1)} %shard_map.101.refs_0_.hidden_in), channel_id=1, source_target_pairs={{16,0},{18,2},{20,4},{22,6},{24,8},{26,10},{28,12},{30,14},{0,16},... | collective-permute-start | bytes 196616 | tf_op jit(solution)/shard_map/ppermute | solution.py:164
  8.8 0.0 collective-permute-done.3
  8.8 2.2 %collective-permute-start.4 = (bf16[2,128,256]{2,1,0:T(8,128)(2,1)S(1)}, bf16[2,128,256]{2,1,0:T(8,128)(2,1)S(1)}, u32[]{:S(2)}, u32[]{:S(2)}) collective-permute-start(bf16[2,128,256]{2,1,0:T(8,128)(2,1)S(1)} %pad_maximum_fusion.2.refs_0_), channel_id=1, source_target_pairs={{24,0},{10,2},{28,4},{14,6},{16,8},{2,10},{20,12},{6,14},{8,16},{2... | collective-permute-start | bytes 393224 | tf_op jit(solution)/shard_map/ppermute | solution.py:164
  11.1 1.7 %collective-permute-done.1.refs_1_ = bf16[128,256]{1,0:T(8,128)(2,1)S(1)} collective-permute-done((bf16[128,256]{1,0:T(8,128)(2,1)S(1)}, bf16[128,256]{1,0:T(8,128)(2,1)S(1)}, u32[]{:S(2)}, u32[]{:S(2)}) %collective-permute-start.1) | collective-permute-done | bytes 65568 | tf_op jit(solution)/shard_map/ppermute | solution.py:164
  12.8 1.7 %collective-permute-start.2 = (bf16[2,128,256]{2,1,0:T(8,128)(2,1)S(1)}, bf16[2,128,256]{2,1,0:T(8,128)(2,1)S(1)}, u32[]{:S(2)}, u32[]{:S(2)}) collective-permute-start(bf16[2,128,256]{2,1,0:T(8,128)(2,1)S(1)} %shard_map.102), channel_id=1, source_target_pairs={{4,0},{6,2},{0,4},{2,6},{12,8},{14,10},{8,12},{10,14},{20,16},{22,... | collective-permute-start | bytes 393224 | tf_op jit(solution)/shard_map/ppermute | solution.py:164
  14.6 1.2 %collective-permute-done.4 = bf16[2,128,256]{2,1,0:T(8,128)(2,1)S(1)} collective-permute-done((bf16[2,128,256]{2,1,0:T(8,128)(2,1)S(1)}, bf16[2,128,256]{2,1,0:T(8,128)(2,1)S(1)}, u32[]{:S(2)}, u32[]{:S(2)}) %collective-permute-start.4) | collective-permute-done | bytes 131104 | tf_op jit(solution)/shard_map/ppermute | solution.py:164
  15.8 1.5 %collective-permute-start.5 = (bf16[2,128,256]{2,1,0:T(8,128)(2,1)S(1)}, bf16[2,128,256]{2,1,0:T(8,128)(2,1)S(1)}, u32[]{:S(2)}, u32[]{:S(2)}) collective-permute-start(bf16[2,128,256]{2,1,0:T(8,128)(2,1)S(1)} %collective-permute-done.4), channel_id=1, source_target_pairs={{4,0},{6,2},{0,4},{2,6},{12,8},{14,10},{8,12},{10,14},{20,16},{22,... | collective-permute-start | bytes 393224 | tf_op jit(solution)/shard_map/ppermute | solution.py:164
  17.9 0.6 %collective-permute-done.2.arrived = bf16[2,128,256]{2,1,0:T(8,128)(2,1)S(1)} collective-permute-done((bf16[2,128,256]{2,1,0:T(8,128)(2,1)S(1)}, bf16[2,128,256]{2,1,0:T(8,128)(2,1)S(1)}, u32[]{:S(2)}, u32[]{:S(2)}) %collective-permute-start.2) | collective-permute-done | bytes 131104 | tf_op jit(solution)/shard_map/ppermute | solution.py:164
  18.5 2.3 %shard_map.103 = (s32[32]{0:T(128)S(1)}, f32[128,1]{1,0:T(8,128)S(1)}, f32[47,1]{1,0:T(8,128)S(1)}, bf16[47,128]{1,0:T(8,128)(2,1)S(1)}, bf16[16,256,256]{2,1,0:...) custom-call(bf16[2,128,256]{2,1,0:T(8,128)(2,1)S(1)} %collective-permute-done.2.arrived, s32[1]{0:T(128)S(6)} %copy.11.live, ...), custom_call_target="tpu_custom_call" | custom-call | flops 268435456 | bytes 268435456 | tf_op jit(solution)/shard_map/pallas_call | solution.py:27
  20.8 0.0 collective-permute-done.5
  20.8 0.1 pad_maximum_fusion.refs_1_
  20.9 0.1 collective-permute-start.6
  21.0 1.8 %collective-permute-done.6.refs_2_ = bf16[7,128,256]{2,1,0:T(8,128)(2,1)S(1)} collective-permute-done((bf16[7,128,256]{2,1,0:T(8,128)(2,1)S(1)}, bf16[7,128,256]{2,1,0:T(8,128)(2,1)S(1)}, u32[]{:S(2)}, u32[]{:S(2)}) %collective-permute-start.6) | collective-permute-done | bytes 458784 | tf_op jit(solution)/shard_map/ppermute | solution.py:164
  22.8 1.4 %shard_map.104 = (f32[136,256]{1,0:T(8,128)S(1)}, f32[136,256]{1,0:T(8,128)S(1)}) custom-call(bf16[2,128,256]{2,1,0:T(8,128)(2,1)S(1)} %pad_maximum_fusion.2.refs_0_, bf16[7,128,256]{2,1,0:T(8,128)(2,1)S(1)} %pad_maximum_fusion.refs_1_, bf16[7,128,256]{2,1,0:T(8,128)(2,1)S(1)} %collective-permute-done.6.refs_2_, ...), custom_call_target="tpu_custom_call" | custom-call | flops 1048576 | bytes 1048576 | tf_op jit(solution)/shard_map/pallas_call | solution.py:27
  24.1 1.6 %collective-permute-start.7 = (f32[136,256]{1,0:T(8,128)S(1)}, f32[136,256]{1,0:T(8,128)S(1)}, u32[]{:S(2)}, u32[]{:S(2)}) collective-permute-start(f32[136,256]{1,0:T(8,128)S(1)} %get-tuple-element.29), channel_id=1, source_target_pairs={{1,0},{0,1},{3,2},{2,3},{5,4},{4,5},{7,6},{6,7},{9,8},{8,9},{11,10... | collective-permute-start | bytes 417800 | tf_op jit(solution)/shard_map/ppermute | solution.py:160
  25.8 4.2 %collective-permute-done.7.rest_0_ = f32[136,256]{1,0:T(8,128)S(1)} collective-permute-done((f32[136,256]{1,0:T(8,128)S(1)}, f32[136,256]{1,0:T(8,128)S(1)}, u32[]{:S(2)}, u32[]{:S(2)}) %collective-permute-start.7) | collective-permute-done | bytes 139296 | tf_op jit(solution)/shard_map/ppermute | solution.py:160
  29.9 0.2 shard_map.105
  30.1 0.0 collective-permute-start.8
  30.1 2.6 %collective-permute-start.9 = (bf16[48,256]{1,0:T(8,128)(2,1)S(1)}, bf16[48,256]{1,0:T(8,128)(2,1)S(1)}, u32[]{:S(2)}, u32[]{:S(2)}) collective-permute-start(bf16[48,256]{1,0:T(8,128)(2,1)S(1)} %get-tuple-element.30.refs_0_.classes_in), channel_id=1, source_target_pairs={{16,0},{18,2},{20,4},{22,6},{24,8},{26,10},{28,12},{30,14},{0,16},... | collective-permute-start | bytes 73736 | tf_op jit(solution)/shard_map/ppermute | solution.py:164
  32.8 0.0 collective-permute-done.8
  32.8 3.1 %collective-permute-start.10 = (bf16[2,48,256]{2,1,0:T(8,128)(2,1)S(1)}, bf16[2,48,256]{2,1,0:T(8,128)(2,1)S(1)}, u32[]{:S(2)}, u32[]{:S(2)}) collective-permute-start(bf16[2,48,256]{2,1,0:T(8,128)(2,1)S(1)} %pad_maximum_fusion.3.refs_0_), channel_id=1, source_target_pairs={{24,0},{10,2},{28,4},{14,6},{16,8},{2,10},{20,12},{6,14},{8,16},{2... | collective-permute-start | bytes 147464 | tf_op jit(solution)/shard_map/ppermute | solution.py:164
  35.8 0.0 collective-permute-done.9.refs_1_
  35.9 1.6 %collective-permute-start.11 = (bf16[2,48,256]{2,1,0:T(8,128)(2,1)S(1)}, bf16[2,48,256]{2,1,0:T(8,128)(2,1)S(1)}, u32[]{:S(2)}, u32[]{:S(2)}) collective-permute-start(bf16[2,48,256]{2,1,0:T(8,128)(2,1)S(1)} %shard_map.106), channel_id=1, source_target_pairs={{4,0},{6,2},{0,4},{2,6},{12,8},{14,10},{8,12},{10,14},{20,16},{22,... | collective-permute-start | bytes 147464 | tf_op jit(solution)/shard_map/ppermute | solution.py:164
  37.4 1.3 %collective-permute-done.10 = bf16[2,48,256]{2,1,0:T(8,128)(2,1)S(1)} collective-permute-done((bf16[2,48,256]{2,1,0:T(8,128)(2,1)S(1)}, bf16[2,48,256]{2,1,0:T(8,128)(2,1)S(1)}, u32[]{:S(2)}, u32[]{:S(2)}) %collective-permute-start.10) | collective-permute-done | bytes 49184 | tf_op jit(solution)/shard_map/ppermute | solution.py:164
  38.8 1.5 %collective-permute-start.12 = (bf16[2,48,256]{2,1,0:T(8,128)(2,1)S(1)}, bf16[2,48,256]{2,1,0:T(8,128)(2,1)S(1)}, u32[]{:S(2)}, u32[]{:S(2)}) collective-permute-start(bf16[2,48,256]{2,1,0:T(8,128)(2,1)S(1)} %collective-permute-done.10), channel_id=1, source_target_pairs={{4,0},{6,2},{0,4},{2,6},{12,8},{14,10},{8,12},{10,14},{20,16},{22,... | collective-permute-start | bytes 147464 | tf_op jit(solution)/shard_map/ppermute | solution.py:164
  40.3 0.1 collective-permute-done.11.arrived
  40.4 2.5 %collective-permute-done.12 = bf16[2,48,256]{2,1,0:T(8,128)(2,1)S(1)} collective-permute-done((bf16[2,48,256]{2,1,0:T(8,128)(2,1)S(1)}, bf16[2,48,256]{2,1,0:T(8,128)(2,1)S(1)}, u32[]{:S(2)}, u32[]{:S(2)}) %collective-permute-start.12) | collective-permute-done | bytes 49184 | tf_op jit(solution)/shard_map/ppermute | solution.py:164
  42.9 0.1 collective-permute-start.13
  43.0 1.4 %collective-permute-done.13.refs_2_ = bf16[7,48,256]{2,1,0:T(8,128)(2,1)S(1)} collective-permute-done((bf16[7,48,256]{2,1,0:T(8,128)(2,1)S(1)}, bf16[7,48,256]{2,1,0:T(8,128)(2,1)S(1)}, u32[]{:S(2)}, u32[]{:S(2)}) %collective-permute-start.13) | collective-permute-done | bytes 172064 | tf_op jit(solution)/shard_map/ppermute | solution.py:164
  44.4 1.3 %shard_map.108 = (f32[48,256]{1,0:T(8,128)S(1)}, f32[48,256]{1,0:T(8,128)S(1)}) custom-call(bf16[2,48,256]{2,1,0:T(8,128)(2,1)S(1)} %pad_maximum_fusion.3.refs_0_, bf16[7,48,256]{2,1,0:T(8,128)(2,1)S(1)} %pad_maximum_fusion.1.refs_1_, bf16[7,48,256]{2,1,0:T(8,128)(2,1)S(1)} %collective-permute-done.13.refs_2_, ...), custom_call_target="tpu_custom_call" | custom-call | flops 1048576 | bytes 1048576 | tf_op jit(solution)/shard_map/pallas_call | solution.py:27
  45.7 1.6 %collective-permute-start.14 = (f32[48,256]{1,0:T(8,128)S(1)}, f32[48,256]{1,0:T(8,128)S(1)}, u32[]{:S(2)}, u32[]{:S(2)}) collective-permute-start(f32[48,256]{1,0:T(8,128)S(1)} %get-tuple-element.34), channel_id=1, source_target_pairs={{1,0},{0,1},{3,2},{2,3},{5,4},{4,5},{7,6},{6,7},{9,8},{8,9},{11,10... | collective-permute-start | bytes 147464 | tf_op jit(solution)/shard_map/ppermute | solution.py:160
  47.2 2.6 %collective-permute-done.14.rest_0_ = f32[48,256]{1,0:T(8,128)S(1)} collective-permute-done((f32[48,256]{1,0:T(8,128)S(1)}, f32[48,256]{1,0:T(8,128)S(1)}, u32[]{:S(2)}, u32[]{:S(2)}) %collective-permute-start.14) | collective-permute-done | bytes 49184 | tf_op jit(solution)/shard_map/ppermute | solution.py:160
  49.8 0.7 %shard_map.109 = f32[47,256]{1,0:T(8,128)} custom-call(bf16[48,256]{1,0:T(8,128)(2,1)S(1)} %get-tuple-element.30.refs_0_.classes_in, f32[1,256]{1,0:T(1,128)S(1)} %get-tuple-element.31.scaling, f32[47,1]{1,0:T(8,128)S(1)} %get-tuple-element.32.bias, f32[48,256]{1,0:T(8,128)S(1)} %get-tuple-element.33.own, f32[48,256]{1,0:T(8,128)S(1)} %collective-permute-done.14.rest_0_), custom_call_target="tpu_custom_call" | custom-call | flops 1048576 | bytes 1048576 | tf_op jit(solution)/shard_map/pallas_call | solution.py:27
  (6 shorter events, 0.1 us)
Async XLA Ops:
  0.0 5.3 %collective-permute-start = (bf16[100,256]{1,0:T(8,128)(2,1)}, bf16[100,256]{1,0:T(8,128)(2,1)S(1)}, u32[]{:S(2)}, u32[]{:S(2)}) collective-permute-start(bf16[100,256]{1,0:T(8,128)(2,1)} %bitcast.18), channel_id=1, source_target_pairs={{1,0},{0,1},{3,2},{2,3},{5,4},{4,5},{7,6},{6,7},{9,8},{8,9},{11,10... | collective-permute-start | bytes 153608 | tf_op jit(solution)/shard_map/ppermute | solution.py:160
  5.5 3.3 %collective-permute-start.3 = (bf16[128,256]{1,0:T(8,128)(2,1)S(1)}, bf16[128,256]{1,0:T(8,128)(2,1)S(1)}, u32[]{:S(2)}, u32[]{:S(2)}) collective-permute-start(bf16[128,256]{1,0:T(8,128)(2,1)S(1)} %shard_map.101.refs_0_.hidden_in), channel_id=1, source_target_pairs={{2,0},{0,2},{6,4},{4,6},{10,8},{8,10},{14,12},{12,14},{18,16},{16,... | collective-permute-start | bytes 196616 | tf_op jit(solution)/shard_map/ppermute | solution.py:164
  5.6 7.2 %collective-permute-start.1 = (bf16[128,256]{1,0:T(8,128)(2,1)S(1)}, bf16[128,256]{1,0:T(8,128)(2,1)S(1)}, u32[]{:S(2)}, u32[]{:S(2)}) collective-permute-start(bf16[128,256]{1,0:T(8,128)(2,1)S(1)} %shard_map.101.refs_0_.hidden_in), channel_id=1, source_target_pairs={{16,0},{18,2},{20,4},{22,6},{24,8},{26,10},{28,12},{30,14},{0,16},... | collective-permute-start | bytes 196616 | tf_op jit(solution)/shard_map/ppermute | solution.py:164
  8.8 6.9 %collective-permute-start.4 = (bf16[2,128,256]{2,1,0:T(8,128)(2,1)S(1)}, bf16[2,128,256]{2,1,0:T(8,128)(2,1)S(1)}, u32[]{:S(2)}, u32[]{:S(2)}) collective-permute-start(bf16[2,128,256]{2,1,0:T(8,128)(2,1)S(1)} %pad_maximum_fusion.2.refs_0_), channel_id=1, source_target_pairs={{24,0},{10,2},{28,4},{14,6},{16,8},{2,10},{20,12},{6,14},{8,16},{2... | collective-permute-start | bytes 393224 | tf_op jit(solution)/shard_map/ppermute | solution.py:164
  12.8 5.7 %collective-permute-start.2 = (bf16[2,128,256]{2,1,0:T(8,128)(2,1)S(1)}, bf16[2,128,256]{2,1,0:T(8,128)(2,1)S(1)}, u32[]{:S(2)}, u32[]{:S(2)}) collective-permute-start(bf16[2,128,256]{2,1,0:T(8,128)(2,1)S(1)} %shard_map.102), channel_id=1, source_target_pairs={{4,0},{6,2},{0,4},{2,6},{12,8},{14,10},{8,12},{10,14},{20,16},{22,... | collective-permute-start | bytes 393224 | tf_op jit(solution)/shard_map/ppermute | solution.py:164
  15.8 5.0 %collective-permute-start.5 = (bf16[2,128,256]{2,1,0:T(8,128)(2,1)S(1)}, bf16[2,128,256]{2,1,0:T(8,128)(2,1)S(1)}, u32[]{:S(2)}, u32[]{:S(2)}) collective-permute-start(bf16[2,128,256]{2,1,0:T(8,128)(2,1)S(1)} %collective-permute-done.4), channel_id=1, source_target_pairs={{4,0},{6,2},{0,4},{2,6},{12,8},{14,10},{8,12},{10,14},{20,16},{22,... | collective-permute-start | bytes 393224 | tf_op jit(solution)/shard_map/ppermute | solution.py:164
  20.9 1.9 %collective-permute-start.6 = (bf16[7,128,256]{2,1,0:T(8,128)(2,1)S(1)}, bf16[7,128,256]{2,1,0:T(8,128)(2,1)S(1)}, u32[]{:S(2)}, u32[]{:S(2)}) collective-permute-start(bf16[7,128,256]{2,1,0:T(8,128)(2,1)S(1)} %pad_maximum_fusion.refs_1_), channel_id=1, source_target_pairs={{2,0},{0,2},{6,4},{4,6},{10,8},{8,10},{14,12},{12,14},{18,16},{16,... | collective-permute-start | bytes 1376264 | tf_op jit(solution)/shard_map/ppermute | solution.py:164
  24.1 5.8 %collective-permute-start.7 = (f32[136,256]{1,0:T(8,128)S(1)}, f32[136,256]{1,0:T(8,128)S(1)}, u32[]{:S(2)}, u32[]{:S(2)}) collective-permute-start(f32[136,256]{1,0:T(8,128)S(1)} %get-tuple-element.29), channel_id=1, source_target_pairs={{1,0},{0,1},{3,2},{2,3},{5,4},{4,5},{7,6},{6,7},{9,8},{8,9},{11,10... | collective-permute-start | bytes 417800 | tf_op jit(solution)/shard_map/ppermute | solution.py:160
  30.1 2.6 %collective-permute-start.8 = (bf16[48,256]{1,0:T(8,128)(2,1)S(1)}, bf16[48,256]{1,0:T(8,128)(2,1)S(1)}, u32[]{:S(2)}, u32[]{:S(2)}) collective-permute-start(bf16[48,256]{1,0:T(8,128)(2,1)S(1)} %get-tuple-element.30.refs_0_.classes_in), channel_id=1, source_target_pairs={{2,0},{0,2},{6,4},{4,6},{10,8},{8,10},{14,12},{12,14},{18,16},{16,... | collective-permute-start | bytes 73736 | tf_op jit(solution)/shard_map/ppermute | solution.py:164
  30.1 5.7 %collective-permute-start.9 = (bf16[48,256]{1,0:T(8,128)(2,1)S(1)}, bf16[48,256]{1,0:T(8,128)(2,1)S(1)}, u32[]{:S(2)}, u32[]{:S(2)}) collective-permute-start(bf16[48,256]{1,0:T(8,128)(2,1)S(1)} %get-tuple-element.30.refs_0_.classes_in), channel_id=1, source_target_pairs={{16,0},{18,2},{20,4},{22,6},{24,8},{26,10},{28,12},{30,14},{0,16},... | collective-permute-start | bytes 73736 | tf_op jit(solution)/shard_map/ppermute | solution.py:164
  32.8 6.0 %collective-permute-start.10 = (bf16[2,48,256]{2,1,0:T(8,128)(2,1)S(1)}, bf16[2,48,256]{2,1,0:T(8,128)(2,1)S(1)}, u32[]{:S(2)}, u32[]{:S(2)}) collective-permute-start(bf16[2,48,256]{2,1,0:T(8,128)(2,1)S(1)} %pad_maximum_fusion.3.refs_0_), channel_id=1, source_target_pairs={{24,0},{10,2},{28,4},{14,6},{16,8},{2,10},{20,12},{6,14},{8,16},{2... | collective-permute-start | bytes 147464 | tf_op jit(solution)/shard_map/ppermute | solution.py:164
  35.9 4.5 %collective-permute-start.11 = (bf16[2,48,256]{2,1,0:T(8,128)(2,1)S(1)}, bf16[2,48,256]{2,1,0:T(8,128)(2,1)S(1)}, u32[]{:S(2)}, u32[]{:S(2)}) collective-permute-start(bf16[2,48,256]{2,1,0:T(8,128)(2,1)S(1)} %shard_map.106), channel_id=1, source_target_pairs={{4,0},{6,2},{0,4},{2,6},{12,8},{14,10},{8,12},{10,14},{20,16},{22,... | collective-permute-start | bytes 147464 | tf_op jit(solution)/shard_map/ppermute | solution.py:164
  38.8 4.1 %collective-permute-start.12 = (bf16[2,48,256]{2,1,0:T(8,128)(2,1)S(1)}, bf16[2,48,256]{2,1,0:T(8,128)(2,1)S(1)}, u32[]{:S(2)}, u32[]{:S(2)}) collective-permute-start(bf16[2,48,256]{2,1,0:T(8,128)(2,1)S(1)} %collective-permute-done.10), channel_id=1, source_target_pairs={{4,0},{6,2},{0,4},{2,6},{12,8},{14,10},{8,12},{10,14},{20,16},{22,... | collective-permute-start | bytes 147464 | tf_op jit(solution)/shard_map/ppermute | solution.py:164
  42.9 1.5 %collective-permute-start.13 = (bf16[7,48,256]{2,1,0:T(8,128)(2,1)S(1)}, bf16[7,48,256]{2,1,0:T(8,128)(2,1)S(1)}, u32[]{:S(2)}, u32[]{:S(2)}) collective-permute-start(bf16[7,48,256]{2,1,0:T(8,128)(2,1)S(1)} %pad_maximum_fusion.1.refs_1_), channel_id=1, source_target_pairs={{2,0},{0,2},{6,4},{4,6},{10,8},{8,10},{14,12},{12,14},{18,16},{16,... | collective-permute-start | bytes 516104 | tf_op jit(solution)/shard_map/ppermute | solution.py:164
  45.7 4.2 %collective-permute-start.14 = (f32[48,256]{1,0:T(8,128)S(1)}, f32[48,256]{1,0:T(8,128)S(1)}, u32[]{:S(2)}, u32[]{:S(2)}) collective-permute-start(f32[48,256]{1,0:T(8,128)S(1)} %get-tuple-element.34), channel_id=1, source_target_pairs={{1,0},{0,1},{3,2},{2,3},{5,4},{4,5},{7,6},{6,7},{9,8},{8,9},{11,10... | collective-permute-start | bytes 147464 | tf_op jit(solution)/shard_map/ppermute | solution.py:160

commit v7 on v6

v7 whole, which is shorter than its diff:
```python
import functools

import jax
import jax.numpy as jnp
from jax import lax
from jax.experimental import pallas as pl
from jax.experimental.pallas import tpu as pltpu
from jax.sharding import PartitionSpec as P

BF16 = jnp.bfloat16
F32 = jnp.float32
ONES_ROWS = 16
VMEM_LIMIT = 32 * 1024 * 1024


def nn(a, b):
    return lax.dot_general(a, b, (((1,), (0,)), ((), ())), preferred_element_type=F32)


def nt(a, b):
    return lax.dot_general(a, b, (((1,), (1,)), ((), ())), preferred_element_type=F32)


def call(kernel, outs, smem=(), vmem=(), hbm=(), scratch=(), smem_outs=0, cost=1 << 20):
    spaces = [pltpu.VMEM] * len(vmem) + [pltpu.SMEM] * len(smem) + [pltpu.HBM] * len(hbm)
    out_spaces = [pltpu.SMEM] * smem_outs + [pltpu.VMEM] * (len(outs) - smem_outs)
    return pl.pallas_call(
        kernel,
        out_shape=outs,
        in_specs=[pl.BlockSpec(memory_space=space) for space in spaces],
        out_specs=[pl.BlockSpec(memory_space=space) for space in out_spaces],
        scratch_shapes=scratch,
        compiler_params=pltpu.CompilerParams(vmem_limit_bytes=VMEM_LIMIT),
        cost_estimate=pl.CostEstimate(flops=cost, bytes_accessed=cost, transcendentals=0),
    )(*vmem, *smem, *[pltpu.with_memory_space_constraint(value, pltpu.HBM) for value in hbm])


def fetched(sources, targets, sems):
    copies = [
        pltpu.make_async_copy(source, target, sems.at[index])
        for index, (source, target) in enumerate(zip(sources, targets))
    ]
    for copy in copies:
        copy.start()
    return copies


def picked(features, wanted, owner):
    tile = features.shape[1]
    source = lax.broadcasted_iota(jnp.int32, (tile, tile), 0) + owner * tile
    return nn(features[...], jnp.where(source == wanted, 1.0, 0.0).astype(BF16))


def prepare(order, features, part, wanted_out, *rest):
    order_in, features_in, sems = rest
    for copy in fetched((order, features), (order_in, features_in), sems):
        copy.wait()
    tile = features.shape[1]
    member = lax.axis_index("rep")
    wanted = order_in[:, pl.ds(pl.multiple_of(member * tile, tile), tile)]
    wanted_out[...] = wanted
    part[...] = picked(features_in, wanted, member)


def arrange(part, wanted, *rest):
    *features, out = rest
    reps = len(features) + 1
    member = lax.axis_index("rep")
    total = part[...]
    for step in range(1, reps):
        owner = lax.rem(member + step, reps)
        total = total + picked(features[step - 1], wanted[...], owner)
    out[...] = total.astype(BF16)


def stage(reps, _, live, *refs):
    sources, (plan, bias_1, bias_2, weight_1, weight_2, tiles), scratch = refs[:7], refs[7:13], refs[13:]
    rows_in, columns_in, row_1, row_2, weight_in, sems = scratch
    slots = tiles.shape[0]
    blocks = lax.axis_size("blk")
    copies = fetched(sources, (rows_in, columns_in, row_1, row_2, weight_in, weight_2, tiles), sems)
    for copy in copies[:5]:
        copy.wait()
    bias_1[...] = jnp.broadcast_to(row_1[...], (8, row_1.shape[1])).T[:, :1]
    bias_2[...] = jnp.broadcast_to(row_2[...], (8, row_2.shape[1])).T[:, :1]
    weight_1[...] = weight_in[...].astype(F32).T.astype(BF16)
    block, member = lax.axis_index("blk"), lax.axis_index("rep")
    for slot in range(slots):
        plan[slot] = lax.clamp(0, columns_in[0, slot] // reps, blocks - 1) ^ block
        local = rows_in[0, slot] - block * reps
        step = lax.rem(local - member + reps, reps)
        plan[slots + slot] = jnp.where((slot < live[0]) & (local >= 0) & (local < reps), step, -1)
    for copy in copies[5:]:
        copy.wait()


def project(weight_t, *refs):
    *stacks, out = refs
    start = 0
    for stack in stacks:
        for index in range(stack.shape[0]):
            out[start + index] = nn(weight_t[...], stack[index]).astype(BF16)
        start += stack.shape[0]


def summed(panels, plan, tiles, count, extra):
    slots, tile = tiles.shape[0], tiles.shape[1]
    height = panels.shape[1] + extra
    total = jnp.zeros((count * height, tile), F32)
    for slot in range(slots):
        values = panels[plan[slot]]
        pieces = []
        for step in range(count):
            used = (plan[slots + slot] == step).astype(F32)
            pieces.append(values * used.astype(BF16))
            if extra:
                pieces.append(jnp.full((extra, tile), used, F32).astype(BF16))
        total = total + nt(jnp.concatenate(pieces, axis=0), tiles[slot])
    return [total[step * height : (step + 1) * height] for step in range(count)]


def in_thirds(row):
    first = row.astype(BF16).astype(F32)
    second = (row - first).astype(BF16).astype(F32)
    return first, second, row - first - second


def aggregate_hidden(projected, far, weight_t, tiles, plan, own, *rest):
    others, panels = rest[:-1], rest[-1]
    mine, opposite = panel_order(panels.shape[0] // 4, lax.axis_index("blk") % 2)
    for index, place in enumerate(mine):
        panels[place] = projected[index]
    for index, place in enumerate(opposite):
        panels[place] = nn(weight_t[...], far[index]).astype(BF16)
    height = panels.shape[1]
    sums = summed(panels, plan, tiles, 1 + len(others), ONES_ROWS)
    own[...] = sums[0][: own.shape[0]]
    row = lax.broadcasted_iota(jnp.int32, (ONES_ROWS, tiles.shape[1]), 0)
    for part, out in zip(sums[1:], others):
        first, second, third = in_thirds(part[height:])
        degree = jnp.where(row == 0, first, jnp.where(row == 1, second, jnp.where(row == 2, third, 0.0)))
        out[...] = jnp.concatenate([part[:height], degree], axis=0).astype(BF16)


def aggregate_classes(near, far, tiles, plan, *rest):
    outs, panels = rest[:-1], rest[-1]
    chip = lax.axis_index("blk") // 2
    for index in range(near.shape[0]):
        panels[2 * (index ^ chip)] = near[index]
        panels[2 * (index ^ chip) + 1] = far[index]
    for out, part in zip(outs, summed(panels, plan, tiles, len(outs), 0)):
        out[...] = part


def combine(hidden_in, bias, weight_t, own, *rest):
    *arrived, out, scale_out = rest
    height = hidden_in.shape[1]
    total, degree = own[:height], own[height : height + 1]
    for part in arrived:
        values = part[...].astype(F32)
        total = total + values[:height]
        terms = [values[height + index : height + index + 1] for index in range(3)]
        degree = degree + (terms[0] + (terms[1] + terms[2]))
    scaling = lax.rsqrt(1.0 + degree)
    hidden = scaling * (total + hidden_in[0].astype(F32)) + bias[...]
    hidden = jnp.maximum(hidden, 0.0).astype(BF16)
    classes = nn(weight_t[...], hidden)
    blank = jnp.zeros((out.shape[0] - classes.shape[0], classes.shape[1]), F32)
    out[...] = jnp.concatenate([classes, blank], axis=0).astype(BF16)
    scale_out[...] = scaling


def finish(classes_in, scaling, bias, own, *rest):
    *arrived, out = rest
    total = own[...]
    for part in arrived:
        total = total + part[...]
    classes = out.shape[0]
    whole = total + classes_in[...].astype(F32)
    out[...] = scaling[...] * whole[:classes] + bias[...]


def shifted(value, axis, step):
    size = lax.axis_size(axis)
    return lax.ppermute(value, axis, [((d + step) % size, d) for d in range(size)])


def swapped(value, masks):
    return lax.ppermute(value, "blk", [(d ^ masks[d % 2], d) for d in range(lax.axis_size("blk"))])


def outer_order(outer):
    first = outer // 2
    rest = [step for step in range(outer - 1, 0, -1) if step != first]
    return first, list(zip(rest[0::2], rest[1::2]))


def panel_order(outer, core):
    first, pairs = outer_order(outer)
    lists = []
    for here in (core, 1 - core):
        across = [jnp.where(here == 0, 4 * pair[0], 4 * pair[1]) + e for pair in pairs for e in range(2)]
        lists.append([4 * first, *across, 2, 4 * first + 2, *[apart + 2 for apart in across]])
    return [0, 1, *lists[0]], [apart ^ 1 for apart in lists[1]]


def packed(parts, after):
    def pack(*refs):
        for index in range(len(parts)):
            refs[-1][index] = refs[index][...]

    out = jax.ShapeDtypeStruct((len(parts), *parts[0].shape), BF16)
    return call(pack, [out], vmem=(*parts, after), cost=1 << 32)[0]


def gather_features(value, aside):
    outer = lax.axis_size("blk") // 4
    first, pairs = outer_order(outer)
    other = swapped(value, (1, 1))
    ahead = swapped(value, (4 * first, 4 * first))
    both = jnp.stack([value, other])
    beside = aside(both)
    across = [swapped(both, (4 * pair[0], 4 * pair[1])) for pair in pairs]
    across = across[0] if len(across) == 1 else jnp.concatenate(across)
    over = swapped(packed((value, ahead), beside[1]), (2, 2))
    beyond = swapped(across, (2, 2))
    near = jnp.concatenate([ahead[None], across, over, beyond])
    return (both, near, swapped(near, (1, 1))), beside


def gather_classes(value):
    size = lax.axis_size("blk")
    groups = [list(range(core, size, 2)) for core in range(2)]
    copies = jnp.broadcast_to(value[None], (size // 2, *value.shape))
    near = lax.all_to_all(copies, "blk", 0, 0, axis_index_groups=groups)
    return near, swapped(near, (1, 1))


def body(
    features,
    node_order,
    tile_values,
    tile_rows,
    tile_columns,
    tile_live,
    first_weight,
    first_bias,
    second_weight,
    second_bias,
):
    tile, width = features.shape
    slots = tile_values.shape[1]
    reps = lax.axis_size("rep")
    blocks = lax.axis_size("blk")
    hidden, classes = second_weight.shape
    padded = -(-classes // 16) * 16
    shape = jax.ShapeDtypeStruct

    def exchanged(sums):
        return [shifted(sums[reps - 1 - step], "rep", step) for step in range(1, reps)]

    own_t = features.T
    others = [shifted(own_t, "rep", step) for step in range(1, reps)]
    prepared = call(
        prepare,
        [shape((width, tile), F32), shape((1, tile), jnp.int32)],
        hbm=(node_order, own_t),
        scratch=[
            pltpu.VMEM(node_order.shape, jnp.int32),
            pltpu.VMEM(own_t.shape, BF16),
            pltpu.SemaphoreType.DMA((2,)),
        ],
    )
    (ordered,) = call(arrange, [shape((width, tile), BF16)], vmem=(*prepared, *others))

    def staged(after):
        return call(
            functools.partial(stage, reps),
            [
                shape((2 * slots,), jnp.int32),
                shape((hidden, 1), F32),
                shape((classes, 1), F32),
                shape((hidden, width), BF16),
                shape((classes, hidden), BF16),
                shape(tile_values.shape[1:], BF16),
            ],
            vmem=(after,),
            smem=(tile_live,),
            hbm=(
                tile_rows,
                tile_columns,
                first_bias[None],
                second_bias[None],
                first_weight,
                second_weight.T,
                tile_values[0],
            ),
            scratch=[
                pltpu.SMEM((1, slots), jnp.int32),
                pltpu.SMEM((1, slots), jnp.int32),
                pltpu.VMEM((1, hidden), F32),
                pltpu.VMEM((1, classes), F32),
                pltpu.VMEM(first_weight.shape, BF16),
                pltpu.SemaphoreType.DMA((7,)),
            ],
            smem_outs=1,
        )

    (both, near, far), values = gather_features(ordered, staged)
    plan, bias_1, bias_2, weight_1, weight_2, tiles = values
    (projected,) = call(
        project,
        [shape((2 + near.shape[0], hidden, tile), BF16)],
        vmem=(weight_1, both, near),
    )
    own, *sums = call(
        aggregate_hidden,
        [shape((hidden + 8, tile), F32)] + [shape((hidden + ONES_ROWS, tile), BF16)] * (reps - 1),
        vmem=(projected, far, weight_1, tiles),
        smem=(plan,),
        scratch=[pltpu.VMEM((blocks, hidden, tile), BF16)],
    )
    classes_in, scaling = call(
        combine,
        [shape((padded, tile), BF16), shape((1, tile), F32)],
        vmem=(projected, bias_1, weight_2, own, *exchanged(sums)),
    )
    own, *sums = call(
        aggregate_classes,
        [shape((padded, tile), F32)] * reps,
        vmem=(*gather_classes(classes_in), tiles),
        smem=(plan,),
        scratch=[pltpu.VMEM((blocks, padded, tile), BF16)],
    )
    (logits,) = call(
        finish,
        [shape((classes, tile), F32)],
        vmem=(classes_in, scaling, bias_2, own, *exchanged(sums)),
    )
    return logits.T


def solution(mesh):
    placed = (
        P(("blk", "rep"), None),
        P("blk", None),
        P(("blk", "rep"), None, None, None),
        P(("blk", "rep"), None),
        P(("blk", "rep"), None),
        P(("blk", "rep")),
        P(),
        P(),
        P(),
        P(),
    )
    return jax.shard_map(
        body, mesh=mesh, in_specs=placed, out_specs=P(("blk", "rep"), None), check_vma=False
    )
```

time: 50.7 us -> 49.8 us (0.982)
  blocking collectives: 0 us -> 13.1 us
  starting transfers between devices: 23.8 us -> 14.1 us
  waiting for transfers between devices: 18.5 us -> 13.9 us
    all_to_all x0 -> x1, blocking collectives: none -> 13.1 us  [gather_classes(): near = lax.all_to_all(copies, 'blk', 0, 0, axis_index_groups=groups)]
    ppermute x12 -> x7, starting transfers between devices: 17.7 us -> 8.02 us  [swapped(): lax.ppermute(value, 'blk', [(d ^ masks[d % 2], d) for d in range(lax.axis...]
    ppermute x12 -> x7, waiting for transfers between devices: 10.6 us -> 7.16 us  [swapped(): lax.ppermute(value, 'blk', [(d ^ masks[d % 2], d) for d in range(lax.axis...]
    ppermute x3, waiting for transfers between devices: 7.85 us -> 6.74 us  [shifted(): lax.ppermute(value, axis, [((d + step) % size, d) for d in range(size)])]
    pallas_call x10 -> x9, Pallas kernels: 7.37 us -> 7.62 us  [call(): pl.pallas_call(kernel, out_shape=outs, in_specs=[pl.BlockSpec(memory_spac...]
  transfers between devices with their start and end apart: 15 -> 10, of which waited for: 11 -> 8; matrix products, arithmetic and copies ran while one was open for 0% -> 0% of each run, Pallas kernels for 7% -> 7%
where the time goes in v7:
time: 49.8 us; the launch traced here: 49.5 us
  starting transfers between devices  14.1 us (28%)
  waiting for transfers between devices  13.9 us (28%)
  blocking collectives  13.1 us (26%)
  Pallas kernels  7.62 us (15%)
  between operations  0.75 us (2%)
    all_to_all x1, blocking collectives, gather_classes(): near = lax.all_to_all(copies, 'blk', 0, 0, axis_index_groups=groups)  13.1 us
    ppermute x7, starting transfers between devices, swapped(): lax.ppermute(value, 'blk', [(d ^ masks[d % 2], d) for d in range(lax.axis...  8.02 us
    pallas_call x9, Pallas kernels, call(): pl.pallas_call(kernel, out_shape=outs, in_specs=[pl.BlockSpec(memory_spac...  7.62 us
    ppermute x7, waiting for transfers between devices, swapped(): lax.ppermute(value, 'blk', [(d ^ masks[d % 2], d) for d in range(lax.axis...  7.16 us
    ppermute x3, waiting for transfers between devices, shifted(): lax.ppermute(value, axis, [((d + step) % size, d) for d in range(size)])  6.74 us
    ppermute x3, starting transfers between devices, shifted(): lax.ppermute(value, axis, [((d + step) % size, d) for d in range(size)])  6.05 us
  transfers between devices with their start and end apart: 10, of which 8 were waited for; matrix products, arithmetic and copies ran while one was open for 0% of the time, Pallas kernels for 7%

profile of v7, /device:TPU:0, one launch (start us, length us, event | category | flops | bytes accessed | tf_op | source)
XLA Modules:
  0.0 49.5 jit_solution(9963336683203399215)
XLA Ops:
  0.0 2.9 %collective-permute-start = (bf16[100,256]{1,0:T(8,128)(2,1)}, bf16[100,256]{1,0:T(8,128)(2,1)S(1)}, u32[]{:S(2)}, u32[]{:S(2)}) collective-permute-start(bf16[100,256]{1,0:T(8,128)(2,1)} %bitcast.12), channel_id=1, source_target_pairs={{1,0},{0,1},{3,2},{2,3},{5,4},{4,5},{7,6},{6,7},{9,8},{8,9},{11,10... | collective-permute-start | bytes 153608 | tf_op jit(solution)/shard_map/ppermute | solution.py:185
  2.9 1.0 %shard_map.100 = (f32[100,256]{1,0:T(8,128)S(1)}, s32[1,256]{1,0:T(1,128)S(1)}) custom-call(s32[1,512]{1,0:T(1,128)} %order.1, bf16[100,256]{1,0:T(8,128)(2,1)} %bitcast.13), custom_call_target="tpu_custom_call" | custom-call | flops 1048576 | bytes 1048576 | tf_op jit(solution)/shard_map/pallas_call | solution.py:27
  4.0 1.3 %collective-permute-done.rest_0_ = bf16[100,256]{1,0:T(8,128)(2,1)S(1)} collective-permute-done((bf16[100,256]{1,0:T(8,128)(2,1)}, bf16[100,256]{1,0:T(8,128)(2,1)S(1)}, u32[]{:S(2)}, u32[]{:S(2)}) %collective-permute-start) | collective-permute-done | bytes 51232 | tf_op jit(solution)/shard_map/ppermute | solution.py:185
  5.3 0.2 shard_map.101.refs_0_
  5.4 0.1 collective-permute-start.1
  6.2 3.2 %collective-permute-start.2 = (bf16[100,256]{1,0:T(8,128)(2,1)S(1)}, bf16[100,256]{1,0:T(8,128)(2,1)S(1)}, u32[]{:S(2)}, u32[]{:S(2)}) collective-permute-start(bf16[100,256]{1,0:T(8,128)(2,1)S(1)} %shard_map.101.refs_0_), channel_id=1, source_target_pairs={{16,0},{18,2},{20,4},{22,6},{24,8},{26,10},{28,12},{30,14},{0,16},... | collective-permute-start | bytes 153608 | tf_op jit(solution)/shard_map/ppermute | solution.py:189
  9.3 0.0 collective-permute-done.1
  9.4 1.6 %collective-permute-start.3 = (bf16[2,100,256]{2,1,0:T(8,128)(2,1)S(1)}, bf16[2,100,256]{2,1,0:T(8,128)(2,1)S(1)}, u32[]{:S(2)}, u32[]{:S(2)}) collective-permute-start(bf16[2,100,256]{2,1,0:T(8,128)(2,1)S(1)} %pad_maximum_fusion.1._.refs_0_), channel_id=1, source_target_pairs={{24,0},{10,2},{28,4},{14,6},{16,8},{2,10},{20,12},{6,14},{8,16},{2... | collective-permute-start | bytes 307208 | tf_op jit(solution)/shard_map/ppermute | solution.py:189
  11.0 2.3 %shard_map.102 = (s32[32]{0:T(128)S(1)}, f32[128,1]{1,0:T(8,128)S(1)}, f32[47,1]{1,0:T(8,128)S(1)}, bf16[128,100]{1,0:T(8,128)(2,1)S(1)}, bf16[47,128]{1,0:T(8,1...) custom-call(bf16[2,100,256]{2,1,0:T(8,128)(2,1)S(1)} %pad_maximum_fusion.1._.refs_0_, s32[1]{0:T(128)S(6)} %copy.11.live, ...), custom_call_target="tpu_custom_call" | custom-call | flops 1048576 | bytes 1048576 | tf_op jit(solution)/shard_map/pallas_call | solution.py:27
  13.3 0.0 collective-permute-done.2.refs_1_
  13.3 1.6 %collective-permute-start.4 = (bf16[2,100,256]{2,1,0:T(8,128)(2,1)S(1)}, bf16[2,100,256]{2,1,0:T(8,128)(2,1)S(1)}, u32[]{:S(2)}, u32[]{:S(2)}) collective-permute-start(bf16[2,100,256]{2,1,0:T(8,128)(2,1)S(1)} %shard_map.103), channel_id=1, source_target_pairs={{4,0},{6,2},{0,4},{2,6},{12,8},{14,10},{8,12},{10,14},{20,16},{22,... | collective-permute-start | bytes 307208 | tf_op jit(solution)/shard_map/ppermute | solution.py:189
  14.9 1.2 %collective-permute-done.3 = bf16[2,100,256]{2,1,0:T(8,128)(2,1)S(1)} collective-permute-done((bf16[2,100,256]{2,1,0:T(8,128)(2,1)S(1)}, bf16[2,100,256]{2,1,0:T(8,128)(2,1)S(1)}, u32[]{:S(2)}, u32[]{:S(2)}) %collective-permute-start.3) | collective-permute-done | bytes 102432 | tf_op jit(solution)/shard_map/ppermute | solution.py:189
  16.0 1.5 %collective-permute-start.5 = (bf16[2,100,256]{2,1,0:T(8,128)(2,1)S(1)}, bf16[2,100,256]{2,1,0:T(8,128)(2,1)S(1)}, u32[]{:S(2)}, u32[]{:S(2)}) collective-permute-start(bf16[2,100,256]{2,1,0:T(8,128)(2,1)S(1)} %collective-permute-done.3), channel_id=1, source_target_pairs={{4,0},{6,2},{0,4},{2,6},{12,8},{14,10},{8,12},{10,14},{20,16},{22,... | collective-permute-start | bytes 307208 | tf_op jit(solution)/shard_map/ppermute | solution.py:189
  17.6 1.6 %collective-permute-done.4 = bf16[2,100,256]{2,1,0:T(8,128)(2,1)S(1)} collective-permute-done((bf16[2,100,256]{2,1,0:T(8,128)(2,1)S(1)}, bf16[2,100,256]{2,1,0:T(8,128)(2,1)S(1)}, u32[]{:S(2)}, u32[]{:S(2)}) %collective-permute-start.4) | collective-permute-done | bytes 102432 | tf_op jit(solution)/shard_map/ppermute | solution.py:189
  19.2 1.5 %collective-permute-done.5 = bf16[2,100,256]{2,1,0:T(8,128)(2,1)S(1)} collective-permute-done((bf16[2,100,256]{2,1,0:T(8,128)(2,1)S(1)}, bf16[2,100,256]{2,1,0:T(8,128)(2,1)S(1)}, u32[]{:S(2)}, u32[]{:S(2)}) %collective-permute-start.5) | collective-permute-done | bytes 102432 | tf_op jit(solution)/shard_map/ppermute | solution.py:189
  20.8 0.1 pad_maximum_fusion.refs_1_
  20.8 0.1 collective-permute-start.6
  20.9 0.3 shard_map.104.projected.hidden_in
  21.2 1.4 %collective-permute-done.6.far = bf16[7,100,256]{2,1,0:T(8,128)(2,1)S(1)} collective-permute-done((bf16[7,100,256]{2,1,0:T(8,128)(2,1)S(1)}, bf16[7,100,256]{2,1,0:T(8,128)(2,1)S(1)}, u32[]{:S(2)}, u32[]{:S(2)}) %collective-permute-start.6) | collective-permute-done | bytes 358432 | tf_op jit(solution)/shard_map/ppermute | solution.py:189
  22.6 1.6 %shard_map.105 = (f32[136,256]{1,0:T(8,128)S(1)}, bf16[144,256]{1,0:T(8,128)(2,1)S(1)}) custom-call(bf16[9,128,256]{2,1,0:T(8,128)(2,1)S(1)} %shard_map.104.projected.hidden_in, bf16[7,100,256]{2,1,0:T(8,128)(2,1)S(1)} %collective-permute-done.6.far, bf16[128,100]{1,0:T(8,128)(2,1)S(1)} %get-tuple-element.21.weight_t, ...), custom_call_target="tpu_custom_call" | custom-call | flops 1048576 | bytes 1048576 | tf_op jit(solution)/shard_map/pallas_call | solution.py:27
  24.2 1.6 %collective-permute-start.7 = (bf16[144,256]{1,0:T(8,128)(2,1)S(1)}, bf16[144,256]{1,0:T(8,128)(2,1)S(1)}, u32[]{:S(2)}, u32[]{:S(2)}) collective-permute-start(bf16[144,256]{1,0:T(8,128)(2,1)S(1)} %get-tuple-element.27), channel_id=1, source_target_pairs={{1,0},{0,1},{3,2},{2,3},{5,4},{4,5},{7,6},{6,7},{9,8},{8,9},{11,10... | collective-permute-start | bytes 221192 | tf_op jit(solution)/shard_map/ppermute | solution.py:185
  25.7 2.9 %collective-permute-done.7.rest_0_ = bf16[144,256]{1,0:T(8,128)(2,1)S(1)} collective-permute-done((bf16[144,256]{1,0:T(8,128)(2,1)S(1)}, bf16[144,256]{1,0:T(8,128)(2,1)S(1)}, u32[]{:S(2)}, u32[]{:S(2)}) %collective-permute-start.7) | collective-permute-done | bytes 73760 | tf_op jit(solution)/shard_map/ppermute | solution.py:185
  28.6 0.2 shard_map.106
  28.8 13.1 %all_to_all.5.near = bf16[8,48,256]{2,1,0:T(8,128)(2,1)S(1)} all-to-all(bf16[8,48,256]{2,1,0:T(8,128)(2,1)S(1)} %broadcast_in_dim.18), channel_id=1, replica_groups={{0,4,8,12,16,20,24,28},{2,6,10,14,18,22,26,30},{1,5,9,13,17,21,25,29},{..., dimensions={0} | all-to-all | bytes 393216 | tf_op jit(solution)/shard_map/all_to_all | solution.py:235
  41.9 0.0 collective-permute-start.8
  41.9 1.4 %collective-permute-done.8.far = bf16[8,48,256]{2,1,0:T(8,128)(2,1)S(1)} collective-permute-done((bf16[8,48,256]{2,1,0:T(8,128)(2,1)S(1)}, bf16[8,48,256]{2,1,0:T(8,128)(2,1)S(1)}, u32[]{:S(2)}, u32[]{:S(2)}) %collective-permute-start.8) | collective-permute-done | bytes 196640 | tf_op jit(solution)/shard_map/ppermute | solution.py:189
  43.4 1.3 %shard_map.107 = (f32[48,256]{1,0:T(8,128)S(1)}, f32[48,256]{1,0:T(8,128)S(1)}) custom-call(bf16[8,48,256]{2,1,0:T(8,128)(2,1)S(1)} %all_to_all.5.near, bf16[8,48,256]{2,1,0:T(8,128)(2,1)S(1)} %collective-permute-done.8.far, bf16[16,256,256]{2,1,0:T(8,128)(2,1)S(1)} %get-tuple-element.24.tiles, s32[32]{0:T(128)S(1)} %get-tuple-element.25.plan), custom_call_target="tpu_custom_call" | custom-call | flops 1048576 | bytes 1048576 | tf_op jit(solution)/shard_map/pallas_call | solution.py:27
  44.7 1.6 %collective-permute-start.9 = (f32[48,256]{1,0:T(8,128)S(1)}, f32[48,256]{1,0:T(8,128)S(1)}, u32[]{:S(2)}, u32[]{:S(2)}) collective-permute-start(f32[48,256]{1,0:T(8,128)S(1)} %get-tuple-element.32), channel_id=1, source_target_pairs={{1,0},{0,1},{3,2},{2,3},{5,4},{4,5},{7,6},{6,7},{9,8},{8,9},{11,10... | collective-permute-start | bytes 147464 | tf_op jit(solution)/shard_map/ppermute | solution.py:185
  46.2 2.6 %collective-permute-done.9.rest_0_ = f32[48,256]{1,0:T(8,128)S(1)} collective-permute-done((f32[48,256]{1,0:T(8,128)S(1)}, f32[48,256]{1,0:T(8,128)S(1)}, u32[]{:S(2)}, u32[]{:S(2)}) %collective-permute-start.9) | collective-permute-done | bytes 49184 | tf_op jit(solution)/shard_map/ppermute | solution.py:185
  48.8 0.7 %shard_map.108 = f32[47,256]{1,0:T(8,128)} custom-call(bf16[48,256]{1,0:T(8,128)(2,1)S(1)} %get-tuple-element.28.classes_in, f32[1,256]{1,0:T(1,128)S(1)} %get-tuple-element.29.scaling, f32[47,1]{1,0:T(8,128)S(1)} %get-tuple-element.30.bias, f32[48,256]{1,0:T(8,128)S(1)} %get-tuple-element.31.own, f32[48,256]{1,0:T(8,128)S(1)} %collective-permute-done.9.rest_0_), custom_call_target="tpu_custom_call" | custom-call | flops 1048576 | bytes 1048576 | tf_op jit(solution)/shard_map/pallas_call | solution.py:27
  (3 shorter events, 0.0 us)
Async XLA Ops:
  0.0 5.3 %collective-permute-start = (bf16[100,256]{1,0:T(8,128)(2,1)}, bf16[100,256]{1,0:T(8,128)(2,1)S(1)}, u32[]{:S(2)}, u32[]{:S(2)}) collective-permute-start(bf16[100,256]{1,0:T(8,128)(2,1)} %bitcast.12), channel_id=1, source_target_pairs={{1,0},{0,1},{3,2},{2,3},{5,4},{4,5},{7,6},{6,7},{9,8},{8,9},{11,10... | collective-permute-start | bytes 153608 | tf_op jit(solution)/shard_map/ppermute | solution.py:185
  5.4 3.9 %collective-permute-start.1 = (bf16[100,256]{1,0:T(8,128)(2,1)S(1)}, bf16[100,256]{1,0:T(8,128)(2,1)S(1)}, u32[]{:S(2)}, u32[]{:S(2)}) collective-permute-start(bf16[100,256]{1,0:T(8,128)(2,1)S(1)} %shard_map.101.refs_0_), channel_id=1, source_target_pairs={{2,0},{0,2},{6,4},{4,6},{10,8},{8,10},{14,12},{12,14},{18,16},{16,... | collective-permute-start | bytes 153608 | tf_op jit(solution)/shard_map/ppermute | solution.py:189
  6.2 7.1 %collective-permute-start.2 = (bf16[100,256]{1,0:T(8,128)(2,1)S(1)}, bf16[100,256]{1,0:T(8,128)(2,1)S(1)}, u32[]{:S(2)}, u32[]{:S(2)}) collective-permute-start(bf16[100,256]{1,0:T(8,128)(2,1)S(1)} %shard_map.101.refs_0_), channel_id=1, source_target_pairs={{16,0},{18,2},{20,4},{22,6},{24,8},{26,10},{28,12},{30,14},{0,16},... | collective-permute-start | bytes 153608 | tf_op jit(solution)/shard_map/ppermute | solution.py:189
  9.4 6.7 %collective-permute-start.3 = (bf16[2,100,256]{2,1,0:T(8,128)(2,1)S(1)}, bf16[2,100,256]{2,1,0:T(8,128)(2,1)S(1)}, u32[]{:S(2)}, u32[]{:S(2)}) collective-permute-start(bf16[2,100,256]{2,1,0:T(8,128)(2,1)S(1)} %pad_maximum_fusion.1._.refs_0_), channel_id=1, source_target_pairs={{24,0},{10,2},{28,4},{14,6},{16,8},{2,10},{20,12},{6,14},{8,16},{2... | collective-permute-start | bytes 307208 | tf_op jit(solution)/shard_map/ppermute | solution.py:189
  13.3 5.9 %collective-permute-start.4 = (bf16[2,100,256]{2,1,0:T(8,128)(2,1)S(1)}, bf16[2,100,256]{2,1,0:T(8,128)(2,1)S(1)}, u32[]{:S(2)}, u32[]{:S(2)}) collective-permute-start(bf16[2,100,256]{2,1,0:T(8,128)(2,1)S(1)} %shard_map.103), channel_id=1, source_target_pairs={{4,0},{6,2},{0,4},{2,6},{12,8},{14,10},{8,12},{10,14},{20,16},{22,... | collective-permute-start | bytes 307208 | tf_op jit(solution)/shard_map/ppermute | solution.py:189
  16.0 4.7 %collective-permute-start.5 = (bf16[2,100,256]{2,1,0:T(8,128)(2,1)S(1)}, bf16[2,100,256]{2,1,0:T(8,128)(2,1)S(1)}, u32[]{:S(2)}, u32[]{:S(2)}) collective-permute-start(bf16[2,100,256]{2,1,0:T(8,128)(2,1)S(1)} %collective-permute-done.3), channel_id=1, source_target_pairs={{4,0},{6,2},{0,4},{2,6},{12,8},{14,10},{8,12},{10,14},{20,16},{22,... | collective-permute-start | bytes 307208 | tf_op jit(solution)/shard_map/ppermute | solution.py:189
  20.8 1.8 %collective-permute-start.6 = (bf16[7,100,256]{2,1,0:T(8,128)(2,1)S(1)}, bf16[7,100,256]{2,1,0:T(8,128)(2,1)S(1)}, u32[]{:S(2)}, u32[]{:S(2)}) collective-permute-start(bf16[7,100,256]{2,1,0:T(8,128)(2,1)S(1)} %pad_maximum_fusion.refs_1_), channel_id=1, source_target_pairs={{2,0},{0,2},{6,4},{4,6},{10,8},{8,10},{14,12},{12,14},{18,16},{16,... | collective-permute-start | bytes 1075208 | tf_op jit(solution)/shard_map/ppermute | solution.py:189
  24.2 4.4 %collective-permute-start.7 = (bf16[144,256]{1,0:T(8,128)(2,1)S(1)}, bf16[144,256]{1,0:T(8,128)(2,1)S(1)}, u32[]{:S(2)}, u32[]{:S(2)}) collective-permute-start(bf16[144,256]{1,0:T(8,128)(2,1)S(1)} %get-tuple-element.27), channel_id=1, source_target_pairs={{1,0},{0,1},{3,2},{2,3},{5,4},{4,5},{7,6},{6,7},{9,8},{8,9},{11,10... | collective-permute-start | bytes 221192 | tf_op jit(solution)/shard_map/ppermute | solution.py:185
  41.9 1.4 %collective-permute-start.8 = (bf16[8,48,256]{2,1,0:T(8,128)(2,1)S(1)}, bf16[8,48,256]{2,1,0:T(8,128)(2,1)S(1)}, u32[]{:S(2)}, u32[]{:S(2)}) collective-permute-start(bf16[8,48,256]{2,1,0:T(8,128)(2,1)S(1)} %all_to_all.5.near), channel_id=1, source_target_pairs={{2,0},{0,2},{6,4},{4,6},{10,8},{8,10},{14,12},{12,14},{18,16},{16,... | collective-permute-start | bytes 589832 | tf_op jit(solution)/shard_map/ppermute | solution.py:189
  44.7 4.2 %collective-permute-start.9 = (f32[48,256]{1,0:T(8,128)S(1)}, f32[48,256]{1,0:T(8,128)S(1)}, u32[]{:S(2)}, u32[]{:S(2)}) collective-permute-start(f32[48,256]{1,0:T(8,128)S(1)} %get-tuple-element.32), channel_id=1, source_target_pairs={{1,0},{0,1},{3,2},{2,3},{5,4},{4,5},{7,6},{6,7},{9,8},{8,9},{11,10... | collective-permute-start | bytes 147464 | tf_op jit(solution)/shard_map/ppermute | solution.py:185

commit v8 on v7

--- a/solution.py
+++ b/solution.py
@@ -190,9 +190,8 @@
 
 
 def outer_order(outer):
-    first = outer // 2
-    rest = [step for step in range(outer - 1, 0, -1) if step != first]
-    return first, list(zip(rest[0::2], rest[1::2]))
+    rest = list(range(2, outer))
+    return 1, list(zip(rest[0::2], rest[1::2]))
 
 
 def panel_order(outer, core):
@@ -204,13 +203,13 @@
     return [0, 1, *lists[0]], [apart ^ 1 for apart in lists[1]]
 
 
-def packed(parts, after):
+def packed(*parts, after=()):
     def pack(*refs):
         for index in range(len(parts)):
             refs[-1][index] = refs[index][...]
 
     out = jax.ShapeDtypeStruct((len(parts), *parts[0].shape), BF16)
-    return call(pack, [out], vmem=(*parts, after), cost=1 << 32)[0]
+    return call(pack, [out], vmem=(*parts, *after), cost=1 << 32)[0]
 
 
 def gather_features(value, aside):
@@ -219,10 +218,12 @@
     other = swapped(value, (1, 1))
     ahead = swapped(value, (4 * first, 4 * first))
     both = jnp.stack([value, other])
-    beside = aside(both)
     across = [swapped(both, (4 * pair[0], 4 * pair[1])) for pair in pairs]
     across = across[0] if len(across) == 1 else jnp.concatenate(across)
-    over = swapped(packed((value, ahead), beside[1]), (2, 2))
+    here = packed(value, ahead)
+    over = swapped(here, (2, 2))
+    beside = aside(here)
+    across = packed(across, after=(beside[1],))[0]
     beyond = swapped(across, (2, 2))
     near = jnp.concatenate([ahead[None], across, over, beyond])
     return (both, near, swapped(near, (1, 1))), beside

time: 49.8 us -> 49.8 us (level)
  blocking collectives: 13.1 us -> 12.4 us
  waiting for transfers between devices: 13.9 us -> 14.5 us
    all_to_all x1, blocking collectives: 13.1 us -> 12.4 us  [gather_classes(): near = lax.all_to_all(copies, 'blk', 0, 0, axis_index_groups=groups)]
    ppermute x7, waiting for transfers between devices: 7.16 us -> 7.72 us  [swapped(): lax.ppermute(value, 'blk', [(d ^ masks[d % 2], d) for d in range(lax.axis...]
    pallas_call x9 -> x10, Pallas kernels: 7.62 us -> 7.63 us  [call(): pl.pallas_call(kernel, out_shape=outs, in_specs=[pl.BlockSpec(memory_spac...]
  transfers between devices with their start and end apart: 10 -> 10, of which waited for: 8 -> 7; matrix products, arithmetic and copies ran while one was open for 0% -> 0% of each run, Pallas kernels for 7% -> 7%
where the time goes in v8:
time: 49.8 us; the launch traced here: 49.6 us
  waiting for transfers between devices  14.5 us (29%)
  starting transfers between devices  14.2 us (29%)
  blocking collectives  12.4 us (25%)
  Pallas kernels  7.63 us (15%)
  between operations  0.74 us (1%)
    all_to_all x1, blocking collectives, gather_classes(): near = lax.all_to_all(copies, 'blk', 0, 0, axis_index_groups=groups)  12.4 us
    ppermute x7, starting transfers between devices, swapped(): lax.ppermute(value, 'blk', [(d ^ masks[d % 2], d) for d in range(lax.axis...  8.14 us
    ppermute x7, waiting for transfers between devices, swapped(): lax.ppermute(value, 'blk', [(d ^ masks[d % 2], d) for d in range(lax.axis...  7.72 us
    pallas_call x10, Pallas kernels, call(): pl.pallas_call(kernel, out_shape=outs, in_specs=[pl.BlockSpec(memory_spac...  7.63 us
    ppermute x3, waiting for transfers between devices, shifted(): lax.ppermute(value, axis, [((d + step) % size, d) for d in range(size)])  6.74 us
    ppermute x3, starting transfers between devices, shifted(): lax.ppermute(value, axis, [((d + step) % size, d) for d in range(size)])  6.05 us
  transfers between devices with their start and end apart: 10, of which 7 were waited for; matrix products, arithmetic and copies ran while one was open for 0% of the time, Pallas kernels for 7%

profile of v8, /device:TPU:0, one launch (start us, length us, event | category | flops | bytes accessed | tf_op | source)
XLA Modules:
  0.0 49.6 jit_solution(1193385143766269036)
XLA Ops:
  0.0 2.9 %collective-permute-start = (bf16[100,256]{1,0:T(8,128)(2,1)}, bf16[100,256]{1,0:T(8,128)(2,1)S(1)}, u32[]{:S(2)}, u32[]{:S(2)}) collective-permute-start(bf16[100,256]{1,0:T(8,128)(2,1)} %bitcast.15), channel_id=1, source_target_pairs={{1,0},{0,1},{3,2},{2,3},{5,4},{4,5},{7,6},{6,7},{9,8},{8,9},{11,10... | collective-permute-start | bytes 153608 | tf_op jit(solution)/shard_map/ppermute | solution.py:185
  2.9 1.0 %shard_map.100 = (f32[100,256]{1,0:T(8,128)S(1)}, s32[1,256]{1,0:T(1,128)S(1)}) custom-call(s32[1,512]{1,0:T(1,128)} %order.1, bf16[100,256]{1,0:T(8,128)(2,1)} %bitcast.16), custom_call_target="tpu_custom_call" | custom-call | flops 1048576 | bytes 1048576 | tf_op jit(solution)/shard_map/pallas_call | solution.py:27
  4.0 1.3 %collective-permute-done.rest_0_ = bf16[100,256]{1,0:T(8,128)(2,1)S(1)} collective-permute-done((bf16[100,256]{1,0:T(8,128)(2,1)}, bf16[100,256]{1,0:T(8,128)(2,1)S(1)}, u32[]{:S(2)}, u32[]{:S(2)}) %collective-permute-start) | collective-permute-done | bytes 51232 | tf_op jit(solution)/shard_map/ppermute | solution.py:185
  5.3 0.2 shard_map.101.refs_0_
  5.4 0.1 collective-permute-start.2
  6.2 2.2 %collective-permute-start.1 = (bf16[100,256]{1,0:T(8,128)(2,1)S(1)}, bf16[100,256]{1,0:T(8,128)(2,1)S(1)}, u32[]{:S(2)}, u32[]{:S(2)}) collective-permute-start(bf16[100,256]{1,0:T(8,128)(2,1)S(1)} %shard_map.101.refs_0_), channel_id=1, source_target_pairs={{8,0},{10,2},{12,4},{14,6},{0,8},{2,10},{4,12},{6,14},{24,16},{26,... | collective-permute-start | bytes 153608 | tf_op jit(solution)/shard_map/ppermute | solution.py:189
  8.3 0.0 collective-permute-done.2
  8.4 2.7 %collective-permute-start.3 = (bf16[2,100,256]{2,1,0:T(8,128)(2,1)S(1)}, bf16[2,100,256]{2,1,0:T(8,128)(2,1)S(1)}, u32[]{:S(2)}, u32[]{:S(2)}) collective-permute-start(bf16[2,100,256]{2,1,0:T(8,128)(2,1)S(1)} %pad_maximum_fusion.1.refs_0_), channel_id=1, source_target_pairs={{16,0},{26,2},{20,4},{30,6},{24,8},{18,10},{28,12},{22,14},{0,16},... | collective-permute-start | bytes 307208 | tf_op jit(solution)/shard_map/ppermute | solution.py:189
  11.0 0.0 collective-permute-done.1.refs_1_
  11.0 1.6 %collective-permute-start.4 = (bf16[2,100,256]{2,1,0:T(8,128)(2,1)S(1)}, bf16[2,100,256]{2,1,0:T(8,128)(2,1)S(1)}, u32[]{:S(2)}, u32[]{:S(2)}) collective-permute-start(bf16[2,100,256]{2,1,0:T(8,128)(2,1)S(1)} %shard_map.102._), channel_id=1, source_target_pairs={{4,0},{6,2},{0,4},{2,6},{12,8},{14,10},{8,12},{10,14},{20,16},{22,... | collective-permute-start | bytes 307208 | tf_op jit(solution)/shard_map/ppermute | solution.py:189
  12.6 2.3 %shard_map.103 = (s32[32]{0:T(128)S(1)}, f32[128,1]{1,0:T(8,128)S(1)}, f32[47,1]{1,0:T(8,128)S(1)}, bf16[128,100]{1,0:T(8,128)(2,1)S(1)}, bf16[47,128]{1,0:T(8,1...) custom-call(bf16[2,100,256]{2,1,0:T(8,128)(2,1)S(1)} %shard_map.102._, s32[1]{0:T(128)S(6)} %copy.11.live, s32[1,16]{1,0:T(1,128)} %refs_0_.1, ...), custom_call_target="tpu_custom_call" | custom-call | flops 1048576 | bytes 1048576 | tf_op jit(solution)/shard_map/pallas_call | solution.py:27
  14.9 1.7 %collective-permute-done.3.refs_0_ = bf16[2,100,256]{2,1,0:T(8,128)(2,1)S(1)} collective-permute-done((bf16[2,100,256]{2,1,0:T(8,128)(2,1)S(1)}, bf16[2,100,256]{2,1,0:T(8,128)(2,1)S(1)}, u32[]{:S(2)}, u32[]{:S(2)}) %collective-permute-start.3) | collective-permute-done | bytes 102432 | tf_op jit(solution)/shard_map/ppermute | solution.py:189
  16.7 1.6 %collective-permute-start.5 = (bf16[2,100,256]{2,1,0:T(8,128)(2,1)S(1)}, bf16[2,100,256]{2,1,0:T(8,128)(2,1)S(1)}, u32[]{:S(2)}, u32[]{:S(2)}) collective-permute-start(bf16[2,100,256]{2,1,0:T(8,128)(2,1)S(1)} %bitcast.11), channel_id=1, source_target_pairs={{4,0},{6,2},{0,4},{2,6},{12,8},{14,10},{8,12},{10,14},{20,16},{22,... | collective-permute-start | bytes 307208 | tf_op jit(solution)/shard_map/ppermute | solution.py:189
  18.2 0.0 collective-permute-done.4
  18.2 3.2 %collective-permute-done.5 = bf16[2,100,256]{2,1,0:T(8,128)(2,1)S(1)} collective-permute-done((bf16[2,100,256]{2,1,0:T(8,128)(2,1)S(1)}, bf16[2,100,256]{2,1,0:T(8,128)(2,1)S(1)}, u32[]{:S(2)}, u32[]{:S(2)}) %collective-permute-start.5) | collective-permute-done | bytes 102432 | tf_op jit(solution)/shard_map/ppermute | solution.py:189
  21.4 0.1 pad_maximum_fusion.refs_1_
  21.5 0.1 collective-permute-start.6
  21.6 0.3 shard_map.105.projected.hidden_in
  21.9 1.4 %collective-permute-done.6.far = bf16[7,100,256]{2,1,0:T(8,128)(2,1)S(1)} collective-permute-done((bf16[7,100,256]{2,1,0:T(8,128)(2,1)S(1)}, bf16[7,100,256]{2,1,0:T(8,128)(2,1)S(1)}, u32[]{:S(2)}, u32[]{:S(2)}) %collective-permute-start.6) | collective-permute-done | bytes 358432 | tf_op jit(solution)/shard_map/ppermute | solution.py:189
  23.2 1.6 %shard_map.106 = (f32[136,256]{1,0:T(8,128)S(1)}, bf16[144,256]{1,0:T(8,128)(2,1)S(1)}) custom-call(bf16[9,128,256]{2,1,0:T(8,128)(2,1)S(1)} %shard_map.105.projected.hidden_in, bf16[7,100,256]{2,1,0:T(8,128)(2,1)S(1)} %collective-permute-done.6.far, bf16[128,100]{1,0:T(8,128)(2,1)S(1)} %get-tuple-element.21.weight_t, ...), custom_call_target="tpu_custom_call" | custom-call | flops 1048576 | bytes 1048576 | tf_op jit(solution)/shard_map/pallas_call | solution.py:27
  24.8 1.6 %collective-permute-start.7 = (bf16[144,256]{1,0:T(8,128)(2,1)S(1)}, bf16[144,256]{1,0:T(8,128)(2,1)S(1)}, u32[]{:S(2)}, u32[]{:S(2)}) collective-permute-start(bf16[144,256]{1,0:T(8,128)(2,1)S(1)} %get-tuple-element.27), channel_id=1, source_target_pairs={{1,0},{0,1},{3,2},{2,3},{5,4},{4,5},{7,6},{6,7},{9,8},{8,9},{11,10... | collective-permute-start | bytes 221192 | tf_op jit(solution)/shard_map/ppermute | solution.py:185
  26.4 2.9 %collective-permute-done.7.rest_0_ = bf16[144,256]{1,0:T(8,128)(2,1)S(1)} collective-permute-done((bf16[144,256]{1,0:T(8,128)(2,1)S(1)}, bf16[144,256]{1,0:T(8,128)(2,1)S(1)}, u32[]{:S(2)}, u32[]{:S(2)}) %collective-permute-start.7) | collective-permute-done | bytes 73760 | tf_op jit(solution)/shard_map/ppermute | solution.py:185
  29.3 0.2 shard_map.107
  29.5 12.4 %all_to_all.5.near = bf16[8,48,256]{2,1,0:T(8,128)(2,1)S(1)} all-to-all(bf16[8,48,256]{2,1,0:T(8,128)(2,1)S(1)} %broadcast_in_dim.18), channel_id=1, replica_groups={{0,4,8,12,16,20,24,28},{2,6,10,14,18,22,26,30},{1,5,9,13,17,21,25,29},{..., dimensions={0} | all-to-all | bytes 393216 | tf_op jit(solution)/shard_map/all_to_all | solution.py:236
  41.9 0.0 collective-permute-start.8
  42.0 1.4 %collective-permute-done.8.far = bf16[8,48,256]{2,1,0:T(8,128)(2,1)S(1)} collective-permute-done((bf16[8,48,256]{2,1,0:T(8,128)(2,1)S(1)}, bf16[8,48,256]{2,1,0:T(8,128)(2,1)S(1)}, u32[]{:S(2)}, u32[]{:S(2)}) %collective-permute-start.8) | collective-permute-done | bytes 196640 | tf_op jit(solution)/shard_map/ppermute | solution.py:189
  43.4 1.3 %shard_map.108 = (f32[48,256]{1,0:T(8,128)S(1)}, f32[48,256]{1,0:T(8,128)S(1)}) custom-call(bf16[8,48,256]{2,1,0:T(8,128)(2,1)S(1)} %all_to_all.5.near, bf16[8,48,256]{2,1,0:T(8,128)(2,1)S(1)} %collective-permute-done.8.far, bf16[16,256,256]{2,1,0:T(8,128)(2,1)S(1)} %get-tuple-element.24.tiles, s32[32]{0:T(128)S(1)} %get-tuple-element.25.plan), custom_call_target="tpu_custom_call" | custom-call | flops 1048576 | bytes 1048576 | tf_op jit(solution)/shard_map/pallas_call | solution.py:27
  44.7 1.6 %collective-permute-start.9 = (f32[48,256]{1,0:T(8,128)S(1)}, f32[48,256]{1,0:T(8,128)S(1)}, u32[]{:S(2)}, u32[]{:S(2)}) collective-permute-start(f32[48,256]{1,0:T(8,128)S(1)} %get-tuple-element.32), channel_id=1, source_target_pairs={{1,0},{0,1},{3,2},{2,3},{5,4},{4,5},{7,6},{6,7},{9,8},{8,9},{11,10... | collective-permute-start | bytes 147464 | tf_op jit(solution)/shard_map/ppermute | solution.py:185
  46.3 2.6 %collective-permute-done.9.rest_0_ = f32[48,256]{1,0:T(8,128)S(1)} collective-permute-done((f32[48,256]{1,0:T(8,128)S(1)}, f32[48,256]{1,0:T(8,128)S(1)}, u32[]{:S(2)}, u32[]{:S(2)}) %collective-permute-start.9) | collective-permute-done | bytes 49184 | tf_op jit(solution)/shard_map/ppermute | solution.py:185
  48.9 0.7 %shard_map.109 = f32[47,256]{1,0:T(8,128)} custom-call(bf16[48,256]{1,0:T(8,128)(2,1)S(1)} %get-tuple-element.28.classes_in, f32[1,256]{1,0:T(1,128)S(1)} %get-tuple-element.29.scaling, f32[47,1]{1,0:T(8,128)S(1)} %get-tuple-element.30.bias, f32[48,256]{1,0:T(8,128)S(1)} %get-tuple-element.31.own, f32[48,256]{1,0:T(8,128)S(1)} %collective-permute-done.9.rest_0_), custom_call_target="tpu_custom_call" | custom-call | flops 1048576 | bytes 1048576 | tf_op jit(solution)/shard_map/pallas_call | solution.py:27
  (4 shorter events, 0.0 us)
Async XLA Ops:
  0.0 5.3 %collective-permute-start = (bf16[100,256]{1,0:T(8,128)(2,1)}, bf16[100,256]{1,0:T(8,128)(2,1)S(1)}, u32[]{:S(2)}, u32[]{:S(2)}) collective-permute-start(bf16[100,256]{1,0:T(8,128)(2,1)} %bitcast.15), channel_id=1, source_target_pairs={{1,0},{0,1},{3,2},{2,3},{5,4},{4,5},{7,6},{6,7},{9,8},{8,9},{11,10... | collective-permute-start | bytes 153608 | tf_op jit(solution)/shard_map/ppermute | solution.py:185
  5.4 2.9 %collective-permute-start.2 = (bf16[100,256]{1,0:T(8,128)(2,1)S(1)}, bf16[100,256]{1,0:T(8,128)(2,1)S(1)}, u32[]{:S(2)}, u32[]{:S(2)}) collective-permute-start(bf16[100,256]{1,0:T(8,128)(2,1)S(1)} %shard_map.101.refs_0_), channel_id=1, source_target_pairs={{2,0},{0,2},{6,4},{4,6},{10,8},{8,10},{14,12},{12,14},{18,16},{16,... | collective-permute-start | bytes 153608 | tf_op jit(solution)/shard_map/ppermute | solution.py:189
  6.2 4.9 %collective-permute-start.1 = (bf16[100,256]{1,0:T(8,128)(2,1)S(1)}, bf16[100,256]{1,0:T(8,128)(2,1)S(1)}, u32[]{:S(2)}, u32[]{:S(2)}) collective-permute-start(bf16[100,256]{1,0:T(8,128)(2,1)S(1)} %shard_map.101.refs_0_), channel_id=1, source_target_pairs={{8,0},{10,2},{12,4},{14,6},{0,8},{2,10},{4,12},{6,14},{24,16},{26,... | collective-permute-start | bytes 153608 | tf_op jit(solution)/shard_map/ppermute | solution.py:189
  8.4 8.3 %collective-permute-start.3 = (bf16[2,100,256]{2,1,0:T(8,128)(2,1)S(1)}, bf16[2,100,256]{2,1,0:T(8,128)(2,1)S(1)}, u32[]{:S(2)}, u32[]{:S(2)}) collective-permute-start(bf16[2,100,256]{2,1,0:T(8,128)(2,1)S(1)} %pad_maximum_fusion.1.refs_0_), channel_id=1, source_target_pairs={{16,0},{26,2},{20,4},{30,6},{24,8},{18,10},{28,12},{22,14},{0,16},... | collective-permute-start | bytes 307208 | tf_op jit(solution)/shard_map/ppermute | solution.py:189
  11.0 7.2 %collective-permute-start.4 = (bf16[2,100,256]{2,1,0:T(8,128)(2,1)S(1)}, bf16[2,100,256]{2,1,0:T(8,128)(2,1)S(1)}, u32[]{:S(2)}, u32[]{:S(2)}) collective-permute-start(bf16[2,100,256]{2,1,0:T(8,128)(2,1)S(1)} %shard_map.102._), channel_id=1, source_target_pairs={{4,0},{6,2},{0,4},{2,6},{12,8},{14,10},{8,12},{10,14},{20,16},{22,... | collective-permute-start | bytes 307208 | tf_op jit(solution)/shard_map/ppermute | solution.py:189
  16.7 4.8 %collective-permute-start.5 = (bf16[2,100,256]{2,1,0:T(8,128)(2,1)S(1)}, bf16[2,100,256]{2,1,0:T(8,128)(2,1)S(1)}, u32[]{:S(2)}, u32[]{:S(2)}) collective-permute-start(bf16[2,100,256]{2,1,0:T(8,128)(2,1)S(1)} %bitcast.11), channel_id=1, source_target_pairs={{4,0},{6,2},{0,4},{2,6},{12,8},{14,10},{8,12},{10,14},{20,16},{22,... | collective-permute-start | bytes 307208 | tf_op jit(solution)/shard_map/ppermute | solution.py:189
  21.5 1.8 %collective-permute-start.6 = (bf16[7,100,256]{2,1,0:T(8,128)(2,1)S(1)}, bf16[7,100,256]{2,1,0:T(8,128)(2,1)S(1)}, u32[]{:S(2)}, u32[]{:S(2)}) collective-permute-start(bf16[7,100,256]{2,1,0:T(8,128)(2,1)S(1)} %pad_maximum_fusion.refs_1_), channel_id=1, source_target_pairs={{2,0},{0,2},{6,4},{4,6},{10,8},{8,10},{14,12},{12,14},{18,16},{16,... | collective-permute-start | bytes 1075208 | tf_op jit(solution)/shard_map/ppermute | solution.py:189
  24.8 4.4 %collective-permute-start.7 = (bf16[144,256]{1,0:T(8,128)(2,1)S(1)}, bf16[144,256]{1,0:T(8,128)(2,1)S(1)}, u32[]{:S(2)}, u32[]{:S(2)}) collective-permute-start(bf16[144,256]{1,0:T(8,128)(2,1)S(1)} %get-tuple-element.27), channel_id=1, source_target_pairs={{1,0},{0,1},{3,2},{2,3},{5,4},{4,5},{7,6},{6,7},{9,8},{8,9},{11,10... | collective-permute-start | bytes 221192 | tf_op jit(solution)/shard_map/ppermute | solution.py:185
  41.9 1.4 %collective-permute-start.8 = (bf16[8,48,256]{2,1,0:T(8,128)(2,1)S(1)}, bf16[8,48,256]{2,1,0:T(8,128)(2,1)S(1)}, u32[]{:S(2)}, u32[]{:S(2)}) collective-permute-start(bf16[8,48,256]{2,1,0:T(8,128)(2,1)S(1)} %all_to_all.5.near), channel_id=1, source_target_pairs={{2,0},{0,2},{6,4},{4,6},{10,8},{8,10},{14,12},{12,14},{18,16},{16,... | collective-permute-start | bytes 589832 | tf_op jit(solution)/shard_map/ppermute | solution.py:189
  44.7 4.2 %collective-permute-start.9 = (f32[48,256]{1,0:T(8,128)S(1)}, f32[48,256]{1,0:T(8,128)S(1)}, u32[]{:S(2)}, u32[]{:S(2)}) collective-permute-start(f32[48,256]{1,0:T(8,128)S(1)} %get-tuple-element.32), channel_id=1, source_target_pairs={{1,0},{0,1},{3,2},{2,3},{5,4},{4,5},{7,6},{6,7},{9,8},{8,9},{11,10... | collective-permute-start | bytes 147464 | tf_op jit(solution)/shard_map/ppermute | solution.py:185

commit v9 on v8

--- a/solution.py
+++ b/solution.py
@@ -103,19 +103,33 @@
         start += stack.shape[0]
 
 
-def summed(panels, plan, tiles, count, extra):
+def turn(tiles, arrived, plan, arrived_out, tiles_t, degrees):
+    arrived_out[...] = arrived[...]
     slots, tile = tiles.shape[0], tiles.shape[1]
-    height = panels.shape[1] + extra
+    count = degrees.shape[0]
+    total = jnp.zeros((count * ONES_ROWS, tile), F32)
+    for slot in range(slots):
+        values = tiles[slot]
+        tiles_t[slot] = values.T
+        ones = [
+            jnp.full((ONES_ROWS, tile), (plan[slots + slot] == step).astype(F32), F32).astype(BF16)
+            for step in range(count)
+        ]
+        total = total + nt(jnp.concatenate(ones, axis=0), values)
+    for step in range(count):
+        degrees[step] = total[step * ONES_ROWS : step * ONES_ROWS + 8]
+
+
+def summed(panels, plan, tiles_t, count):
+    slots, tile = tiles_t.shape[0], tiles_t.shape[1]
+    height = panels.shape[1]
     total = jnp.zeros((count * height, tile), F32)
     for slot in range(slots):
         values = panels[plan[slot]]
-        pieces = []
-        for step in range(count):
-            used = (plan[slots + slot] == step).astype(F32)
-            pieces.append(values * used.astype(BF16))
-            if extra:
-                pieces.append(jnp.full((extra, tile), used, F32).astype(BF16))
-        total = total + nt(jnp.concatenate(pieces, axis=0), tiles[slot])
+        pieces = [
+            values * (plan[slots + slot] == step).astype(F32).astype(BF16) for step in range(count)
+        ]
+        total = total + nn(jnp.concatenate(pieces, axis=0), tiles_t[slot])
     return [total[step * height : (step + 1) * height] for step in range(count)]
 
 
@@ -125,37 +139,36 @@
     return first, second, row - first - second
 
 
-def aggregate_hidden(projected, far, weight_t, tiles, plan, own, *rest):
+def aggregate_hidden(projected, far, weight_t, tiles_t, degrees, plan, own, *rest):
     others, panels = rest[:-1], rest[-1]
     mine, opposite = panel_order(panels.shape[0] // 4, lax.axis_index("blk") % 2)
     for index, place in enumerate(mine):
         panels[place] = projected[index]
     for index, place in enumerate(opposite):
         panels[place] = nn(weight_t[...], far[index]).astype(BF16)
-    height = panels.shape[1]
-    sums = summed(panels, plan, tiles, 1 + len(others), ONES_ROWS)
-    own[...] = sums[0][: own.shape[0]]
-    row = lax.broadcasted_iota(jnp.int32, (ONES_ROWS, tiles.shape[1]), 0)
-    for part, out in zip(sums[1:], others):
-        first, second, third = in_thirds(part[height:])
-        degree = jnp.where(row == 0, first, jnp.where(row == 1, second, jnp.where(row == 2, third, 0.0)))
-        out[...] = jnp.concatenate([part[:height], degree], axis=0).astype(BF16)
-
-
-def aggregate_classes(near, far, tiles, plan, *rest):
+    sums = summed(panels, plan, tiles_t, 1 + len(others))
+    own[...] = sums[0]
+    row = lax.broadcasted_iota(jnp.int32, (8, own.shape[1]), 0)
+    for step, (part, out) in enumerate(zip(sums[1:], others), 1):
+        first, second, third = in_thirds(degrees[step])
+        terms = jnp.where(row == 0, first, jnp.where(row == 1, second, jnp.where(row == 2, third, 0.0)))
+        out[...] = jnp.concatenate([part, terms, jnp.zeros_like(terms)], axis=0).astype(BF16)
+
+
+def aggregate_classes(near, far, tiles_t, plan, *rest):
     outs, panels = rest[:-1], rest[-1]
     chip = lax.axis_index("blk") // 2
     for index in range(near.shape[0]):
         panels[2 * (index ^ chip)] = near[index]
         panels[2 * (index ^ chip) + 1] = far[index]
-    for out, part in zip(outs, summed(panels, plan, tiles, len(outs), 0)):
+    for out, part in zip(outs, summed(panels, plan, tiles_t, len(outs))):
         out[...] = part
 
 
-def combine(hidden_in, bias, weight_t, own, *rest):
+def combine(hidden_in, bias, weight_t, degrees, own, *rest):
     *arrived, out, scale_out = rest
     height = hidden_in.shape[1]
-    total, degree = own[:height], own[height : height + 1]
+    total, degree = own[...], degrees[0, :1]
     for part in arrived:
         values = part[...].astype(F32)
         total = total + values[:height]
@@ -212,7 +225,7 @@
     return call(pack, [out], vmem=(*parts, *after), cost=1 << 32)[0]
 
 
-def gather_features(value, aside):
+def gather_features(value, aside, later):
     outer = lax.axis_size("blk") // 4
     first, pairs = outer_order(outer)
     other = swapped(value, (1, 1))
@@ -225,8 +238,9 @@
     beside = aside(here)
     across = packed(across, after=(beside[1],))[0]
     beyond = swapped(across, (2, 2))
+    over, *behind = later(over, beside)
     near = jnp.concatenate([ahead[None], across, over, beyond])
-    return (both, near, swapped(near, (1, 1))), beside
+    return (both, near, swapped(near, (1, 1))), beside, behind
 
 
 def gather_classes(value):
@@ -307,8 +321,21 @@
             smem_outs=1,
         )
 
-    (both, near, far), values = gather_features(ordered, staged)
-    plan, bias_1, bias_2, weight_1, weight_2, tiles = values
+    def turned(arrived, values):
+        tiles = values[-1]
+        return call(
+            turn,
+            [
+                shape(arrived.shape, BF16),
+                shape(tiles.shape, BF16),
+                shape((reps, 8, tile), F32),
+            ],
+            vmem=(tiles, arrived),
+            smem=(values[0],),
+        )
+
+    (both, near, far), values, (tiles, degrees) = gather_features(ordered, staged, turned)
+    plan, bias_1, bias_2, weight_1, weight_2, _ = values
     (projected,) = call(
         project,
         [shape((2 + near.shape[0], hidden, tile), BF16)],
@@ -316,15 +343,15 @@
     )
     own, *sums = call(
         aggregate_hidden,
-        [shape((hidden + 8, tile), F32)] + [shape((hidden + ONES_ROWS, tile), BF16)] * (reps - 1),
-        vmem=(projected, far, weight_1, tiles),
+        [shape((hidden, tile), F32)] + [shape((hidden + ONES_ROWS, tile), BF16)] * (reps - 1),
+        vmem=(projected, far, weight_1, tiles, degrees),
         smem=(plan,),
         scratch=[pltpu.VMEM((blocks, hidden, tile), BF16)],
     )
     classes_in, scaling = call(
         combine,
         [shape((padded, tile), BF16), shape((1, tile), F32)],
-        vmem=(projected, bias_1, weight_2, own, *exchanged(sums)),
+        vmem=(projected, bias_1, weight_2, degrees, own, *exchanged(sums)),
     )
     own, *sums = call(
         aggregate_classes,

time: 49.8 us -> 49.5 us (level)
  waiting for transfers between devices: 14.5 us -> 13.2 us
  Pallas kernels: 7.63 us -> 8.59 us
    ppermute x7, waiting for transfers between devices: 7.72 us -> 6.44 us  [swapped(): lax.ppermute(value, 'blk', [(d ^ masks[d % 2], d) for d in range(lax.axis...]
    pallas_call x10 -> x11, Pallas kernels: 7.63 us -> 8.59 us  [call(): pl.pallas_call(kernel, out_shape=outs, in_specs=[pl.BlockSpec(memory_spac...]
  transfers between devices with their start and end apart: 10 -> 10, of which waited for: 7 -> 7; matrix products, arithmetic and copies ran while one was open for 0% -> 0% of each run, Pallas kernels for 7% -> 10%
where the time goes in v9:
time: 49.5 us; the launch traced here: 49.2 us
  starting transfers between devices  14.2 us (29%)
  waiting for transfers between devices  13.2 us (27%)
  blocking collectives  12.5 us (25%)
  Pallas kernels  8.59 us (17%)
  between operations  0.74 us (1%)
    all_to_all x1, blocking collectives, gather_classes(): near = lax.all_to_all(copies, 'blk', 0, 0, axis_index_groups=groups)  12.5 us
    pallas_call x11, Pallas kernels, call(): pl.pallas_call(kernel, out_shape=outs, in_specs=[pl.BlockSpec(memory_spac...  8.59 us
    ppermute x7, starting transfers between devices, swapped(): lax.ppermute(value, 'blk', [(d ^ masks[d % 2], d) for d in range(lax.axis...  8.14 us
    ppermute x3, waiting for transfers between devices, shifted(): lax.ppermute(value, axis, [((d + step) % size, d) for d in range(size)])  6.74 us
    ppermute x7, waiting for transfers between devices, swapped(): lax.ppermute(value, 'blk', [(d ^ masks[d % 2], d) for d in range(lax.axis...  6.44 us
    ppermute x3, starting transfers between devices, shifted(): lax.ppermute(value, axis, [((d + step) % size, d) for d in range(size)])  6.05 us
  transfers between devices with their start and end apart: 10, of which 7 were waited for; matrix products, arithmetic and copies ran while one was open for 0% of the time, Pallas kernels for 10%

profile of v9, /device:TPU:0, one launch (start us, length us, event | category | flops | bytes accessed | tf_op | source)
XLA Modules:
  0.0 49.2 jit_solution(9045991486008105233)
XLA Ops:
  0.0 2.9 %collective-permute-start = (bf16[100,256]{1,0:T(8,128)(2,1)}, bf16[100,256]{1,0:T(8,128)(2,1)S(1)}, u32[]{:S(2)}, u32[]{:S(2)}) collective-permute-start(bf16[100,256]{1,0:T(8,128)(2,1)} %bitcast.15), channel_id=1, source_target_pairs={{1,0},{0,1},{3,2},{2,3},{5,4},{4,5},{7,6},{6,7},{9,8},{8,9},{11,10... | collective-permute-start | bytes 153608 | tf_op jit(solution)/shard_map/ppermute | solution.py:198
  2.9 1.0 %shard_map.100 = (f32[100,256]{1,0:T(8,128)S(1)}, s32[1,256]{1,0:T(1,128)S(1)}) custom-call(s32[1,512]{1,0:T(1,128)} %order.1, bf16[100,256]{1,0:T(8,128)(2,1)} %bitcast.16), custom_call_target="tpu_custom_call" | custom-call | flops 1048576 | bytes 1048576 | tf_op jit(solution)/shard_map/pallas_call | solution.py:27
  4.0 1.3 %collective-permute-done.rest_0_ = bf16[100,256]{1,0:T(8,128)(2,1)S(1)} collective-permute-done((bf16[100,256]{1,0:T(8,128)(2,1)}, bf16[100,256]{1,0:T(8,128)(2,1)S(1)}, u32[]{:S(2)}, u32[]{:S(2)}) %collective-permute-start) | collective-permute-done | bytes 51232 | tf_op jit(solution)/shard_map/ppermute | solution.py:198
  5.3 0.2 shard_map.101.refs_0_
  5.4 0.1 collective-permute-start.2
  6.2 2.2 %collective-permute-start.1 = (bf16[100,256]{1,0:T(8,128)(2,1)S(1)}, bf16[100,256]{1,0:T(8,128)(2,1)S(1)}, u32[]{:S(2)}, u32[]{:S(2)}) collective-permute-start(bf16[100,256]{1,0:T(8,128)(2,1)S(1)} %shard_map.101.refs_0_), channel_id=1, source_target_pairs={{8,0},{10,2},{12,4},{14,6},{0,8},{2,10},{4,12},{6,14},{24,16},{26,... | collective-permute-start | bytes 153608 | tf_op jit(solution)/shard_map/ppermute | solution.py:202
  8.3 0.0 collective-permute-done.2
  8.4 2.7 %collective-permute-start.3 = (bf16[2,100,256]{2,1,0:T(8,128)(2,1)S(1)}, bf16[2,100,256]{2,1,0:T(8,128)(2,1)S(1)}, u32[]{:S(2)}, u32[]{:S(2)}) collective-permute-start(bf16[2,100,256]{2,1,0:T(8,128)(2,1)S(1)} %pad_maximum_fusion.1.refs_0_), channel_id=1, source_target_pairs={{16,0},{26,2},{20,4},{30,6},{24,8},{18,10},{28,12},{22,14},{0,16},... | collective-permute-start | bytes 307208 | tf_op jit(solution)/shard_map/ppermute | solution.py:202
  11.0 0.0 collective-permute-done.1.refs_1_
  11.0 1.6 %collective-permute-start.4 = (bf16[2,100,256]{2,1,0:T(8,128)(2,1)S(1)}, bf16[2,100,256]{2,1,0:T(8,128)(2,1)S(1)}, u32[]{:S(2)}, u32[]{:S(2)}) collective-permute-start(bf16[2,100,256]{2,1,0:T(8,128)(2,1)S(1)} %shard_map.102._), channel_id=1, source_target_pairs={{4,0},{6,2},{0,4},{2,6},{12,8},{14,10},{8,12},{10,14},{20,16},{22,... | collective-permute-start | bytes 307208 | tf_op jit(solution)/shard_map/ppermute | solution.py:202
  12.6 2.3 %shard_map.103 = (s32[32]{0:T(128)S(1)}, f32[128,1]{1,0:T(8,128)S(1)}, f32[47,1]{1,0:T(8,128)S(1)}, bf16[128,100]{1,0:T(8,128)(2,1)S(1)}, bf16[47,128]{1,0:T(8,1...) custom-call(bf16[2,100,256]{2,1,0:T(8,128)(2,1)S(1)} %shard_map.102._, s32[1]{0:T(128)S(6)} %copy.11.live, s32[1,16]{1,0:T(1,128)} %refs_0_.1, ...), custom_call_target="tpu_custom_call" | custom-call | flops 1048576 | bytes 1048576 | tf_op jit(solution)/shard_map/pallas_call | solution.py:27
  14.9 1.7 %collective-permute-done.3.refs_0_ = bf16[2,100,256]{2,1,0:T(8,128)(2,1)S(1)} collective-permute-done((bf16[2,100,256]{2,1,0:T(8,128)(2,1)S(1)}, bf16[2,100,256]{2,1,0:T(8,128)(2,1)S(1)}, u32[]{:S(2)}, u32[]{:S(2)}) %collective-permute-start.3) | collective-permute-done | bytes 102432 | tf_op jit(solution)/shard_map/ppermute | solution.py:202
  16.7 1.6 %collective-permute-start.5 = (bf16[2,100,256]{2,1,0:T(8,128)(2,1)S(1)}, bf16[2,100,256]{2,1,0:T(8,128)(2,1)S(1)}, u32[]{:S(2)}, u32[]{:S(2)}) collective-permute-start(bf16[2,100,256]{2,1,0:T(8,128)(2,1)S(1)} %bitcast.11), channel_id=1, source_target_pairs={{4,0},{6,2},{0,4},{2,6},{12,8},{14,10},{8,12},{10,14},{20,16},{22,... | collective-permute-start | bytes 307208 | tf_op jit(solution)/shard_map/ppermute | solution.py:202
  18.2 0.0 collective-permute-done.4.arrived
  18.2 1.3 %shard_map.105 = (bf16[2,100,256]{2,1,0:T(8,128)(2,1)S(1)}, bf16[16,256,256]{2,1,0:T(8,128)(2,1)S(1)}, f32[2,8,256]{2,1,0:T(8,128)S(1)}) custom-call(bf16[16,256,256]{2,1,0:T(8,128)(2,1)S(1)} %get-tuple-element.26.tiles, bf16[2,100,256]{2,1,0:T(8,128)(2,1)S(1)} %collective-permute-done.4.arrived, s32[32]{0:T(128)S(1)} %get-tuple-element.27.plan), custom_call_target="tpu_custom_call" | custom-call | flops 1048576 | bytes 1048576 | tf_op jit(solution)/shard_map/pallas_call | solution.py:27
  19.5 1.9 %collective-permute-done.5 = bf16[2,100,256]{2,1,0:T(8,128)(2,1)S(1)} collective-permute-done((bf16[2,100,256]{2,1,0:T(8,128)(2,1)S(1)}, bf16[2,100,256]{2,1,0:T(8,128)(2,1)S(1)}, u32[]{:S(2)}, u32[]{:S(2)}) %collective-permute-start.5) | collective-permute-done | bytes 102432 | tf_op jit(solution)/shard_map/ppermute | solution.py:202
  21.4 0.1 pad_maximum_fusion.refs_1_
  21.5 0.1 collective-permute-start.6
  21.6 0.3 shard_map.106.projected.hidden_in
  21.9 1.4 %collective-permute-done.6.far = bf16[7,100,256]{2,1,0:T(8,128)(2,1)S(1)} collective-permute-done((bf16[7,100,256]{2,1,0:T(8,128)(2,1)S(1)}, bf16[7,100,256]{2,1,0:T(8,128)(2,1)S(1)}, u32[]{:S(2)}, u32[]{:S(2)}) %collective-permute-start.6) | collective-permute-done | bytes 358432 | tf_op jit(solution)/shard_map/ppermute | solution.py:202
  23.2 1.5 %shard_map.107 = (f32[128,256]{1,0:T(8,128)S(1)}, bf16[144,256]{1,0:T(8,128)(2,1)S(1)}) custom-call(bf16[9,128,256]{2,1,0:T(8,128)(2,1)S(1)} %shard_map.106.projected.hidden_in, bf16[7,100,256]{2,1,0:T(8,128)(2,1)S(1)} %collective-permute-done.6.far, bf16[128,100]{1,0:T(8,128)(2,1)S(1)} %get-tuple-element.24.weight_t, ...), custom_call_target="tpu_custom_call" | custom-call | flops 1048576 | bytes 1048576 | tf_op jit(solution)/shard_map/pallas_call | solution.py:27
  24.8 1.6 %collective-permute-start.7 = (bf16[144,256]{1,0:T(8,128)(2,1)S(1)}, bf16[144,256]{1,0:T(8,128)(2,1)S(1)}, u32[]{:S(2)}, u32[]{:S(2)}) collective-permute-start(bf16[144,256]{1,0:T(8,128)(2,1)S(1)} %get-tuple-element.33), channel_id=1, source_target_pairs={{1,0},{0,1},{3,2},{2,3},{5,4},{4,5},{7,6},{6,7},{9,8},{8,9},{11,10... | collective-permute-start | bytes 221192 | tf_op jit(solution)/shard_map/ppermute | solution.py:198
  26.3 2.9 %collective-permute-done.7.rest_0_ = bf16[144,256]{1,0:T(8,128)(2,1)S(1)} collective-permute-done((bf16[144,256]{1,0:T(8,128)(2,1)S(1)}, bf16[144,256]{1,0:T(8,128)(2,1)S(1)}, u32[]{:S(2)}, u32[]{:S(2)}) %collective-permute-start.7) | collective-permute-done | bytes 73760 | tf_op jit(solution)/shard_map/ppermute | solution.py:198
  29.2 0.2 shard_map.108
  29.5 12.5 %all_to_all.5.near = bf16[8,48,256]{2,1,0:T(8,128)(2,1)S(1)} all-to-all(bf16[8,48,256]{2,1,0:T(8,128)(2,1)S(1)} %broadcast_in_dim.18), channel_id=1, replica_groups={{0,4,8,12,16,20,24,28},{2,6,10,14,18,22,26,30},{1,5,9,13,17,21,25,29},{..., dimensions={0} | all-to-all | bytes 393216 | tf_op jit(solution)/shard_map/all_to_all | solution.py:250
  41.9 0.0 collective-permute-start.8
  41.9 1.4 %collective-permute-done.8.far = bf16[8,48,256]{2,1,0:T(8,128)(2,1)S(1)} collective-permute-done((bf16[8,48,256]{2,1,0:T(8,128)(2,1)S(1)}, bf16[8,48,256]{2,1,0:T(8,128)(2,1)S(1)}, u32[]{:S(2)}, u32[]{:S(2)}) %collective-permute-start.8) | collective-permute-done | bytes 196640 | tf_op jit(solution)/shard_map/ppermute | solution.py:202
  43.3 1.0 %shard_map.109 = (f32[48,256]{1,0:T(8,128)S(1)}, f32[48,256]{1,0:T(8,128)S(1)}) custom-call(bf16[8,48,256]{2,1,0:T(8,128)(2,1)S(1)} %all_to_all.5.near, bf16[8,48,256]{2,1,0:T(8,128)(2,1)S(1)} %collective-permute-done.8.far, bf16[16,256,256]{2,1,0:T(8,128)(2,1)S(1)} %get-tuple-element.31.tiles_t, s32[32]{0:T(128)S(1)} %get-tuple-element.27.plan), custom_call_target="tpu_custom_call" | custom-call | flops 1048576 | bytes 1048576 | tf_op jit(solution)/shard_map/pallas_call | solution.py:27
  44.4 1.6 %collective-permute-start.9 = (f32[48,256]{1,0:T(8,128)S(1)}, f32[48,256]{1,0:T(8,128)S(1)}, u32[]{:S(2)}, u32[]{:S(2)}) collective-permute-start(f32[48,256]{1,0:T(8,128)S(1)} %get-tuple-element.38), channel_id=1, source_target_pairs={{1,0},{0,1},{3,2},{2,3},{5,4},{4,5},{7,6},{6,7},{9,8},{8,9},{11,10... | collective-permute-start | bytes 147464 | tf_op jit(solution)/shard_map/ppermute | solution.py:198
  45.9 2.6 %collective-permute-done.9.rest_0_ = f32[48,256]{1,0:T(8,128)S(1)} collective-permute-done((f32[48,256]{1,0:T(8,128)S(1)}, f32[48,256]{1,0:T(8,128)S(1)}, u32[]{:S(2)}, u32[]{:S(2)}) %collective-permute-start.9) | collective-permute-done | bytes 49184 | tf_op jit(solution)/shard_map/ppermute | solution.py:198
  48.5 0.7 %shard_map.110 = f32[47,256]{1,0:T(8,128)} custom-call(bf16[48,256]{1,0:T(8,128)(2,1)S(1)} %get-tuple-element.34.classes_in, f32[1,256]{1,0:T(1,128)S(1)} %get-tuple-element.35.scaling, f32[47,1]{1,0:T(8,128)S(1)} %get-tuple-element.36.bias, f32[48,256]{1,0:T(8,128)S(1)} %get-tuple-element.37.own, f32[48,256]{1,0:T(8,128)S(1)} %collective-permute-done.9.rest_0_), custom_call_target="tpu_custom_call" | custom-call | flops 1048576 | bytes 1048576 | tf_op jit(solution)/shard_map/pallas_call | solution.py:27
  (4 shorter events, 0.0 us)
Async XLA Ops:
  0.0 5.3 %collective-permute-start = (bf16[100,256]{1,0:T(8,128)(2,1)}, bf16[100,256]{1,0:T(8,128)(2,1)S(1)}, u32[]{:S(2)}, u32[]{:S(2)}) collective-permute-start(bf16[100,256]{1,0:T(8,128)(2,1)} %bitcast.15), channel_id=1, source_target_pairs={{1,0},{0,1},{3,2},{2,3},{5,4},{4,5},{7,6},{6,7},{9,8},{8,9},{11,10... | collective-permute-start | bytes 153608 | tf_op jit(solution)/shard_map/ppermute | solution.py:198
  5.4 2.9 %collective-permute-start.2 = (bf16[100,256]{1,0:T(8,128)(2,1)S(1)}, bf16[100,256]{1,0:T(8,128)(2,1)S(1)}, u32[]{:S(2)}, u32[]{:S(2)}) collective-permute-start(bf16[100,256]{1,0:T(8,128)(2,1)S(1)} %shard_map.101.refs_0_), channel_id=1, source_target_pairs={{2,0},{0,2},{6,4},{4,6},{10,8},{8,10},{14,12},{12,14},{18,16},{16,... | collective-permute-start | bytes 153608 | tf_op jit(solution)/shard_map/ppermute | solution.py:202
  6.2 4.9 %collective-permute-start.1 = (bf16[100,256]{1,0:T(8,128)(2,1)S(1)}, bf16[100,256]{1,0:T(8,128)(2,1)S(1)}, u32[]{:S(2)}, u32[]{:S(2)}) collective-permute-start(bf16[100,256]{1,0:T(8,128)(2,1)S(1)} %shard_map.101.refs_0_), channel_id=1, source_target_pairs={{8,0},{10,2},{12,4},{14,6},{0,8},{2,10},{4,12},{6,14},{24,16},{26,... | collective-permute-start | bytes 153608 | tf_op jit(solution)/shard_map/ppermute | solution.py:202
  8.4 8.3 %collective-permute-start.3 = (bf16[2,100,256]{2,1,0:T(8,128)(2,1)S(1)}, bf16[2,100,256]{2,1,0:T(8,128)(2,1)S(1)}, u32[]{:S(2)}, u32[]{:S(2)}) collective-permute-start(bf16[2,100,256]{2,1,0:T(8,128)(2,1)S(1)} %pad_maximum_fusion.1.refs_0_), channel_id=1, source_target_pairs={{16,0},{26,2},{20,4},{30,6},{24,8},{18,10},{28,12},{22,14},{0,16},... | collective-permute-start | bytes 307208 | tf_op jit(solution)/shard_map/ppermute | solution.py:202
  11.0 7.2 %collective-permute-start.4 = (bf16[2,100,256]{2,1,0:T(8,128)(2,1)S(1)}, bf16[2,100,256]{2,1,0:T(8,128)(2,1)S(1)}, u32[]{:S(2)}, u32[]{:S(2)}) collective-permute-start(bf16[2,100,256]{2,1,0:T(8,128)(2,1)S(1)} %shard_map.102._), channel_id=1, source_target_pairs={{4,0},{6,2},{0,4},{2,6},{12,8},{14,10},{8,12},{10,14},{20,16},{22,... | collective-permute-start | bytes 307208 | tf_op jit(solution)/shard_map/ppermute | solution.py:202
  16.7 4.8 %collective-permute-start.5 = (bf16[2,100,256]{2,1,0:T(8,128)(2,1)S(1)}, bf16[2,100,256]{2,1,0:T(8,128)(2,1)S(1)}, u32[]{:S(2)}, u32[]{:S(2)}) collective-permute-start(bf16[2,100,256]{2,1,0:T(8,128)(2,1)S(1)} %bitcast.11), channel_id=1, source_target_pairs={{4,0},{6,2},{0,4},{2,6},{12,8},{14,10},{8,12},{10,14},{20,16},{22,... | collective-permute-start | bytes 307208 | tf_op jit(solution)/shard_map/ppermute | solution.py:202
  21.5 1.8 %collective-permute-start.6 = (bf16[7,100,256]{2,1,0:T(8,128)(2,1)S(1)}, bf16[7,100,256]{2,1,0:T(8,128)(2,1)S(1)}, u32[]{:S(2)}, u32[]{:S(2)}) collective-permute-start(bf16[7,100,256]{2,1,0:T(8,128)(2,1)S(1)} %pad_maximum_fusion.refs_1_), channel_id=1, source_target_pairs={{2,0},{0,2},{6,4},{4,6},{10,8},{8,10},{14,12},{12,14},{18,16},{16,... | collective-permute-start | bytes 1075208 | tf_op jit(solution)/shard_map/ppermute | solution.py:202
  24.8 4.4 %collective-permute-start.7 = (bf16[144,256]{1,0:T(8,128)(2,1)S(1)}, bf16[144,256]{1,0:T(8,128)(2,1)S(1)}, u32[]{:S(2)}, u32[]{:S(2)}) collective-permute-start(bf16[144,256]{1,0:T(8,128)(2,1)S(1)} %get-tuple-element.33), channel_id=1, source_target_pairs={{1,0},{0,1},{3,2},{2,3},{5,4},{4,5},{7,6},{6,7},{9,8},{8,9},{11,10... | collective-permute-start | bytes 221192 | tf_op jit(solution)/shard_map/ppermute | solution.py:198
  41.9 1.4 %collective-permute-start.8 = (bf16[8,48,256]{2,1,0:T(8,128)(2,1)S(1)}, bf16[8,48,256]{2,1,0:T(8,128)(2,1)S(1)}, u32[]{:S(2)}, u32[]{:S(2)}) collective-permute-start(bf16[8,48,256]{2,1,0:T(8,128)(2,1)S(1)} %all_to_all.5.near), channel_id=1, source_target_pairs={{2,0},{0,2},{6,4},{4,6},{10,8},{8,10},{14,12},{12,14},{18,16},{16,... | collective-permute-start | bytes 589832 | tf_op jit(solution)/shard_map/ppermute | solution.py:202
  44.4 4.2 %collective-permute-start.9 = (f32[48,256]{1,0:T(8,128)S(1)}, f32[48,256]{1,0:T(8,128)S(1)}, u32[]{:S(2)}, u32[]{:S(2)}) collective-permute-start(f32[48,256]{1,0:T(8,128)S(1)} %get-tuple-element.38), channel_id=1, source_target_pairs={{1,0},{0,1},{3,2},{2,3},{5,4},{4,5},{7,6},{6,7},{9,8},{8,9},{11,10... | collective-permute-start | bytes 147464 | tf_op jit(solution)/shard_map/ppermute | solution.py:198

commit v10 on v9

--- a/solution.py
+++ b/solution.py
@@ -19,6 +19,10 @@
 
 def nt(a, b):
     return lax.dot_general(a, b, (((1,), (1,)), ((), ())), preferred_element_type=F32)
+
+
+def in_smem(value):
+    return value if value.size == 1 else pltpu.with_memory_space_constraint(value, pltpu.SMEM)
 
 
 def call(kernel, outs, smem=(), vmem=(), hbm=(), scratch=(), smem_outs=0, cost=1 << 20):
@@ -32,7 +36,7 @@
         scratch_shapes=scratch,
         compiler_params=pltpu.CompilerParams(vmem_limit_bytes=VMEM_LIMIT),
         cost_estimate=pl.CostEstimate(flops=cost, bytes_accessed=cost, transcendentals=0),
-    )(*vmem, *smem, *[pltpu.with_memory_space_constraint(value, pltpu.HBM) for value in hbm])
+    )(*vmem, *[in_smem(value) for value in smem], *[pltpu.with_memory_space_constraint(value, pltpu.HBM) for value in hbm])
 
 
 def fetched(sources, targets, sems):
@@ -51,15 +55,17 @@
     return nn(features[...], jnp.where(source == wanted, 1.0, 0.0).astype(BF16))
 
 
-def prepare(order, features, part, wanted_out, *rest):
+def prepare(order, features, tiles, part, wanted_out, tiles_out, *rest):
     order_in, features_in, sems = rest
-    for copy in fetched((order, features), (order_in, features_in), sems):
+    copies = fetched((order, features, tiles), (order_in, features_in, tiles_out), sems)
+    for copy in copies[:2]:
         copy.wait()
     tile = features.shape[1]
     member = lax.axis_index("rep")
     wanted = order_in[:, pl.ds(pl.multiple_of(member * tile, tile), tile)]
     wanted_out[...] = wanted
     part[...] = picked(features_in, wanted, member)
+    copies[2].wait()
 
 
 def arrange(part, wanted, *rest):
@@ -74,12 +80,11 @@
 
 
 def stage(reps, _, live, *refs):
-    sources, (plan, bias_1, bias_2, weight_1, weight_2, tiles), scratch = refs[:7], refs[7:13], refs[13:]
+    sources, (plan, bias_1, bias_2, weight_1, weight_2), scratch = refs[:6], refs[6:11], refs[11:]
     rows_in, columns_in, row_1, row_2, weight_in, sems = scratch
-    slots = tiles.shape[0]
+    slots = rows_in.shape[1]
     blocks = lax.axis_size("blk")
-    copies = fetched(sources, (rows_in, columns_in, row_1, row_2, weight_in, weight_2, tiles), sems)
-    for copy in copies[:5]:
+    for copy in fetched(sources, (rows_in, columns_in, row_1, row_2, weight_in, weight_2), sems):
         copy.wait()
     bias_1[...] = jnp.broadcast_to(row_1[...], (8, row_1.shape[1])).T[:, :1]
     bias_2[...] = jnp.broadcast_to(row_2[...], (8, row_2.shape[1])).T[:, :1]
@@ -90,17 +95,11 @@
         local = rows_in[0, slot] - block * reps
         step = lax.rem(local - member + reps, reps)
         plan[slots + slot] = jnp.where((slot < live[0]) & (local >= 0) & (local < reps), step, -1)
-    for copy in copies[5:]:
-        copy.wait()
-
-
-def project(weight_t, *refs):
-    *stacks, out = refs
-    start = 0
-    for stack in stacks:
-        for index in range(stack.shape[0]):
-            out[start + index] = nn(weight_t[...], stack[index]).astype(BF16)
-        start += stack.shape[0]
+
+
+def project(weight_t, stack, out):
+    for index in range(stack.shape[0]):
+        out[index] = nn(weight_t[...], stack[index]).astype(BF16)
 
 
 def turn(tiles, arrived, plan, arrived_out, tiles_t, degrees):
@@ -207,40 +206,42 @@
     return 1, list(zip(rest[0::2], rest[1::2]))
 
 
+def two_ways(pairs):
+    return pairs + [(pair[1], pair[0]) for pair in pairs]
+
+
 def panel_order(outer, core):
     first, pairs = outer_order(outer)
     lists = []
     for here in (core, 1 - core):
-        across = [jnp.where(here == 0, 4 * pair[0], 4 * pair[1]) + e for pair in pairs for e in range(2)]
-        lists.append([4 * first, *across, 2, 4 * first + 2, *[apart + 2 for apart in across]])
-    return [0, 1, *lists[0]], [apart ^ 1 for apart in lists[1]]
-
-
-def packed(*parts, after=()):
+        across = [jnp.where(here == 0, *sides) for sides in two_ways(pairs)]
+        across = [4 * first, *[4 * apart for apart in across]]
+        lists.append([0, *across, 2, *[apart + 2 for apart in across]])
+    return lists[0], [apart ^ 1 for apart in lists[1]]
+
+
+def packed(*parts):
     def pack(*refs):
         for index in range(len(parts)):
             refs[-1][index] = refs[index][...]
 
     out = jax.ShapeDtypeStruct((len(parts), *parts[0].shape), BF16)
-    return call(pack, [out], vmem=(*parts, *after), cost=1 << 32)[0]
+    return call(pack, [out], vmem=parts)[0]
 
 
 def gather_features(value, aside, later):
     outer = lax.axis_size("blk") // 4
     first, pairs = outer_order(outer)
-    other = swapped(value, (1, 1))
     ahead = swapped(value, (4 * first, 4 * first))
-    both = jnp.stack([value, other])
-    across = [swapped(both, (4 * pair[0], 4 * pair[1])) for pair in pairs]
-    across = across[0] if len(across) == 1 else jnp.concatenate(across)
+    across = [swapped(value, (4 * sides[0], 4 * sides[1])) for sides in two_ways(pairs)]
     here = packed(value, ahead)
     over = swapped(here, (2, 2))
-    beside = aside(here)
-    across = packed(across, after=(beside[1],))[0]
-    beyond = swapped(across, (2, 2))
+    early, late = packed(*across[: len(pairs)]), packed(*across[len(pairs) :])
+    beyond = [swapped(early, (2, 2)), swapped(late, (2, 2))]
+    beside = aside(over)
     over, *behind = later(over, beside)
-    near = jnp.concatenate([ahead[None], across, over, beyond])
-    return (both, near, swapped(near, (1, 1))), beside, behind
+    near = jnp.concatenate([here, early, late, over, *beyond])
+    return (near, swapped(near, (1, 1))), beside, behind
 
 
 def gather_classes(value):
@@ -276,28 +277,31 @@
 
     own_t = features.T
     others = [shifted(own_t, "rep", step) for step in range(1, reps)]
-    prepared = call(
+    part, wanted, tiles = call(
         prepare,
-        [shape((width, tile), F32), shape((1, tile), jnp.int32)],
-        hbm=(node_order, own_t),
+        [
+            shape((width, tile), F32),
+            shape((1, tile), jnp.int32),
+            shape(tile_values.shape[1:], BF16),
+        ],
+        hbm=(node_order, own_t, tile_values[0]),
         scratch=[
             pltpu.VMEM(node_order.shape, jnp.int32),
             pltpu.VMEM(own_t.shape, BF16),
-            pltpu.SemaphoreType.DMA((2,)),
+            pltpu.SemaphoreType.DMA((3,)),
         ],
     )
-    (ordered,) = call(arrange, [shape((width, tile), BF16)], vmem=(*prepared, *others))
+    (ordered,) = call(arrange, [shape((width, tile), BF16)], vmem=(part, wanted, *others))
 
     def staged(after):
         return call(
             functools.partial(stage, reps),
             [
-                shape((2 * slots,), jnp.int32),
+                pltpu.SMEM((2 * slots,), jnp.int32),
                 shape((hidden, 1), F32),
                 shape((classes, 1), F32),
                 shape((hidden, width), BF16),
                 shape((classes, hidden), BF16),
-                shape(tile_values.shape[1:], BF16),
             ],
             vmem=(after,),
             smem=(tile_live,),
@@ -308,7 +312,6 @@
                 second_bias[None],
                 first_weight,
                 second_weight.T,
-                tile_values[0],
             ),
             scratch=[
                 pltpu.SMEM((1, slots), jnp.int32),
@@ -316,13 +319,12 @@
                 pltpu.VMEM((1, hidden), F32),
                 pltpu.VMEM((1, classes), F32),
                 pltpu.VMEM(first_weight.shape, BF16),
-                pltpu.SemaphoreType.DMA((7,)),
+                pltpu.SemaphoreType.DMA((6,)),
             ],
             smem_outs=1,
         )
 
     def turned(arrived, values):
-        tiles = values[-1]
         return call(
             turn,
             [
@@ -334,17 +336,17 @@
             smem=(values[0],),
         )
 
-    (both, near, far), values, (tiles, degrees) = gather_features(ordered, staged, turned)
-    plan, bias_1, bias_2, weight_1, weight_2, _ = values
+    (near, far), values, (tiles_t, degrees) = gather_features(ordered, staged, turned)
+    plan, bias_1, bias_2, weight_1, weight_2 = values
     (projected,) = call(
         project,
-        [shape((2 + near.shape[0], hidden, tile), BF16)],
-        vmem=(weight_1, both, near),
+        [shape((near.shape[0], hidden, tile), BF16)],
+        vmem=(weight_1, near),
     )
     own, *sums = call(
         aggregate_hidden,
         [shape((hidden, tile), F32)] + [shape((hidden + ONES_ROWS, tile), BF16)] * (reps - 1),
-        vmem=(projected, far, weight_1, tiles, degrees),
+        vmem=(projected, far, weight_1, tiles_t, degrees),
         smem=(plan,),
         scratch=[pltpu.VMEM((blocks, hidden, tile), BF16)],
     )
@@ -356,7 +358,7 @@
     own, *sums = call(
         aggregate_classes,
         [shape((padded, tile), F32)] * reps,
-        vmem=(*gather_classes(classes_in), tiles),
+        vmem=(*gather_classes(classes_in), tiles_t),
         smem=(plan,),
         scratch=[pltpu.VMEM((blocks, padded, tile), BF16)],
     )

time: 49.5 us -> 45.9 us (0.927)
  Pallas kernels: 8.59 us -> 6.24 us
  blocking collectives: 12.5 us -> 10.5 us
  starting transfers between devices: 14.2 us -> 15.8 us
  waiting for transfers between devices: 13.2 us -> 12.3 us
    pallas_call x11 -> x12, Pallas kernels: 8.59 us -> 6.24 us  [call(): pl.pallas_call(kernel, out_shape=outs, in_specs=[pl.BlockSpec(memory_spac...]
    all_to_all x1, blocking collectives: 12.5 us -> 10.5 us  [gather_classes(): near = lax.all_to_all(copies, 'blk', 0, 0, axis_index_groups=groups)]
    ppermute x7 -> x8, starting transfers between devices: 8.14 us -> 9.75 us  [swapped(): lax.ppermute(value, 'blk', [(d ^ masks[d % 2], d) for d in range(lax.axis...]
    ppermute x3, waiting for transfers between devices: 6.74 us -> 6.11 us  [shifted(): lax.ppermute(value, axis, [((d + step) % size, d) for d in range(size)])]
    ppermute x7 -> x8, waiting for transfers between devices: 6.44 us -> 6.21 us  [swapped(): lax.ppermute(value, 'blk', [(d ^ masks[d % 2], d) for d in range(lax.axis...]
  transfers between devices with their start and end apart: 10 -> 11, of which waited for: 7 -> 8; matrix products, arithmetic and copies ran while one was open for 0% -> 0% of each run, Pallas kernels for 10% -> 8%
where the time goes in v10:
time: 45.9 us; the launch traced here: 45.7 us
  starting transfers between devices  15.8 us (34%)
  waiting for transfers between devices  12.3 us (27%)
  blocking collectives  10.5 us (23%)
  Pallas kernels  6.24 us (14%)
  between operations  0.75 us (2%)
    all_to_all x1, blocking collectives, gather_classes(): near = lax.all_to_all(copies, 'blk', 0, 0, axis_index_groups=groups)  10.5 us
    ppermute x8, starting transfers between devices, swapped(): lax.ppermute(value, 'blk', [(d ^ masks[d % 2], d) for d in range(lax.axis...  9.75 us
    pallas_call x12, Pallas kernels, call(): pl.pallas_call(kernel, out_shape=outs, in_specs=[pl.BlockSpec(memory_spac...  6.24 us
    ppermute x8, waiting for transfers between devices, swapped(): lax.ppermute(value, 'blk', [(d ^ masks[d % 2], d) for d in range(lax.axis...  6.21 us
    ppermute x3, waiting for transfers between devices, shifted(): lax.ppermute(value, axis, [((d + step) % size, d) for d in range(size)])  6.11 us
    ppermute x3, starting transfers between devices, shifted(): lax.ppermute(value, axis, [((d + step) % size, d) for d in range(size)])  6.05 us
  transfers between devices with their start and end apart: 11, of which 8 were waited for; matrix products, arithmetic and copies ran while one was open for 0% of the time, Pallas kernels for 8%

profile of v10, /device:TPU:0, one launch (start us, length us, event | category | flops | bytes accessed | tf_op | source)
XLA Modules:
  0.0 45.7 jit_solution(9505908100692218050)
XLA Ops:
  0.0 2.9 %collective-permute-start = (bf16[100,256]{1,0:T(8,128)(2,1)}, bf16[100,256]{1,0:T(8,128)(2,1)S(1)}, u32[]{:S(2)}, u32[]{:S(2)}) collective-permute-start(bf16[100,256]{1,0:T(8,128)(2,1)} %bitcast.7), channel_id=1, source_target_pairs={{1,0},{0,1},{3,2},{2,3},{5,4},{4,5},{7,6},{6,7},{9,8},{8,9},{11,10... | collective-permute-start | bytes 153608 | tf_op jit(solution)/shard_map/ppermute | solution.py:197
  2.9 1.7 %shard_map.100 = (f32[100,256]{1,0:T(8,128)S(1)}, s32[1,256]{1,0:T(1,128)S(1)}, bf16[16,256,256]{2,1,0:T(8,128)(2,1)S(1)}) custom-call(s32[1,512]{1,0:T(1,128)} %order.1, bf16[100,256]{1,0:T(8,128)(2,1)} %bitcast.8, bf16[16,256,256]{2,1,0:T(8,128)(2,1)} %bitcast.6), custom_call_target="tpu_custom_call" | custom-call | flops 1048576 | bytes 1048576 | tf_op jit(solution)/shard_map/pallas_call | solution.py:31
  4.6 0.6 %collective-permute-done.rest_0_ = bf16[100,256]{1,0:T(8,128)(2,1)S(1)} collective-permute-done((bf16[100,256]{1,0:T(8,128)(2,1)}, bf16[100,256]{1,0:T(8,128)(2,1)S(1)}, u32[]{:S(2)}, u32[]{:S(2)}) %collective-permute-start) | collective-permute-done | bytes 51232 | tf_op jit(solution)/shard_map/ppermute | solution.py:197
  5.3 0.2 shard_map.101.refs_0_
  5.4 2.2 %collective-permute-start.1 = (bf16[100,256]{1,0:T(8,128)(2,1)S(1)}, bf16[100,256]{1,0:T(8,128)(2,1)S(1)}, u32[]{:S(2)}, u32[]{:S(2)}) collective-permute-start(bf16[100,256]{1,0:T(8,128)(2,1)S(1)} %shard_map.101.refs_0_), channel_id=1, source_target_pairs={{8,0},{10,2},{12,4},{14,6},{0,8},{2,10},{4,12},{6,14},{24,16},{26,... | collective-permute-start | bytes 153608 | tf_op jit(solution)/shard_map/ppermute | solution.py:201
  8.3 2.7 %collective-permute-start.3 = (bf16[100,256]{1,0:T(8,128)(2,1)S(1)}, bf16[100,256]{1,0:T(8,128)(2,1)S(1)}, u32[]{:S(2)}, u32[]{:S(2)}) collective-permute-start(bf16[100,256]{1,0:T(8,128)(2,1)S(1)} %shard_map.101.refs_0_), channel_id=1, source_target_pairs={{16,0},{26,2},{20,4},{30,6},{24,8},{18,10},{28,12},{22,14},{0,16},... | collective-permute-start | bytes 153608 | tf_op jit(solution)/shard_map/ppermute | solution.py:201
  10.9 0.0 collective-permute-start.4
  10.9 0.0 collective-permute-done.1.refs_1_
  10.9 1.8 %collective-permute-start.2 = (bf16[2,100,256]{2,1,0:T(8,128)(2,1)S(1)}, bf16[2,100,256]{2,1,0:T(8,128)(2,1)S(1)}, u32[]{:S(2)}, u32[]{:S(2)}) collective-permute-start(bf16[2,100,256]{2,1,0:T(8,128)(2,1)S(1)} %shard_map.102), channel_id=1, source_target_pairs={{4,0},{6,2},{0,4},{2,6},{12,8},{14,10},{8,12},{10,14},{20,16},{22,... | collective-permute-start | bytes 307208 | tf_op jit(solution)/shard_map/ppermute | solution.py:201
  12.7 1.9 %collective-permute-done.3.refs_0_ = bf16[100,256]{1,0:T(8,128)(2,1)S(1)} collective-permute-done((bf16[100,256]{1,0:T(8,128)(2,1)S(1)}, bf16[100,256]{1,0:T(8,128)(2,1)S(1)}, u32[]{:S(2)}, u32[]{:S(2)}) %collective-permute-start.3) | collective-permute-done | bytes 51232 | tf_op jit(solution)/shard_map/ppermute | solution.py:201
  14.6 1.6 %collective-permute-start.5 = (bf16[1,100,256]{2,1,0:T(8,128)(2,1)S(1)}, bf16[1,100,256]{2,1,0:T(8,128)(2,1)S(1)}, u32[]{:S(2)}, u32[]{:S(2)}) collective-permute-start(bf16[1,100,256]{2,1,0:T(8,128)(2,1)S(1)} %shard_map.104), channel_id=1, source_target_pairs={{4,0},{6,2},{0,4},{2,6},{12,8},{14,10},{8,12},{10,14},{20,16},{22,... | collective-permute-start | bytes 153608 | tf_op jit(solution)/shard_map/ppermute | solution.py:201
  16.2 0.6 %collective-permute-done.4.refs_0_ = bf16[100,256]{1,0:T(8,128)(2,1)S(1)} collective-permute-done((bf16[100,256]{1,0:T(8,128)(2,1)S(1)}, bf16[100,256]{1,0:T(8,128)(2,1)S(1)}, u32[]{:S(2)}, u32[]{:S(2)}) %collective-permute-start.4) | collective-permute-done | bytes 51232 | tf_op jit(solution)/shard_map/ppermute | solution.py:201
  16.9 1.5 %collective-permute-start.6 = (bf16[1,100,256]{2,1,0:T(8,128)(2,1)S(1)}, bf16[1,100,256]{2,1,0:T(8,128)(2,1)S(1)}, u32[]{:S(2)}, u32[]{:S(2)}) collective-permute-start(bf16[1,100,256]{2,1,0:T(8,128)(2,1)S(1)} %shard_map.105), channel_id=1, source_target_pairs={{4,0},{6,2},{0,4},{2,6},{12,8},{14,10},{8,12},{10,14},{20,16},{22,... | collective-permute-start | bytes 153608 | tf_op jit(solution)/shard_map/ppermute | solution.py:201
  18.4 0.0 collective-permute-done.2._.arrived
  18.4 1.0 %shard_map.103 = (s32[32]{0:T(128)S(4)}, f32[128,1]{1,0:T(8,128)S(1)}, f32[47,1]{1,0:T(8,128)S(1)}, bf16[128,100]{1,0:T(8,128)(2,1)S(1)}, bf16[47,128]{1,0:T(8,128)(2,1)S(1)}) custom-call(bf16[2,100,256]{2,1,0:T(8,128)(2,1)S(1)} %collective-permute-done.2._.arrived, s32[1]{0:T(128)S(6)} %copy.16.live, s32[1,16]{1,0:T(1,128)} %refs_0_.1, s32[1,16]{1,0:T(1,128)} %refs_1_.1, ...), custom_call_target="tpu_custom_call" | custom-call | flops 1048576 | bytes 1048576 | tf_op jit(solution)/shard_map/pallas_call | solution.py:31
  19.4 0.7 %shard_map.106 = (bf16[2,100,256]{2,1,0:T(8,128)(2,1)S(1)}, bf16[16,256,256]{2,1,0:T(8,128)(2,1)S(1)}, f32[2,8,256]{2,1,0:T(8,128)S(1)}) custom-call(bf16[16,256,256]{2,1,0:T(8,128)(2,1)S(1)} %get-tuple-element.25.tiles, bf16[2,100,256]{2,1,0:T(8,128)(2,1)S(1)} %collective-permute-done.2._.arrived, s32[32]{0:T(128)S(4)} %get-tuple-element.26.plan), custom_call_target="tpu_custom_call" | custom-call | flops 1048576 | bytes 1048576 | tf_op jit(solution)/shard_map/pallas_call | solution.py:31
  20.2 0.0 collective-permute-done.5
  20.2 0.8 %collective-permute-done.6 = bf16[1,100,256]{2,1,0:T(8,128)(2,1)S(1)} collective-permute-done((bf16[1,100,256]{2,1,0:T(8,128)(2,1)S(1)}, bf16[1,100,256]{2,1,0:T(8,128)(2,1)S(1)}, u32[]{:S(2)}, u32[]{:S(2)}) %collective-permute-start.6) | collective-permute-done | bytes 51232 | tf_op jit(solution)/shard_map/ppermute | solution.py:201
  21.0 0.0 collective-permute-start.7
  21.0 0.3 shard_map.107.projected.hidden_in
  21.3 1.5 %collective-permute-done.7.far = bf16[8,100,256]{2,1,0:T(8,128)(2,1)S(1)} collective-permute-done((bf16[8,100,256]{2,1,0:T(8,128)(2,1)S(1)}, bf16[8,100,256]{2,1,0:T(8,128)(2,1)S(1)}, u32[]{:S(2)}, u32[]{:S(2)}) %collective-permute-start.7) | collective-permute-done | bytes 409632 | tf_op jit(solution)/shard_map/ppermute | solution.py:201
  22.8 1.0 %shard_map.108 = (f32[128,256]{1,0:T(8,128)S(1)}, bf16[144,256]{1,0:T(8,128)(2,1)S(1)}) custom-call(bf16[8,128,256]{2,1,0:T(8,128)(2,1)S(1)} %shard_map.107.projected.hidden_in, bf16[8,100,256]{2,1,0:T(8,128)(2,1)S(1)} %collective-permute-done.7.far, bf16[128,100]{1,0:T(8,128)(2,1)S(1)} %get-tuple-element.24.weight_t, ...), custom_call_target="tpu_custom_call" | custom-call | flops 1048576 | bytes 1048576 | tf_op jit(solution)/shard_map/pallas_call | solution.py:31
  23.7 1.6 %collective-permute-start.8 = (bf16[144,256]{1,0:T(8,128)(2,1)S(1)}, bf16[144,256]{1,0:T(8,128)(2,1)S(1)}, u32[]{:S(2)}, u32[]{:S(2)}) collective-permute-start(bf16[144,256]{1,0:T(8,128)(2,1)S(1)} %get-tuple-element.33), channel_id=1, source_target_pairs={{1,0},{0,1},{3,2},{2,3},{5,4},{4,5},{7,6},{6,7},{9,8},{8,9},{11,10... | collective-permute-start | bytes 221192 | tf_op jit(solution)/shard_map/ppermute | solution.py:197
  25.3 2.9 %collective-permute-done.8.rest_0_ = bf16[144,256]{1,0:T(8,128)(2,1)S(1)} collective-permute-done((bf16[144,256]{1,0:T(8,128)(2,1)S(1)}, bf16[144,256]{1,0:T(8,128)(2,1)S(1)}, u32[]{:S(2)}, u32[]{:S(2)}) %collective-permute-start.8) | collective-permute-done | bytes 73760 | tf_op jit(solution)/shard_map/ppermute | solution.py:197
  28.2 0.2 shard_map.109
  28.4 10.5 %all_to_all.5.near = bf16[8,48,256]{2,1,0:T(8,128)(2,1)S(1)} all-to-all(bf16[8,48,256]{2,1,0:T(8,128)(2,1)S(1)} %broadcast_in_dim.14), channel_id=1, replica_groups={{0,4,8,12,16,20,24,28},{2,6,10,14,18,22,26,30},{1,5,9,13,17,21,25,29},{..., dimensions={0} | all-to-all | bytes 393216 | tf_op jit(solution)/shard_map/all_to_all | solution.py:251
  38.9 0.0 collective-permute-start.9
  38.9 1.4 %collective-permute-done.9.far = bf16[8,48,256]{2,1,0:T(8,128)(2,1)S(1)} collective-permute-done((bf16[8,48,256]{2,1,0:T(8,128)(2,1)S(1)}, bf16[8,48,256]{2,1,0:T(8,128)(2,1)S(1)}, u32[]{:S(2)}, u32[]{:S(2)}) %collective-permute-start.9) | collective-permute-done | bytes 196640 | tf_op jit(solution)/shard_map/ppermute | solution.py:201
  40.3 0.5 %shard_map.110 = (f32[48,256]{1,0:T(8,128)S(1)}, f32[48,256]{1,0:T(8,128)S(1)}) custom-call(bf16[8,48,256]{2,1,0:T(8,128)(2,1)S(1)} %all_to_all.5.near, bf16[8,48,256]{2,1,0:T(8,128)(2,1)S(1)} %collective-permute-done.9.far, bf16[16,256,256]{2,1,0:T(8,128)(2,1)S(1)} %get-tuple-element.31.tiles_t, s32[32]{0:T(128)S(4)} %get-tuple-element.26.plan), custom_call_target="tpu_custom_call" | custom-call | flops 1048576 | bytes 1048576 | tf_op jit(solution)/shard_map/pallas_call | solution.py:31
  40.8 1.6 %collective-permute-start.10 = (f32[48,256]{1,0:T(8,128)S(1)}, f32[48,256]{1,0:T(8,128)S(1)}, u32[]{:S(2)}, u32[]{:S(2)}) collective-permute-start(f32[48,256]{1,0:T(8,128)S(1)} %get-tuple-element.38), channel_id=1, source_target_pairs={{1,0},{0,1},{3,2},{2,3},{5,4},{4,5},{7,6},{6,7},{9,8},{8,9},{11,10... | collective-permute-start | bytes 147464 | tf_op jit(solution)/shard_map/ppermute | solution.py:197
  42.4 2.6 %collective-permute-done.10.rest_0_ = f32[48,256]{1,0:T(8,128)S(1)} collective-permute-done((f32[48,256]{1,0:T(8,128)S(1)}, f32[48,256]{1,0:T(8,128)S(1)}, u32[]{:S(2)}, u32[]{:S(2)}) %collective-permute-start.10) | collective-permute-done | bytes 49184 | tf_op jit(solution)/shard_map/ppermute | solution.py:197
  45.0 0.7 %shard_map.111 = f32[47,256]{1,0:T(8,128)} custom-call(bf16[48,256]{1,0:T(8,128)(2,1)S(1)} %get-tuple-element.34.classes_in, f32[1,256]{1,0:T(1,128)S(1)} %get-tuple-element.35.scaling, f32[47,1]{1,0:T(8,128)S(1)} %get-tuple-element.36.bias, f32[48,256]{1,0:T(8,128)S(1)} %get-tuple-element.37.own, f32[48,256]{1,0:T(8,128)S(1)} %collective-permute-done.10.rest_0_), custom_call_target="tpu_custom_call" | custom-call | flops 1048576 | bytes 1048576 | tf_op jit(solution)/shard_map/pallas_call | solution.py:31
  (10 shorter events, 0.1 us)
Async XLA Ops:
  0.0 5.3 %collective-permute-start = (bf16[100,256]{1,0:T(8,128)(2,1)}, bf16[100,256]{1,0:T(8,128)(2,1)S(1)}, u32[]{:S(2)}, u32[]{:S(2)}) collective-permute-start(bf16[100,256]{1,0:T(8,128)(2,1)} %bitcast.7), channel_id=1, source_target_pairs={{1,0},{0,1},{3,2},{2,3},{5,4},{4,5},{7,6},{6,7},{9,8},{8,9},{11,10... | collective-permute-start | bytes 153608 | tf_op jit(solution)/shard_map/ppermute | solution.py:197
  5.4 5.5 %collective-permute-start.1 = (bf16[100,256]{1,0:T(8,128)(2,1)S(1)}, bf16[100,256]{1,0:T(8,128)(2,1)S(1)}, u32[]{:S(2)}, u32[]{:S(2)}) collective-permute-start(bf16[100,256]{1,0:T(8,128)(2,1)S(1)} %shard_map.101.refs_0_), channel_id=1, source_target_pairs={{8,0},{10,2},{12,4},{14,6},{0,8},{2,10},{4,12},{6,14},{24,16},{26,... | collective-permute-start | bytes 153608 | tf_op jit(solution)/shard_map/ppermute | solution.py:201
  8.3 6.4 %collective-permute-start.3 = (bf16[100,256]{1,0:T(8,128)(2,1)S(1)}, bf16[100,256]{1,0:T(8,128)(2,1)S(1)}, u32[]{:S(2)}, u32[]{:S(2)}) collective-permute-start(bf16[100,256]{1,0:T(8,128)(2,1)S(1)} %shard_map.101.refs_0_), channel_id=1, source_target_pairs={{16,0},{26,2},{20,4},{30,6},{24,8},{18,10},{28,12},{22,14},{0,16},... | collective-permute-start | bytes 153608 | tf_op jit(solution)/shard_map/ppermute | solution.py:201
  10.9 5.9 %collective-permute-start.4 = (bf16[100,256]{1,0:T(8,128)(2,1)S(1)}, bf16[100,256]{1,0:T(8,128)(2,1)S(1)}, u32[]{:S(2)}, u32[]{:S(2)}) collective-permute-start(bf16[100,256]{1,0:T(8,128)(2,1)S(1)} %shard_map.101.refs_0_), channel_id=1, source_target_pairs={{24,0},{18,2},{28,4},{22,6},{16,8},{26,10},{20,12},{30,14},{8,16},... | collective-permute-start | bytes 153608 | tf_op jit(solution)/shard_map/ppermute | solution.py:201
  10.9 7.4 %collective-permute-start.2 = (bf16[2,100,256]{2,1,0:T(8,128)(2,1)S(1)}, bf16[2,100,256]{2,1,0:T(8,128)(2,1)S(1)}, u32[]{:S(2)}, u32[]{:S(2)}) collective-permute-start(bf16[2,100,256]{2,1,0:T(8,128)(2,1)S(1)} %shard_map.102), channel_id=1, source_target_pairs={{4,0},{6,2},{0,4},{2,6},{12,8},{14,10},{8,12},{10,14},{20,16},{22,... | collective-permute-start | bytes 307208 | tf_op jit(solution)/shard_map/ppermute | solution.py:201
  14.6 5.5 %collective-permute-start.5 = (bf16[1,100,256]{2,1,0:T(8,128)(2,1)S(1)}, bf16[1,100,256]{2,1,0:T(8,128)(2,1)S(1)}, u32[]{:S(2)}, u32[]{:S(2)}) collective-permute-start(bf16[1,100,256]{2,1,0:T(8,128)(2,1)S(1)} %shard_map.104), channel_id=1, source_target_pairs={{4,0},{6,2},{0,4},{2,6},{12,8},{14,10},{8,12},{10,14},{20,16},{22,... | collective-permute-start | bytes 153608 | tf_op jit(solution)/shard_map/ppermute | solution.py:201
  16.9 4.1 %collective-permute-start.6 = (bf16[1,100,256]{2,1,0:T(8,128)(2,1)S(1)}, bf16[1,100,256]{2,1,0:T(8,128)(2,1)S(1)}, u32[]{:S(2)}, u32[]{:S(2)}) collective-permute-start(bf16[1,100,256]{2,1,0:T(8,128)(2,1)S(1)} %shard_map.105), channel_id=1, source_target_pairs={{4,0},{6,2},{0,4},{2,6},{12,8},{14,10},{8,12},{10,14},{20,16},{22,... | collective-permute-start | bytes 153608 | tf_op jit(solution)/shard_map/ppermute | solution.py:201
  21.0 1.8 %collective-permute-start.7 = (bf16[8,100,256]{2,1,0:T(8,128)(2,1)S(1)}, bf16[8,100,256]{2,1,0:T(8,128)(2,1)S(1)}, u32[]{:S(2)}, u32[]{:S(2)}) collective-permute-start(bf16[8,100,256]{2,1,0:T(8,128)(2,1)S(1)} %constant_dynamic-update-slice_fusion.stack), channel_id=1, source_target_pairs={{2,0},{0,2},{6,4},{4,6},{10,8},{8,10},{14,12},{12,14},{18,16},{16,... | collective-permute-start | bytes 1228808 | tf_op jit(solution)/shard_map/ppermute | solution.py:201
  23.7 4.4 %collective-permute-start.8 = (bf16[144,256]{1,0:T(8,128)(2,1)S(1)}, bf16[144,256]{1,0:T(8,128)(2,1)S(1)}, u32[]{:S(2)}, u32[]{:S(2)}) collective-permute-start(bf16[144,256]{1,0:T(8,128)(2,1)S(1)} %get-tuple-element.33), channel_id=1, source_target_pairs={{1,0},{0,1},{3,2},{2,3},{5,4},{4,5},{7,6},{6,7},{9,8},{8,9},{11,10... | collective-permute-start | bytes 221192 | tf_op jit(solution)/shard_map/ppermute | solution.py:197
  38.9 1.4 %collective-permute-start.9 = (bf16[8,48,256]{2,1,0:T(8,128)(2,1)S(1)}, bf16[8,48,256]{2,1,0:T(8,128)(2,1)S(1)}, u32[]{:S(2)}, u32[]{:S(2)}) collective-permute-start(bf16[8,48,256]{2,1,0:T(8,128)(2,1)S(1)} %all_to_all.5.near), channel_id=1, source_target_pairs={{2,0},{0,2},{6,4},{4,6},{10,8},{8,10},{14,12},{12,14},{18,16},{16,... | collective-permute-start | bytes 589832 | tf_op jit(solution)/shard_map/ppermute | solution.py:201
  40.8 4.2 %collective-permute-start.10 = (f32[48,256]{1,0:T(8,128)S(1)}, f32[48,256]{1,0:T(8,128)S(1)}, u32[]{:S(2)}, u32[]{:S(2)}) collective-permute-start(f32[48,256]{1,0:T(8,128)S(1)} %get-tuple-element.38), channel_id=1, source_target_pairs={{1,0},{0,1},{3,2},{2,3},{5,4},{4,5},{7,6},{6,7},{9,8},{8,9},{11,10... | collective-permute-start | bytes 147464 | tf_op jit(solution)/shard_map/ppermute | solution.py:197

commit v11 on v10

--- a/solution.py
+++ b/solution.py
@@ -55,7 +55,8 @@
     return nn(features[...], jnp.where(source == wanted, 1.0, 0.0).astype(BF16))
 
 
-def prepare(order, features, tiles, part, wanted_out, tiles_out, *rest):
+def prepare(live, order, features, tiles, live_out, part, wanted_out, tiles_out, *rest):
+    live_out[0] = live[0]
     order_in, features_in, sems = rest
     copies = fetched((order, features, tiles), (order_in, features_in, tiles_out), sems)
     for copy in copies[:2]:
@@ -132,10 +133,21 @@
     return [total[step * height : (step + 1) * height] for step in range(count)]
 
 
+def coded(values):
+    top = jnp.max(jnp.abs(values), axis=0, keepdims=True)
+    power = jnp.ceil(jnp.log2(jnp.maximum(top, 1e-30)))
+    return jnp.round(values * jnp.exp2(14.0 - power)).astype(jnp.int32), power.astype(jnp.int32)
+
+
+def decoded(codes, power):
+    return codes.astype(F32) * jnp.exp2(power.astype(F32) - 14.0)
+
+
 def in_thirds(row):
-    first = row.astype(BF16).astype(F32)
-    second = (row - first).astype(BF16).astype(F32)
-    return first, second, row - first - second
+    first = jnp.floor(row)
+    second = jnp.floor((row - first) * 16384.0)
+    third = jnp.round(((row - first) * 16384.0 - second) * 16384.0)
+    return [part.astype(jnp.int32) for part in (first, second, third)]
 
 
 def aggregate_hidden(projected, far, weight_t, tiles_t, degrees, plan, own, *rest):
@@ -147,21 +159,27 @@
         panels[place] = nn(weight_t[...], far[index]).astype(BF16)
     sums = summed(panels, plan, tiles_t, 1 + len(others))
     own[...] = sums[0]
-    row = lax.broadcasted_iota(jnp.int32, (8, own.shape[1]), 0)
+    row = lax.broadcasted_iota(jnp.int32, (ONES_ROWS, own.shape[1]), 0)
     for step, (part, out) in enumerate(zip(sums[1:], others), 1):
-        first, second, third = in_thirds(degrees[step])
-        terms = jnp.where(row == 0, first, jnp.where(row == 1, second, jnp.where(row == 2, third, 0.0)))
-        out[...] = jnp.concatenate([part, terms, jnp.zeros_like(terms)], axis=0).astype(BF16)
-
-
-def aggregate_classes(near, far, tiles_t, plan, *rest):
-    outs, panels = rest[:-1], rest[-1]
+        codes, power = coded(part)
+        terms = jnp.zeros(row.shape, jnp.int32)
+        for index, term in enumerate([power, *in_thirds(degrees[step, :1])]):
+            terms = jnp.where(row == index, term, terms)
+        out[...] = jnp.concatenate([codes, terms], axis=0).astype(jnp.int16)
+
+
+def aggregate_classes(near, far, tiles_t, plan, own, *rest):
+    others, panels = rest[:-1], rest[-1]
     chip = lax.axis_index("blk") // 2
     for index in range(near.shape[0]):
         panels[2 * (index ^ chip)] = near[index]
         panels[2 * (index ^ chip) + 1] = far[index]
-    for out, part in zip(outs, summed(panels, plan, tiles_t, len(outs))):
-        out[...] = part
+    sums = summed(panels, plan, tiles_t, 1 + len(others))
+    own[...] = sums[0]
+    row = lax.broadcasted_iota(jnp.int32, own.shape, 0)
+    for part, out in zip(sums[1:], others):
+        codes, power = coded(part)
+        out[...] = jnp.where(row == own.shape[0] - 1, power, codes).astype(jnp.int16)
 
 
 def combine(hidden_in, bias, weight_t, degrees, own, *rest):
@@ -169,10 +187,10 @@
     height = hidden_in.shape[1]
     total, degree = own[...], degrees[0, :1]
     for part in arrived:
-        values = part[...].astype(F32)
-        total = total + values[:height]
-        terms = [values[height + index : height + index + 1] for index in range(3)]
-        degree = degree + (terms[0] + (terms[1] + terms[2]))
+        codes = part[...].astype(jnp.int32)
+        total = total + decoded(codes[:height], codes[height : height + 1])
+        terms = [codes[height + 1 + index : height + 2 + index].astype(F32) for index in range(3)]
+        degree = degree + (terms[0] + (terms[1] + terms[2] * 2.0**-14) * 2.0**-14)
     scaling = lax.rsqrt(1.0 + degree)
     hidden = scaling * (total + hidden_in[0].astype(F32)) + bias[...]
     hidden = jnp.maximum(hidden, 0.0).astype(BF16)
@@ -184,10 +202,11 @@
 
 def finish(classes_in, scaling, bias, own, *rest):
     *arrived, out = rest
+    classes = out.shape[0]
     total = own[...]
     for part in arrived:
-        total = total + part[...]
-    classes = out.shape[0]
+        codes = part[...].astype(jnp.int32)
+        total = total + decoded(codes, codes[-1:])
     whole = total + classes_in[...].astype(F32)
     out[...] = scaling[...] * whole[:classes] + bias[...]
 
@@ -269,7 +288,7 @@
     reps = lax.axis_size("rep")
     blocks = lax.axis_size("blk")
     hidden, classes = second_weight.shape
-    padded = -(-classes // 16) * 16
+    padded = -(-(classes + 1) // 16) * 16
     shape = jax.ShapeDtypeStruct
 
     def exchanged(sums):
@@ -277,19 +296,22 @@
 
     own_t = features.T
     others = [shifted(own_t, "rep", step) for step in range(1, reps)]
-    part, wanted, tiles = call(
+    live, part, wanted, tiles = call(
         prepare,
         [
+            pltpu.SMEM((8,), jnp.int32),
             shape((width, tile), F32),
             shape((1, tile), jnp.int32),
             shape(tile_values.shape[1:], BF16),
         ],
+        smem=(tile_live,),
         hbm=(node_order, own_t, tile_values[0]),
         scratch=[
             pltpu.VMEM(node_order.shape, jnp.int32),
             pltpu.VMEM(own_t.shape, BF16),
             pltpu.SemaphoreType.DMA((3,)),
         ],
+        smem_outs=1,
     )
     (ordered,) = call(arrange, [shape((width, tile), BF16)], vmem=(part, wanted, *others))
 
@@ -304,7 +326,7 @@
                 shape((classes, hidden), BF16),
             ],
             vmem=(after,),
-            smem=(tile_live,),
+            smem=(live,),
             hbm=(
                 tile_rows,
                 tile_columns,
@@ -345,7 +367,7 @@
     )
     own, *sums = call(
         aggregate_hidden,
-        [shape((hidden, tile), F32)] + [shape((hidden + ONES_ROWS, tile), BF16)] * (reps - 1),
+        [shape((hidden, tile), F32)] + [shape((hidden + ONES_ROWS, tile), jnp.int16)] * (reps - 1),
         vmem=(projected, far, weight_1, tiles_t, degrees),
         smem=(plan,),
         scratch=[pltpu.VMEM((blocks, hidden, tile), BF16)],
@@ -357,7 +379,7 @@
     )
     own, *sums = call(
         aggregate_classes,
-        [shape((padded, tile), F32)] * reps,
+        [shape((padded, tile), F32)] + [shape((padded, tile), jnp.int16)] * (reps - 1),
         vmem=(*gather_classes(classes_in), tiles_t),
         smem=(plan,),
         scratch=[pltpu.VMEM((blocks, padded, tile), BF16)],

time: 45.9 us -> 45.7 us (level)
  blocking collectives: 10.5 us -> 11.1 us
  waiting for transfers between devices: 12.3 us -> 11.8 us
    all_to_all x1, blocking collectives: 10.5 us -> 11.1 us  [gather_classes(): near = lax.all_to_all(copies, 'blk', 0, 0, axis_index_groups=groups)]
    ppermute x3, waiting for transfers between devices: 6.11 us -> 5.49 us  [shifted(): lax.ppermute(value, axis, [((d + step) % size, d) for d in range(size)])]
  transfers between devices with their start and end apart: 11 -> 11, of which waited for: 8 -> 7; matrix products, arithmetic and copies ran while one was open for 0% -> 0% of each run, Pallas kernels for 8% -> 8%
where the time goes in v11:
time: 45.7 us; the launch traced here: 45.4 us
  starting transfers between devices  15.4 us (34%)
  waiting for transfers between devices  11.8 us (26%)
  blocking collectives  11.1 us (24%)
  Pallas kernels  6.32 us (14%)
  between operations  0.77 us (2%)
    all_to_all x1, blocking collectives, gather_classes(): near = lax.all_to_all(copies, 'blk', 0, 0, axis_index_groups=groups)  11.1 us
    ppermute x8, starting transfers between devices, swapped(): lax.ppermute(value, 'blk', [(d ^ masks[d % 2], d) for d in range(lax.axis...  9.59 us
    pallas_call x12, Pallas kernels, call(): pl.pallas_call(kernel, out_shape=outs, in_specs=[pl.BlockSpec(memory_spac...  6.32 us
    ppermute x8, waiting for transfers between devices, swapped(): lax.ppermute(value, 'blk', [(d ^ masks[d % 2], d) for d in range(lax.axis...  6.28 us
    ppermute x3, starting transfers between devices, shifted(): lax.ppermute(value, axis, [((d + step) % size, d) for d in range(size)])  5.76 us
    ppermute x3, waiting for transfers between devices, shifted(): lax.ppermute(value, axis, [((d + step) % size, d) for d in range(size)])  5.49 us
  transfers between devices with their start and end apart: 11, of which 7 were waited for; matrix products, arithmetic and copies ran while one was open for 0% of the time, Pallas kernels for 8%

profile of v11, /device:TPU:0, one launch (start us, length us, event | category | flops | bytes accessed | tf_op | source)
XLA Modules:
  0.0 45.4 jit_solution(6533288941353832517)
XLA Ops:
  0.0 2.9 %collective-permute-start = (bf16[100,256]{1,0:T(8,128)(2,1)}, bf16[100,256]{1,0:T(8,128)(2,1)S(1)}, u32[]{:S(2)}, u32[]{:S(2)}) collective-permute-start(bf16[100,256]{1,0:T(8,128)(2,1)} %bitcast.7), channel_id=1, source_target_pairs={{1,0},{0,1},{3,2},{2,3},{5,4},{4,5},{7,6},{6,7},{9,8},{8,9},{11,10... | collective-permute-start | bytes 153608 | tf_op jit(solution)/shard_map/ppermute | solution.py:216
  3.6 1.7 %shard_map.100 = (s32[8]{0:T(128)S(4)}, f32[100,256]{1,0:T(8,128)S(1)}, s32[1,256]{1,0:T(1,128)S(1)}, bf16[16,256,256]{2,1,0:T(8,128)(2,1)S(1)}) custom-call(s32[1]{0:T(128)S(6)} %copy.16.live, s32[1,512]{1,0:T(1,128)} %order.1, bf16[100,256]{1,0:T(8,128)(2,1)} %bitcast.8, bf16[16,256,256]{2,1,0:T(8,128)(2,1)} %bitcast.6), custom_call_target="tpu_custom_call" | custom-call | flops 1048576 | bytes 1048576 | tf_op jit(solution)/shard_map/pallas_call | solution.py:31
  5.3 0.0 collective-permute-done.rest_0_
  5.3 0.2 shard_map.101.refs_0_
  5.5 2.2 %collective-permute-start.1 = (bf16[100,256]{1,0:T(8,128)(2,1)S(1)}, bf16[100,256]{1,0:T(8,128)(2,1)S(1)}, u32[]{:S(2)}, u32[]{:S(2)}) collective-permute-start(bf16[100,256]{1,0:T(8,128)(2,1)S(1)} %shard_map.101.refs_0_), channel_id=1, source_target_pairs={{8,0},{10,2},{12,4},{14,6},{0,8},{2,10},{4,12},{6,14},{24,16},{26,... | collective-permute-start | bytes 153608 | tf_op jit(solution)/shard_map/ppermute | solution.py:220
  7.6 2.6 %collective-permute-start.3 = (bf16[100,256]{1,0:T(8,128)(2,1)S(1)}, bf16[100,256]{1,0:T(8,128)(2,1)S(1)}, u32[]{:S(2)}, u32[]{:S(2)}) collective-permute-start(bf16[100,256]{1,0:T(8,128)(2,1)S(1)} %shard_map.101.refs_0_), channel_id=1, source_target_pairs={{16,0},{26,2},{20,4},{30,6},{24,8},{18,10},{28,12},{22,14},{0,16},... | collective-permute-start | bytes 153608 | tf_op jit(solution)/shard_map/ppermute | solution.py:220
  10.2 0.0 collective-permute-start.4
  10.2 0.0 collective-permute-done.1.refs_1_
  10.2 1.8 %collective-permute-start.2 = (bf16[2,100,256]{2,1,0:T(8,128)(2,1)S(1)}, bf16[2,100,256]{2,1,0:T(8,128)(2,1)S(1)}, u32[]{:S(2)}, u32[]{:S(2)}) collective-permute-start(bf16[2,100,256]{2,1,0:T(8,128)(2,1)S(1)} %shard_map.102), channel_id=1, source_target_pairs={{4,0},{6,2},{0,4},{2,6},{12,8},{14,10},{8,12},{10,14},{20,16},{22,... | collective-permute-start | bytes 307208 | tf_op jit(solution)/shard_map/ppermute | solution.py:220
  12.0 2.3 %collective-permute-done.3.refs_0_ = bf16[100,256]{1,0:T(8,128)(2,1)S(1)} collective-permute-done((bf16[100,256]{1,0:T(8,128)(2,1)S(1)}, bf16[100,256]{1,0:T(8,128)(2,1)S(1)}, u32[]{:S(2)}, u32[]{:S(2)}) %collective-permute-start.3) | collective-permute-done | bytes 51232 | tf_op jit(solution)/shard_map/ppermute | solution.py:220
  14.3 1.5 %collective-permute-start.5 = (bf16[1,100,256]{2,1,0:T(8,128)(2,1)S(1)}, bf16[1,100,256]{2,1,0:T(8,128)(2,1)S(1)}, u32[]{:S(2)}, u32[]{:S(2)}) collective-permute-start(bf16[1,100,256]{2,1,0:T(8,128)(2,1)S(1)} %shard_map.104), channel_id=1, source_target_pairs={{4,0},{6,2},{0,4},{2,6},{12,8},{14,10},{8,12},{10,14},{20,16},{22,... | collective-permute-start | bytes 153608 | tf_op jit(solution)/shard_map/ppermute | solution.py:220
  15.9 0.3 collective-permute-done.4.refs_0_
  16.1 1.5 %collective-permute-start.6 = (bf16[1,100,256]{2,1,0:T(8,128)(2,1)S(1)}, bf16[1,100,256]{2,1,0:T(8,128)(2,1)S(1)}, u32[]{:S(2)}, u32[]{:S(2)}) collective-permute-start(bf16[1,100,256]{2,1,0:T(8,128)(2,1)S(1)} %shard_map.105), channel_id=1, source_target_pairs={{4,0},{6,2},{0,4},{2,6},{12,8},{14,10},{8,12},{10,14},{20,16},{22,... | collective-permute-start | bytes 153608 | tf_op jit(solution)/shard_map/ppermute | solution.py:220
  17.7 0.0 collective-permute-done.2._.arrived
  17.7 1.0 %shard_map.103 = (s32[32]{0:T(128)S(4)}, f32[128,1]{1,0:T(8,128)S(1)}, f32[47,1]{1,0:T(8,128)S(1)}, bf16[128,100]{1,0:T(8,128)(2,1)S(1)}, bf16[47,128]{1,0:T(8,128)(2,1)S(1)}) custom-call(bf16[2,100,256]{2,1,0:T(8,128)(2,1)S(1)} %collective-permute-done.2._.arrived, s32[8]{0:T(128)S(4)} %get-tuple-element.25.live, s32[1,16]{1,0:T(1,128)} %refs_0_.1, ...), custom_call_target="tpu_custom_call" | custom-call | flops 1048576 | bytes 1048576 | tf_op jit(solution)/shard_map/pallas_call | solution.py:31
  18.7 0.7 %shard_map.106 = (bf16[2,100,256]{2,1,0:T(8,128)(2,1)S(1)}, bf16[16,256,256]{2,1,0:T(8,128)(2,1)S(1)}, f32[2,8,256]{2,1,0:T(8,128)S(1)}) custom-call(bf16[16,256,256]{2,1,0:T(8,128)(2,1)S(1)} %get-tuple-element.27.tiles, bf16[2,100,256]{2,1,0:T(8,128)(2,1)S(1)} %collective-permute-done.2._.arrived, s32[32]{0:T(128)S(4)} %get-tuple-element.28.plan), custom_call_target="tpu_custom_call" | custom-call | flops 1048576 | bytes 1048576 | tf_op jit(solution)/shard_map/pallas_call | solution.py:31
  19.5 0.0 collective-permute-done.5
  19.5 0.8 %collective-permute-done.6 = bf16[1,100,256]{2,1,0:T(8,128)(2,1)S(1)} collective-permute-done((bf16[1,100,256]{2,1,0:T(8,128)(2,1)S(1)}, bf16[1,100,256]{2,1,0:T(8,128)(2,1)S(1)}, u32[]{:S(2)}, u32[]{:S(2)}) %collective-permute-start.6) | collective-permute-done | bytes 51232 | tf_op jit(solution)/shard_map/ppermute | solution.py:220
  20.3 0.0 collective-permute-start.7
  20.3 0.3 shard_map.107.projected.hidden_in
  20.6 1.5 %collective-permute-done.7.far = bf16[8,100,256]{2,1,0:T(8,128)(2,1)S(1)} collective-permute-done((bf16[8,100,256]{2,1,0:T(8,128)(2,1)S(1)}, bf16[8,100,256]{2,1,0:T(8,128)(2,1)S(1)}, u32[]{:S(2)}, u32[]{:S(2)}) %collective-permute-start.7) | collective-permute-done | bytes 409632 | tf_op jit(solution)/shard_map/ppermute | solution.py:220
  22.0 1.0 %shard_map.108 = (f32[128,256]{1,0:T(8,128)S(1)}, s16[144,256]{1,0:T(8,128)(2,1)S(1)}) custom-call(bf16[8,128,256]{2,1,0:T(8,128)(2,1)S(1)} %shard_map.107.projected.hidden_in, bf16[8,100,256]{2,1,0:T(8,128)(2,1)S(1)} %collective-permute-done.7.far, bf16[128,100]{1,0:T(8,128)(2,1)S(1)} %get-tuple-element.26.weight_t, ...), custom_call_target="tpu_custom_call" | custom-call | flops 1048576 | bytes 1048576 | tf_op jit(solution)/shard_map/pallas_call | solution.py:31
  23.1 1.6 %collective-permute-start.8 = (s16[144,256]{1,0:T(8,128)(2,1)S(1)}, s16[144,256]{1,0:T(8,128)(2,1)S(1)}, u32[]{:S(2)}, u32[]{:S(2)}) collective-permute-start(s16[144,256]{1,0:T(8,128)(2,1)S(1)} %get-tuple-element.35), channel_id=1, source_target_pairs={{1,0},{0,1},{3,2},{2,3},{5,4},{4,5},{7,6},{6,7},{9,8},{8,9},{11,10... | collective-permute-start | bytes 221192 | tf_op jit(solution)/shard_map/ppermute | solution.py:216
  24.6 2.9 %collective-permute-done.8.rest_0_ = s16[144,256]{1,0:T(8,128)(2,1)S(1)} collective-permute-done((s16[144,256]{1,0:T(8,128)(2,1)S(1)}, s16[144,256]{1,0:T(8,128)(2,1)S(1)}, u32[]{:S(2)}, u32[]{:S(2)}) %collective-permute-start.8) | collective-permute-done | bytes 73760 | tf_op jit(solution)/shard_map/ppermute | solution.py:216
  27.5 0.2 shard_map.109
  27.7 11.1 %all_to_all.5.near = bf16[8,48,256]{2,1,0:T(8,128)(2,1)S(1)} all-to-all(bf16[8,48,256]{2,1,0:T(8,128)(2,1)S(1)} %broadcast_in_dim.14), channel_id=1, replica_groups={{0,4,8,12,16,20,24,28},{2,6,10,14,18,22,26,30},{1,5,9,13,17,21,25,29},{..., dimensions={0} | all-to-all | bytes 393216 | tf_op jit(solution)/shard_map/all_to_all | solution.py:270
  38.9 0.0 collective-permute-start.9
  38.9 1.4 %collective-permute-done.9.far = bf16[8,48,256]{2,1,0:T(8,128)(2,1)S(1)} collective-permute-done((bf16[8,48,256]{2,1,0:T(8,128)(2,1)S(1)}, bf16[8,48,256]{2,1,0:T(8,128)(2,1)S(1)}, u32[]{:S(2)}, u32[]{:S(2)}) %collective-permute-start.9) | collective-permute-done | bytes 196640 | tf_op jit(solution)/shard_map/ppermute | solution.py:220
  40.3 0.5 %shard_map.110 = (f32[48,256]{1,0:T(8,128)S(1)}, s16[48,256]{1,0:T(8,128)(2,1)S(1)}) custom-call(bf16[8,48,256]{2,1,0:T(8,128)(2,1)S(1)} %all_to_all.5.near, bf16[8,48,256]{2,1,0:T(8,128)(2,1)S(1)} %collective-permute-done.9.far, bf16[16,256,256]{2,1,0:T(8,128)(2,1)S(1)} %get-tuple-element.33.tiles_t, s32[32]{0:T(128)S(4)} %get-tuple-element.28.plan), custom_call_target="tpu_custom_call" | custom-call | flops 1048576 | bytes 1048576 | tf_op jit(solution)/shard_map/pallas_call | solution.py:31
  40.8 1.3 %collective-permute-start.10 = (s16[48,256]{1,0:T(8,128)(2,1)S(1)}, s16[48,256]{1,0:T(8,128)(2,1)S(1)}, u32[]{:S(2)}, u32[]{:S(2)}) collective-permute-start(s16[48,256]{1,0:T(8,128)(2,1)S(1)} %get-tuple-element.40), channel_id=1, source_target_pairs={{1,0},{0,1},{3,2},{2,3},{5,4},{4,5},{7,6},{6,7},{9,8},{8,9},{11,10... | collective-permute-start | bytes 73736 | tf_op jit(solution)/shard_map/ppermute | solution.py:216
  42.1 2.6 %collective-permute-done.10.rest_0_ = s16[48,256]{1,0:T(8,128)(2,1)S(1)} collective-permute-done((s16[48,256]{1,0:T(8,128)(2,1)S(1)}, s16[48,256]{1,0:T(8,128)(2,1)S(1)}, u32[]{:S(2)}, u32[]{:S(2)}) %collective-permute-start.10) | collective-permute-done | bytes 24608 | tf_op jit(solution)/shard_map/ppermute | solution.py:216
  44.7 0.7 %shard_map.111 = f32[47,256]{1,0:T(8,128)} custom-call(bf16[48,256]{1,0:T(8,128)(2,1)S(1)} %get-tuple-element.36.classes_in, f32[1,256]{1,0:T(1,128)S(1)} %get-tuple-element.37.scaling, f32[47,1]{1,0:T(8,128)S(1)} %get-tuple-element.38.bias, f32[48,256]{1,0:T(8,128)S(1)} %get-tuple-element.39.own, s16[48,256]{1,0:T(8,128)(2,1)S(1)} %collective-permute-done.10.rest_0_), custom_call_target="tpu_custom_call" | custom-call | flops 1048576 | bytes 1048576 | tf_op jit(solution)/shard_map/pallas_call | solution.py:31
  (10 shorter events, 0.1 us)
Async XLA Ops:
  0.0 5.3 %collective-permute-start = (bf16[100,256]{1,0:T(8,128)(2,1)}, bf16[100,256]{1,0:T(8,128)(2,1)S(1)}, u32[]{:S(2)}, u32[]{:S(2)}) collective-permute-start(bf16[100,256]{1,0:T(8,128)(2,1)} %bitcast.7), channel_id=1, source_target_pairs={{1,0},{0,1},{3,2},{2,3},{5,4},{4,5},{7,6},{6,7},{9,8},{8,9},{11,10... | collective-permute-start | bytes 153608 | tf_op jit(solution)/shard_map/ppermute | solution.py:216
  5.5 4.8 %collective-permute-start.1 = (bf16[100,256]{1,0:T(8,128)(2,1)S(1)}, bf16[100,256]{1,0:T(8,128)(2,1)S(1)}, u32[]{:S(2)}, u32[]{:S(2)}) collective-permute-start(bf16[100,256]{1,0:T(8,128)(2,1)S(1)} %shard_map.101.refs_0_), channel_id=1, source_target_pairs={{8,0},{10,2},{12,4},{14,6},{0,8},{2,10},{4,12},{6,14},{24,16},{26,... | collective-permute-start | bytes 153608 | tf_op jit(solution)/shard_map/ppermute | solution.py:220
  7.6 6.7 %collective-permute-start.3 = (bf16[100,256]{1,0:T(8,128)(2,1)S(1)}, bf16[100,256]{1,0:T(8,128)(2,1)S(1)}, u32[]{:S(2)}, u32[]{:S(2)}) collective-permute-start(bf16[100,256]{1,0:T(8,128)(2,1)S(1)} %shard_map.101.refs_0_), channel_id=1, source_target_pairs={{16,0},{26,2},{20,4},{30,6},{24,8},{18,10},{28,12},{22,14},{0,16},... | collective-permute-start | bytes 153608 | tf_op jit(solution)/shard_map/ppermute | solution.py:220
  10.2 5.9 %collective-permute-start.4 = (bf16[100,256]{1,0:T(8,128)(2,1)S(1)}, bf16[100,256]{1,0:T(8,128)(2,1)S(1)}, u32[]{:S(2)}, u32[]{:S(2)}) collective-permute-start(bf16[100,256]{1,0:T(8,128)(2,1)S(1)} %shard_map.101.refs_0_), channel_id=1, source_target_pairs={{24,0},{18,2},{28,4},{22,6},{16,8},{26,10},{20,12},{30,14},{8,16},... | collective-permute-start | bytes 153608 | tf_op jit(solution)/shard_map/ppermute | solution.py:220
  10.2 7.4 %collective-permute-start.2 = (bf16[2,100,256]{2,1,0:T(8,128)(2,1)S(1)}, bf16[2,100,256]{2,1,0:T(8,128)(2,1)S(1)}, u32[]{:S(2)}, u32[]{:S(2)}) collective-permute-start(bf16[2,100,256]{2,1,0:T(8,128)(2,1)S(1)} %shard_map.102), channel_id=1, source_target_pairs={{4,0},{6,2},{0,4},{2,6},{12,8},{14,10},{8,12},{10,14},{20,16},{22,... | collective-permute-start | bytes 307208 | tf_op jit(solution)/shard_map/ppermute | solution.py:220
  14.3 5.1 %collective-permute-start.5 = (bf16[1,100,256]{2,1,0:T(8,128)(2,1)S(1)}, bf16[1,100,256]{2,1,0:T(8,128)(2,1)S(1)}, u32[]{:S(2)}, u32[]{:S(2)}) collective-permute-start(bf16[1,100,256]{2,1,0:T(8,128)(2,1)S(1)} %shard_map.104), channel_id=1, source_target_pairs={{4,0},{6,2},{0,4},{2,6},{12,8},{14,10},{8,12},{10,14},{20,16},{22,... | collective-permute-start | bytes 153608 | tf_op jit(solution)/shard_map/ppermute | solution.py:220
  16.1 4.1 %collective-permute-start.6 = (bf16[1,100,256]{2,1,0:T(8,128)(2,1)S(1)}, bf16[1,100,256]{2,1,0:T(8,128)(2,1)S(1)}, u32[]{:S(2)}, u32[]{:S(2)}) collective-permute-start(bf16[1,100,256]{2,1,0:T(8,128)(2,1)S(1)} %shard_map.105), channel_id=1, source_target_pairs={{4,0},{6,2},{0,4},{2,6},{12,8},{14,10},{8,12},{10,14},{20,16},{22,... | collective-permute-start | bytes 153608 | tf_op jit(solution)/shard_map/ppermute | solution.py:220
  20.3 1.8 %collective-permute-start.7 = (bf16[8,100,256]{2,1,0:T(8,128)(2,1)S(1)}, bf16[8,100,256]{2,1,0:T(8,128)(2,1)S(1)}, u32[]{:S(2)}, u32[]{:S(2)}) collective-permute-start(bf16[8,100,256]{2,1,0:T(8,128)(2,1)S(1)} %constant_dynamic-update-slice_fusion.stack), channel_id=1, source_target_pairs={{2,0},{0,2},{6,4},{4,6},{10,8},{8,10},{14,12},{12,14},{18,16},{16,... | collective-permute-start | bytes 1228808 | tf_op jit(solution)/shard_map/ppermute | solution.py:220
  23.1 4.4 %collective-permute-start.8 = (s16[144,256]{1,0:T(8,128)(2,1)S(1)}, s16[144,256]{1,0:T(8,128)(2,1)S(1)}, u32[]{:S(2)}, u32[]{:S(2)}) collective-permute-start(s16[144,256]{1,0:T(8,128)(2,1)S(1)} %get-tuple-element.35), channel_id=1, source_target_pairs={{1,0},{0,1},{3,2},{2,3},{5,4},{4,5},{7,6},{6,7},{9,8},{8,9},{11,10... | collective-permute-start | bytes 221192 | tf_op jit(solution)/shard_map/ppermute | solution.py:216
  38.9 1.4 %collective-permute-start.9 = (bf16[8,48,256]{2,1,0:T(8,128)(2,1)S(1)}, bf16[8,48,256]{2,1,0:T(8,128)(2,1)S(1)}, u32[]{:S(2)}, u32[]{:S(2)}) collective-permute-start(bf16[8,48,256]{2,1,0:T(8,128)(2,1)S(1)} %all_to_all.5.near), channel_id=1, source_target_pairs={{2,0},{0,2},{6,4},{4,6},{10,8},{8,10},{14,12},{12,14},{18,16},{16,... | collective-permute-start | bytes 589832 | tf_op jit(solution)/shard_map/ppermute | solution.py:220
  40.8 3.9 %collective-permute-start.10 = (s16[48,256]{1,0:T(8,128)(2,1)S(1)}, s16[48,256]{1,0:T(8,128)(2,1)S(1)}, u32[]{:S(2)}, u32[]{:S(2)}) collective-permute-start(s16[48,256]{1,0:T(8,128)(2,1)S(1)} %get-tuple-element.40), channel_id=1, source_target_pairs={{1,0},{0,1},{3,2},{2,3},{5,4},{4,5},{7,6},{6,7},{9,8},{8,9},{11,10... | collective-permute-start | bytes 73736 | tf_op jit(solution)/shard_map/ppermute | solution.py:216

commit v12 on v11

--- a/solution.py
+++ b/solution.py
@@ -226,16 +226,16 @@
 
 
 def two_ways(pairs):
-    return pairs + [(pair[1], pair[0]) for pair in pairs]
+    return pairs, [(pair[1], pair[0]) for pair in pairs]
 
 
 def panel_order(outer, core):
     first, pairs = outer_order(outer)
     lists = []
     for here in (core, 1 - core):
-        across = [jnp.where(here == 0, *sides) for sides in two_ways(pairs)]
-        across = [4 * first, *[4 * apart for apart in across]]
-        lists.append([0, *across, 2, *[apart + 2 for apart in across]])
+        early, late = ([4 * jnp.where(here == 0, *sides) for sides in way] for way in two_ways(pairs))
+        mine = [0, *early, 4 * first, *late]
+        lists.append(mine + [apart + 2 for apart in mine])
     return lists[0], [apart ^ 1 for apart in lists[1]]
 
 
@@ -251,15 +251,13 @@
 def gather_features(value, aside, later):
     outer = lax.axis_size("blk") // 4
     first, pairs = outer_order(outer)
+    early, late = ([swapped(value, (4 * a, 4 * b)) for a, b in way] for way in two_ways(pairs))
     ahead = swapped(value, (4 * first, 4 * first))
-    across = [swapped(value, (4 * sides[0], 4 * sides[1])) for sides in two_ways(pairs)]
-    here = packed(value, ahead)
-    over = swapped(here, (2, 2))
-    early, late = packed(*across[: len(pairs)]), packed(*across[len(pairs) :])
-    beyond = [swapped(early, (2, 2)), swapped(late, (2, 2))]
-    beside = aside(over)
-    over, *behind = later(over, beside)
-    near = jnp.concatenate([here, early, late, over, *beyond])
+    stacks = packed(value, *early), packed(ahead, *late)
+    over = [swapped(stack, (2, 2)) for stack in stacks]
+    beside = aside(over[0])
+    over[0], *behind = later(over[0], beside)
+    near = jnp.concatenate([*stacks, *over])
     return (near, swapped(near, (1, 1))), beside, behind
 
 

time: 45.7 us -> 46.7 us (1.022)
  waiting for transfers between devices: 11.8 us -> 14 us
  starting transfers between devices: 15.4 us -> 13.9 us
    ppermute x8 -> x7, waiting for transfers between devices: 6.28 us -> 8.41 us  [swapped(): lax.ppermute(value, 'blk', [(d ^ masks[d % 2], d) for d in range(lax.axis...]
    ppermute x8 -> x7, starting transfers between devices: 9.59 us -> 8.24 us  [swapped(): lax.ppermute(value, 'blk', [(d ^ masks[d % 2], d) for d in range(lax.axis...]
    pallas_call x12 -> x11, Pallas kernels: 6.32 us -> 6.31 us  [call(): pl.pallas_call(kernel, out_shape=outs, in_specs=[pl.BlockSpec(memory_spac...]
  transfers between devices with their start and end apart: 11 -> 10, of which waited for: 7 -> 8; matrix products, arithmetic and copies ran while one was open for 0% -> 0% of each run, Pallas kernels for 8% -> 8%
where the time goes in v12:
time: 46.7 us; the launch traced here: 46.4 us
  waiting for transfers between devices  14 us (30%)
  starting transfers between devices  13.9 us (30%)
  blocking collectives  11.4 us (24%)
  Pallas kernels  6.31 us (14%)
  between operations  0.74 us (2%)
    all_to_all x1, blocking collectives, gather_classes(): near = lax.all_to_all(copies, 'blk', 0, 0, axis_index_groups=groups)  11.4 us
    ppermute x7, waiting for transfers between devices, swapped(): lax.ppermute(value, 'blk', [(d ^ masks[d % 2], d) for d in range(lax.axis...  8.41 us
    ppermute x7, starting transfers between devices, swapped(): lax.ppermute(value, 'blk', [(d ^ masks[d % 2], d) for d in range(lax.axis...  8.24 us
    pallas_call x11, Pallas kernels, call(): pl.pallas_call(kernel, out_shape=outs, in_specs=[pl.BlockSpec(memory_spac...  6.31 us
    ppermute x3, starting transfers between devices, shifted(): lax.ppermute(value, axis, [((d + step) % size, d) for d in range(size)])  5.7 us
    ppermute x3, waiting for transfers between devices, shifted(): lax.ppermute(value, axis, [((d + step) % size, d) for d in range(size)])  5.55 us
  transfers between devices with their start and end apart: 10, of which 8 were waited for; matrix products, arithmetic and copies ran while one was open for 0% of the time, Pallas kernels for 8%

profile of v12, /device:TPU:0, one launch (start us, length us, event | category | flops | bytes accessed | tf_op | source)
XLA Modules:
  0.0 46.4 jit_solution(2396219518433184718)
XLA Ops:
  0.0 2.9 %collective-permute-start = (bf16[100,256]{1,0:T(8,128)(2,1)}, bf16[100,256]{1,0:T(8,128)(2,1)S(1)}, u32[]{:S(2)}, u32[]{:S(2)}) collective-permute-start(bf16[100,256]{1,0:T(8,128)(2,1)} %bitcast.7), channel_id=1, source_target_pairs={{1,0},{0,1},{3,2},{2,3},{5,4},{4,5},{7,6},{6,7},{9,8},{8,9},{11,10... | collective-permute-start | bytes 153608 | tf_op jit(solution)/shard_map/ppermute | solution.py:216
  3.6 1.7 %shard_map.100 = (s32[8]{0:T(128)S(4)}, f32[100,256]{1,0:T(8,128)S(1)}, s32[1,256]{1,0:T(1,128)S(1)}, bf16[16,256,256]{2,1,0:T(8,128)(2,1)S(1)}) custom-call(s32[1]{0:T(128)S(6)} %copy.11.live, s32[1,512]{1,0:T(1,128)} %order.1, bf16[100,256]{1,0:T(8,128)(2,1)} %bitcast.8, bf16[16,256,256]{2,1,0:T(8,128)(2,1)} %bitcast.6), custom_call_target="tpu_custom_call" | custom-call | flops 1048576 | bytes 1048576 | tf_op jit(solution)/shard_map/pallas_call | solution.py:31
  5.3 0.0 collective-permute-done.rest_0_
  5.3 0.2 shard_map.101.refs_0_
  5.5 3.2 %collective-permute-start.1 = (bf16[100,256]{1,0:T(8,128)(2,1)S(1)}, bf16[100,256]{1,0:T(8,128)(2,1)S(1)}, u32[]{:S(2)}, u32[]{:S(2)}) collective-permute-start(bf16[100,256]{1,0:T(8,128)(2,1)S(1)} %shard_map.101.refs_0_), channel_id=1, source_target_pairs={{16,0},{26,2},{20,4},{30,6},{24,8},{18,10},{28,12},{22,14},{0,16},... | collective-permute-start | bytes 153608 | tf_op jit(solution)/shard_map/ppermute | solution.py:220
  8.6 1.6 %collective-permute-start.3 = (bf16[100,256]{1,0:T(8,128)(2,1)S(1)}, bf16[100,256]{1,0:T(8,128)(2,1)S(1)}, u32[]{:S(2)}, u32[]{:S(2)}) collective-permute-start(bf16[100,256]{1,0:T(8,128)(2,1)S(1)} %shard_map.101.refs_0_), channel_id=1, source_target_pairs={{8,0},{10,2},{12,4},{14,6},{0,8},{2,10},{4,12},{6,14},{24,16},{26,... | collective-permute-start | bytes 153608 | tf_op jit(solution)/shard_map/ppermute | solution.py:220
  10.2 0.0 collective-permute-start.4
  10.2 0.6 %collective-permute-done.1.refs_1_ = bf16[100,256]{1,0:T(8,128)(2,1)S(1)} collective-permute-done((bf16[100,256]{1,0:T(8,128)(2,1)S(1)}, bf16[100,256]{1,0:T(8,128)(2,1)S(1)}, u32[]{:S(2)}, u32[]{:S(2)}) %collective-permute-start.1) | collective-permute-done | bytes 51232 | tf_op jit(solution)/shard_map/ppermute | solution.py:220
  10.8 1.8 %collective-permute-start.2 = (bf16[2,100,256]{2,1,0:T(8,128)(2,1)S(1)}, bf16[2,100,256]{2,1,0:T(8,128)(2,1)S(1)}, u32[]{:S(2)}, u32[]{:S(2)}) collective-permute-start(bf16[2,100,256]{2,1,0:T(8,128)(2,1)S(1)} %shard_map.102), channel_id=1, source_target_pairs={{4,0},{6,2},{0,4},{2,6},{12,8},{14,10},{8,12},{10,14},{20,16},{22,... | collective-permute-start | bytes 307208 | tf_op jit(solution)/shard_map/ppermute | solution.py:220
  12.7 0.6 %collective-permute-done.3.refs_0_ = bf16[100,256]{1,0:T(8,128)(2,1)S(1)} collective-permute-done((bf16[100,256]{1,0:T(8,128)(2,1)S(1)}, bf16[100,256]{1,0:T(8,128)(2,1)S(1)}, u32[]{:S(2)}, u32[]{:S(2)}) %collective-permute-start.3) | collective-permute-done | bytes 51232 | tf_op jit(solution)/shard_map/ppermute | solution.py:220
  13.2 2.9 %collective-permute-done.4.refs_1_ = bf16[100,256]{1,0:T(8,128)(2,1)S(1)} collective-permute-done((bf16[100,256]{1,0:T(8,128)(2,1)S(1)}, bf16[100,256]{1,0:T(8,128)(2,1)S(1)}, u32[]{:S(2)}, u32[]{:S(2)}) %collective-permute-start.4) | collective-permute-done | bytes 51232 | tf_op jit(solution)/shard_map/ppermute | solution.py:220
  16.1 1.6 %collective-permute-start.5 = (bf16[2,100,256]{2,1,0:T(8,128)(2,1)S(1)}, bf16[2,100,256]{2,1,0:T(8,128)(2,1)S(1)}, u32[]{:S(2)}, u32[]{:S(2)}) collective-permute-start(bf16[2,100,256]{2,1,0:T(8,128)(2,1)S(1)} %shard_map.104), channel_id=1, source_target_pairs={{4,0},{6,2},{0,4},{2,6},{12,8},{14,10},{8,12},{10,14},{20,16},{22,... | collective-permute-start | bytes 307208 | tf_op jit(solution)/shard_map/ppermute | solution.py:220
  17.7 0.0 collective-permute-done.2._.arrived
  17.7 1.0 %shard_map.103 = (s32[32]{0:T(128)S(4)}, f32[128,1]{1,0:T(8,128)S(1)}, f32[47,1]{1,0:T(8,128)S(1)}, bf16[128,100]{1,0:T(8,128)(2,1)S(1)}, bf16[47,128]{1,0:T(8,128)(2,1)S(1)}) custom-call(bf16[2,100,256]{2,1,0:T(8,128)(2,1)S(1)} %collective-permute-done.2._.arrived, s32[8]{0:T(128)S(4)} %get-tuple-element.25.live, s32[1,16]{1,0:T(1,128)} %refs_0_.1, ...), custom_call_target="tpu_custom_call" | custom-call | flops 1048576 | bytes 1048576 | tf_op jit(solution)/shard_map/pallas_call | solution.py:31
  18.8 0.7 %shard_map.105 = (bf16[2,100,256]{2,1,0:T(8,128)(2,1)S(1)}, bf16[16,256,256]{2,1,0:T(8,128)(2,1)S(1)}, f32[2,8,256]{2,1,0:T(8,128)S(1)}) custom-call(bf16[16,256,256]{2,1,0:T(8,128)(2,1)S(1)} %get-tuple-element.27.tiles, bf16[2,100,256]{2,1,0:T(8,128)(2,1)S(1)} %collective-permute-done.2._.arrived, s32[32]{0:T(128)S(4)} %get-tuple-element.28.plan), custom_call_target="tpu_custom_call" | custom-call | flops 1048576 | bytes 1048576 | tf_op jit(solution)/shard_map/pallas_call | solution.py:31
  19.5 1.4 %collective-permute-done.5 = bf16[2,100,256]{2,1,0:T(8,128)(2,1)S(1)} collective-permute-done((bf16[2,100,256]{2,1,0:T(8,128)(2,1)S(1)}, bf16[2,100,256]{2,1,0:T(8,128)(2,1)S(1)}, u32[]{:S(2)}, u32[]{:S(2)}) %collective-permute-start.5) | collective-permute-done | bytes 102432 | tf_op jit(solution)/shard_map/ppermute | solution.py:220
  20.9 0.1 pad_maximum_fusion.stack
  21.0 0.1 collective-permute-start.6
  21.1 0.3 shard_map.106.projected.hidden_in
  21.3 1.5 %collective-permute-done.6.far = bf16[8,100,256]{2,1,0:T(8,128)(2,1)S(1)} collective-permute-done((bf16[8,100,256]{2,1,0:T(8,128)(2,1)S(1)}, bf16[8,100,256]{2,1,0:T(8,128)(2,1)S(1)}, u32[]{:S(2)}, u32[]{:S(2)}) %collective-permute-start.6) | collective-permute-done | bytes 409632 | tf_op jit(solution)/shard_map/ppermute | solution.py:220
  22.8 1.0 %shard_map.107 = (f32[128,256]{1,0:T(8,128)S(1)}, s16[144,256]{1,0:T(8,128)(2,1)S(1)}) custom-call(bf16[8,128,256]{2,1,0:T(8,128)(2,1)S(1)} %shard_map.106.projected.hidden_in, bf16[8,100,256]{2,1,0:T(8,128)(2,1)S(1)} %collective-permute-done.6.far, bf16[128,100]{1,0:T(8,128)(2,1)S(1)} %get-tuple-element.26.weight_t, ...), custom_call_target="tpu_custom_call" | custom-call | flops 1048576 | bytes 1048576 | tf_op jit(solution)/shard_map/pallas_call | solution.py:31
  23.8 1.6 %collective-permute-start.7 = (s16[144,256]{1,0:T(8,128)(2,1)S(1)}, s16[144,256]{1,0:T(8,128)(2,1)S(1)}, u32[]{:S(2)}, u32[]{:S(2)}) collective-permute-start(s16[144,256]{1,0:T(8,128)(2,1)S(1)} %get-tuple-element.35), channel_id=1, source_target_pairs={{1,0},{0,1},{3,2},{2,3},{5,4},{4,5},{7,6},{6,7},{9,8},{8,9},{11,10... | collective-permute-start | bytes 221192 | tf_op jit(solution)/shard_map/ppermute | solution.py:216
  25.4 2.9 %collective-permute-done.7.rest_0_ = s16[144,256]{1,0:T(8,128)(2,1)S(1)} collective-permute-done((s16[144,256]{1,0:T(8,128)(2,1)S(1)}, s16[144,256]{1,0:T(8,128)(2,1)S(1)}, u32[]{:S(2)}, u32[]{:S(2)}) %collective-permute-start.7) | collective-permute-done | bytes 73760 | tf_op jit(solution)/shard_map/ppermute | solution.py:216
  28.2 0.2 shard_map.108
  28.5 11.4 %all_to_all.5.near = bf16[8,48,256]{2,1,0:T(8,128)(2,1)S(1)} all-to-all(bf16[8,48,256]{2,1,0:T(8,128)(2,1)S(1)} %broadcast_in_dim.14), channel_id=1, replica_groups={{0,4,8,12,16,20,24,28},{2,6,10,14,18,22,26,30},{1,5,9,13,17,21,25,29},{..., dimensions={0} | all-to-all | bytes 393216 | tf_op jit(solution)/shard_map/all_to_all | solution.py:268
  39.8 0.0 collective-permute-start.8
  39.9 1.4 %collective-permute-done.8.far = bf16[8,48,256]{2,1,0:T(8,128)(2,1)S(1)} collective-permute-done((bf16[8,48,256]{2,1,0:T(8,128)(2,1)S(1)}, bf16[8,48,256]{2,1,0:T(8,128)(2,1)S(1)}, u32[]{:S(2)}, u32[]{:S(2)}) %collective-permute-start.8) | collective-permute-done | bytes 196640 | tf_op jit(solution)/shard_map/ppermute | solution.py:220
  41.3 0.5 %shard_map.109 = (f32[48,256]{1,0:T(8,128)S(1)}, s16[48,256]{1,0:T(8,128)(2,1)S(1)}) custom-call(bf16[8,48,256]{2,1,0:T(8,128)(2,1)S(1)} %all_to_all.5.near, bf16[8,48,256]{2,1,0:T(8,128)(2,1)S(1)} %collective-permute-done.8.far, bf16[16,256,256]{2,1,0:T(8,128)(2,1)S(1)} %get-tuple-element.33.tiles_t, s32[32]{0:T(128)S(4)} %get-tuple-element.28.plan), custom_call_target="tpu_custom_call" | custom-call | flops 1048576 | bytes 1048576 | tf_op jit(solution)/shard_map/pallas_call | solution.py:31
  41.8 1.2 %collective-permute-start.9 = (s16[48,256]{1,0:T(8,128)(2,1)S(1)}, s16[48,256]{1,0:T(8,128)(2,1)S(1)}, u32[]{:S(2)}, u32[]{:S(2)}) collective-permute-start(s16[48,256]{1,0:T(8,128)(2,1)S(1)} %get-tuple-element.40), channel_id=1, source_target_pairs={{1,0},{0,1},{3,2},{2,3},{5,4},{4,5},{7,6},{6,7},{9,8},{8,9},{11,10... | collective-permute-start | bytes 73736 | tf_op jit(solution)/shard_map/ppermute | solution.py:216
  43.0 2.7 %collective-permute-done.9.rest_0_ = s16[48,256]{1,0:T(8,128)(2,1)S(1)} collective-permute-done((s16[48,256]{1,0:T(8,128)(2,1)S(1)}, s16[48,256]{1,0:T(8,128)(2,1)S(1)}, u32[]{:S(2)}, u32[]{:S(2)}) %collective-permute-start.9) | collective-permute-done | bytes 24608 | tf_op jit(solution)/shard_map/ppermute | solution.py:216
  45.7 0.7 %shard_map.110 = f32[47,256]{1,0:T(8,128)} custom-call(bf16[48,256]{1,0:T(8,128)(2,1)S(1)} %get-tuple-element.36.classes_in, f32[1,256]{1,0:T(1,128)S(1)} %get-tuple-element.37.scaling, f32[47,1]{1,0:T(8,128)S(1)} %get-tuple-element.38.bias, f32[48,256]{1,0:T(8,128)S(1)} %get-tuple-element.39.own, s16[48,256]{1,0:T(8,128)(2,1)S(1)} %collective-permute-done.9.rest_0_), custom_call_target="tpu_custom_call" | custom-call | flops 1048576 | bytes 1048576 | tf_op jit(solution)/shard_map/pallas_call | solution.py:31
  (3 shorter events, 0.0 us)
Async XLA Ops:
  0.0 5.3 %collective-permute-start = (bf16[100,256]{1,0:T(8,128)(2,1)}, bf16[100,256]{1,0:T(8,128)(2,1)S(1)}, u32[]{:S(2)}, u32[]{:S(2)}) collective-permute-start(bf16[100,256]{1,0:T(8,128)(2,1)} %bitcast.7), channel_id=1, source_target_pairs={{1,0},{0,1},{3,2},{2,3},{5,4},{4,5},{7,6},{6,7},{9,8},{8,9},{11,10... | collective-permute-start | bytes 153608 | tf_op jit(solution)/shard_map/ppermute | solution.py:216
  5.5 5.4 %collective-permute-start.1 = (bf16[100,256]{1,0:T(8,128)(2,1)S(1)}, bf16[100,256]{1,0:T(8,128)(2,1)S(1)}, u32[]{:S(2)}, u32[]{:S(2)}) collective-permute-start(bf16[100,256]{1,0:T(8,128)(2,1)S(1)} %shard_map.101.refs_0_), channel_id=1, source_target_pairs={{16,0},{26,2},{20,4},{30,6},{24,8},{18,10},{28,12},{22,14},{0,16},... | collective-permute-start | bytes 153608 | tf_op jit(solution)/shard_map/ppermute | solution.py:220
  8.6 4.6 %collective-permute-start.3 = (bf16[100,256]{1,0:T(8,128)(2,1)S(1)}, bf16[100,256]{1,0:T(8,128)(2,1)S(1)}, u32[]{:S(2)}, u32[]{:S(2)}) collective-permute-start(bf16[100,256]{1,0:T(8,128)(2,1)S(1)} %shard_map.101.refs_0_), channel_id=1, source_target_pairs={{8,0},{10,2},{12,4},{14,6},{0,8},{2,10},{4,12},{6,14},{24,16},{26,... | collective-permute-start | bytes 153608 | tf_op jit(solution)/shard_map/ppermute | solution.py:220
  10.2 5.9 %collective-permute-start.4 = (bf16[100,256]{1,0:T(8,128)(2,1)S(1)}, bf16[100,256]{1,0:T(8,128)(2,1)S(1)}, u32[]{:S(2)}, u32[]{:S(2)}) collective-permute-start(bf16[100,256]{1,0:T(8,128)(2,1)S(1)} %shard_map.101.refs_0_), channel_id=1, source_target_pairs={{24,0},{18,2},{28,4},{22,6},{16,8},{26,10},{20,12},{30,14},{8,16},... | collective-permute-start | bytes 153608 | tf_op jit(solution)/shard_map/ppermute | solution.py:220
  10.8 6.9 %collective-permute-start.2 = (bf16[2,100,256]{2,1,0:T(8,128)(2,1)S(1)}, bf16[2,100,256]{2,1,0:T(8,128)(2,1)S(1)}, u32[]{:S(2)}, u32[]{:S(2)}) collective-permute-start(bf16[2,100,256]{2,1,0:T(8,128)(2,1)S(1)} %shard_map.102), channel_id=1, source_target_pairs={{4,0},{6,2},{0,4},{2,6},{12,8},{14,10},{8,12},{10,14},{20,16},{22,... | collective-permute-start | bytes 307208 | tf_op jit(solution)/shard_map/ppermute | solution.py:220
  16.1 4.8 %collective-permute-start.5 = (bf16[2,100,256]{2,1,0:T(8,128)(2,1)S(1)}, bf16[2,100,256]{2,1,0:T(8,128)(2,1)S(1)}, u32[]{:S(2)}, u32[]{:S(2)}) collective-permute-start(bf16[2,100,256]{2,1,0:T(8,128)(2,1)S(1)} %shard_map.104), channel_id=1, source_target_pairs={{4,0},{6,2},{0,4},{2,6},{12,8},{14,10},{8,12},{10,14},{20,16},{22,... | collective-permute-start | bytes 307208 | tf_op jit(solution)/shard_map/ppermute | solution.py:220
  21.0 1.8 %collective-permute-start.6 = (bf16[8,100,256]{2,1,0:T(8,128)(2,1)S(1)}, bf16[8,100,256]{2,1,0:T(8,128)(2,1)S(1)}, u32[]{:S(2)}, u32[]{:S(2)}) collective-permute-start(bf16[8,100,256]{2,1,0:T(8,128)(2,1)S(1)} %pad_maximum_fusion.stack), channel_id=1, source_target_pairs={{2,0},{0,2},{6,4},{4,6},{10,8},{8,10},{14,12},{12,14},{18,16},{16,... | collective-permute-start | bytes 1228808 | tf_op jit(solution)/shard_map/ppermute | solution.py:220
  23.8 4.4 %collective-permute-start.7 = (s16[144,256]{1,0:T(8,128)(2,1)S(1)}, s16[144,256]{1,0:T(8,128)(2,1)S(1)}, u32[]{:S(2)}, u32[]{:S(2)}) collective-permute-start(s16[144,256]{1,0:T(8,128)(2,1)S(1)} %get-tuple-element.35), channel_id=1, source_target_pairs={{1,0},{0,1},{3,2},{2,3},{5,4},{4,5},{7,6},{6,7},{9,8},{8,9},{11,10... | collective-permute-start | bytes 221192 | tf_op jit(solution)/shard_map/ppermute | solution.py:216
  39.8 1.4 %collective-permute-start.8 = (bf16[8,48,256]{2,1,0:T(8,128)(2,1)S(1)}, bf16[8,48,256]{2,1,0:T(8,128)(2,1)S(1)}, u32[]{:S(2)}, u32[]{:S(2)}) collective-permute-start(bf16[8,48,256]{2,1,0:T(8,128)(2,1)S(1)} %all_to_all.5.near), channel_id=1, source_target_pairs={{2,0},{0,2},{6,4},{4,6},{10,8},{8,10},{14,12},{12,14},{18,16},{16,... | collective-permute-start | bytes 589832 | tf_op jit(solution)/shard_map/ppermute | solution.py:220
  41.8 3.9 %collective-permute-start.9 = (s16[48,256]{1,0:T(8,128)(2,1)S(1)}, s16[48,256]{1,0:T(8,128)(2,1)S(1)}, u32[]{:S(2)}, u32[]{:S(2)}) collective-permute-start(s16[48,256]{1,0:T(8,128)(2,1)S(1)} %get-tuple-element.40), channel_id=1, source_target_pairs={{1,0},{0,1},{3,2},{2,3},{5,4},{4,5},{7,6},{6,7},{9,8},{8,9},{11,10... | collective-permute-start | bytes 73736 | tf_op jit(solution)/shard_map/ppermute | solution.py:216

commit v13 on v12

--- a/solution.py
+++ b/solution.py
@@ -182,7 +182,7 @@
         out[...] = jnp.where(row == own.shape[0] - 1, power, codes).astype(jnp.int16)
 
 
-def combine(hidden_in, bias, weight_t, degrees, own, *rest):
+def combine(place, hidden_in, bias, weight_t, degrees, own, *rest):
     *arrived, out, scale_out = rest
     height = hidden_in.shape[1]
     total, degree = own[...], degrees[0, :1]
@@ -192,7 +192,7 @@
         terms = [codes[height + 1 + index : height + 2 + index].astype(F32) for index in range(3)]
         degree = degree + (terms[0] + (terms[1] + terms[2] * 2.0**-14) * 2.0**-14)
     scaling = lax.rsqrt(1.0 + degree)
-    hidden = scaling * (total + hidden_in[0].astype(F32)) + bias[...]
+    hidden = scaling * (total + hidden_in[place].astype(F32)) + bias[...]
     hidden = jnp.maximum(hidden, 0.0).astype(BF16)
     classes = nn(weight_t[...], hidden)
     blank = jnp.zeros((out.shape[0] - classes.shape[0], classes.shape[1]), F32)
@@ -234,7 +234,7 @@
     lists = []
     for here in (core, 1 - core):
         early, late = ([4 * jnp.where(here == 0, *sides) for sides in way] for way in two_ways(pairs))
-        mine = [0, *early, 4 * first, *late]
+        mine = [*early, 0, 4 * first, *late]
         lists.append(mine + [apart + 2 for apart in mine])
     return lists[0], [apart ^ 1 for apart in lists[1]]
 
@@ -253,9 +253,9 @@
     first, pairs = outer_order(outer)
     early, late = ([swapped(value, (4 * a, 4 * b)) for a, b in way] for way in two_ways(pairs))
     ahead = swapped(value, (4 * first, 4 * first))
-    stacks = packed(value, *early), packed(ahead, *late)
+    stacks = packed(*early), packed(value, ahead), packed(*late)
     over = [swapped(stack, (2, 2)) for stack in stacks]
-    beside = aside(over[0])
+    beside = aside(stacks[1])
     over[0], *behind = later(over[0], beside)
     near = jnp.concatenate([*stacks, *over])
     return (near, swapped(near, (1, 1))), beside, behind
@@ -371,7 +371,7 @@
         scratch=[pltpu.VMEM((blocks, hidden, tile), BF16)],
     )
     classes_in, scaling = call(
-        combine,
+        functools.partial(combine, len(outer_order(blocks // 4)[1])),
         [shape((padded, tile), BF16), shape((1, tile), F32)],
         vmem=(projected, bias_1, weight_2, degrees, own, *exchanged(sums)),
     )

time: 46.7 us -> 46.4 us (level)
  waiting for transfers between devices: 14 us -> 11.8 us
  starting transfers between devices: 13.9 us -> 15.3 us
    ppermute x7 -> x8, waiting for transfers between devices: 8.41 us -> 6.26 us  [swapped(): lax.ppermute(value, 'blk', [(d ^ masks[d % 2], d) for d in range(lax.axis...]
    ppermute x7 -> x8, starting transfers between devices: 8.24 us -> 9.62 us  [swapped(): lax.ppermute(value, 'blk', [(d ^ masks[d % 2], d) for d in range(lax.axis...]
    pallas_call x11 -> x12, Pallas kernels: 6.31 us -> 6.33 us  [call(): pl.pallas_call(kernel, out_shape=outs, in_specs=[pl.BlockSpec(memory_spac...]
  transfers between devices with their start and end apart: 10 -> 11, of which waited for: 8 -> 8; matrix products, arithmetic and copies ran while one was open for 0% -> 0% of each run, Pallas kernels for 8% -> 8%
where the time goes in v13:
time: 46.4 us; the launch traced here: 46.1 us
  starting transfers between devices  15.3 us (33%)
  waiting for transfers between devices  11.8 us (25%)
  blocking collectives  11.8 us (25%)
  Pallas kernels  6.33 us (14%)
  between operations  0.77 us (2%)
    all_to_all x1, blocking collectives, gather_classes(): near = lax.all_to_all(copies, 'blk', 0, 0, axis_index_groups=groups)  11.8 us
    ppermute x8, starting transfers between devices, swapped(): lax.ppermute(value, 'blk', [(d ^ masks[d % 2], d) for d in range(lax.axis...  9.62 us
    pallas_call x12, Pallas kernels, call(): pl.pallas_call(kernel, out_shape=outs, in_specs=[pl.BlockSpec(memory_spac...  6.33 us
    ppermute x8, waiting for transfers between devices, swapped(): lax.ppermute(value, 'blk', [(d ^ masks[d % 2], d) for d in range(lax.axis...  6.26 us
    ppermute x3, starting transfers between devices, shifted(): lax.ppermute(value, axis, [((d + step) % size, d) for d in range(size)])  5.69 us
    ppermute x3, waiting for transfers between devices, shifted(): lax.ppermute(value, axis, [((d + step) % size, d) for d in range(size)])  5.56 us
  transfers between devices with their start and end apart: 11, of which 8 were waited for; matrix products, arithmetic and copies ran while one was open for 0% of the time, Pallas kernels for 8%

profile of v13, /device:TPU:0, one launch (start us, length us, event | category | flops | bytes accessed | tf_op | source)
XLA Modules:
  0.0 46.1 jit_solution(6891476619464380540)
XLA Ops:
  0.0 2.9 %collective-permute-start = (bf16[100,256]{1,0:T(8,128)(2,1)}, bf16[100,256]{1,0:T(8,128)(2,1)S(1)}, u32[]{:S(2)}, u32[]{:S(2)}) collective-permute-start(bf16[100,256]{1,0:T(8,128)(2,1)} %bitcast.7), channel_id=1, source_target_pairs={{1,0},{0,1},{3,2},{2,3},{5,4},{4,5},{7,6},{6,7},{9,8},{8,9},{11,10... | collective-permute-start | bytes 153608 | tf_op jit(solution)/shard_map/ppermute | solution.py:216
  3.6 1.7 %shard_map.100 = (s32[8]{0:T(128)S(4)}, f32[100,256]{1,0:T(8,128)S(1)}, s32[1,256]{1,0:T(1,128)S(1)}, bf16[16,256,256]{2,1,0:T(8,128)(2,1)S(1)}) custom-call(s32[1]{0:T(128)S(6)} %copy.16.live, s32[1,512]{1,0:T(1,128)} %order.1, bf16[100,256]{1,0:T(8,128)(2,1)} %bitcast.8, bf16[16,256,256]{2,1,0:T(8,128)(2,1)} %bitcast.6), custom_call_target="tpu_custom_call" | custom-call | flops 1048576 | bytes 1048576 | tf_op jit(solution)/shard_map/pallas_call | solution.py:31
  5.3 0.0 collective-permute-done.rest_0_
  5.3 0.2 shard_map.101.refs_0_
  5.5 3.2 %collective-permute-start.2 = (bf16[100,256]{1,0:T(8,128)(2,1)S(1)}, bf16[100,256]{1,0:T(8,128)(2,1)S(1)}, u32[]{:S(2)}, u32[]{:S(2)}) collective-permute-start(bf16[100,256]{1,0:T(8,128)(2,1)S(1)} %shard_map.101.refs_0_), channel_id=1, source_target_pairs={{16,0},{26,2},{20,4},{30,6},{24,8},{18,10},{28,12},{22,14},{0,16},... | collective-permute-start | bytes 153608 | tf_op jit(solution)/shard_map/ppermute | solution.py:220
  8.6 1.6 %collective-permute-start.1 = (bf16[100,256]{1,0:T(8,128)(2,1)S(1)}, bf16[100,256]{1,0:T(8,128)(2,1)S(1)}, u32[]{:S(2)}, u32[]{:S(2)}) collective-permute-start(bf16[100,256]{1,0:T(8,128)(2,1)S(1)} %shard_map.101.refs_0_), channel_id=1, source_target_pairs={{8,0},{10,2},{12,4},{14,6},{0,8},{2,10},{4,12},{6,14},{24,16},{26,... | collective-permute-start | bytes 153608 | tf_op jit(solution)/shard_map/ppermute | solution.py:220
  10.2 0.0 collective-permute-start.3
  10.2 0.6 %collective-permute-done.2.refs_0_ = bf16[100,256]{1,0:T(8,128)(2,1)S(1)} collective-permute-done((bf16[100,256]{1,0:T(8,128)(2,1)S(1)}, bf16[100,256]{1,0:T(8,128)(2,1)S(1)}, u32[]{:S(2)}, u32[]{:S(2)}) %collective-permute-start.2) | collective-permute-done | bytes 51232 | tf_op jit(solution)/shard_map/ppermute | solution.py:220
  10.8 1.8 %collective-permute-start.4 = (bf16[1,100,256]{2,1,0:T(8,128)(2,1)S(1)}, bf16[1,100,256]{2,1,0:T(8,128)(2,1)S(1)}, u32[]{:S(2)}, u32[]{:S(2)}) collective-permute-start(bf16[1,100,256]{2,1,0:T(8,128)(2,1)S(1)} %shard_map.104), channel_id=1, source_target_pairs={{4,0},{6,2},{0,4},{2,6},{12,8},{14,10},{8,12},{10,14},{20,16},{22,... | collective-permute-start | bytes 153608 | tf_op jit(solution)/shard_map/ppermute | solution.py:220
  12.6 0.6 %collective-permute-done.1.refs_1_ = bf16[100,256]{1,0:T(8,128)(2,1)S(1)} collective-permute-done((bf16[100,256]{1,0:T(8,128)(2,1)S(1)}, bf16[100,256]{1,0:T(8,128)(2,1)S(1)}, u32[]{:S(2)}, u32[]{:S(2)}) %collective-permute-start.1) | collective-permute-done | bytes 51232 | tf_op jit(solution)/shard_map/ppermute | solution.py:220
  13.2 1.6 %collective-permute-start.5 = (bf16[2,100,256]{2,1,0:T(8,128)(2,1)S(1)}, bf16[2,100,256]{2,1,0:T(8,128)(2,1)S(1)}, u32[]{:S(2)}, u32[]{:S(2)}) collective-permute-start(bf16[2,100,256]{2,1,0:T(8,128)(2,1)S(1)} %shard_map.102._), channel_id=1, source_target_pairs={{4,0},{6,2},{0,4},{2,6},{12,8},{14,10},{8,12},{10,14},{20,16},{22,... | collective-permute-start | bytes 307208 | tf_op jit(solution)/shard_map/ppermute | solution.py:220
  14.8 1.3 %collective-permute-done.3.refs_0_ = bf16[100,256]{1,0:T(8,128)(2,1)S(1)} collective-permute-done((bf16[100,256]{1,0:T(8,128)(2,1)S(1)}, bf16[100,256]{1,0:T(8,128)(2,1)S(1)}, u32[]{:S(2)}, u32[]{:S(2)}) %collective-permute-start.3) | collective-permute-done | bytes 51232 | tf_op jit(solution)/shard_map/ppermute | solution.py:220
  16.1 1.5 %collective-permute-start.6 = (bf16[1,100,256]{2,1,0:T(8,128)(2,1)S(1)}, bf16[1,100,256]{2,1,0:T(8,128)(2,1)S(1)}, u32[]{:S(2)}, u32[]{:S(2)}) collective-permute-start(bf16[1,100,256]{2,1,0:T(8,128)(2,1)S(1)} %shard_map.105), channel_id=1, source_target_pairs={{4,0},{6,2},{0,4},{2,6},{12,8},{14,10},{8,12},{10,14},{20,16},{22,... | collective-permute-start | bytes 153608 | tf_op jit(solution)/shard_map/ppermute | solution.py:220
  17.7 1.0 %shard_map.103 = (s32[32]{0:T(128)S(4)}, f32[128,1]{1,0:T(8,128)S(1)}, f32[47,1]{1,0:T(8,128)S(1)}, bf16[128,100]{1,0:T(8,128)(2,1)S(1)}, bf16[47,128]{1,0:T(8,128)(2,1)S(1)}) custom-call(bf16[2,100,256]{2,1,0:T(8,128)(2,1)S(1)} %shard_map.102._, s32[8]{0:T(128)S(4)} %get-tuple-element.25.live, s32[1,16]{1,0:T(1,128)} %refs_0_.1, s32[1,16]{1,0:T(1,128)} %refs_1_.1, ...), custom_call_target="tpu_custom_call" | custom-call | flops 1048576 | bytes 1048576 | tf_op jit(solution)/shard_map/pallas_call | solution.py:31
  18.7 0.0 collective-permute-done.4.arrived
  18.7 0.7 %shard_map.106 = (bf16[1,100,256]{2,1,0:T(8,128)(2,1)S(1)}, bf16[16,256,256]{2,1,0:T(8,128)(2,1)S(1)}, f32[2,8,256]{2,1,0:T(8,128)S(1)}) custom-call(bf16[16,256,256]{2,1,0:T(8,128)(2,1)S(1)} %get-tuple-element.27.tiles, bf16[1,100,256]{2,1,0:T(8,128)(2,1)S(1)} %collective-permute-done.4.arrived, s32[32]{0:T(128)S(4)} %get-tuple-element.28.plan), custom_call_target="tpu_custom_call" | custom-call | flops 1048576 | bytes 1048576 | tf_op jit(solution)/shard_map/pallas_call | solution.py:31
  19.4 0.0 collective-permute-done.5
  19.5 0.8 %collective-permute-done.6 = bf16[1,100,256]{2,1,0:T(8,128)(2,1)S(1)} collective-permute-done((bf16[1,100,256]{2,1,0:T(8,128)(2,1)S(1)}, bf16[1,100,256]{2,1,0:T(8,128)(2,1)S(1)}, u32[]{:S(2)}, u32[]{:S(2)}) %collective-permute-start.6) | collective-permute-done | bytes 51232 | tf_op jit(solution)/shard_map/ppermute | solution.py:220
  20.3 0.0 collective-permute-start.7
  20.3 0.3 shard_map.107.projected.hidden_in
  20.6 1.5 %collective-permute-done.7.far = bf16[8,100,256]{2,1,0:T(8,128)(2,1)S(1)} collective-permute-done((bf16[8,100,256]{2,1,0:T(8,128)(2,1)S(1)}, bf16[8,100,256]{2,1,0:T(8,128)(2,1)S(1)}, u32[]{:S(2)}, u32[]{:S(2)}) %collective-permute-start.7) | collective-permute-done | bytes 409632 | tf_op jit(solution)/shard_map/ppermute | solution.py:220
  22.0 1.0 %shard_map.108 = (f32[128,256]{1,0:T(8,128)S(1)}, s16[144,256]{1,0:T(8,128)(2,1)S(1)}) custom-call(bf16[8,128,256]{2,1,0:T(8,128)(2,1)S(1)} %shard_map.107.projected.hidden_in, bf16[8,100,256]{2,1,0:T(8,128)(2,1)S(1)} %collective-permute-done.7.far, bf16[128,100]{1,0:T(8,128)(2,1)S(1)} %get-tuple-element.26.weight_t, ...), custom_call_target="tpu_custom_call" | custom-call | flops 1048576 | bytes 1048576 | tf_op jit(solution)/shard_map/pallas_call | solution.py:31
  23.1 1.6 %collective-permute-start.8 = (s16[144,256]{1,0:T(8,128)(2,1)S(1)}, s16[144,256]{1,0:T(8,128)(2,1)S(1)}, u32[]{:S(2)}, u32[]{:S(2)}) collective-permute-start(s16[144,256]{1,0:T(8,128)(2,1)S(1)} %get-tuple-element.35), channel_id=1, source_target_pairs={{1,0},{0,1},{3,2},{2,3},{5,4},{4,5},{7,6},{6,7},{9,8},{8,9},{11,10... | collective-permute-start | bytes 221192 | tf_op jit(solution)/shard_map/ppermute | solution.py:216
  24.6 2.9 %collective-permute-done.8.rest_0_ = s16[144,256]{1,0:T(8,128)(2,1)S(1)} collective-permute-done((s16[144,256]{1,0:T(8,128)(2,1)S(1)}, s16[144,256]{1,0:T(8,128)(2,1)S(1)}, u32[]{:S(2)}, u32[]{:S(2)}) %collective-permute-start.8) | collective-permute-done | bytes 73760 | tf_op jit(solution)/shard_map/ppermute | solution.py:216
  27.5 0.2 shard_map.109
  27.7 11.8 %all_to_all.5.near = bf16[8,48,256]{2,1,0:T(8,128)(2,1)S(1)} all-to-all(bf16[8,48,256]{2,1,0:T(8,128)(2,1)S(1)} %broadcast_in_dim.14), channel_id=1, replica_groups={{0,4,8,12,16,20,24,28},{2,6,10,14,18,22,26,30},{1,5,9,13,17,21,25,29},{..., dimensions={0} | all-to-all | bytes 393216 | tf_op jit(solution)/shard_map/all_to_all | solution.py:268
  39.6 0.0 collective-permute-start.9
  39.6 1.4 %collective-permute-done.9.far = bf16[8,48,256]{2,1,0:T(8,128)(2,1)S(1)} collective-permute-done((bf16[8,48,256]{2,1,0:T(8,128)(2,1)S(1)}, bf16[8,48,256]{2,1,0:T(8,128)(2,1)S(1)}, u32[]{:S(2)}, u32[]{:S(2)}) %collective-permute-start.9) | collective-permute-done | bytes 196640 | tf_op jit(solution)/shard_map/ppermute | solution.py:220
  41.0 0.5 %shard_map.110 = (f32[48,256]{1,0:T(8,128)S(1)}, s16[48,256]{1,0:T(8,128)(2,1)S(1)}) custom-call(bf16[8,48,256]{2,1,0:T(8,128)(2,1)S(1)} %all_to_all.5.near, bf16[8,48,256]{2,1,0:T(8,128)(2,1)S(1)} %collective-permute-done.9.far, bf16[16,256,256]{2,1,0:T(8,128)(2,1)S(1)} %get-tuple-element.33.tiles_t, s32[32]{0:T(128)S(4)} %get-tuple-element.28.plan), custom_call_target="tpu_custom_call" | custom-call | flops 1048576 | bytes 1048576 | tf_op jit(solution)/shard_map/pallas_call | solution.py:31
  41.5 1.2 %collective-permute-start.10 = (s16[48,256]{1,0:T(8,128)(2,1)S(1)}, s16[48,256]{1,0:T(8,128)(2,1)S(1)}, u32[]{:S(2)}, u32[]{:S(2)}) collective-permute-start(s16[48,256]{1,0:T(8,128)(2,1)S(1)} %get-tuple-element.40), channel_id=1, source_target_pairs={{1,0},{0,1},{3,2},{2,3},{5,4},{4,5},{7,6},{6,7},{9,8},{8,9},{11,10... | collective-permute-start | bytes 73736 | tf_op jit(solution)/shard_map/ppermute | solution.py:216
  42.7 2.7 %collective-permute-done.10.rest_0_ = s16[48,256]{1,0:T(8,128)(2,1)S(1)} collective-permute-done((s16[48,256]{1,0:T(8,128)(2,1)S(1)}, s16[48,256]{1,0:T(8,128)(2,1)S(1)}, u32[]{:S(2)}, u32[]{:S(2)}) %collective-permute-start.10) | collective-permute-done | bytes 24608 | tf_op jit(solution)/shard_map/ppermute | solution.py:216
  45.4 0.7 %shard_map.111 = f32[47,256]{1,0:T(8,128)} custom-call(bf16[48,256]{1,0:T(8,128)(2,1)S(1)} %get-tuple-element.36.classes_in, f32[1,256]{1,0:T(1,128)S(1)} %get-tuple-element.37.scaling, f32[47,1]{1,0:T(8,128)S(1)} %get-tuple-element.38.bias, f32[48,256]{1,0:T(8,128)S(1)} %get-tuple-element.39.own, s16[48,256]{1,0:T(8,128)(2,1)S(1)} %collective-permute-done.10.rest_0_), custom_call_target="tpu_custom_call" | custom-call | flops 1048576 | bytes 1048576 | tf_op jit(solution)/shard_map/pallas_call | solution.py:31
  (10 shorter events, 0.1 us)
Async XLA Ops:
  0.0 5.3 %collective-permute-start = (bf16[100,256]{1,0:T(8,128)(2,1)}, bf16[100,256]{1,0:T(8,128)(2,1)S(1)}, u32[]{:S(2)}, u32[]{:S(2)}) collective-permute-start(bf16[100,256]{1,0:T(8,128)(2,1)} %bitcast.7), channel_id=1, source_target_pairs={{1,0},{0,1},{3,2},{2,3},{5,4},{4,5},{7,6},{6,7},{9,8},{8,9},{11,10... | collective-permute-start | bytes 153608 | tf_op jit(solution)/shard_map/ppermute | solution.py:216
  5.5 5.4 %collective-permute-start.2 = (bf16[100,256]{1,0:T(8,128)(2,1)S(1)}, bf16[100,256]{1,0:T(8,128)(2,1)S(1)}, u32[]{:S(2)}, u32[]{:S(2)}) collective-permute-start(bf16[100,256]{1,0:T(8,128)(2,1)S(1)} %shard_map.101.refs_0_), channel_id=1, source_target_pairs={{16,0},{26,2},{20,4},{30,6},{24,8},{18,10},{28,12},{22,14},{0,16},... | collective-permute-start | bytes 153608 | tf_op jit(solution)/shard_map/ppermute | solution.py:220
  8.6 4.6 %collective-permute-start.1 = (bf16[100,256]{1,0:T(8,128)(2,1)S(1)}, bf16[100,256]{1,0:T(8,128)(2,1)S(1)}, u32[]{:S(2)}, u32[]{:S(2)}) collective-permute-start(bf16[100,256]{1,0:T(8,128)(2,1)S(1)} %shard_map.101.refs_0_), channel_id=1, source_target_pairs={{8,0},{10,2},{12,4},{14,6},{0,8},{2,10},{4,12},{6,14},{24,16},{26,... | collective-permute-start | bytes 153608 | tf_op jit(solution)/shard_map/ppermute | solution.py:220
  10.2 5.9 %collective-permute-start.3 = (bf16[100,256]{1,0:T(8,128)(2,1)S(1)}, bf16[100,256]{1,0:T(8,128)(2,1)S(1)}, u32[]{:S(2)}, u32[]{:S(2)}) collective-permute-start(bf16[100,256]{1,0:T(8,128)(2,1)S(1)} %shard_map.101.refs_0_), channel_id=1, source_target_pairs={{24,0},{18,2},{28,4},{22,6},{16,8},{26,10},{20,12},{30,14},{8,16},... | collective-permute-start | bytes 153608 | tf_op jit(solution)/shard_map/ppermute | solution.py:220
  10.8 7.9 %collective-permute-start.4 = (bf16[1,100,256]{2,1,0:T(8,128)(2,1)S(1)}, bf16[1,100,256]{2,1,0:T(8,128)(2,1)S(1)}, u32[]{:S(2)}, u32[]{:S(2)}) collective-permute-start(bf16[1,100,256]{2,1,0:T(8,128)(2,1)S(1)} %shard_map.104), channel_id=1, source_target_pairs={{4,0},{6,2},{0,4},{2,6},{12,8},{14,10},{8,12},{10,14},{20,16},{22,... | collective-permute-start | bytes 153608 | tf_op jit(solution)/shard_map/ppermute | solution.py:220
  13.2 6.2 %collective-permute-start.5 = (bf16[2,100,256]{2,1,0:T(8,128)(2,1)S(1)}, bf16[2,100,256]{2,1,0:T(8,128)(2,1)S(1)}, u32[]{:S(2)}, u32[]{:S(2)}) collective-permute-start(bf16[2,100,256]{2,1,0:T(8,128)(2,1)S(1)} %shard_map.102._), channel_id=1, source_target_pairs={{4,0},{6,2},{0,4},{2,6},{12,8},{14,10},{8,12},{10,14},{20,16},{22,... | collective-permute-start | bytes 307208 | tf_op jit(solution)/shard_map/ppermute | solution.py:220
  16.1 4.1 %collective-permute-start.6 = (bf16[1,100,256]{2,1,0:T(8,128)(2,1)S(1)}, bf16[1,100,256]{2,1,0:T(8,128)(2,1)S(1)}, u32[]{:S(2)}, u32[]{:S(2)}) collective-permute-start(bf16[1,100,256]{2,1,0:T(8,128)(2,1)S(1)} %shard_map.105), channel_id=1, source_target_pairs={{4,0},{6,2},{0,4},{2,6},{12,8},{14,10},{8,12},{10,14},{20,16},{22,... | collective-permute-start | bytes 153608 | tf_op jit(solution)/shard_map/ppermute | solution.py:220
  20.3 1.8 %collective-permute-start.7 = (bf16[8,100,256]{2,1,0:T(8,128)(2,1)S(1)}, bf16[8,100,256]{2,1,0:T(8,128)(2,1)S(1)}, u32[]{:S(2)}, u32[]{:S(2)}) collective-permute-start(bf16[8,100,256]{2,1,0:T(8,128)(2,1)S(1)} %constant_dynamic-update-slice_fusion.stack), channel_id=1, source_target_pairs={{2,0},{0,2},{6,4},{4,6},{10,8},{8,10},{14,12},{12,14},{18,16},{16,... | collective-permute-start | bytes 1228808 | tf_op jit(solution)/shard_map/ppermute | solution.py:220
  23.1 4.4 %collective-permute-start.8 = (s16[144,256]{1,0:T(8,128)(2,1)S(1)}, s16[144,256]{1,0:T(8,128)(2,1)S(1)}, u32[]{:S(2)}, u32[]{:S(2)}) collective-permute-start(s16[144,256]{1,0:T(8,128)(2,1)S(1)} %get-tuple-element.35), channel_id=1, source_target_pairs={{1,0},{0,1},{3,2},{2,3},{5,4},{4,5},{7,6},{6,7},{9,8},{8,9},{11,10... | collective-permute-start | bytes 221192 | tf_op jit(solution)/shard_map/ppermute | solution.py:216
  39.6 1.4 %collective-permute-start.9 = (bf16[8,48,256]{2,1,0:T(8,128)(2,1)S(1)}, bf16[8,48,256]{2,1,0:T(8,128)(2,1)S(1)}, u32[]{:S(2)}, u32[]{:S(2)}) collective-permute-start(bf16[8,48,256]{2,1,0:T(8,128)(2,1)S(1)} %all_to_all.5.near), channel_id=1, source_target_pairs={{2,0},{0,2},{6,4},{4,6},{10,8},{8,10},{14,12},{12,14},{18,16},{16,... | collective-permute-start | bytes 589832 | tf_op jit(solution)/shard_map/ppermute | solution.py:220
  41.5 3.9 %collective-permute-start.10 = (s16[48,256]{1,0:T(8,128)(2,1)S(1)}, s16[48,256]{1,0:T(8,128)(2,1)S(1)}, u32[]{:S(2)}, u32[]{:S(2)}) collective-permute-start(s16[48,256]{1,0:T(8,128)(2,1)S(1)} %get-tuple-element.40), channel_id=1, source_target_pairs={{1,0},{0,1},{3,2},{2,3},{5,4},{4,5},{7,6},{6,7},{9,8},{8,9},{11,10... | collective-permute-start | bytes 73736 | tf_op jit(solution)/shard_map/ppermute | solution.py:216

commit v14 on v13

--- a/solution.py
+++ b/solution.py
@@ -152,7 +152,7 @@
 
 def aggregate_hidden(projected, far, weight_t, tiles_t, degrees, plan, own, *rest):
     others, panels = rest[:-1], rest[-1]
-    mine, opposite = panel_order(panels.shape[0] // 4, lax.axis_index("blk") % 2)
+    mine, opposite = panel_order(panels.shape[0] // 4)
     for index, place in enumerate(mine):
         panels[place] = projected[index]
     for index, place in enumerate(opposite):
@@ -216,27 +216,15 @@
     return lax.ppermute(value, axis, [((d + step) % size, d) for d in range(size)])
 
 
-def swapped(value, masks):
-    return lax.ppermute(value, "blk", [(d ^ masks[d % 2], d) for d in range(lax.axis_size("blk"))])
-
-
-def outer_order(outer):
-    rest = list(range(2, outer))
-    return 1, list(zip(rest[0::2], rest[1::2]))
-
-
-def two_ways(pairs):
-    return pairs, [(pair[1], pair[0]) for pair in pairs]
-
-
-def panel_order(outer, core):
-    first, pairs = outer_order(outer)
-    lists = []
-    for here in (core, 1 - core):
-        early, late = ([4 * jnp.where(here == 0, *sides) for sides in way] for way in two_ways(pairs))
-        mine = [*early, 0, 4 * first, *late]
-        lists.append(mine + [apart + 2 for apart in mine])
-    return lists[0], [apart ^ 1 for apart in lists[1]]
+def swapped(value, mask):
+    return lax.ppermute(value, "blk", [(d ^ mask, d) for d in range(lax.axis_size("blk"))])
+
+
+def panel_order(outer):
+    direct = [4 * step for step in range(2, outer, 2)]
+    mine = [*direct, 0, 4, *[apart + 4 for apart in direct]]
+    mine = mine + [apart + 2 for apart in mine]
+    return mine, [apart ^ 1 for apart in mine]
 
 
 def packed(*parts):
@@ -250,15 +238,15 @@
 
 def gather_features(value, aside, later):
     outer = lax.axis_size("blk") // 4
-    first, pairs = outer_order(outer)
-    early, late = ([swapped(value, (4 * a, 4 * b)) for a, b in way] for way in two_ways(pairs))
-    ahead = swapped(value, (4 * first, 4 * first))
-    stacks = packed(*early), packed(value, ahead), packed(*late)
-    over = [swapped(stack, (2, 2)) for stack in stacks]
-    beside = aside(stacks[1])
+    direct = packed(*[swapped(value, 4 * step) for step in range(2, outer, 2)])
+    ahead = swapped(value, 4)
+    relayed = swapped(direct, 4)
+    stacks = direct, packed(value, ahead), packed(relayed)[0]
+    over = [swapped(stack, 2) for stack in stacks]
+    beside = aside(over[0])
     over[0], *behind = later(over[0], beside)
     near = jnp.concatenate([*stacks, *over])
-    return (near, swapped(near, (1, 1))), beside, behind
+    return (near, swapped(near, 1)), beside, behind
 
 
 def gather_classes(value):
@@ -266,7 +254,7 @@
     groups = [list(range(core, size, 2)) for core in range(2)]
     copies = jnp.broadcast_to(value[None], (size // 2, *value.shape))
     near = lax.all_to_all(copies, "blk", 0, 0, axis_index_groups=groups)
-    return near, swapped(near, (1, 1))
+    return near, swapped(near, 1)
 
 
 def body(
@@ -371,7 +359,7 @@
         scratch=[pltpu.VMEM((blocks, hidden, tile), BF16)],
     )
     classes_in, scaling = call(
-        functools.partial(combine, len(outer_order(blocks // 4)[1])),
+        functools.partial(combine, blocks // 8 - 1),
         [shape((padded, tile), BF16), shape((1, tile), F32)],
         vmem=(projected, bias_1, weight_2, degrees, own, *exchanged(sums)),
     )

time: 46.4 us -> 47.5 us (1.024)
  blocking collectives: 11.8 us -> 13.7 us
  waiting for transfers between devices: 11.8 us -> 9.92 us
  starting transfers between devices: 15.3 us -> 16.5 us
    all_to_all x1, blocking collectives: 11.8 us -> 13.7 us  [gather_classes(): near = lax.all_to_all(copies, 'blk', 0, 0, axis_index_groups=groups)]
    ppermute x8, waiting for transfers between devices: 6.26 us -> 4.72 us  [swapped(): lax.ppermute(value, 'blk', [(d ^ mask, d) for d in range(lax.axis_size('b...]
    ppermute x8, starting transfers between devices: 9.62 us -> 10.4 us  [swapped(): lax.ppermute(value, 'blk', [(d ^ mask, d) for d in range(lax.axis_size('b...]
where the time goes in v14:
time: 47.5 us; the launch traced here: 47.2 us
  starting transfers between devices  16.5 us (35%)
  blocking collectives  13.7 us (29%)
  waiting for transfers between devices  9.92 us (21%)
  Pallas kernels  6.34 us (13%)
  between operations  0.76 us (2%)
    all_to_all x1, blocking collectives, gather_classes(): near = lax.all_to_all(copies, 'blk', 0, 0, axis_index_groups=groups)  13.7 us
    ppermute x8, starting transfers between devices, swapped(): lax.ppermute(value, 'blk', [(d ^ mask, d) for d in range(lax.axis_size('b...  10.4 us
    pallas_call x12, Pallas kernels, call(): pl.pallas_call(kernel, out_shape=outs, in_specs=[pl.BlockSpec(memory_spac...  6.34 us
    ppermute x3, starting transfers between devices, shifted(): lax.ppermute(value, axis, [((d + step) % size, d) for d in range(size)])  6.05 us
    ppermute x3, waiting for transfers between devices, shifted(): lax.ppermute(value, axis, [((d + step) % size, d) for d in range(size)])  5.2 us
    ppermute x8, waiting for transfers between devices, swapped(): lax.ppermute(value, 'blk', [(d ^ mask, d) for d in range(lax.axis_size('b...  4.72 us
  transfers between devices with their start and end apart: 11, of which 8 were waited for; matrix products, arithmetic and copies ran while one was open for 0% of the time, Pallas kernels for 8%

profile of v14, /device:TPU:0, one launch (start us, length us, event | category | flops | bytes accessed | tf_op | source)
XLA Modules:
  0.0 47.2 jit_solution(15132380673050173373)
XLA Ops:
  0.0 2.9 %collective-permute-start = (bf16[100,256]{1,0:T(8,128)(2,1)}, bf16[100,256]{1,0:T(8,128)(2,1)S(1)}, u32[]{:S(2)}, u32[]{:S(2)}) collective-permute-start(bf16[100,256]{1,0:T(8,128)(2,1)} %bitcast.10), channel_id=1, source_target_pairs={{1,0},{0,1},{3,2},{2,3},{5,4},{4,5},{7,6},{6,7},{9,8},{8,9},{11,10... | collective-permute-start | bytes 153608 | tf_op jit(solution)/shard_map/ppermute | solution.py:216
  3.6 1.7 %shard_map.100 = (s32[8]{0:T(128)S(4)}, f32[100,256]{1,0:T(8,128)S(1)}, s32[1,256]{1,0:T(1,128)S(1)}, bf16[16,256,256]{2,1,0:T(8,128)(2,1)S(1)}) custom-call(s32[1]{0:T(128)S(6)} %copy.16.live, s32[1,512]{1,0:T(1,128)} %order.1, bf16[100,256]{1,0:T(8,128)(2,1)} %bitcast.11, bf16[16,256,256]{2,1,0:T(8,128)(2,1)} %bitcast.9), custom_call_target="tpu_custom_call" | custom-call | flops 1048576 | bytes 1048576 | tf_op jit(solution)/shard_map/pallas_call | solution.py:31
  5.3 0.0 collective-permute-done.rest_0_
  5.3 0.2 shard_map.101.refs_0_
  5.5 3.2 %collective-permute-start.1 = (bf16[100,256]{1,0:T(8,128)(2,1)S(1)}, bf16[100,256]{1,0:T(8,128)(2,1)S(1)}, u32[]{:S(2)}, u32[]{:S(2)}) collective-permute-start(bf16[100,256]{1,0:T(8,128)(2,1)S(1)} %shard_map.101.refs_0_), channel_id=1, source_target_pairs={{16,0},{18,2},{20,4},{22,6},{24,8},{26,10},{28,12},{30,14},{0,16},... | collective-permute-start | bytes 153608 | tf_op jit(solution)/shard_map/ppermute | solution.py:220
  8.6 1.6 %collective-permute-start.3 = (bf16[100,256]{1,0:T(8,128)(2,1)S(1)}, bf16[100,256]{1,0:T(8,128)(2,1)S(1)}, u32[]{:S(2)}, u32[]{:S(2)}) collective-permute-start(bf16[100,256]{1,0:T(8,128)(2,1)S(1)} %shard_map.101.refs_0_), channel_id=1, source_target_pairs={{8,0},{10,2},{12,4},{14,6},{0,8},{2,10},{4,12},{6,14},{24,16},{26,... | collective-permute-start | bytes 153608 | tf_op jit(solution)/shard_map/ppermute | solution.py:220
  10.2 0.6 %collective-permute-done.1.refs_0_ = bf16[100,256]{1,0:T(8,128)(2,1)S(1)} collective-permute-done((bf16[100,256]{1,0:T(8,128)(2,1)S(1)}, bf16[100,256]{1,0:T(8,128)(2,1)S(1)}, u32[]{:S(2)}, u32[]{:S(2)}) %collective-permute-start.1) | collective-permute-done | bytes 51232 | tf_op jit(solution)/shard_map/ppermute | solution.py:220
  10.8 1.8 %collective-permute-start.4 = (bf16[1,100,256]{2,1,0:T(8,128)(2,1)S(1)}, bf16[1,100,256]{2,1,0:T(8,128)(2,1)S(1)}, u32[]{:S(2)}, u32[]{:S(2)}) collective-permute-start(bf16[1,100,256]{2,1,0:T(8,128)(2,1)S(1)} %shard_map.102), channel_id=1, source_target_pairs={{8,0},{10,2},{12,4},{14,6},{0,8},{2,10},{4,12},{6,14},{24,16},{26,... | collective-permute-start | bytes 153608 | tf_op jit(solution)/shard_map/ppermute | solution.py:220
  12.6 1.5 %collective-permute-start.2 = (bf16[1,100,256]{2,1,0:T(8,128)(2,1)S(1)}, bf16[1,100,256]{2,1,0:T(8,128)(2,1)S(1)}, u32[]{:S(2)}, u32[]{:S(2)}) collective-permute-start(bf16[1,100,256]{2,1,0:T(8,128)(2,1)S(1)} %shard_map.102), channel_id=1, source_target_pairs={{4,0},{6,2},{0,4},{2,6},{12,8},{14,10},{8,12},{10,14},{20,16},{22,... | collective-permute-start | bytes 153608 | tf_op jit(solution)/shard_map/ppermute | solution.py:220
  14.2 0.0 collective-permute-done.3.refs_1_
  14.2 0.6 %collective-permute-start.5 = (bf16[2,100,256]{2,1,0:T(8,128)(2,1)S(1)}, bf16[2,100,256]{2,1,0:T(8,128)(2,1)S(1)}, u32[]{:S(2)}, u32[]{:S(2)}) collective-permute-start(bf16[2,100,256]{2,1,0:T(8,128)(2,1)S(1)} %shard_map.104), channel_id=1, source_target_pairs={{4,0},{6,2},{0,4},{2,6},{12,8},{14,10},{8,12},{10,14},{20,16},{22,... | collective-permute-start | bytes 307208 | tf_op jit(solution)/shard_map/ppermute | solution.py:220
  14.8 0.2 collective-permute-done.4.refs_0_
  15.0 1.8 %collective-permute-start.6 = (bf16[1,100,256]{2,1,0:T(8,128)(2,1)S(1)}, bf16[1,100,256]{2,1,0:T(8,128)(2,1)S(1)}, u32[]{:S(2)}, u32[]{:S(2)}) collective-permute-start(bf16[1,100,256]{2,1,0:T(8,128)(2,1)S(1)} %bitcast.8), channel_id=1, source_target_pairs={{4,0},{6,2},{0,4},{2,6},{12,8},{14,10},{8,12},{10,14},{20,16},{22,... | collective-permute-start | bytes 153608 | tf_op jit(solution)/shard_map/ppermute | solution.py:220
  16.8 0.0 collective-permute-done.2._.arrived
  16.8 1.0 %shard_map.103 = (s32[32]{0:T(128)S(4)}, f32[128,1]{1,0:T(8,128)S(1)}, f32[47,1]{1,0:T(8,128)S(1)}, bf16[128,100]{1,0:T(8,128)(2,1)S(1)}, bf16[47,128]{1,0:T(8,128)(2,1)S(1)}) custom-call(bf16[1,100,256]{2,1,0:T(8,128)(2,1)S(1)} %collective-permute-done.2._.arrived, s32[8]{0:T(128)S(4)} %get-tuple-element.25.live, s32[1,16]{1,0:T(1,128)} %refs_0_.1, ...), custom_call_target="tpu_custom_call" | custom-call | flops 1048576 | bytes 1048576 | tf_op jit(solution)/shard_map/pallas_call | solution.py:31
  17.8 0.7 %shard_map.106 = (bf16[1,100,256]{2,1,0:T(8,128)(2,1)S(1)}, bf16[16,256,256]{2,1,0:T(8,128)(2,1)S(1)}, f32[2,8,256]{2,1,0:T(8,128)S(1)}) custom-call(bf16[16,256,256]{2,1,0:T(8,128)(2,1)S(1)} %get-tuple-element.27.tiles, bf16[1,100,256]{2,1,0:T(8,128)(2,1)S(1)} %collective-permute-done.2._.arrived, s32[32]{0:T(128)S(4)} %get-tuple-element.28.plan), custom_call_target="tpu_custom_call" | custom-call | flops 1048576 | bytes 1048576 | tf_op jit(solution)/shard_map/pallas_call | solution.py:31
  18.6 0.4 collective-permute-done.5
  19.0 0.6 %collective-permute-done.6 = bf16[1,100,256]{2,1,0:T(8,128)(2,1)S(1)} collective-permute-done((bf16[1,100,256]{2,1,0:T(8,128)(2,1)S(1)}, bf16[1,100,256]{2,1,0:T(8,128)(2,1)S(1)}, u32[]{:S(2)}, u32[]{:S(2)}) %collective-permute-start.6) | collective-permute-done | bytes 51232 | tf_op jit(solution)/shard_map/ppermute | solution.py:220
  19.5 0.0 collective-permute-start.7
  19.5 0.3 shard_map.107.projected.hidden_in
  19.8 1.5 %collective-permute-done.7.far = bf16[8,100,256]{2,1,0:T(8,128)(2,1)S(1)} collective-permute-done((bf16[8,100,256]{2,1,0:T(8,128)(2,1)S(1)}, bf16[8,100,256]{2,1,0:T(8,128)(2,1)S(1)}, u32[]{:S(2)}, u32[]{:S(2)}) %collective-permute-start.7) | collective-permute-done | bytes 409632 | tf_op jit(solution)/shard_map/ppermute | solution.py:220
  21.3 1.0 %shard_map.108 = (f32[128,256]{1,0:T(8,128)S(1)}, s16[144,256]{1,0:T(8,128)(2,1)S(1)}) custom-call(bf16[8,128,256]{2,1,0:T(8,128)(2,1)S(1)} %shard_map.107.projected.hidden_in, bf16[8,100,256]{2,1,0:T(8,128)(2,1)S(1)} %collective-permute-done.7.far, bf16[128,100]{1,0:T(8,128)(2,1)S(1)} %get-tuple-element.26.weight_t, ...), custom_call_target="tpu_custom_call" | custom-call | flops 1048576 | bytes 1048576 | tf_op jit(solution)/shard_map/pallas_call | solution.py:31
  22.4 1.6 %collective-permute-start.8 = (s16[144,256]{1,0:T(8,128)(2,1)S(1)}, s16[144,256]{1,0:T(8,128)(2,1)S(1)}, u32[]{:S(2)}, u32[]{:S(2)}) collective-permute-start(s16[144,256]{1,0:T(8,128)(2,1)S(1)} %get-tuple-element.35), channel_id=1, source_target_pairs={{1,0},{0,1},{3,2},{2,3},{5,4},{4,5},{7,6},{6,7},{9,8},{8,9},{11,10... | collective-permute-start | bytes 221192 | tf_op jit(solution)/shard_map/ppermute | solution.py:216
  23.9 2.9 %collective-permute-done.8.rest_0_ = s16[144,256]{1,0:T(8,128)(2,1)S(1)} collective-permute-done((s16[144,256]{1,0:T(8,128)(2,1)S(1)}, s16[144,256]{1,0:T(8,128)(2,1)S(1)}, u32[]{:S(2)}, u32[]{:S(2)}) %collective-permute-start.8) | collective-permute-done | bytes 73760 | tf_op jit(solution)/shard_map/ppermute | solution.py:216
  26.8 0.2 shard_map.109
  27.0 13.7 %all_to_all.5.near = bf16[8,48,256]{2,1,0:T(8,128)(2,1)S(1)} all-to-all(bf16[8,48,256]{2,1,0:T(8,128)(2,1)S(1)} %broadcast_in_dim.14), channel_id=1, replica_groups={{0,4,8,12,16,20,24,28},{2,6,10,14,18,22,26,30},{1,5,9,13,17,21,25,29},{..., dimensions={0} | all-to-all | bytes 393216 | tf_op jit(solution)/shard_map/all_to_all | solution.py:256
  40.7 0.0 collective-permute-start.9
  40.7 1.4 %collective-permute-done.9.far = bf16[8,48,256]{2,1,0:T(8,128)(2,1)S(1)} collective-permute-done((bf16[8,48,256]{2,1,0:T(8,128)(2,1)S(1)}, bf16[8,48,256]{2,1,0:T(8,128)(2,1)S(1)}, u32[]{:S(2)}, u32[]{:S(2)}) %collective-permute-start.9) | collective-permute-done | bytes 196640 | tf_op jit(solution)/shard_map/ppermute | solution.py:220
  42.1 0.5 %shard_map.110 = (f32[48,256]{1,0:T(8,128)S(1)}, s16[48,256]{1,0:T(8,128)(2,1)S(1)}) custom-call(bf16[8,48,256]{2,1,0:T(8,128)(2,1)S(1)} %all_to_all.5.near, bf16[8,48,256]{2,1,0:T(8,128)(2,1)S(1)} %collective-permute-done.9.far, bf16[16,256,256]{2,1,0:T(8,128)(2,1)S(1)} %get-tuple-element.33.tiles_t, s32[32]{0:T(128)S(4)} %get-tuple-element.28.plan), custom_call_target="tpu_custom_call" | custom-call | flops 1048576 | bytes 1048576 | tf_op jit(solution)/shard_map/pallas_call | solution.py:31
  42.6 1.6 %collective-permute-start.10 = (s16[48,256]{1,0:T(8,128)(2,1)S(1)}, s16[48,256]{1,0:T(8,128)(2,1)S(1)}, u32[]{:S(2)}, u32[]{:S(2)}) collective-permute-start(s16[48,256]{1,0:T(8,128)(2,1)S(1)} %get-tuple-element.40), channel_id=1, source_target_pairs={{1,0},{0,1},{3,2},{2,3},{5,4},{4,5},{7,6},{6,7},{9,8},{8,9},{11,10... | collective-permute-start | bytes 73736 | tf_op jit(solution)/shard_map/ppermute | solution.py:216
  44.2 2.3 %collective-permute-done.10.rest_0_ = s16[48,256]{1,0:T(8,128)(2,1)S(1)} collective-permute-done((s16[48,256]{1,0:T(8,128)(2,1)S(1)}, s16[48,256]{1,0:T(8,128)(2,1)S(1)}, u32[]{:S(2)}, u32[]{:S(2)}) %collective-permute-start.10) | collective-permute-done | bytes 24608 | tf_op jit(solution)/shard_map/ppermute | solution.py:216
  46.5 0.7 %shard_map.111 = f32[47,256]{1,0:T(8,128)} custom-call(bf16[48,256]{1,0:T(8,128)(2,1)S(1)} %get-tuple-element.36.classes_in, f32[1,256]{1,0:T(1,128)S(1)} %get-tuple-element.37.scaling, f32[47,1]{1,0:T(8,128)S(1)} %get-tuple-element.38.bias, f32[48,256]{1,0:T(8,128)S(1)} %get-tuple-element.39.own, s16[48,256]{1,0:T(8,128)(2,1)S(1)} %collective-permute-done.10.rest_0_), custom_call_target="tpu_custom_call" | custom-call | flops 1048576 | bytes 1048576 | tf_op jit(solution)/shard_map/pallas_call | solution.py:31
  (10 shorter events, 0.1 us)
Async XLA Ops:
  0.0 5.3 %collective-permute-start = (bf16[100,256]{1,0:T(8,128)(2,1)}, bf16[100,256]{1,0:T(8,128)(2,1)S(1)}, u32[]{:S(2)}, u32[]{:S(2)}) collective-permute-start(bf16[100,256]{1,0:T(8,128)(2,1)} %bitcast.10), channel_id=1, source_target_pairs={{1,0},{0,1},{3,2},{2,3},{5,4},{4,5},{7,6},{6,7},{9,8},{8,9},{11,10... | collective-permute-start | bytes 153608 | tf_op jit(solution)/shard_map/ppermute | solution.py:216
  5.5 5.4 %collective-permute-start.1 = (bf16[100,256]{1,0:T(8,128)(2,1)S(1)}, bf16[100,256]{1,0:T(8,128)(2,1)S(1)}, u32[]{:S(2)}, u32[]{:S(2)}) collective-permute-start(bf16[100,256]{1,0:T(8,128)(2,1)S(1)} %shard_map.101.refs_0_), channel_id=1, source_target_pairs={{16,0},{18,2},{20,4},{22,6},{24,8},{26,10},{28,12},{30,14},{0,16},... | collective-permute-start | bytes 153608 | tf_op jit(solution)/shard_map/ppermute | solution.py:220
  8.6 5.6 %collective-permute-start.3 = (bf16[100,256]{1,0:T(8,128)(2,1)S(1)}, bf16[100,256]{1,0:T(8,128)(2,1)S(1)}, u32[]{:S(2)}, u32[]{:S(2)}) collective-permute-start(bf16[100,256]{1,0:T(8,128)(2,1)S(1)} %shard_map.101.refs_0_), channel_id=1, source_target_pairs={{8,0},{10,2},{12,4},{14,6},{0,8},{2,10},{4,12},{6,14},{24,16},{26,... | collective-permute-start | bytes 153608 | tf_op jit(solution)/shard_map/ppermute | solution.py:220
  10.8 4.1 %collective-permute-start.4 = (bf16[1,100,256]{2,1,0:T(8,128)(2,1)S(1)}, bf16[1,100,256]{2,1,0:T(8,128)(2,1)S(1)}, u32[]{:S(2)}, u32[]{:S(2)}) collective-permute-start(bf16[1,100,256]{2,1,0:T(8,128)(2,1)S(1)} %shard_map.102), channel_id=1, source_target_pairs={{8,0},{10,2},{12,4},{14,6},{0,8},{2,10},{4,12},{6,14},{24,16},{26,... | collective-permute-start | bytes 153608 | tf_op jit(solution)/shard_map/ppermute | solution.py:220
  12.6 4.1 %collective-permute-start.2 = (bf16[1,100,256]{2,1,0:T(8,128)(2,1)S(1)}, bf16[1,100,256]{2,1,0:T(8,128)(2,1)S(1)}, u32[]{:S(2)}, u32[]{:S(2)}) collective-permute-start(bf16[1,100,256]{2,1,0:T(8,128)(2,1)S(1)} %shard_map.102), channel_id=1, source_target_pairs={{4,0},{6,2},{0,4},{2,6},{12,8},{14,10},{8,12},{10,14},{20,16},{22,... | collective-permute-start | bytes 153608 | tf_op jit(solution)/shard_map/ppermute | solution.py:220
  14.2 4.8 %collective-permute-start.5 = (bf16[2,100,256]{2,1,0:T(8,128)(2,1)S(1)}, bf16[2,100,256]{2,1,0:T(8,128)(2,1)S(1)}, u32[]{:S(2)}, u32[]{:S(2)}) collective-permute-start(bf16[2,100,256]{2,1,0:T(8,128)(2,1)S(1)} %shard_map.104), channel_id=1, source_target_pairs={{4,0},{6,2},{0,4},{2,6},{12,8},{14,10},{8,12},{10,14},{20,16},{22,... | collective-permute-start | bytes 307208 | tf_op jit(solution)/shard_map/ppermute | solution.py:220
  15.0 4.5 %collective-permute-start.6 = (bf16[1,100,256]{2,1,0:T(8,128)(2,1)S(1)}, bf16[1,100,256]{2,1,0:T(8,128)(2,1)S(1)}, u32[]{:S(2)}, u32[]{:S(2)}) collective-permute-start(bf16[1,100,256]{2,1,0:T(8,128)(2,1)S(1)} %bitcast.8), channel_id=1, source_target_pairs={{4,0},{6,2},{0,4},{2,6},{12,8},{14,10},{8,12},{10,14},{20,16},{22,... | collective-permute-start | bytes 153608 | tf_op jit(solution)/shard_map/ppermute | solution.py:220
  19.5 1.8 %collective-permute-start.7 = (bf16[8,100,256]{2,1,0:T(8,128)(2,1)S(1)}, bf16[8,100,256]{2,1,0:T(8,128)(2,1)S(1)}, u32[]{:S(2)}, u32[]{:S(2)}) collective-permute-start(bf16[8,100,256]{2,1,0:T(8,128)(2,1)S(1)} %constant_dynamic-update-slice_fusion.stack), channel_id=1, source_target_pairs={{2,0},{0,2},{6,4},{4,6},{10,8},{8,10},{14,12},{12,14},{18,16},{16,... | collective-permute-start | bytes 1228808 | tf_op jit(solution)/shard_map/ppermute | solution.py:220
  22.4 4.4 %collective-permute-start.8 = (s16[144,256]{1,0:T(8,128)(2,1)S(1)}, s16[144,256]{1,0:T(8,128)(2,1)S(1)}, u32[]{:S(2)}, u32[]{:S(2)}) collective-permute-start(s16[144,256]{1,0:T(8,128)(2,1)S(1)} %get-tuple-element.35), channel_id=1, source_target_pairs={{1,0},{0,1},{3,2},{2,3},{5,4},{4,5},{7,6},{6,7},{9,8},{8,9},{11,10... | collective-permute-start | bytes 221192 | tf_op jit(solution)/shard_map/ppermute | solution.py:216
  40.7 1.4 %collective-permute-start.9 = (bf16[8,48,256]{2,1,0:T(8,128)(2,1)S(1)}, bf16[8,48,256]{2,1,0:T(8,128)(2,1)S(1)}, u32[]{:S(2)}, u32[]{:S(2)}) collective-permute-start(bf16[8,48,256]{2,1,0:T(8,128)(2,1)S(1)} %all_to_all.5.near), channel_id=1, source_target_pairs={{2,0},{0,2},{6,4},{4,6},{10,8},{8,10},{14,12},{12,14},{18,16},{16,... | collective-permute-start | bytes 589832 | tf_op jit(solution)/shard_map/ppermute | solution.py:220
  42.6 3.9 %collective-permute-start.10 = (s16[48,256]{1,0:T(8,128)(2,1)S(1)}, s16[48,256]{1,0:T(8,128)(2,1)S(1)}, u32[]{:S(2)}, u32[]{:S(2)}) collective-permute-start(s16[48,256]{1,0:T(8,128)(2,1)S(1)} %get-tuple-element.40), channel_id=1, source_target_pairs={{1,0},{0,1},{3,2},{2,3},{5,4},{4,5},{7,6},{6,7},{9,8},{8,9},{11,10... | collective-permute-start | bytes 73736 | tf_op jit(solution)/shard_map/ppermute | solution.py:216

commit v15 on v12

--- a/solution.py
+++ b/solution.py
@@ -234,7 +234,7 @@
     lists = []
     for here in (core, 1 - core):
         early, late = ([4 * jnp.where(here == 0, *sides) for sides in way] for way in two_ways(pairs))
-        mine = [0, *early, 4 * first, *late]
+        mine = [0, 4 * first, *early, *late]
         lists.append(mine + [apart + 2 for apart in mine])
     return lists[0], [apart ^ 1 for apart in lists[1]]
 
@@ -251,13 +251,14 @@
 def gather_features(value, aside, later):
     outer = lax.axis_size("blk") // 4
     first, pairs = outer_order(outer)
+    ahead = swapped(value, (4 * first, 4 * first))
     early, late = ([swapped(value, (4 * a, 4 * b)) for a, b in way] for way in two_ways(pairs))
-    ahead = swapped(value, (4 * first, 4 * first))
-    stacks = packed(value, *early), packed(ahead, *late)
-    over = [swapped(stack, (2, 2)) for stack in stacks]
-    beside = aside(over[0])
+    crossed = [swapped(value, (4 * a + 2, 4 * b + 2)) for a, b in two_ways(pairs)[1]]
+    here, early = packed(value, ahead), packed(*early)
+    over = [swapped(here, (2, 2)), swapped(early, (2, 2))]
+    beside = aside(here)
     over[0], *behind = later(over[0], beside)
-    near = jnp.concatenate([*stacks, *over])
+    near = jnp.concatenate([here, early, packed(*late), *over, packed(*crossed)])
     return (near, swapped(near, (1, 1))), beside, behind
 
 

time: 46.7 us -> 45.9 us (0.983)
  waiting for transfers between devices: 14 us -> 9.77 us
  starting transfers between devices: 13.9 us -> 17.7 us
    ppermute x7 -> x8, waiting for transfers between devices: 8.41 us -> 4.44 us  [swapped(): lax.ppermute(value, 'blk', [(d ^ masks[d % 2], d) for d in range(lax.axis...]
    ppermute x7 -> x8, starting transfers between devices: 8.24 us -> 11.8 us  [swapped(): lax.ppermute(value, 'blk', [(d ^ masks[d % 2], d) for d in range(lax.axis...]
  transfers between devices with their start and end apart: 10 -> 11, of which waited for: 8 -> 5; matrix products, arithmetic and copies ran while one was open for 0% -> 0% of each run, Pallas kernels for 8% -> 8%
where the time goes in v15:
time: 45.9 us; the launch traced here: 45.7 us
  starting transfers between devices  17.7 us (39%)
  blocking collectives  11 us (24%)
  waiting for transfers between devices  9.77 us (21%)
  Pallas kernels  6.32 us (14%)
  between operations  0.8 us (2%)
    ppermute x8, starting transfers between devices, swapped(): lax.ppermute(value, 'blk', [(d ^ masks[d % 2], d) for d in range(lax.axis...  11.8 us
    all_to_all x1, blocking collectives, gather_classes(): near = lax.all_to_all(copies, 'blk', 0, 0, axis_index_groups=groups)  11 us
    pallas_call x11, Pallas kernels, call(): pl.pallas_call(kernel, out_shape=outs, in_specs=[pl.BlockSpec(memory_spac...  6.32 us
    ppermute x3, starting transfers between devices, shifted(): lax.ppermute(value, axis, [((d + step) % size, d) for d in range(size)])  5.92 us
    ppermute x3, waiting for transfers between devices, shifted(): lax.ppermute(value, axis, [((d + step) % size, d) for d in range(size)])  5.33 us
    ppermute x8, waiting for transfers between devices, swapped(): lax.ppermute(value, 'blk', [(d ^ masks[d % 2], d) for d in range(lax.axis...  4.44 us
  transfers between devices with their start and end apart: 11, of which 5 were waited for; matrix products, arithmetic and copies ran while one was open for 0% of the time, Pallas kernels for 8%

profile of v15, /device:TPU:0, one launch (start us, length us, event | category | flops | bytes accessed | tf_op | source)
XLA Modules:
  0.0 45.7 jit_solution(8184682214308818456)
XLA Ops:
  0.0 2.9 %collective-permute-start = (bf16[100,256]{1,0:T(8,128)(2,1)}, bf16[100,256]{1,0:T(8,128)(2,1)S(1)}, u32[]{:S(2)}, u32[]{:S(2)}) collective-permute-start(bf16[100,256]{1,0:T(8,128)(2,1)} %bitcast.7), channel_id=1, source_target_pairs={{1,0},{0,1},{3,2},{2,3},{5,4},{4,5},{7,6},{6,7},{9,8},{8,9},{11,10... | collective-permute-start | bytes 153608 | tf_op jit(solution)/shard_map/ppermute | solution.py:216
  3.6 1.7 %shard_map.100 = (s32[8]{0:T(128)S(4)}, f32[100,256]{1,0:T(8,128)S(1)}, s32[1,256]{1,0:T(1,128)S(1)}, bf16[16,256,256]{2,1,0:T(8,128)(2,1)S(1)}) custom-call(s32[1]{0:T(128)S(6)} %copy.16.live, s32[1,512]{1,0:T(1,128)} %order.1, bf16[100,256]{1,0:T(8,128)(2,1)} %bitcast.8, bf16[16,256,256]{2,1,0:T(8,128)(2,1)} %bitcast.6), custom_call_target="tpu_custom_call" | custom-call | flops 1048576 | bytes 1048576 | tf_op jit(solution)/shard_map/pallas_call | solution.py:31
  5.3 0.0 collective-permute-done.rest_0_
  5.3 0.2 shard_map.101.refs_0_
  5.5 2.2 %collective-permute-start.1 = (bf16[100,256]{1,0:T(8,128)(2,1)S(1)}, bf16[100,256]{1,0:T(8,128)(2,1)S(1)}, u32[]{:S(2)}, u32[]{:S(2)}) collective-permute-start(bf16[100,256]{1,0:T(8,128)(2,1)S(1)} %shard_map.101.refs_0_), channel_id=1, source_target_pairs={{8,0},{10,2},{12,4},{14,6},{0,8},{2,10},{4,12},{6,14},{24,16},{26,... | collective-permute-start | bytes 153608 | tf_op jit(solution)/shard_map/ppermute | solution.py:220
  7.6 2.6 %collective-permute-start.2 = (bf16[100,256]{1,0:T(8,128)(2,1)S(1)}, bf16[100,256]{1,0:T(8,128)(2,1)S(1)}, u32[]{:S(2)}, u32[]{:S(2)}) collective-permute-start(bf16[100,256]{1,0:T(8,128)(2,1)S(1)} %shard_map.101.refs_0_), channel_id=1, source_target_pairs={{16,0},{26,2},{20,4},{30,6},{24,8},{18,10},{28,12},{22,14},{0,16},... | collective-permute-start | bytes 153608 | tf_op jit(solution)/shard_map/ppermute | solution.py:220
  10.2 0.0 collective-permute-start.3
  10.2 4.8 %collective-permute-start.6 = (bf16[100,256]{1,0:T(8,128)(2,1)S(1)}, bf16[100,256]{1,0:T(8,128)(2,1)S(1)}, u32[]{:S(2)}, u32[]{:S(2)}) collective-permute-start(bf16[100,256]{1,0:T(8,128)(2,1)S(1)} %shard_map.101.refs_0_), channel_id=1, source_target_pairs={{28,0},{22,2},{24,4},{18,6},{20,8},{30,10},{16,12},{26,14},{12,16}... | collective-permute-start | bytes 153608 | tf_op jit(solution)/shard_map/ppermute | solution.py:220
  15.0 0.0 collective-permute-done.1.refs_1_
  15.0 0.6 %collective-permute-start.4 = (bf16[2,100,256]{2,1,0:T(8,128)(2,1)S(1)}, bf16[2,100,256]{2,1,0:T(8,128)(2,1)S(1)}, u32[]{:S(2)}, u32[]{:S(2)}) collective-permute-start(bf16[2,100,256]{2,1,0:T(8,128)(2,1)S(1)} %shard_map.102._), channel_id=1, source_target_pairs={{4,0},{6,2},{0,4},{2,6},{12,8},{14,10},{8,12},{10,14},{20,16},{22,... | collective-permute-start | bytes 307208 | tf_op jit(solution)/shard_map/ppermute | solution.py:220
  15.6 0.0 collective-permute-done.2.refs_0_
  15.6 1.6 %collective-permute-start.5 = (bf16[1,100,256]{2,1,0:T(8,128)(2,1)S(1)}, bf16[1,100,256]{2,1,0:T(8,128)(2,1)S(1)}, u32[]{:S(2)}, u32[]{:S(2)}) collective-permute-start(bf16[1,100,256]{2,1,0:T(8,128)(2,1)S(1)} %shard_map.104), channel_id=1, source_target_pairs={{4,0},{6,2},{0,4},{2,6},{12,8},{14,10},{8,12},{10,14},{20,16},{22,... | collective-permute-start | bytes 153608 | tf_op jit(solution)/shard_map/ppermute | solution.py:220
  17.2 0.0 collective-permute-done.3
  17.2 1.0 %shard_map.103 = (s32[32]{0:T(128)S(4)}, f32[128,1]{1,0:T(8,128)S(1)}, f32[47,1]{1,0:T(8,128)S(1)}, bf16[128,100]{1,0:T(8,128)(2,1)S(1)}, bf16[47,128]{1,0:T(8,128)(2,1)S(1)}) custom-call(bf16[2,100,256]{2,1,0:T(8,128)(2,1)S(1)} %shard_map.102._, s32[8]{0:T(128)S(4)} %get-tuple-element.25.live, s32[1,16]{1,0:T(1,128)} %refs_0_.1, s32[1,16]{1,0:T(1,128)} %refs_1_.1, ...), custom_call_target="tpu_custom_call" | custom-call | flops 1048576 | bytes 1048576 | tf_op jit(solution)/shard_map/pallas_call | solution.py:31
  18.2 1.5 %collective-permute-done.4.arrived = bf16[2,100,256]{2,1,0:T(8,128)(2,1)S(1)} collective-permute-done((bf16[2,100,256]{2,1,0:T(8,128)(2,1)S(1)}, bf16[2,100,256]{2,1,0:T(8,128)(2,1)S(1)}, u32[]{:S(2)}, u32[]{:S(2)}) %collective-permute-start.4) | collective-permute-done | bytes 102432 | tf_op jit(solution)/shard_map/ppermute | solution.py:220
  19.8 0.7 %shard_map.105 = (bf16[2,100,256]{2,1,0:T(8,128)(2,1)S(1)}, bf16[16,256,256]{2,1,0:T(8,128)(2,1)S(1)}, f32[2,8,256]{2,1,0:T(8,128)S(1)}) custom-call(bf16[16,256,256]{2,1,0:T(8,128)(2,1)S(1)} %get-tuple-element.27.tiles, bf16[2,100,256]{2,1,0:T(8,128)(2,1)S(1)} %collective-permute-done.4.arrived, s32[32]{0:T(128)S(4)} %get-tuple-element.28.plan), custom_call_target="tpu_custom_call" | custom-call | flops 1048576 | bytes 1048576 | tf_op jit(solution)/shard_map/pallas_call | solution.py:31
  20.5 0.0 collective-permute-done.5
  20.5 0.0 collective-permute-done.6
  20.6 0.1 collective-permute-start.7
  20.7 0.3 shard_map.106.projected.hidden_in
  20.9 1.5 %collective-permute-done.7.far = bf16[8,100,256]{2,1,0:T(8,128)(2,1)S(1)} collective-permute-done((bf16[8,100,256]{2,1,0:T(8,128)(2,1)S(1)}, bf16[8,100,256]{2,1,0:T(8,128)(2,1)S(1)}, u32[]{:S(2)}, u32[]{:S(2)}) %collective-permute-start.7) | collective-permute-done | bytes 409632 | tf_op jit(solution)/shard_map/ppermute | solution.py:220
  22.4 1.0 %shard_map.107 = (f32[128,256]{1,0:T(8,128)S(1)}, s16[144,256]{1,0:T(8,128)(2,1)S(1)}) custom-call(bf16[8,128,256]{2,1,0:T(8,128)(2,1)S(1)} %shard_map.106.projected.hidden_in, bf16[8,100,256]{2,1,0:T(8,128)(2,1)S(1)} %collective-permute-done.7.far, bf16[128,100]{1,0:T(8,128)(2,1)S(1)} %get-tuple-element.26.weight_t, ...), custom_call_target="tpu_custom_call" | custom-call | flops 1048576 | bytes 1048576 | tf_op jit(solution)/shard_map/pallas_call | solution.py:31
  23.4 1.6 %collective-permute-start.8 = (s16[144,256]{1,0:T(8,128)(2,1)S(1)}, s16[144,256]{1,0:T(8,128)(2,1)S(1)}, u32[]{:S(2)}, u32[]{:S(2)}) collective-permute-start(s16[144,256]{1,0:T(8,128)(2,1)S(1)} %get-tuple-element.35), channel_id=1, source_target_pairs={{1,0},{0,1},{3,2},{2,3},{5,4},{4,5},{7,6},{6,7},{9,8},{8,9},{11,10... | collective-permute-start | bytes 221192 | tf_op jit(solution)/shard_map/ppermute | solution.py:216
  25.0 2.9 %collective-permute-done.8.rest_0_ = s16[144,256]{1,0:T(8,128)(2,1)S(1)} collective-permute-done((s16[144,256]{1,0:T(8,128)(2,1)S(1)}, s16[144,256]{1,0:T(8,128)(2,1)S(1)}, u32[]{:S(2)}, u32[]{:S(2)}) %collective-permute-start.8) | collective-permute-done | bytes 73760 | tf_op jit(solution)/shard_map/ppermute | solution.py:216
  27.8 0.2 shard_map.108
  28.1 11.0 %all_to_all.5.near = bf16[8,48,256]{2,1,0:T(8,128)(2,1)S(1)} all-to-all(bf16[8,48,256]{2,1,0:T(8,128)(2,1)S(1)} %broadcast_in_dim.14), channel_id=1, replica_groups={{0,4,8,12,16,20,24,28},{2,6,10,14,18,22,26,30},{1,5,9,13,17,21,25,29},{..., dimensions={0} | all-to-all | bytes 393216 | tf_op jit(solution)/shard_map/all_to_all | solution.py:269
  39.1 0.0 collective-permute-start.9
  39.1 1.4 %collective-permute-done.9.far = bf16[8,48,256]{2,1,0:T(8,128)(2,1)S(1)} collective-permute-done((bf16[8,48,256]{2,1,0:T(8,128)(2,1)S(1)}, bf16[8,48,256]{2,1,0:T(8,128)(2,1)S(1)}, u32[]{:S(2)}, u32[]{:S(2)}) %collective-permute-start.9) | collective-permute-done | bytes 196640 | tf_op jit(solution)/shard_map/ppermute | solution.py:220
  40.6 0.5 %shard_map.109 = (f32[48,256]{1,0:T(8,128)S(1)}, s16[48,256]{1,0:T(8,128)(2,1)S(1)}) custom-call(bf16[8,48,256]{2,1,0:T(8,128)(2,1)S(1)} %all_to_all.5.near, bf16[8,48,256]{2,1,0:T(8,128)(2,1)S(1)} %collective-permute-done.9.far, bf16[16,256,256]{2,1,0:T(8,128)(2,1)S(1)} %get-tuple-element.33.tiles_t, s32[32]{0:T(128)S(4)} %get-tuple-element.28.plan), custom_call_target="tpu_custom_call" | custom-call | flops 1048576 | bytes 1048576 | tf_op jit(solution)/shard_map/pallas_call | solution.py:31
  41.1 1.4 %collective-permute-start.10 = (s16[48,256]{1,0:T(8,128)(2,1)S(1)}, s16[48,256]{1,0:T(8,128)(2,1)S(1)}, u32[]{:S(2)}, u32[]{:S(2)}) collective-permute-start(s16[48,256]{1,0:T(8,128)(2,1)S(1)} %get-tuple-element.40), channel_id=1, source_target_pairs={{1,0},{0,1},{3,2},{2,3},{5,4},{4,5},{7,6},{6,7},{9,8},{8,9},{11,10... | collective-permute-start | bytes 73736 | tf_op jit(solution)/shard_map/ppermute | solution.py:216
  42.5 2.5 %collective-permute-done.10.rest_0_ = s16[48,256]{1,0:T(8,128)(2,1)S(1)} collective-permute-done((s16[48,256]{1,0:T(8,128)(2,1)S(1)}, s16[48,256]{1,0:T(8,128)(2,1)S(1)}, u32[]{:S(2)}, u32[]{:S(2)}) %collective-permute-start.10) | collective-permute-done | bytes 24608 | tf_op jit(solution)/shard_map/ppermute | solution.py:216
  45.0 0.7 %shard_map.110 = f32[47,256]{1,0:T(8,128)} custom-call(bf16[48,256]{1,0:T(8,128)(2,1)S(1)} %get-tuple-element.36.classes_in, f32[1,256]{1,0:T(1,128)S(1)} %get-tuple-element.37.scaling, f32[47,1]{1,0:T(8,128)S(1)} %get-tuple-element.38.bias, f32[48,256]{1,0:T(8,128)S(1)} %get-tuple-element.39.own, s16[48,256]{1,0:T(8,128)(2,1)S(1)} %collective-permute-done.10.rest_0_), custom_call_target="tpu_custom_call" | custom-call | flops 1048576 | bytes 1048576 | tf_op jit(solution)/shard_map/pallas_call | solution.py:31
  (9 shorter events, 0.1 us)
Async XLA Ops:
  0.0 5.3 %collective-permute-start = (bf16[100,256]{1,0:T(8,128)(2,1)}, bf16[100,256]{1,0:T(8,128)(2,1)S(1)}, u32[]{:S(2)}, u32[]{:S(2)}) collective-permute-start(bf16[100,256]{1,0:T(8,128)(2,1)} %bitcast.7), channel_id=1, source_target_pairs={{1,0},{0,1},{3,2},{2,3},{5,4},{4,5},{7,6},{6,7},{9,8},{8,9},{11,10... | collective-permute-start | bytes 153608 | tf_op jit(solution)/shard_map/ppermute | solution.py:216
  5.5 9.5 %collective-permute-start.1 = (bf16[100,256]{1,0:T(8,128)(2,1)S(1)}, bf16[100,256]{1,0:T(8,128)(2,1)S(1)}, u32[]{:S(2)}, u32[]{:S(2)}) collective-permute-start(bf16[100,256]{1,0:T(8,128)(2,1)S(1)} %shard_map.101.refs_0_), channel_id=1, source_target_pairs={{8,0},{10,2},{12,4},{14,6},{0,8},{2,10},{4,12},{6,14},{24,16},{26,... | collective-permute-start | bytes 153608 | tf_op jit(solution)/shard_map/ppermute | solution.py:220
  7.6 8.0 %collective-permute-start.2 = (bf16[100,256]{1,0:T(8,128)(2,1)S(1)}, bf16[100,256]{1,0:T(8,128)(2,1)S(1)}, u32[]{:S(2)}, u32[]{:S(2)}) collective-permute-start(bf16[100,256]{1,0:T(8,128)(2,1)S(1)} %shard_map.101.refs_0_), channel_id=1, source_target_pairs={{16,0},{26,2},{20,4},{30,6},{24,8},{18,10},{28,12},{22,14},{0,16},... | collective-permute-start | bytes 153608 | tf_op jit(solution)/shard_map/ppermute | solution.py:220
  10.2 7.0 %collective-permute-start.3 = (bf16[100,256]{1,0:T(8,128)(2,1)S(1)}, bf16[100,256]{1,0:T(8,128)(2,1)S(1)}, u32[]{:S(2)}, u32[]{:S(2)}) collective-permute-start(bf16[100,256]{1,0:T(8,128)(2,1)S(1)} %shard_map.101.refs_0_), channel_id=1, source_target_pairs={{24,0},{18,2},{28,4},{22,6},{16,8},{26,10},{20,12},{30,14},{8,16},... | collective-permute-start | bytes 153608 | tf_op jit(solution)/shard_map/ppermute | solution.py:220
  10.2 10.3 %collective-permute-start.6 = (bf16[100,256]{1,0:T(8,128)(2,1)S(1)}, bf16[100,256]{1,0:T(8,128)(2,1)S(1)}, u32[]{:S(2)}, u32[]{:S(2)}) collective-permute-start(bf16[100,256]{1,0:T(8,128)(2,1)S(1)} %shard_map.101.refs_0_), channel_id=1, source_target_pairs={{28,0},{22,2},{24,4},{18,6},{20,8},{30,10},{16,12},{26,14},{12,16}... | collective-permute-start | bytes 153608 | tf_op jit(solution)/shard_map/ppermute | solution.py:220
  15.0 4.8 %collective-permute-start.4 = (bf16[2,100,256]{2,1,0:T(8,128)(2,1)S(1)}, bf16[2,100,256]{2,1,0:T(8,128)(2,1)S(1)}, u32[]{:S(2)}, u32[]{:S(2)}) collective-permute-start(bf16[2,100,256]{2,1,0:T(8,128)(2,1)S(1)} %shard_map.102._), channel_id=1, source_target_pairs={{4,0},{6,2},{0,4},{2,6},{12,8},{14,10},{8,12},{10,14},{20,16},{22,... | collective-permute-start | bytes 307208 | tf_op jit(solution)/shard_map/ppermute | solution.py:220
  15.6 4.9 %collective-permute-start.5 = (bf16[1,100,256]{2,1,0:T(8,128)(2,1)S(1)}, bf16[1,100,256]{2,1,0:T(8,128)(2,1)S(1)}, u32[]{:S(2)}, u32[]{:S(2)}) collective-permute-start(bf16[1,100,256]{2,1,0:T(8,128)(2,1)S(1)} %shard_map.104), channel_id=1, source_target_pairs={{4,0},{6,2},{0,4},{2,6},{12,8},{14,10},{8,12},{10,14},{20,16},{22,... | collective-permute-start | bytes 153608 | tf_op jit(solution)/shard_map/ppermute | solution.py:220
  20.6 1.8 %collective-permute-start.7 = (bf16[8,100,256]{2,1,0:T(8,128)(2,1)S(1)}, bf16[8,100,256]{2,1,0:T(8,128)(2,1)S(1)}, u32[]{:S(2)}, u32[]{:S(2)}) collective-permute-start(bf16[8,100,256]{2,1,0:T(8,128)(2,1)S(1)} %shard_map.111.stack), channel_id=1, source_target_pairs={{2,0},{0,2},{6,4},{4,6},{10,8},{8,10},{14,12},{12,14},{18,16},{16,... | collective-permute-start | bytes 1228808 | tf_op jit(solution)/shard_map/ppermute | solution.py:220
  23.4 4.4 %collective-permute-start.8 = (s16[144,256]{1,0:T(8,128)(2,1)S(1)}, s16[144,256]{1,0:T(8,128)(2,1)S(1)}, u32[]{:S(2)}, u32[]{:S(2)}) collective-permute-start(s16[144,256]{1,0:T(8,128)(2,1)S(1)} %get-tuple-element.35), channel_id=1, source_target_pairs={{1,0},{0,1},{3,2},{2,3},{5,4},{4,5},{7,6},{6,7},{9,8},{8,9},{11,10... | collective-permute-start | bytes 221192 | tf_op jit(solution)/shard_map/ppermute | solution.py:216
  39.1 1.4 %collective-permute-start.9 = (bf16[8,48,256]{2,1,0:T(8,128)(2,1)S(1)}, bf16[8,48,256]{2,1,0:T(8,128)(2,1)S(1)}, u32[]{:S(2)}, u32[]{:S(2)}) collective-permute-start(bf16[8,48,256]{2,1,0:T(8,128)(2,1)S(1)} %all_to_all.5.near), channel_id=1, source_target_pairs={{2,0},{0,2},{6,4},{4,6},{10,8},{8,10},{14,12},{12,14},{18,16},{16,... | collective-permute-start | bytes 589832 | tf_op jit(solution)/shard_map/ppermute | solution.py:220
  41.1 3.9 %collective-permute-start.10 = (s16[48,256]{1,0:T(8,128)(2,1)S(1)}, s16[48,256]{1,0:T(8,128)(2,1)S(1)}, u32[]{:S(2)}, u32[]{:S(2)}) collective-permute-start(s16[48,256]{1,0:T(8,128)(2,1)S(1)} %get-tuple-element.40), channel_id=1, source_target_pairs={{1,0},{0,1},{3,2},{2,3},{5,4},{4,5},{7,6},{6,7},{9,8},{8,9},{11,10... | collective-permute-start | bytes 73736 | tf_op jit(solution)/shard_map/ppermute | solution.py:216

commit v16 on v15

--- a/solution.py
+++ b/solution.py
@@ -55,18 +55,34 @@
     return nn(features[...], jnp.where(source == wanted, 1.0, 0.0).astype(BF16))
 
 
-def prepare(live, order, features, tiles, live_out, part, wanted_out, tiles_out, *rest):
-    live_out[0] = live[0]
-    order_in, features_in, sems = rest
-    copies = fetched((order, features, tiles), (order_in, features_in, tiles_out), sems)
-    for copy in copies[:2]:
+def prepare(reps, live, *refs):
+    order, features, tiles, rows, columns, *sources = refs[:9]
+    plan, part, wanted_out, tiles_out, bias_1, bias_2, weight_1, weight_2 = refs[9:17]
+    order_in, features_in, rows_in, columns_in, row_1, row_2, weight_in, sems = refs[17:]
+    copies = fetched(
+        (order, features, rows, columns, *sources, tiles),
+        (order_in, features_in, rows_in, columns_in, row_1, row_2, weight_in, weight_2, tiles_out),
+        sems,
+    )
+    for copy in copies[:7]:
         copy.wait()
     tile = features.shape[1]
-    member = lax.axis_index("rep")
+    slots = rows_in.shape[1]
+    blocks = lax.axis_size("blk")
+    block, member = lax.axis_index("blk"), lax.axis_index("rep")
     wanted = order_in[:, pl.ds(pl.multiple_of(member * tile, tile), tile)]
     wanted_out[...] = wanted
     part[...] = picked(features_in, wanted, member)
-    copies[2].wait()
+    bias_1[...] = jnp.broadcast_to(row_1[...], (8, row_1.shape[1])).T[:, :1]
+    bias_2[...] = jnp.broadcast_to(row_2[...], (8, row_2.shape[1])).T[:, :1]
+    weight_1[...] = weight_in[...].astype(F32).T.astype(BF16)
+    for slot in range(slots):
+        plan[slot] = lax.clamp(0, columns_in[0, slot] // reps, blocks - 1) ^ block
+        local = rows_in[0, slot] - block * reps
+        step = lax.rem(local - member + reps, reps)
+        plan[slots + slot] = jnp.where((slot < live[0]) & (local >= 0) & (local < reps), step, -1)
+    for copy in copies[7:]:
+        copy.wait()
 
 
 def arrange(part, wanted, *rest):
@@ -80,31 +96,12 @@
     out[...] = total.astype(BF16)
 
 
-def stage(reps, _, live, *refs):
-    sources, (plan, bias_1, bias_2, weight_1, weight_2), scratch = refs[:6], refs[6:11], refs[11:]
-    rows_in, columns_in, row_1, row_2, weight_in, sems = scratch
-    slots = rows_in.shape[1]
-    blocks = lax.axis_size("blk")
-    for copy in fetched(sources, (rows_in, columns_in, row_1, row_2, weight_in, weight_2), sems):
-        copy.wait()
-    bias_1[...] = jnp.broadcast_to(row_1[...], (8, row_1.shape[1])).T[:, :1]
-    bias_2[...] = jnp.broadcast_to(row_2[...], (8, row_2.shape[1])).T[:, :1]
-    weight_1[...] = weight_in[...].astype(F32).T.astype(BF16)
-    block, member = lax.axis_index("blk"), lax.axis_index("rep")
-    for slot in range(slots):
-        plan[slot] = lax.clamp(0, columns_in[0, slot] // reps, blocks - 1) ^ block
-        local = rows_in[0, slot] - block * reps
-        step = lax.rem(local - member + reps, reps)
-        plan[slots + slot] = jnp.where((slot < live[0]) & (local >= 0) & (local < reps), step, -1)
-
-
 def project(weight_t, stack, out):
     for index in range(stack.shape[0]):
         out[index] = nn(weight_t[...], stack[index]).astype(BF16)
 
 
-def turn(tiles, arrived, plan, arrived_out, tiles_t, degrees):
-    arrived_out[...] = arrived[...]
+def turn(tiles, plan, tiles_t, degrees):
     slots, tile = tiles.shape[0], tiles.shape[1]
     count = degrees.shape[0]
     total = jnp.zeros((count * ONES_ROWS, tile), F32)
@@ -234,8 +231,8 @@
     lists = []
     for here in (core, 1 - core):
         early, late = ([4 * jnp.where(here == 0, *sides) for sides in way] for way in two_ways(pairs))
-        mine = [0, 4 * first, *early, *late]
-        lists.append(mine + [apart + 2 for apart in mine])
+        crossed, over = [apart + 2 for apart in late], [apart + 2 for apart in early]
+        lists.append([0, 4 * first, *crossed, *late, *early, 2, 4 * first + 2, *over])
     return lists[0], [apart ^ 1 for apart in lists[1]]
 
 
@@ -248,7 +245,7 @@
     return call(pack, [out], vmem=parts)[0]
 
 
-def gather_features(value, aside, later):
+def gather_features(value):
     outer = lax.axis_size("blk") // 4
     first, pairs = outer_order(outer)
     ahead = swapped(value, (4 * first, 4 * first))
@@ -256,10 +253,8 @@
     crossed = [swapped(value, (4 * a + 2, 4 * b + 2)) for a, b in two_ways(pairs)[1]]
     here, early = packed(value, ahead), packed(*early)
     over = [swapped(here, (2, 2)), swapped(early, (2, 2))]
-    beside = aside(here)
-    over[0], *behind = later(over[0], beside)
-    near = jnp.concatenate([here, early, packed(*late), *over, packed(*crossed)])
-    return (near, swapped(near, (1, 1))), beside, behind
+    near = jnp.concatenate([here, packed(*crossed), packed(*late), early, *over])
+    return near, swapped(near, (1, 1))
 
 
 def gather_classes(value):
@@ -295,70 +290,50 @@
 
     own_t = features.T
     others = [shifted(own_t, "rep", step) for step in range(1, reps)]
-    live, part, wanted, tiles = call(
-        prepare,
+    plan, part, wanted, tiles, bias_1, bias_2, weight_1, weight_2 = call(
+        functools.partial(prepare, reps),
         [
-            pltpu.SMEM((8,), jnp.int32),
+            pltpu.SMEM((2 * slots,), jnp.int32),
             shape((width, tile), F32),
             shape((1, tile), jnp.int32),
             shape(tile_values.shape[1:], BF16),
+            shape((hidden, 1), F32),
+            shape((classes, 1), F32),
+            shape((hidden, width), BF16),
+            shape((classes, hidden), BF16),
         ],
         smem=(tile_live,),
-        hbm=(node_order, own_t, tile_values[0]),
+        hbm=(
+            node_order,
+            own_t,
+            tile_values[0],
+            tile_rows,
+            tile_columns,
+            first_bias[None],
+            second_bias[None],
+            first_weight,
+            second_weight.T,
+        ),
         scratch=[
             pltpu.VMEM(node_order.shape, jnp.int32),
             pltpu.VMEM(own_t.shape, BF16),
-            pltpu.SemaphoreType.DMA((3,)),
+            pltpu.SMEM((1, slots), jnp.int32),
+            pltpu.SMEM((1, slots), jnp.int32),
+            pltpu.VMEM((1, hidden), F32),
+            pltpu.VMEM((1, classes), F32),
+            pltpu.VMEM(first_weight.shape, BF16),
+            pltpu.SemaphoreType.DMA((9,)),
         ],
         smem_outs=1,
     )
     (ordered,) = call(arrange, [shape((width, tile), BF16)], vmem=(part, wanted, *others))
-
-    def staged(after):
-        return call(
-            functools.partial(stage, reps),
-            [
-                pltpu.SMEM((2 * slots,), jnp.int32),
-                shape((hidden, 1), F32),
-                shape((classes, 1), F32),
-                shape((hidden, width), BF16),
-                shape((classes, hidden), BF16),
-            ],
-            vmem=(after,),
-            smem=(live,),
-            hbm=(
-                tile_rows,
-                tile_columns,
-                first_bias[None],
-                second_bias[None],
-                first_weight,
-                second_weight.T,
-            ),
-            scratch=[
-                pltpu.SMEM((1, slots), jnp.int32),
-                pltpu.SMEM((1, slots), jnp.int32),
-                pltpu.VMEM((1, hidden), F32),
-                pltpu.VMEM((1, classes), F32),
-                pltpu.VMEM(first_weight.shape, BF16),
-                pltpu.SemaphoreType.DMA((6,)),
-            ],
-            smem_outs=1,
-        )
-
-    def turned(arrived, values):
-        return call(
-            turn,
-            [
-                shape(arrived.shape, BF16),
-                shape(tiles.shape, BF16),
-                shape((reps, 8, tile), F32),
-            ],
-            vmem=(tiles, arrived),
-            smem=(values[0],),
-        )
-
-    (near, far), values, (tiles_t, degrees) = gather_features(ordered, staged, turned)
-    plan, bias_1, bias_2, weight_1, weight_2 = values
+    near, far = gather_features(ordered)
+    tiles_t, degrees = call(
+        turn,
+        [shape(tiles.shape, BF16), shape((reps, 8, tile), F32)],
+        vmem=(tiles,),
+        smem=(plan,),
+    )
     (projected,) = call(
         project,
         [shape((near.shape[0], hidden, tile), BF16)],

time: 45.9 us -> 45.8 us (level)
  Pallas kernels: 6.32 us -> 5.43 us
  waiting for transfers between devices: 9.77 us -> 10.6 us
    pallas_call x11 -> x10, Pallas kernels: 6.32 us -> 5.43 us  [call(): pl.pallas_call(kernel, out_shape=outs, in_specs=[pl.BlockSpec(memory_spac...]
    ppermute x8, waiting for transfers between devices: 4.44 us -> 5.27 us  [swapped(): lax.ppermute(value, 'blk', [(d ^ masks[d % 2], d) for d in range(lax.axis...]
  transfers between devices with their start and end apart: 11 -> 11, of which waited for: 5 -> 7; matrix products, arithmetic and copies ran while one was open for 0% -> 0% of each run, Pallas kernels for 8% -> 6%
where the time goes in v16:
time: 45.8 us; the launch traced here: 45.6 us
  starting transfers between devices  17.5 us (38%)
  blocking collectives  11.2 us (24%)
  waiting for transfers between devices  10.6 us (23%)
  Pallas kernels  5.43 us (12%)
  between operations  0.76 us (2%)
    ppermute x8, starting transfers between devices, swapped(): lax.ppermute(value, 'blk', [(d ^ masks[d % 2], d) for d in range(lax.axis...  11.6 us
    all_to_all x1, blocking collectives, gather_classes(): near = lax.all_to_all(copies, 'blk', 0, 0, axis_index_groups=groups)  11.2 us
    ppermute x3, starting transfers between devices, shifted(): lax.ppermute(value, axis, [((d + step) % size, d) for d in range(size)])  5.91 us
    pallas_call x10, Pallas kernels, call(): pl.pallas_call(kernel, out_shape=outs, in_specs=[pl.BlockSpec(memory_spac...  5.43 us
    ppermute x3, waiting for transfers between devices, shifted(): lax.ppermute(value, axis, [((d + step) % size, d) for d in range(size)])  5.34 us
    ppermute x8, waiting for transfers between devices, swapped(): lax.ppermute(value, 'blk', [(d ^ masks[d % 2], d) for d in range(lax.axis...  5.27 us
  transfers between devices with their start and end apart: 11, of which 7 were waited for; matrix products, arithmetic and copies ran while one was open for 0% of the time, Pallas kernels for 6%

profile of v16, /device:TPU:0, one launch (start us, length us, event | category | flops | bytes accessed | tf_op | source)
XLA Modules:
  0.0 45.6 jit_solution(18413463167747990121)
XLA Ops:
  0.0 2.9 %collective-permute-start = (bf16[100,256]{1,0:T(8,128)(2,1)}, bf16[100,256]{1,0:T(8,128)(2,1)S(1)}, u32[]{:S(2)}, u32[]{:S(2)}) collective-permute-start(bf16[100,256]{1,0:T(8,128)(2,1)} %bitcast.7), channel_id=1, source_target_pairs={{1,0},{0,1},{3,2},{2,3},{5,4},{4,5},{7,6},{6,7},{9,8},{8,9},{11,10... | collective-permute-start | bytes 153608 | tf_op jit(solution)/shard_map/ppermute | solution.py:213
  3.6 1.8 %shard_map.100 = (s32[32]{0:T(128)S(4)}, f32[100,256]{1,0:T(8,128)S(1)}, s32[1,256]{1,0:T(1,128)S(1)}, bf16[16,256,256]{2,1,0:T(8,128)(2,1)S(1)}, f32[128,1]{1,0...) custom-call(s32[1]{0:T(128)S(6)} %copy.16.live, s32[1,512]{1,0:T(1,128)} %refs_0_.1, ...), custom_call_target="tpu_custom_call" | custom-call | flops 1048576 | bytes 1048576 | tf_op jit(solution)/shard_map/pallas_call | solution.py:31
  5.4 0.0 collective-permute-done.rest_0_
  5.4 0.2 shard_map.101.refs_0_
  5.6 2.0 %collective-permute-start.1 = (bf16[100,256]{1,0:T(8,128)(2,1)S(1)}, bf16[100,256]{1,0:T(8,128)(2,1)S(1)}, u32[]{:S(2)}, u32[]{:S(2)}) collective-permute-start(bf16[100,256]{1,0:T(8,128)(2,1)S(1)} %shard_map.101.refs_0_), channel_id=1, source_target_pairs={{8,0},{10,2},{12,4},{14,6},{0,8},{2,10},{4,12},{6,14},{24,16},{26,... | collective-permute-start | bytes 153608 | tf_op jit(solution)/shard_map/ppermute | solution.py:217
  7.6 2.6 %collective-permute-start.4 = (bf16[100,256]{1,0:T(8,128)(2,1)S(1)}, bf16[100,256]{1,0:T(8,128)(2,1)S(1)}, u32[]{:S(2)}, u32[]{:S(2)}) collective-permute-start(bf16[100,256]{1,0:T(8,128)(2,1)S(1)} %shard_map.101.refs_0_), channel_id=1, source_target_pairs={{16,0},{26,2},{20,4},{30,6},{24,8},{18,10},{28,12},{22,14},{0,16},... | collective-permute-start | bytes 153608 | tf_op jit(solution)/shard_map/ppermute | solution.py:217
  10.2 0.0 collective-permute-start.3
  10.2 4.8 %collective-permute-start.2 = (bf16[100,256]{1,0:T(8,128)(2,1)S(1)}, bf16[100,256]{1,0:T(8,128)(2,1)S(1)}, u32[]{:S(2)}, u32[]{:S(2)}) collective-permute-start(bf16[100,256]{1,0:T(8,128)(2,1)S(1)} %shard_map.101.refs_0_), channel_id=1, source_target_pairs={{28,0},{22,2},{24,4},{18,6},{20,8},{30,10},{16,12},{26,14},{12,16}... | collective-permute-start | bytes 153608 | tf_op jit(solution)/shard_map/ppermute | solution.py:217
  15.0 0.0 collective-permute-done.1.refs_1_
  15.0 0.6 %collective-permute-start.5 = (bf16[2,100,256]{2,1,0:T(8,128)(2,1)S(1)}, bf16[2,100,256]{2,1,0:T(8,128)(2,1)S(1)}, u32[]{:S(2)}, u32[]{:S(2)}) collective-permute-start(bf16[2,100,256]{2,1,0:T(8,128)(2,1)S(1)} %shard_map.102), channel_id=1, source_target_pairs={{4,0},{6,2},{0,4},{2,6},{12,8},{14,10},{8,12},{10,14},{20,16},{22,... | collective-permute-start | bytes 307208 | tf_op jit(solution)/shard_map/ppermute | solution.py:217
  15.6 0.0 collective-permute-done.4.refs_0_
  15.6 1.6 %collective-permute-start.6 = (bf16[1,100,256]{2,1,0:T(8,128)(2,1)S(1)}, bf16[1,100,256]{2,1,0:T(8,128)(2,1)S(1)}, u32[]{:S(2)}, u32[]{:S(2)}) collective-permute-start(bf16[1,100,256]{2,1,0:T(8,128)(2,1)S(1)} %shard_map.103), channel_id=1, source_target_pairs={{4,0},{6,2},{0,4},{2,6},{12,8},{14,10},{8,12},{10,14},{20,16},{22,... | collective-permute-start | bytes 153608 | tf_op jit(solution)/shard_map/ppermute | solution.py:217
  17.2 0.6 %collective-permute-done.2 = bf16[100,256]{1,0:T(8,128)(2,1)S(1)} collective-permute-done((bf16[100,256]{1,0:T(8,128)(2,1)S(1)}, bf16[100,256]{1,0:T(8,128)(2,1)S(1)}, u32[]{:S(2)}, u32[]{:S(2)}) %collective-permute-start.2) | collective-permute-done | bytes 51232 | tf_op jit(solution)/shard_map/ppermute | solution.py:217
  17.8 0.0 collective-permute-done.3
  17.8 2.0 %collective-permute-done.5 = bf16[2,100,256]{2,1,0:T(8,128)(2,1)S(1)} collective-permute-done((bf16[2,100,256]{2,1,0:T(8,128)(2,1)S(1)}, bf16[2,100,256]{2,1,0:T(8,128)(2,1)S(1)}, u32[]{:S(2)}, u32[]{:S(2)}) %collective-permute-start.5) | collective-permute-done | bytes 102432 | tf_op jit(solution)/shard_map/ppermute | solution.py:217
  19.8 0.6 %collective-permute-done.6 = bf16[1,100,256]{2,1,0:T(8,128)(2,1)S(1)} collective-permute-done((bf16[1,100,256]{2,1,0:T(8,128)(2,1)S(1)}, bf16[1,100,256]{2,1,0:T(8,128)(2,1)S(1)}, u32[]{:S(2)}, u32[]{:S(2)}) %collective-permute-start.6) | collective-permute-done | bytes 51232 | tf_op jit(solution)/shard_map/ppermute | solution.py:217
  20.3 0.0 collective-permute-start.7
  20.3 0.7 %shard_map.105 = (bf16[16,256,256]{2,1,0:T(8,128)(2,1)S(1)}, f32[2,8,256]{2,1,0:T(8,128)S(1)}) custom-call(bf16[16,256,256]{2,1,0:T(8,128)(2,1)S(1)} %get-tuple-element.26.tiles, s32[32]{0:T(128)S(4)} %get-tuple-element.27.plan), custom_call_target="tpu_custom_call" | custom-call | flops 1048576 | bytes 1048576 | tf_op jit(solution)/shard_map/pallas_call | solution.py:31
  21.1 0.3 shard_map.104.projected.hidden_in
  21.4 0.7 %collective-permute-done.7.far = bf16[8,100,256]{2,1,0:T(8,128)(2,1)S(1)} collective-permute-done((bf16[8,100,256]{2,1,0:T(8,128)(2,1)S(1)}, bf16[8,100,256]{2,1,0:T(8,128)(2,1)S(1)}, u32[]{:S(2)}, u32[]{:S(2)}) %collective-permute-start.7) | collective-permute-done | bytes 409632 | tf_op jit(solution)/shard_map/ppermute | solution.py:217
  22.1 1.0 %shard_map.106 = (f32[128,256]{1,0:T(8,128)S(1)}, s16[144,256]{1,0:T(8,128)(2,1)S(1)}) custom-call(bf16[8,128,256]{2,1,0:T(8,128)(2,1)S(1)} %shard_map.104.projected.hidden_in, bf16[8,100,256]{2,1,0:T(8,128)(2,1)S(1)} %collective-permute-done.7.far, bf16[128,100]{1,0:T(8,128)(2,1)S(1)} %get-tuple-element.21.weight_t, ...), custom_call_target="tpu_custom_call" | custom-call | flops 1048576 | bytes 1048576 | tf_op jit(solution)/shard_map/pallas_call | solution.py:31
  23.1 1.6 %collective-permute-start.8 = (s16[144,256]{1,0:T(8,128)(2,1)S(1)}, s16[144,256]{1,0:T(8,128)(2,1)S(1)}, u32[]{:S(2)}, u32[]{:S(2)}) collective-permute-start(s16[144,256]{1,0:T(8,128)(2,1)S(1)} %get-tuple-element.31), channel_id=1, source_target_pairs={{1,0},{0,1},{3,2},{2,3},{5,4},{4,5},{7,6},{6,7},{9,8},{8,9},{11,10... | collective-permute-start | bytes 221192 | tf_op jit(solution)/shard_map/ppermute | solution.py:213
  24.7 2.9 %collective-permute-done.8.rest_0_ = s16[144,256]{1,0:T(8,128)(2,1)S(1)} collective-permute-done((s16[144,256]{1,0:T(8,128)(2,1)S(1)}, s16[144,256]{1,0:T(8,128)(2,1)S(1)}, u32[]{:S(2)}, u32[]{:S(2)}) %collective-permute-start.8) | collective-permute-done | bytes 73760 | tf_op jit(solution)/shard_map/ppermute | solution.py:213
  27.5 0.2 shard_map.107
  27.8 11.2 %all_to_all.5.near = bf16[8,48,256]{2,1,0:T(8,128)(2,1)S(1)} all-to-all(bf16[8,48,256]{2,1,0:T(8,128)(2,1)S(1)} %broadcast_in_dim.14), channel_id=1, replica_groups={{0,4,8,12,16,20,24,28},{2,6,10,14,18,22,26,30},{1,5,9,13,17,21,25,29},{..., dimensions={0} | all-to-all | bytes 393216 | tf_op jit(solution)/shard_map/all_to_all | solution.py:264
  39.0 0.0 collective-permute-start.9
  39.0 1.4 %collective-permute-done.9.far = bf16[8,48,256]{2,1,0:T(8,128)(2,1)S(1)} collective-permute-done((bf16[8,48,256]{2,1,0:T(8,128)(2,1)S(1)}, bf16[8,48,256]{2,1,0:T(8,128)(2,1)S(1)}, u32[]{:S(2)}, u32[]{:S(2)}) %collective-permute-start.9) | collective-permute-done | bytes 196640 | tf_op jit(solution)/shard_map/ppermute | solution.py:217
  40.5 0.5 %shard_map.108 = (f32[48,256]{1,0:T(8,128)S(1)}, s16[48,256]{1,0:T(8,128)(2,1)S(1)}) custom-call(bf16[8,48,256]{2,1,0:T(8,128)(2,1)S(1)} %all_to_all.5.near, bf16[8,48,256]{2,1,0:T(8,128)(2,1)S(1)} %collective-permute-done.9.far, bf16[16,256,256]{2,1,0:T(8,128)(2,1)S(1)} %get-tuple-element.29.tiles_t, s32[32]{0:T(128)S(4)} %get-tuple-element.27.plan), custom_call_target="tpu_custom_call" | custom-call | flops 1048576 | bytes 1048576 | tf_op jit(solution)/shard_map/pallas_call | solution.py:31
  41.0 1.4 %collective-permute-start.10 = (s16[48,256]{1,0:T(8,128)(2,1)S(1)}, s16[48,256]{1,0:T(8,128)(2,1)S(1)}, u32[]{:S(2)}, u32[]{:S(2)}) collective-permute-start(s16[48,256]{1,0:T(8,128)(2,1)S(1)} %get-tuple-element.36), channel_id=1, source_target_pairs={{1,0},{0,1},{3,2},{2,3},{5,4},{4,5},{7,6},{6,7},{9,8},{8,9},{11,10... | collective-permute-start | bytes 73736 | tf_op jit(solution)/shard_map/ppermute | solution.py:213
  42.4 2.5 %collective-permute-done.10.rest_0_ = s16[48,256]{1,0:T(8,128)(2,1)S(1)} collective-permute-done((s16[48,256]{1,0:T(8,128)(2,1)S(1)}, s16[48,256]{1,0:T(8,128)(2,1)S(1)}, u32[]{:S(2)}, u32[]{:S(2)}) %collective-permute-start.10) | collective-permute-done | bytes 24608 | tf_op jit(solution)/shard_map/ppermute | solution.py:213
  44.9 0.7 %shard_map.109 = f32[47,256]{1,0:T(8,128)} custom-call(bf16[48,256]{1,0:T(8,128)(2,1)S(1)} %get-tuple-element.32.classes_in, f32[1,256]{1,0:T(1,128)S(1)} %get-tuple-element.33.scaling, f32[47,1]{1,0:T(8,128)S(1)} %get-tuple-element.34.bias, f32[48,256]{1,0:T(8,128)S(1)} %get-tuple-element.35.own, s16[48,256]{1,0:T(8,128)(2,1)S(1)} %collective-permute-done.10.rest_0_), custom_call_target="tpu_custom_call" | custom-call | flops 1048576 | bytes 1048576 | tf_op jit(solution)/shard_map/pallas_call | solution.py:31
  (9 shorter events, 0.1 us)
Async XLA Ops:
  0.0 5.4 %collective-permute-start = (bf16[100,256]{1,0:T(8,128)(2,1)}, bf16[100,256]{1,0:T(8,128)(2,1)S(1)}, u32[]{:S(2)}, u32[]{:S(2)}) collective-permute-start(bf16[100,256]{1,0:T(8,128)(2,1)} %bitcast.7), channel_id=1, source_target_pairs={{1,0},{0,1},{3,2},{2,3},{5,4},{4,5},{7,6},{6,7},{9,8},{8,9},{11,10... | collective-permute-start | bytes 153608 | tf_op jit(solution)/shard_map/ppermute | solution.py:213
  5.6 9.4 %collective-permute-start.1 = (bf16[100,256]{1,0:T(8,128)(2,1)S(1)}, bf16[100,256]{1,0:T(8,128)(2,1)S(1)}, u32[]{:S(2)}, u32[]{:S(2)}) collective-permute-start(bf16[100,256]{1,0:T(8,128)(2,1)S(1)} %shard_map.101.refs_0_), channel_id=1, source_target_pairs={{8,0},{10,2},{12,4},{14,6},{0,8},{2,10},{4,12},{6,14},{24,16},{26,... | collective-permute-start | bytes 153608 | tf_op jit(solution)/shard_map/ppermute | solution.py:217
  7.6 8.0 %collective-permute-start.4 = (bf16[100,256]{1,0:T(8,128)(2,1)S(1)}, bf16[100,256]{1,0:T(8,128)(2,1)S(1)}, u32[]{:S(2)}, u32[]{:S(2)}) collective-permute-start(bf16[100,256]{1,0:T(8,128)(2,1)S(1)} %shard_map.101.refs_0_), channel_id=1, source_target_pairs={{16,0},{26,2},{20,4},{30,6},{24,8},{18,10},{28,12},{22,14},{0,16},... | collective-permute-start | bytes 153608 | tf_op jit(solution)/shard_map/ppermute | solution.py:217
  10.2 7.6 %collective-permute-start.3 = (bf16[100,256]{1,0:T(8,128)(2,1)S(1)}, bf16[100,256]{1,0:T(8,128)(2,1)S(1)}, u32[]{:S(2)}, u32[]{:S(2)}) collective-permute-start(bf16[100,256]{1,0:T(8,128)(2,1)S(1)} %shard_map.101.refs_0_), channel_id=1, source_target_pairs={{24,0},{18,2},{28,4},{22,6},{16,8},{26,10},{20,12},{30,14},{8,16},... | collective-permute-start | bytes 153608 | tf_op jit(solution)/shard_map/ppermute | solution.py:217
  10.2 7.6 %collective-permute-start.2 = (bf16[100,256]{1,0:T(8,128)(2,1)S(1)}, bf16[100,256]{1,0:T(8,128)(2,1)S(1)}, u32[]{:S(2)}, u32[]{:S(2)}) collective-permute-start(bf16[100,256]{1,0:T(8,128)(2,1)S(1)} %shard_map.101.refs_0_), channel_id=1, source_target_pairs={{28,0},{22,2},{24,4},{18,6},{20,8},{30,10},{16,12},{26,14},{12,16}... | collective-permute-start | bytes 153608 | tf_op jit(solution)/shard_map/ppermute | solution.py:217
  15.0 4.8 %collective-permute-start.5 = (bf16[2,100,256]{2,1,0:T(8,128)(2,1)S(1)}, bf16[2,100,256]{2,1,0:T(8,128)(2,1)S(1)}, u32[]{:S(2)}, u32[]{:S(2)}) collective-permute-start(bf16[2,100,256]{2,1,0:T(8,128)(2,1)S(1)} %shard_map.102), channel_id=1, source_target_pairs={{4,0},{6,2},{0,4},{2,6},{12,8},{14,10},{8,12},{10,14},{20,16},{22,... | collective-permute-start | bytes 307208 | tf_op jit(solution)/shard_map/ppermute | solution.py:217
  15.6 4.7 %collective-permute-start.6 = (bf16[1,100,256]{2,1,0:T(8,128)(2,1)S(1)}, bf16[1,100,256]{2,1,0:T(8,128)(2,1)S(1)}, u32[]{:S(2)}, u32[]{:S(2)}) collective-permute-start(bf16[1,100,256]{2,1,0:T(8,128)(2,1)S(1)} %shard_map.103), channel_id=1, source_target_pairs={{4,0},{6,2},{0,4},{2,6},{12,8},{14,10},{8,12},{10,14},{20,16},{22,... | collective-permute-start | bytes 153608 | tf_op jit(solution)/shard_map/ppermute | solution.py:217
  20.3 1.8 %collective-permute-start.7 = (bf16[8,100,256]{2,1,0:T(8,128)(2,1)S(1)}, bf16[8,100,256]{2,1,0:T(8,128)(2,1)S(1)}, u32[]{:S(2)}, u32[]{:S(2)}) collective-permute-start(bf16[8,100,256]{2,1,0:T(8,128)(2,1)S(1)} %constant_dynamic-update-slice_fusion.stack), channel_id=1, source_target_pairs={{2,0},{0,2},{6,4},{4,6},{10,8},{8,10},{14,12},{12,14},{18,16},{16,... | collective-permute-start | bytes 1228808 | tf_op jit(solution)/shard_map/ppermute | solution.py:217
  23.1 4.4 %collective-permute-start.8 = (s16[144,256]{1,0:T(8,128)(2,1)S(1)}, s16[144,256]{1,0:T(8,128)(2,1)S(1)}, u32[]{:S(2)}, u32[]{:S(2)}) collective-permute-start(s16[144,256]{1,0:T(8,128)(2,1)S(1)} %get-tuple-element.31), channel_id=1, source_target_pairs={{1,0},{0,1},{3,2},{2,3},{5,4},{4,5},{7,6},{6,7},{9,8},{8,9},{11,10... | collective-permute-start | bytes 221192 | tf_op jit(solution)/shard_map/ppermute | solution.py:213
  39.0 1.4 %collective-permute-start.9 = (bf16[8,48,256]{2,1,0:T(8,128)(2,1)S(1)}, bf16[8,48,256]{2,1,0:T(8,128)(2,1)S(1)}, u32[]{:S(2)}, u32[]{:S(2)}) collective-permute-start(bf16[8,48,256]{2,1,0:T(8,128)(2,1)S(1)} %all_to_all.5.near), channel_id=1, source_target_pairs={{2,0},{0,2},{6,4},{4,6},{10,8},{8,10},{14,12},{12,14},{18,16},{16,... | collective-permute-start | bytes 589832 | tf_op jit(solution)/shard_map/ppermute | solution.py:217
  41.0 3.9 %collective-permute-start.10 = (s16[48,256]{1,0:T(8,128)(2,1)S(1)}, s16[48,256]{1,0:T(8,128)(2,1)S(1)}, u32[]{:S(2)}, u32[]{:S(2)}) collective-permute-start(s16[48,256]{1,0:T(8,128)(2,1)S(1)} %get-tuple-element.36), channel_id=1, source_target_pairs={{1,0},{0,1},{3,2},{2,3},{5,4},{4,5},{7,6},{6,7},{9,8},{8,9},{11,10... | collective-permute-start | bytes 73736 | tf_op jit(solution)/shard_map/ppermute | solution.py:213

commit v17 on v16

--- a/solution.py
+++ b/solution.py
@@ -167,10 +167,10 @@
 
 def aggregate_classes(near, far, tiles_t, plan, own, *rest):
     others, panels = rest[:-1], rest[-1]
-    chip = lax.axis_index("blk") // 2
-    for index in range(near.shape[0]):
-        panels[2 * (index ^ chip)] = near[index]
-        panels[2 * (index ^ chip) + 1] = far[index]
+    mine, opposite = panel_order(panels.shape[0] // 4, lax.axis_index("blk") % 2)
+    for index, (here, there) in enumerate(zip(mine, opposite)):
+        panels[here] = near[index]
+        panels[there] = far[index]
     sums = summed(panels, plan, tiles_t, 1 + len(others))
     own[...] = sums[0]
     row = lax.broadcasted_iota(jnp.int32, own.shape, 0)
@@ -231,8 +231,8 @@
     lists = []
     for here in (core, 1 - core):
         early, late = ([4 * jnp.where(here == 0, *sides) for sides in way] for way in two_ways(pairs))
-        crossed, over = [apart + 2 for apart in late], [apart + 2 for apart in early]
-        lists.append([0, 4 * first, *crossed, *late, *early, 2, 4 * first + 2, *over])
+        over = [apart + 2 for apart in [0, 4 * first, *early, *late]]
+        lists.append([0, 4 * first, *late, *early, *over])
     return lists[0], [apart ^ 1 for apart in lists[1]]
 
 
@@ -245,23 +245,14 @@
     return call(pack, [out], vmem=parts)[0]
 
 
-def gather_features(value):
+def gather(value):
     outer = lax.axis_size("blk") // 4
     first, pairs = outer_order(outer)
     ahead = swapped(value, (4 * first, 4 * first))
     early, late = ([swapped(value, (4 * a, 4 * b)) for a, b in way] for way in two_ways(pairs))
-    crossed = [swapped(value, (4 * a + 2, 4 * b + 2)) for a, b in two_ways(pairs)[1]]
-    here, early = packed(value, ahead), packed(*early)
-    over = [swapped(here, (2, 2)), swapped(early, (2, 2))]
-    near = jnp.concatenate([here, packed(*crossed), packed(*late), early, *over])
-    return near, swapped(near, (1, 1))
-
-
-def gather_classes(value):
-    size = lax.axis_size("blk")
-    groups = [list(range(core, size, 2)) for core in range(2)]
-    copies = jnp.broadcast_to(value[None], (size // 2, *value.shape))
-    near = lax.all_to_all(copies, "blk", 0, 0, axis_index_groups=groups)
+    stacks = packed(value, ahead), packed(*early), packed(*late)
+    over = [swapped(stack, (2, 2)) for stack in stacks]
+    near = jnp.concatenate([stacks[0], stacks[2], stacks[1], *over])
     return near, swapped(near, (1, 1))
 
 
@@ -327,7 +318,7 @@
         smem_outs=1,
     )
     (ordered,) = call(arrange, [shape((width, tile), BF16)], vmem=(part, wanted, *others))
-    near, far = gather_features(ordered)
+    near, far = gather(ordered)
     tiles_t, degrees = call(
         turn,
         [shape(tiles.shape, BF16), shape((reps, 8, tile), F32)],
@@ -354,7 +345,7 @@
     own, *sums = call(
         aggregate_classes,
         [shape((padded, tile), F32)] + [shape((padded, tile), jnp.int16)] * (reps - 1),
-        vmem=(*gather_classes(classes_in), tiles_t),
+        vmem=(*gather(classes_in), tiles_t),
         smem=(plan,),
         scratch=[pltpu.VMEM((blocks, padded, tile), BF16)],
     )

time: 45.8 us -> 46.7 us (1.020)
  blocking collectives: 11.2 us -> 0 us
  waiting for transfers between devices: 10.6 us -> 19 us
  starting transfers between devices: 17.5 us -> 21.3 us
    all_to_all x1 -> x0, blocking collectives: 11.2 us -> none  [gather_classes(): near = lax.all_to_all(copies, 'blk', 0, 0, axis_index_groups=groups)]
    ppermute x8 -> x14, waiting for transfers between devices: 5.27 us -> 12.5 us  [swapped(): lax.ppermute(value, 'blk', [(d ^ masks[d % 2], d) for d in range(lax.axis...]
    ppermute x8 -> x14, starting transfers between devices: 11.6 us -> 16.5 us  [swapped(): lax.ppermute(value, 'blk', [(d ^ masks[d % 2], d) for d in range(lax.axis...]
    ppermute x3, waiting for transfers between devices: 5.34 us -> 6.44 us  [shifted(): lax.ppermute(value, axis, [((d + step) % size, d) for d in range(size)])]
    ppermute x3, starting transfers between devices: 5.91 us -> 4.81 us  [shifted(): lax.ppermute(value, axis, [((d + step) % size, d) for d in range(size)])]
    pallas_call x10 -> x14, Pallas kernels: 5.43 us -> 5.44 us  [call(): pl.pallas_call(kernel, out_shape=outs, in_specs=[pl.BlockSpec(memory_spac...]
  transfers between devices with their start and end apart: 11 -> 17, of which waited for: 7 -> 11; matrix products, arithmetic and copies ran while one was open for 0% -> 0% of each run, Pallas kernels for 6% -> 6%
where the time goes in v17:
time: 46.7 us; the launch traced here: 46.6 us
  starting transfers between devices  21.3 us (46%)
  waiting for transfers between devices  19 us (41%)
  Pallas kernels  5.44 us (12%)
  between operations  0.77 us (2%)
    ppermute x14, starting transfers between devices, swapped(): lax.ppermute(value, 'blk', [(d ^ masks[d % 2], d) for d in range(lax.axis...  16.5 us
    ppermute x14, waiting for transfers between devices, swapped(): lax.ppermute(value, 'blk', [(d ^ masks[d % 2], d) for d in range(lax.axis...  12.5 us
    ppermute x3, waiting for transfers between devices, shifted(): lax.ppermute(value, axis, [((d + step) % size, d) for d in range(size)])  6.44 us
    pallas_call x14, Pallas kernels, call(): pl.pallas_call(kernel, out_shape=outs, in_specs=[pl.BlockSpec(memory_spac...  5.44 us
    ppermute x3, starting transfers between devices, shifted(): lax.ppermute(value, axis, [((d + step) % size, d) for d in range(size)])  4.81 us
  transfers between devices with their start and end apart: 17, of which 11 were waited for; matrix products, arithmetic and copies ran while one was open for 0% of the time, Pallas kernels for 6%

profile of v17, /device:TPU:0, one launch (start us, length us, event | category | flops | bytes accessed | tf_op | source)
XLA Modules:
  0.0 46.6 jit_solution(16847956993008647254)
XLA Ops:
  0.0 2.9 %collective-permute-start = (bf16[100,256]{1,0:T(8,128)(2,1)}, bf16[100,256]{1,0:T(8,128)(2,1)S(1)}, u32[]{:S(2)}, u32[]{:S(2)}) collective-permute-start(bf16[100,256]{1,0:T(8,128)(2,1)} %bitcast.7), channel_id=1, source_target_pairs={{1,0},{0,1},{3,2},{2,3},{5,4},{4,5},{7,6},{6,7},{9,8},{8,9},{11,10... | collective-permute-start | bytes 153608 | tf_op jit(solution)/shard_map/ppermute | solution.py:213
  3.6 1.8 %shard_map.100 = (s32[32]{0:T(128)S(4)}, f32[100,256]{1,0:T(8,128)S(1)}, s32[1,256]{1,0:T(1,128)S(1)}, bf16[16,256,256]{2,1,0:T(8,128)(2,1)S(1)}, f32[128,1]{1,0...) custom-call(s32[1]{0:T(128)S(6)} %copy.21.live, s32[1,512]{1,0:T(1,128)} %refs_0_.1, ...), custom_call_target="tpu_custom_call" | custom-call | flops 1048576 | bytes 1048576 | tf_op jit(solution)/shard_map/pallas_call | solution.py:31
  5.4 0.0 collective-permute-done.rest_0_
  5.4 0.2 shard_map.101.refs_0_
  5.6 2.0 %collective-permute-start.1 = (bf16[100,256]{1,0:T(8,128)(2,1)S(1)}, bf16[100,256]{1,0:T(8,128)(2,1)S(1)}, u32[]{:S(2)}, u32[]{:S(2)}) collective-permute-start(bf16[100,256]{1,0:T(8,128)(2,1)S(1)} %shard_map.101.refs_0_), channel_id=1, source_target_pairs={{8,0},{10,2},{12,4},{14,6},{0,8},{2,10},{4,12},{6,14},{24,16},{26,... | collective-permute-start | bytes 153608 | tf_op jit(solution)/shard_map/ppermute | solution.py:217
  7.6 2.6 %collective-permute-start.3 = (bf16[100,256]{1,0:T(8,128)(2,1)S(1)}, bf16[100,256]{1,0:T(8,128)(2,1)S(1)}, u32[]{:S(2)}, u32[]{:S(2)}) collective-permute-start(bf16[100,256]{1,0:T(8,128)(2,1)S(1)} %shard_map.101.refs_0_), channel_id=1, source_target_pairs={{16,0},{26,2},{20,4},{30,6},{24,8},{18,10},{28,12},{22,14},{0,16},... | collective-permute-start | bytes 153608 | tf_op jit(solution)/shard_map/ppermute | solution.py:217
  10.2 0.0 collective-permute-start.2
  10.2 0.0 collective-permute-done.1.refs_1_
  10.2 1.8 %collective-permute-start.4 = (bf16[2,100,256]{2,1,0:T(8,128)(2,1)S(1)}, bf16[2,100,256]{2,1,0:T(8,128)(2,1)S(1)}, u32[]{:S(2)}, u32[]{:S(2)}) collective-permute-start(bf16[2,100,256]{2,1,0:T(8,128)(2,1)S(1)} %shard_map.102), channel_id=1, source_target_pairs={{4,0},{6,2},{0,4},{2,6},{12,8},{14,10},{8,12},{10,14},{20,16},{22,... | collective-permute-start | bytes 307208 | tf_op jit(solution)/shard_map/ppermute | solution.py:217
  12.0 2.2 %collective-permute-done.3.refs_0_ = bf16[100,256]{1,0:T(8,128)(2,1)S(1)} collective-permute-done((bf16[100,256]{1,0:T(8,128)(2,1)S(1)}, bf16[100,256]{1,0:T(8,128)(2,1)S(1)}, u32[]{:S(2)}, u32[]{:S(2)}) %collective-permute-start.3) | collective-permute-done | bytes 51232 | tf_op jit(solution)/shard_map/ppermute | solution.py:217
  14.2 1.5 %collective-permute-start.5 = (bf16[1,100,256]{2,1,0:T(8,128)(2,1)S(1)}, bf16[1,100,256]{2,1,0:T(8,128)(2,1)S(1)}, u32[]{:S(2)}, u32[]{:S(2)}) collective-permute-start(bf16[1,100,256]{2,1,0:T(8,128)(2,1)S(1)} %shard_map.104), channel_id=1, source_target_pairs={{4,0},{6,2},{0,4},{2,6},{12,8},{14,10},{8,12},{10,14},{20,16},{22,... | collective-permute-start | bytes 153608 | tf_op jit(solution)/shard_map/ppermute | solution.py:217
  15.8 0.4 collective-permute-done.2.refs_0_
  16.1 1.5 %collective-permute-start.6 = (bf16[1,100,256]{2,1,0:T(8,128)(2,1)S(1)}, bf16[1,100,256]{2,1,0:T(8,128)(2,1)S(1)}, u32[]{:S(2)}, u32[]{:S(2)}) collective-permute-start(bf16[1,100,256]{2,1,0:T(8,128)(2,1)S(1)} %shard_map.103), channel_id=1, source_target_pairs={{4,0},{6,2},{0,4},{2,6},{12,8},{14,10},{8,12},{10,14},{20,16},{22,... | collective-permute-start | bytes 153608 | tf_op jit(solution)/shard_map/ppermute | solution.py:217
  17.7 0.0 collective-permute-done.4
  17.7 0.7 %collective-permute-done.5 = bf16[1,100,256]{2,1,0:T(8,128)(2,1)S(1)} collective-permute-done((bf16[1,100,256]{2,1,0:T(8,128)(2,1)S(1)}, bf16[1,100,256]{2,1,0:T(8,128)(2,1)S(1)}, u32[]{:S(2)}, u32[]{:S(2)}) %collective-permute-start.5) | collective-permute-done | bytes 51232 | tf_op jit(solution)/shard_map/ppermute | solution.py:217
  18.4 1.9 %collective-permute-done.6 = bf16[1,100,256]{2,1,0:T(8,128)(2,1)S(1)} collective-permute-done((bf16[1,100,256]{2,1,0:T(8,128)(2,1)S(1)}, bf16[1,100,256]{2,1,0:T(8,128)(2,1)S(1)}, u32[]{:S(2)}, u32[]{:S(2)}) %collective-permute-start.6) | collective-permute-done | bytes 51232 | tf_op jit(solution)/shard_map/ppermute | solution.py:217
  20.3 0.0 collective-permute-start.7
  20.3 0.7 %shard_map.106 = (bf16[16,256,256]{2,1,0:T(8,128)(2,1)S(1)}, f32[2,8,256]{2,1,0:T(8,128)S(1)}) custom-call(bf16[16,256,256]{2,1,0:T(8,128)(2,1)S(1)} %get-tuple-element.26.tiles, s32[32]{0:T(128)S(4)} %get-tuple-element.27.plan), custom_call_target="tpu_custom_call" | custom-call | flops 1048576 | bytes 1048576 | tf_op jit(solution)/shard_map/pallas_call | solution.py:31
  21.0 0.3 shard_map.105.projected.hidden_in
  21.3 0.7 %collective-permute-done.7.far = bf16[8,100,256]{2,1,0:T(8,128)(2,1)S(1)} collective-permute-done((bf16[8,100,256]{2,1,0:T(8,128)(2,1)S(1)}, bf16[8,100,256]{2,1,0:T(8,128)(2,1)S(1)}, u32[]{:S(2)}, u32[]{:S(2)}) %collective-permute-start.7) | collective-permute-done | bytes 409632 | tf_op jit(solution)/shard_map/ppermute | solution.py:217
  22.0 1.0 %shard_map.107 = (f32[128,256]{1,0:T(8,128)S(1)}, s16[144,256]{1,0:T(8,128)(2,1)S(1)}) custom-call(bf16[8,128,256]{2,1,0:T(8,128)(2,1)S(1)} %shard_map.105.projected.hidden_in, bf16[8,100,256]{2,1,0:T(8,128)(2,1)S(1)} %collective-permute-done.7.far, bf16[128,100]{1,0:T(8,128)(2,1)S(1)} %get-tuple-element.21.weight_t, ...), custom_call_target="tpu_custom_call" | custom-call | flops 1048576 | bytes 1048576 | tf_op jit(solution)/shard_map/pallas_call | solution.py:31
  23.1 1.6 %collective-permute-start.8 = (s16[144,256]{1,0:T(8,128)(2,1)S(1)}, s16[144,256]{1,0:T(8,128)(2,1)S(1)}, u32[]{:S(2)}, u32[]{:S(2)}) collective-permute-start(s16[144,256]{1,0:T(8,128)(2,1)S(1)} %get-tuple-element.31), channel_id=1, source_target_pairs={{1,0},{0,1},{3,2},{2,3},{5,4},{4,5},{7,6},{6,7},{9,8},{8,9},{11,10... | collective-permute-start | bytes 221192 | tf_op jit(solution)/shard_map/ppermute | solution.py:213
  24.6 2.9 %collective-permute-done.8.rest_0_ = s16[144,256]{1,0:T(8,128)(2,1)S(1)} collective-permute-done((s16[144,256]{1,0:T(8,128)(2,1)S(1)}, s16[144,256]{1,0:T(8,128)(2,1)S(1)}, u32[]{:S(2)}, u32[]{:S(2)}) %collective-permute-start.8) | collective-permute-done | bytes 73760 | tf_op jit(solution)/shard_map/ppermute | solution.py:213
  27.5 0.2 shard_map.108
  27.7 0.0 collective-permute-start.9
  27.7 2.8 %collective-permute-start.11 = (bf16[48,256]{1,0:T(8,128)(2,1)S(1)}, bf16[48,256]{1,0:T(8,128)(2,1)S(1)}, u32[]{:S(2)}, u32[]{:S(2)}) collective-permute-start(bf16[48,256]{1,0:T(8,128)(2,1)S(1)} %get-tuple-element.32.refs_0_.classes_in), channel_id=1, source_target_pairs={{16,0},{26,2},{20,4},{30,6},{24,8},{18,10},{28,12},{22,14},{0,16},... | collective-permute-start | bytes 73736 | tf_op jit(solution)/shard_map/ppermute | solution.py:217
  30.6 1.5 %collective-permute-start.10 = (bf16[48,256]{1,0:T(8,128)(2,1)S(1)}, bf16[48,256]{1,0:T(8,128)(2,1)S(1)}, u32[]{:S(2)}, u32[]{:S(2)}) collective-permute-start(bf16[48,256]{1,0:T(8,128)(2,1)S(1)} %get-tuple-element.32.refs_0_.classes_in), channel_id=1, source_target_pairs={{24,0},{18,2},{28,4},{22,6},{16,8},{26,10},{20,12},{30,14},{8,16},... | collective-permute-start | bytes 73736 | tf_op jit(solution)/shard_map/ppermute | solution.py:217
  32.1 0.0 collective-permute-done.9.refs_1_
  32.1 1.6 %collective-permute-start.12 = (bf16[2,48,256]{2,1,0:T(8,128)(2,1)S(1)}, bf16[2,48,256]{2,1,0:T(8,128)(2,1)S(1)}, u32[]{:S(2)}, u32[]{:S(2)}) collective-permute-start(bf16[2,48,256]{2,1,0:T(8,128)(2,1)S(1)} %shard_map.109), channel_id=1, source_target_pairs={{4,0},{6,2},{0,4},{2,6},{12,8},{14,10},{8,12},{10,14},{20,16},{22,... | collective-permute-start | bytes 147464 | tf_op jit(solution)/shard_map/ppermute | solution.py:217
  33.7 0.0 collective-permute-done.11.refs_0_
  33.7 0.6 %collective-permute-start.13 = (bf16[1,48,256]{2,1,0:T(8,128)(2,1)S(1)}, bf16[1,48,256]{2,1,0:T(8,128)(2,1)S(1)}, u32[]{:S(2)}, u32[]{:S(2)}) collective-permute-start(bf16[1,48,256]{2,1,0:T(8,128)(2,1)S(1)} %shard_map.111), channel_id=1, source_target_pairs={{4,0},{6,2},{0,4},{2,6},{12,8},{14,10},{8,12},{10,14},{20,16},{22,... | collective-permute-start | bytes 73736 | tf_op jit(solution)/shard_map/ppermute | solution.py:217
  34.3 1.9 %collective-permute-done.10.refs_0_ = bf16[48,256]{1,0:T(8,128)(2,1)S(1)} collective-permute-done((bf16[48,256]{1,0:T(8,128)(2,1)S(1)}, bf16[48,256]{1,0:T(8,128)(2,1)S(1)}, u32[]{:S(2)}, u32[]{:S(2)}) %collective-permute-start.10) | collective-permute-done | bytes 24608 | tf_op jit(solution)/shard_map/ppermute | solution.py:217
  36.2 0.5 %collective-permute-start.14 = (bf16[1,48,256]{2,1,0:T(8,128)(2,1)S(1)}, bf16[1,48,256]{2,1,0:T(8,128)(2,1)S(1)}, u32[]{:S(2)}, u32[]{:S(2)}) collective-permute-start(bf16[1,48,256]{2,1,0:T(8,128)(2,1)S(1)} %shard_map.110), channel_id=1, source_target_pairs={{4,0},{6,2},{0,4},{2,6},{12,8},{14,10},{8,12},{10,14},{20,16},{22,... | collective-permute-start | bytes 73736 | tf_op jit(solution)/shard_map/ppermute | solution.py:217
  36.7 0.0 collective-permute-done.12
  36.7 0.9 %collective-permute-done.13 = bf16[1,48,256]{2,1,0:T(8,128)(2,1)S(1)} collective-permute-done((bf16[1,48,256]{2,1,0:T(8,128)(2,1)S(1)}, bf16[1,48,256]{2,1,0:T(8,128)(2,1)S(1)}, u32[]{:S(2)}, u32[]{:S(2)}) %collective-permute-start.13) | collective-permute-done | bytes 24608 | tf_op jit(solution)/shard_map/ppermute | solution.py:217
  37.6 2.4 %collective-permute-done.14 = bf16[1,48,256]{2,1,0:T(8,128)(2,1)S(1)} collective-permute-done((bf16[1,48,256]{2,1,0:T(8,128)(2,1)S(1)}, bf16[1,48,256]{2,1,0:T(8,128)(2,1)S(1)}, u32[]{:S(2)}, u32[]{:S(2)}) %collective-permute-start.14) | collective-permute-done | bytes 24608 | tf_op jit(solution)/shard_map/ppermute | solution.py:217
  40.0 0.0 collective-permute-start.15
  40.0 1.4 %collective-permute-done.15.far = bf16[8,48,256]{2,1,0:T(8,128)(2,1)S(1)} collective-permute-done((bf16[8,48,256]{2,1,0:T(8,128)(2,1)S(1)}, bf16[8,48,256]{2,1,0:T(8,128)(2,1)S(1)}, u32[]{:S(2)}, u32[]{:S(2)}) %collective-permute-start.15) | collective-permute-done | bytes 196640 | tf_op jit(solution)/shard_map/ppermute | solution.py:217
  41.5 0.5 %shard_map.112 = (f32[48,256]{1,0:T(8,128)S(1)}, s16[48,256]{1,0:T(8,128)(2,1)S(1)}) custom-call(bf16[8,48,256]{2,1,0:T(8,128)(2,1)S(1)} %constant_dynamic-update-slice_fusion.6.near, bf16[8,48,256]{2,1,0:T(8,128)(2,1)S(1)} %collective-permute-done.15.far, bf16[16,256,256]{2,1,0:T(8,128)(2,1)S(1)} %get-tuple-element.29.tiles_t, s32[32]{0:T(128)S(4)} %get-tuple-element.27.plan), custom_call_target="tpu_custom_call" | custom-call | flops 1048576 | bytes 1048576 | tf_op jit(solution)/shard_map/pallas_call | solution.py:31
  42.0 0.3 collective-permute-start.16
  42.3 3.6 %collective-permute-done.16.rest_0_ = s16[48,256]{1,0:T(8,128)(2,1)S(1)} collective-permute-done((s16[48,256]{1,0:T(8,128)(2,1)S(1)}, s16[48,256]{1,0:T(8,128)(2,1)S(1)}, u32[]{:S(2)}, u32[]{:S(2)}) %collective-permute-start.16) | collective-permute-done | bytes 24608 | tf_op jit(solution)/shard_map/ppermute | solution.py:213
  45.9 0.7 %shard_map.113 = f32[47,256]{1,0:T(8,128)} custom-call(bf16[48,256]{1,0:T(8,128)(2,1)S(1)} %get-tuple-element.32.refs_0_.classes_in, f32[1,256]{1,0:T(1,128)S(1)} %get-tuple-element.33.scaling, f32[47,1]{1,0:T(8,128)S(1)} %get-tuple-element.34.bias, f32[48,256]{1,0:T(8,128)S(1)} %get-tuple-element.35.own, s16[48,256]{1,0:T(8,128)(2,1)S(1)} %collective-permute-done.16.rest_0_), custom_call_target="tpu_custom_call" | custom-call | flops 1048576 | bytes 1048576 | tf_op jit(solution)/shard_map/pallas_call | solution.py:31
  (18 shorter events, 0.1 us)
Async XLA Ops:
  0.0 5.4 %collective-permute-start = (bf16[100,256]{1,0:T(8,128)(2,1)}, bf16[100,256]{1,0:T(8,128)(2,1)S(1)}, u32[]{:S(2)}, u32[]{:S(2)}) collective-permute-start(bf16[100,256]{1,0:T(8,128)(2,1)} %bitcast.7), channel_id=1, source_target_pairs={{1,0},{0,1},{3,2},{2,3},{5,4},{4,5},{7,6},{6,7},{9,8},{8,9},{11,10... | collective-permute-start | bytes 153608 | tf_op jit(solution)/shard_map/ppermute | solution.py:213
  5.6 4.6 %collective-permute-start.1 = (bf16[100,256]{1,0:T(8,128)(2,1)S(1)}, bf16[100,256]{1,0:T(8,128)(2,1)S(1)}, u32[]{:S(2)}, u32[]{:S(2)}) collective-permute-start(bf16[100,256]{1,0:T(8,128)(2,1)S(1)} %shard_map.101.refs_0_), channel_id=1, source_target_pairs={{8,0},{10,2},{12,4},{14,6},{0,8},{2,10},{4,12},{6,14},{24,16},{26,... | collective-permute-start | bytes 153608 | tf_op jit(solution)/shard_map/ppermute | solution.py:217
  7.6 6.6 %collective-permute-start.3 = (bf16[100,256]{1,0:T(8,128)(2,1)S(1)}, bf16[100,256]{1,0:T(8,128)(2,1)S(1)}, u32[]{:S(2)}, u32[]{:S(2)}) collective-permute-start(bf16[100,256]{1,0:T(8,128)(2,1)S(1)} %shard_map.101.refs_0_), channel_id=1, source_target_pairs={{16,0},{26,2},{20,4},{30,6},{24,8},{18,10},{28,12},{22,14},{0,16},... | collective-permute-start | bytes 153608 | tf_op jit(solution)/shard_map/ppermute | solution.py:217
  10.2 5.9 %collective-permute-start.2 = (bf16[100,256]{1,0:T(8,128)(2,1)S(1)}, bf16[100,256]{1,0:T(8,128)(2,1)S(1)}, u32[]{:S(2)}, u32[]{:S(2)}) collective-permute-start(bf16[100,256]{1,0:T(8,128)(2,1)S(1)} %shard_map.101.refs_0_), channel_id=1, source_target_pairs={{24,0},{18,2},{28,4},{22,6},{16,8},{26,10},{20,12},{30,14},{8,16},... | collective-permute-start | bytes 153608 | tf_op jit(solution)/shard_map/ppermute | solution.py:217
  10.2 7.5 %collective-permute-start.4 = (bf16[2,100,256]{2,1,0:T(8,128)(2,1)S(1)}, bf16[2,100,256]{2,1,0:T(8,128)(2,1)S(1)}, u32[]{:S(2)}, u32[]{:S(2)}) collective-permute-start(bf16[2,100,256]{2,1,0:T(8,128)(2,1)S(1)} %shard_map.102), channel_id=1, source_target_pairs={{4,0},{6,2},{0,4},{2,6},{12,8},{14,10},{8,12},{10,14},{20,16},{22,... | collective-permute-start | bytes 307208 | tf_op jit(solution)/shard_map/ppermute | solution.py:217
  14.2 4.1 %collective-permute-start.5 = (bf16[1,100,256]{2,1,0:T(8,128)(2,1)S(1)}, bf16[1,100,256]{2,1,0:T(8,128)(2,1)S(1)}, u32[]{:S(2)}, u32[]{:S(2)}) collective-permute-start(bf16[1,100,256]{2,1,0:T(8,128)(2,1)S(1)} %shard_map.104), channel_id=1, source_target_pairs={{4,0},{6,2},{0,4},{2,6},{12,8},{14,10},{8,12},{10,14},{20,16},{22,... | collective-permute-start | bytes 153608 | tf_op jit(solution)/shard_map/ppermute | solution.py:217
  16.1 4.1 %collective-permute-start.6 = (bf16[1,100,256]{2,1,0:T(8,128)(2,1)S(1)}, bf16[1,100,256]{2,1,0:T(8,128)(2,1)S(1)}, u32[]{:S(2)}, u32[]{:S(2)}) collective-permute-start(bf16[1,100,256]{2,1,0:T(8,128)(2,1)S(1)} %shard_map.103), channel_id=1, source_target_pairs={{4,0},{6,2},{0,4},{2,6},{12,8},{14,10},{8,12},{10,14},{20,16},{22,... | collective-permute-start | bytes 153608 | tf_op jit(solution)/shard_map/ppermute | solution.py:217
  20.3 1.8 %collective-permute-start.7 = (bf16[8,100,256]{2,1,0:T(8,128)(2,1)S(1)}, bf16[8,100,256]{2,1,0:T(8,128)(2,1)S(1)}, u32[]{:S(2)}, u32[]{:S(2)}) collective-permute-start(bf16[8,100,256]{2,1,0:T(8,128)(2,1)S(1)} %constant_dynamic-update-slice_fusion.stack), channel_id=1, source_target_pairs={{2,0},{0,2},{6,4},{4,6},{10,8},{8,10},{14,12},{12,14},{18,16},{16,... | collective-permute-start | bytes 1228808 | tf_op jit(solution)/shard_map/ppermute | solution.py:217
  23.1 4.4 %collective-permute-start.8 = (s16[144,256]{1,0:T(8,128)(2,1)S(1)}, s16[144,256]{1,0:T(8,128)(2,1)S(1)}, u32[]{:S(2)}, u32[]{:S(2)}) collective-permute-start(s16[144,256]{1,0:T(8,128)(2,1)S(1)} %get-tuple-element.31), channel_id=1, source_target_pairs={{1,0},{0,1},{3,2},{2,3},{5,4},{4,5},{7,6},{6,7},{9,8},{8,9},{11,10... | collective-permute-start | bytes 221192 | tf_op jit(solution)/shard_map/ppermute | solution.py:213
  27.7 4.4 %collective-permute-start.9 = (bf16[48,256]{1,0:T(8,128)(2,1)S(1)}, bf16[48,256]{1,0:T(8,128)(2,1)S(1)}, u32[]{:S(2)}, u32[]{:S(2)}) collective-permute-start(bf16[48,256]{1,0:T(8,128)(2,1)S(1)} %get-tuple-element.32.refs_0_.classes_in), channel_id=1, source_target_pairs={{8,0},{10,2},{12,4},{14,6},{0,8},{2,10},{4,12},{6,14},{24,16},{26,... | collective-permute-start | bytes 73736 | tf_op jit(solution)/shard_map/ppermute | solution.py:217
  27.7 6.0 %collective-permute-start.11 = (bf16[48,256]{1,0:T(8,128)(2,1)S(1)}, bf16[48,256]{1,0:T(8,128)(2,1)S(1)}, u32[]{:S(2)}, u32[]{:S(2)}) collective-permute-start(bf16[48,256]{1,0:T(8,128)(2,1)S(1)} %get-tuple-element.32.refs_0_.classes_in), channel_id=1, source_target_pairs={{16,0},{26,2},{20,4},{30,6},{24,8},{18,10},{28,12},{22,14},{0,16},... | collective-permute-start | bytes 73736 | tf_op jit(solution)/shard_map/ppermute | solution.py:217
  30.6 5.6 %collective-permute-start.10 = (bf16[48,256]{1,0:T(8,128)(2,1)S(1)}, bf16[48,256]{1,0:T(8,128)(2,1)S(1)}, u32[]{:S(2)}, u32[]{:S(2)}) collective-permute-start(bf16[48,256]{1,0:T(8,128)(2,1)S(1)} %get-tuple-element.32.refs_0_.classes_in), channel_id=1, source_target_pairs={{24,0},{18,2},{28,4},{22,6},{16,8},{26,10},{20,12},{30,14},{8,16},... | collective-permute-start | bytes 73736 | tf_op jit(solution)/shard_map/ppermute | solution.py:217
  32.1 4.6 %collective-permute-start.12 = (bf16[2,48,256]{2,1,0:T(8,128)(2,1)S(1)}, bf16[2,48,256]{2,1,0:T(8,128)(2,1)S(1)}, u32[]{:S(2)}, u32[]{:S(2)}) collective-permute-start(bf16[2,48,256]{2,1,0:T(8,128)(2,1)S(1)} %shard_map.109), channel_id=1, source_target_pairs={{4,0},{6,2},{0,4},{2,6},{12,8},{14,10},{8,12},{10,14},{20,16},{22,... | collective-permute-start | bytes 147464 | tf_op jit(solution)/shard_map/ppermute | solution.py:217
  33.7 3.9 %collective-permute-start.13 = (bf16[1,48,256]{2,1,0:T(8,128)(2,1)S(1)}, bf16[1,48,256]{2,1,0:T(8,128)(2,1)S(1)}, u32[]{:S(2)}, u32[]{:S(2)}) collective-permute-start(bf16[1,48,256]{2,1,0:T(8,128)(2,1)S(1)} %shard_map.111), channel_id=1, source_target_pairs={{4,0},{6,2},{0,4},{2,6},{12,8},{14,10},{8,12},{10,14},{20,16},{22,... | collective-permute-start | bytes 73736 | tf_op jit(solution)/shard_map/ppermute | solution.py:217
  36.2 3.8 %collective-permute-start.14 = (bf16[1,48,256]{2,1,0:T(8,128)(2,1)S(1)}, bf16[1,48,256]{2,1,0:T(8,128)(2,1)S(1)}, u32[]{:S(2)}, u32[]{:S(2)}) collective-permute-start(bf16[1,48,256]{2,1,0:T(8,128)(2,1)S(1)} %shard_map.110), channel_id=1, source_target_pairs={{4,0},{6,2},{0,4},{2,6},{12,8},{14,10},{8,12},{10,14},{20,16},{22,... | collective-permute-start | bytes 73736 | tf_op jit(solution)/shard_map/ppermute | solution.py:217
  40.0 1.4 %collective-permute-start.15 = (bf16[8,48,256]{2,1,0:T(8,128)(2,1)S(1)}, bf16[8,48,256]{2,1,0:T(8,128)(2,1)S(1)}, u32[]{:S(2)}, u32[]{:S(2)}) collective-permute-start(bf16[8,48,256]{2,1,0:T(8,128)(2,1)S(1)} %constant_dynamic-update-slice_fusion.6.near), channel_id=1, source_target_pairs={{2,0},{0,2},{6,4},{4,6},{10,8},{8,10},{14,12},{12,14},{18,16},{16,... | collective-permute-start | bytes 589832 | tf_op jit(solution)/shard_map/ppermute | solution.py:217
  42.0 3.9 %collective-permute-start.16 = (s16[48,256]{1,0:T(8,128)(2,1)S(1)}, s16[48,256]{1,0:T(8,128)(2,1)S(1)}, u32[]{:S(2)}, u32[]{:S(2)}) collective-permute-start(s16[48,256]{1,0:T(8,128)(2,1)S(1)} %get-tuple-element.36), channel_id=1, source_target_pairs={{1,0},{0,1},{3,2},{2,3},{5,4},{4,5},{7,6},{6,7},{9,8},{8,9},{11,10... | collective-permute-start | bytes 73736 | tf_op jit(solution)/shard_map/ppermute | solution.py:213

commit v18 on v16

--- a/solution.py
+++ b/solution.py
@@ -214,7 +214,9 @@
 
 
 def swapped(value, masks):
-    return lax.ppermute(value, "blk", [(d ^ masks[d % 2], d) for d in range(lax.axis_size("blk"))])
+    size = lax.axis_size("blk")
+    pairs = [(d ^ masks[d % 2], d) for d in range(size) if masks[d % 2] is not None]
+    return lax.ppermute(value, "blk", pairs)
 
 
 def outer_order(outer):
@@ -232,7 +234,7 @@
     for here in (core, 1 - core):
         early, late = ([4 * jnp.where(here == 0, *sides) for sides in way] for way in two_ways(pairs))
         crossed, over = [apart + 2 for apart in late], [apart + 2 for apart in early]
-        lists.append([0, 4 * first, *crossed, *late, *early, 2, 4 * first + 2, *over])
+        lists.append([0, 4 * first, *late, *crossed, *early, 2, 4 * first + 2, *over])
     return lists[0], [apart ^ 1 for apart in lists[1]]
 
 
@@ -250,10 +252,11 @@
     first, pairs = outer_order(outer)
     ahead = swapped(value, (4 * first, 4 * first))
     early, late = ([swapped(value, (4 * a, 4 * b)) for a, b in way] for way in two_ways(pairs))
-    crossed = [swapped(value, (4 * a + 2, 4 * b + 2)) for a, b in two_ways(pairs)[1]]
-    here, early = packed(value, ahead), packed(*early)
+    crossed = [swapped(value, (4 * a + 2, None)) for a, b in two_ways(pairs)[1]]
+    here, early, late = packed(value, ahead), packed(*early), packed(*late)
     over = [swapped(here, (2, 2)), swapped(early, (2, 2))]
-    near = jnp.concatenate([here, packed(*crossed), packed(*late), early, *over])
+    beyond = swapped(late, (None, 2)) + jnp.stack(crossed)
+    near = jnp.concatenate([here, late, beyond, early, *over])
     return near, swapped(near, (1, 1))
 
 

time: 45.8 us -> 46.8 us (1.022)
  starting transfers between devices: 17.5 us -> 20.2 us
  blocking collectives: 11.2 us -> 10.3 us
  waiting for transfers between devices: 10.6 us -> 9.78 us
    ppermute x8 -> x9, starting transfers between devices: 11.6 us -> 14.2 us  [swapped(): return lax.ppermute(value, 'blk', pairs)]
    all_to_all x1, blocking collectives: 11.2 us -> 10.3 us  [gather_classes(): near = lax.all_to_all(copies, 'blk', 0, 0, axis_index_groups=groups)]
    ppermute x8 -> x9, waiting for transfers between devices: 5.27 us -> 4.58 us  [swapped(): return lax.ppermute(value, 'blk', pairs)]
    pallas_call x10 -> x11, Pallas kernels: 5.43 us -> 5.43 us  [call(): pl.pallas_call(kernel, out_shape=outs, in_specs=[pl.BlockSpec(memory_spac...]
  transfers between devices with their start and end apart: 11 -> 12, of which waited for: 7 -> 7; matrix products, arithmetic and copies ran while one was open for 0% -> 0% of each run, Pallas kernels for 6% -> 6%
where the time goes in v18:
time: 46.8 us; the launch traced here: 46.6 us
  starting transfers between devices  20.2 us (43%)
  blocking collectives  10.3 us (22%)
  waiting for transfers between devices  9.78 us (21%)
  Pallas kernels  5.43 us (12%)
  between operations  0.8 us (2%)
    ppermute x9, starting transfers between devices, swapped(): return lax.ppermute(value, 'blk', pairs)  14.2 us
    all_to_all x1, blocking collectives, gather_classes(): near = lax.all_to_all(copies, 'blk', 0, 0, axis_index_groups=groups)  10.3 us
    ppermute x3, starting transfers between devices, shifted(): lax.ppermute(value, axis, [((d + step) % size, d) for d in range(size)])  6.06 us
    pallas_call x11, Pallas kernels, call(): pl.pallas_call(kernel, out_shape=outs, in_specs=[pl.BlockSpec(memory_spac...  5.43 us
    ppermute x3, waiting for transfers between devices, shifted(): lax.ppermute(value, axis, [((d + step) % size, d) for d in range(size)])  5.2 us
    ppermute x9, waiting for transfers between devices, swapped(): return lax.ppermute(value, 'blk', pairs)  4.58 us
  transfers between devices with their start and end apart: 12, of which 7 were waited for; matrix products, arithmetic and copies ran while one was open for 0% of the time, Pallas kernels for 6%

profile of v18, /device:TPU:0, one launch (start us, length us, event | category | flops | bytes accessed | tf_op | source)
XLA Modules:
  0.0 46.6 jit_solution(15192382950055486493)
XLA Ops:
  0.0 2.9 %collective-permute-start = (bf16[100,256]{1,0:T(8,128)(2,1)}, bf16[100,256]{1,0:T(8,128)(2,1)S(1)}, u32[]{:S(2)}, u32[]{:S(2)}) collective-permute-start(bf16[100,256]{1,0:T(8,128)(2,1)} %bitcast.11), channel_id=1, source_target_pairs={{1,0},{0,1},{3,2},{2,3},{5,4},{4,5},{7,6},{6,7},{9,8},{8,9},{11,10... | collective-permute-start | bytes 153608 | tf_op jit(solution)/shard_map/ppermute | solution.py:213
  3.6 1.8 %shard_map.100 = (s32[32]{0:T(128)S(4)}, f32[100,256]{1,0:T(8,128)S(1)}, s32[1,256]{1,0:T(1,128)S(1)}, bf16[16,256,256]{2,1,0:T(8,128)(2,1)S(1)}, f32[128,1]{1,0...) custom-call(s32[1]{0:T(128)S(6)} %copy.16.live, s32[1,512]{1,0:T(1,128)} %refs_0_.1, ...), custom_call_target="tpu_custom_call" | custom-call | flops 1048576 | bytes 1048576 | tf_op jit(solution)/shard_map/pallas_call | solution.py:31
  5.4 0.0 collective-permute-done.rest_0_
  5.4 0.2 shard_map.101.refs_0_
  5.6 2.0 %collective-permute-start.1 = (bf16[100,256]{1,0:T(8,128)(2,1)S(1)}, bf16[100,256]{1,0:T(8,128)(2,1)S(1)}, u32[]{:S(2)}, u32[]{:S(2)}) collective-permute-start(bf16[100,256]{1,0:T(8,128)(2,1)S(1)} %shard_map.101.refs_0_), channel_id=1, source_target_pairs={{8,0},{10,2},{12,4},{14,6},{0,8},{2,10},{4,12},{6,14},{24,16},{26,... | collective-permute-start | bytes 153608 | tf_op jit(solution)/shard_map/ppermute | solution.py:219
  7.6 2.6 %collective-permute-start.5 = (bf16[100,256]{1,0:T(8,128)(2,1)S(1)}, bf16[100,256]{1,0:T(8,128)(2,1)S(1)}, u32[]{:S(2)}, u32[]{:S(2)}) collective-permute-start(bf16[100,256]{1,0:T(8,128)(2,1)S(1)} %shard_map.101.refs_0_), channel_id=1, source_target_pairs={{16,0},{26,2},{20,4},{30,6},{24,8},{18,10},{28,12},{22,14},{0,16},... | collective-permute-start | bytes 153608 | tf_op jit(solution)/shard_map/ppermute | solution.py:219
  10.2 3.1 %collective-permute-start.4 = (bf16[100,256]{1,0:T(8,128)(2,1)S(1)}, bf16[100,256]{1,0:T(8,128)(2,1)S(1)}, u32[]{:S(2)}, u32[]{:S(2)}) collective-permute-start(bf16[100,256]{1,0:T(8,128)(2,1)S(1)} %shard_map.101.refs_0_), channel_id=1, source_target_pairs={{28,0},{24,4},{20,8},{16,12},{12,16},{8,20},{4,24},{0,28},{29,1},{... | collective-permute-start | bytes 153608 | tf_op jit(solution)/shard_map/ppermute | solution.py:219
  13.3 3.7 %collective-permute-start.2 = (bf16[100,256]{1,0:T(8,128)(2,1)S(1)}, bf16[100,256]{1,0:T(8,128)(2,1)S(1)}, u32[]{:S(2)}, u32[]{:S(2)}) collective-permute-start(bf16[100,256]{1,0:T(8,128)(2,1)S(1)} %shard_map.101.refs_0_), channel_id=1, source_target_pairs={{24,0},{18,2},{28,4},{22,6},{16,8},{26,10},{20,12},{30,14},{8,16},... | collective-permute-start | bytes 153608 | tf_op jit(solution)/shard_map/ppermute | solution.py:219
  16.9 0.0 collective-permute-done.1.refs_1_
  17.0 0.6 %collective-permute-start.6 = (bf16[2,100,256]{2,1,0:T(8,128)(2,1)S(1)}, bf16[2,100,256]{2,1,0:T(8,128)(2,1)S(1)}, u32[]{:S(2)}, u32[]{:S(2)}) collective-permute-start(bf16[2,100,256]{2,1,0:T(8,128)(2,1)S(1)} %shard_map.102), channel_id=1, source_target_pairs={{4,0},{6,2},{0,4},{2,6},{12,8},{14,10},{8,12},{10,14},{20,16},{22,... | collective-permute-start | bytes 307208 | tf_op jit(solution)/shard_map/ppermute | solution.py:219
  17.5 0.0 collective-permute-done.5.refs_0_
  17.6 1.6 %collective-permute-start.7 = (bf16[1,100,256]{2,1,0:T(8,128)(2,1)S(1)}, bf16[1,100,256]{2,1,0:T(8,128)(2,1)S(1)}, u32[]{:S(2)}, u32[]{:S(2)}) collective-permute-start(bf16[1,100,256]{2,1,0:T(8,128)(2,1)S(1)} %shard_map.104), channel_id=1, source_target_pairs={{4,0},{6,2},{0,4},{2,6},{12,8},{14,10},{8,12},{10,14},{20,16},{22,... | collective-permute-start | bytes 153608 | tf_op jit(solution)/shard_map/ppermute | solution.py:219
  19.2 0.4 collective-permute-done.2.refs_0_
  19.5 0.7 %collective-permute-start.3 = (bf16[1,100,256]{2,1,0:T(8,128)(2,1)S(1)}, bf16[1,100,256]{2,1,0:T(8,128)(2,1)S(1)}, u32[]{:S(2)}, u32[]{:S(2)}) collective-permute-start(bf16[1,100,256]{2,1,0:T(8,128)(2,1)S(1)} %shard_map.103), channel_id=1, source_target_pairs={{6,2},{2,6},{14,10},{10,14},{22,18},{18,22},{30,26},{26,30},{7,3},... | collective-permute-start | bytes 153608 | tf_op jit(solution)/shard_map/ppermute | solution.py:219
  20.2 0.0 collective-permute-done.4
  20.2 0.0 collective-permute-done.3
  20.3 1.5 %collective-permute-done.6 = bf16[2,100,256]{2,1,0:T(8,128)(2,1)S(1)} collective-permute-done((bf16[2,100,256]{2,1,0:T(8,128)(2,1)S(1)}, bf16[2,100,256]{2,1,0:T(8,128)(2,1)S(1)}, u32[]{:S(2)}, u32[]{:S(2)}) %collective-permute-start.6) | collective-permute-done | bytes 102432 | tf_op jit(solution)/shard_map/ppermute | solution.py:219
  21.7 0.6 %collective-permute-done.7 = bf16[1,100,256]{2,1,0:T(8,128)(2,1)S(1)} collective-permute-done((bf16[1,100,256]{2,1,0:T(8,128)(2,1)S(1)}, bf16[1,100,256]{2,1,0:T(8,128)(2,1)S(1)}, u32[]{:S(2)}, u32[]{:S(2)}) %collective-permute-start.7) | collective-permute-done | bytes 51232 | tf_op jit(solution)/shard_map/ppermute | solution.py:219
  22.3 0.0 collective-permute-start.8
  22.3 0.7 %shard_map.106 = (bf16[16,256,256]{2,1,0:T(8,128)(2,1)S(1)}, f32[2,8,256]{2,1,0:T(8,128)S(1)}) custom-call(bf16[16,256,256]{2,1,0:T(8,128)(2,1)S(1)} %get-tuple-element.26.tiles, s32[32]{0:T(128)S(4)} %get-tuple-element.27.plan), custom_call_target="tpu_custom_call" | custom-call | flops 1048576 | bytes 1048576 | tf_op jit(solution)/shard_map/pallas_call | solution.py:31
  23.0 0.3 shard_map.105.projected.hidden_in
  23.3 0.7 %collective-permute-done.8.far = bf16[8,100,256]{2,1,0:T(8,128)(2,1)S(1)} collective-permute-done((bf16[8,100,256]{2,1,0:T(8,128)(2,1)S(1)}, bf16[8,100,256]{2,1,0:T(8,128)(2,1)S(1)}, u32[]{:S(2)}, u32[]{:S(2)}) %collective-permute-start.8) | collective-permute-done | bytes 409632 | tf_op jit(solution)/shard_map/ppermute | solution.py:219
  24.1 1.0 %shard_map.107 = (f32[128,256]{1,0:T(8,128)S(1)}, s16[144,256]{1,0:T(8,128)(2,1)S(1)}) custom-call(bf16[8,128,256]{2,1,0:T(8,128)(2,1)S(1)} %shard_map.105.projected.hidden_in, bf16[8,100,256]{2,1,0:T(8,128)(2,1)S(1)} %collective-permute-done.8.far, bf16[128,100]{1,0:T(8,128)(2,1)S(1)} %get-tuple-element.21.weight_t, ...), custom_call_target="tpu_custom_call" | custom-call | flops 1048576 | bytes 1048576 | tf_op jit(solution)/shard_map/pallas_call | solution.py:31
  25.1 1.6 %collective-permute-start.9 = (s16[144,256]{1,0:T(8,128)(2,1)S(1)}, s16[144,256]{1,0:T(8,128)(2,1)S(1)}, u32[]{:S(2)}, u32[]{:S(2)}) collective-permute-start(s16[144,256]{1,0:T(8,128)(2,1)S(1)} %get-tuple-element.31), channel_id=1, source_target_pairs={{1,0},{0,1},{3,2},{2,3},{5,4},{4,5},{7,6},{6,7},{9,8},{8,9},{11,10... | collective-permute-start | bytes 221192 | tf_op jit(solution)/shard_map/ppermute | solution.py:213
  26.7 2.9 %collective-permute-done.9.rest_0_ = s16[144,256]{1,0:T(8,128)(2,1)S(1)} collective-permute-done((s16[144,256]{1,0:T(8,128)(2,1)S(1)}, s16[144,256]{1,0:T(8,128)(2,1)S(1)}, u32[]{:S(2)}, u32[]{:S(2)}) %collective-permute-start.9) | collective-permute-done | bytes 73760 | tf_op jit(solution)/shard_map/ppermute | solution.py:213
  29.5 0.2 shard_map.108
  29.8 10.3 %all_to_all.5.near = bf16[8,48,256]{2,1,0:T(8,128)(2,1)S(1)} all-to-all(bf16[8,48,256]{2,1,0:T(8,128)(2,1)S(1)} %broadcast_in_dim.14), channel_id=1, replica_groups={{0,4,8,12,16,20,24,28},{2,6,10,14,18,22,26,30},{1,5,9,13,17,21,25,29},{..., dimensions={0} | all-to-all | bytes 393216 | tf_op jit(solution)/shard_map/all_to_all | solution.py:267
  40.0 0.0 collective-permute-start.10
  40.0 1.4 %collective-permute-done.10.far = bf16[8,48,256]{2,1,0:T(8,128)(2,1)S(1)} collective-permute-done((bf16[8,48,256]{2,1,0:T(8,128)(2,1)S(1)}, bf16[8,48,256]{2,1,0:T(8,128)(2,1)S(1)}, u32[]{:S(2)}, u32[]{:S(2)}) %collective-permute-start.10) | collective-permute-done | bytes 196640 | tf_op jit(solution)/shard_map/ppermute | solution.py:219
  41.5 0.5 %shard_map.109 = (f32[48,256]{1,0:T(8,128)S(1)}, s16[48,256]{1,0:T(8,128)(2,1)S(1)}) custom-call(bf16[8,48,256]{2,1,0:T(8,128)(2,1)S(1)} %all_to_all.5.near, bf16[8,48,256]{2,1,0:T(8,128)(2,1)S(1)} %collective-permute-done.10.far, bf16[16,256,256]{2,1,0:T(8,128)(2,1)S(1)} %get-tuple-element.29.tiles_t, s32[32]{0:T(128)S(4)} %get-tuple-element.27.plan), custom_call_target="tpu_custom_call" | custom-call | flops 1048576 | bytes 1048576 | tf_op jit(solution)/shard_map/pallas_call | solution.py:31
  42.0 1.6 %collective-permute-start.11 = (s16[48,256]{1,0:T(8,128)(2,1)S(1)}, s16[48,256]{1,0:T(8,128)(2,1)S(1)}, u32[]{:S(2)}, u32[]{:S(2)}) collective-permute-start(s16[48,256]{1,0:T(8,128)(2,1)S(1)} %get-tuple-element.36), channel_id=1, source_target_pairs={{1,0},{0,1},{3,2},{2,3},{5,4},{4,5},{7,6},{6,7},{9,8},{8,9},{11,10... | collective-permute-start | bytes 73736 | tf_op jit(solution)/shard_map/ppermute | solution.py:213
  43.6 2.3 %collective-permute-done.11.rest_0_ = s16[48,256]{1,0:T(8,128)(2,1)S(1)} collective-permute-done((s16[48,256]{1,0:T(8,128)(2,1)S(1)}, s16[48,256]{1,0:T(8,128)(2,1)S(1)}, u32[]{:S(2)}, u32[]{:S(2)}) %collective-permute-start.11) | collective-permute-done | bytes 24608 | tf_op jit(solution)/shard_map/ppermute | solution.py:213
  45.9 0.7 %shard_map.110 = f32[47,256]{1,0:T(8,128)} custom-call(bf16[48,256]{1,0:T(8,128)(2,1)S(1)} %get-tuple-element.32.classes_in, f32[1,256]{1,0:T(1,128)S(1)} %get-tuple-element.33.scaling, f32[47,1]{1,0:T(8,128)S(1)} %get-tuple-element.34.bias, f32[48,256]{1,0:T(8,128)S(1)} %get-tuple-element.35.own, s16[48,256]{1,0:T(8,128)(2,1)S(1)} %collective-permute-done.11.rest_0_), custom_call_target="tpu_custom_call" | custom-call | flops 1048576 | bytes 1048576 | tf_op jit(solution)/shard_map/pallas_call | solution.py:31
  (10 shorter events, 0.1 us)
Async XLA Ops:
  0.0 5.4 %collective-permute-start = (bf16[100,256]{1,0:T(8,128)(2,1)}, bf16[100,256]{1,0:T(8,128)(2,1)S(1)}, u32[]{:S(2)}, u32[]{:S(2)}) collective-permute-start(bf16[100,256]{1,0:T(8,128)(2,1)} %bitcast.11), channel_id=1, source_target_pairs={{1,0},{0,1},{3,2},{2,3},{5,4},{4,5},{7,6},{6,7},{9,8},{8,9},{11,10... | collective-permute-start | bytes 153608 | tf_op jit(solution)/shard_map/ppermute | solution.py:213
  5.6 11.4 %collective-permute-start.1 = (bf16[100,256]{1,0:T(8,128)(2,1)S(1)}, bf16[100,256]{1,0:T(8,128)(2,1)S(1)}, u32[]{:S(2)}, u32[]{:S(2)}) collective-permute-start(bf16[100,256]{1,0:T(8,128)(2,1)S(1)} %shard_map.101.refs_0_), channel_id=1, source_target_pairs={{8,0},{10,2},{12,4},{14,6},{0,8},{2,10},{4,12},{6,14},{24,16},{26,... | collective-permute-start | bytes 153608 | tf_op jit(solution)/shard_map/ppermute | solution.py:219
  7.6 9.9 %collective-permute-start.5 = (bf16[100,256]{1,0:T(8,128)(2,1)S(1)}, bf16[100,256]{1,0:T(8,128)(2,1)S(1)}, u32[]{:S(2)}, u32[]{:S(2)}) collective-permute-start(bf16[100,256]{1,0:T(8,128)(2,1)S(1)} %shard_map.101.refs_0_), channel_id=1, source_target_pairs={{16,0},{26,2},{20,4},{30,6},{24,8},{18,10},{28,12},{22,14},{0,16},... | collective-permute-start | bytes 153608 | tf_op jit(solution)/shard_map/ppermute | solution.py:219
  10.2 10.0 %collective-permute-start.4 = (bf16[100,256]{1,0:T(8,128)(2,1)S(1)}, bf16[100,256]{1,0:T(8,128)(2,1)S(1)}, u32[]{:S(2)}, u32[]{:S(2)}) collective-permute-start(bf16[100,256]{1,0:T(8,128)(2,1)S(1)} %shard_map.101.refs_0_), channel_id=1, source_target_pairs={{28,0},{24,4},{20,8},{16,12},{12,16},{8,20},{4,24},{0,28},{29,1},{... | collective-permute-start | bytes 153608 | tf_op jit(solution)/shard_map/ppermute | solution.py:219
  13.3 6.3 %collective-permute-start.2 = (bf16[100,256]{1,0:T(8,128)(2,1)S(1)}, bf16[100,256]{1,0:T(8,128)(2,1)S(1)}, u32[]{:S(2)}, u32[]{:S(2)}) collective-permute-start(bf16[100,256]{1,0:T(8,128)(2,1)S(1)} %shard_map.101.refs_0_), channel_id=1, source_target_pairs={{24,0},{18,2},{28,4},{22,6},{16,8},{26,10},{20,12},{30,14},{8,16},... | collective-permute-start | bytes 153608 | tf_op jit(solution)/shard_map/ppermute | solution.py:219
  17.0 4.8 %collective-permute-start.6 = (bf16[2,100,256]{2,1,0:T(8,128)(2,1)S(1)}, bf16[2,100,256]{2,1,0:T(8,128)(2,1)S(1)}, u32[]{:S(2)}, u32[]{:S(2)}) collective-permute-start(bf16[2,100,256]{2,1,0:T(8,128)(2,1)S(1)} %shard_map.102), channel_id=1, source_target_pairs={{4,0},{6,2},{0,4},{2,6},{12,8},{14,10},{8,12},{10,14},{20,16},{22,... | collective-permute-start | bytes 307208 | tf_op jit(solution)/shard_map/ppermute | solution.py:219
  17.6 4.7 %collective-permute-start.7 = (bf16[1,100,256]{2,1,0:T(8,128)(2,1)S(1)}, bf16[1,100,256]{2,1,0:T(8,128)(2,1)S(1)}, u32[]{:S(2)}, u32[]{:S(2)}) collective-permute-start(bf16[1,100,256]{2,1,0:T(8,128)(2,1)S(1)} %shard_map.104), channel_id=1, source_target_pairs={{4,0},{6,2},{0,4},{2,6},{12,8},{14,10},{8,12},{10,14},{20,16},{22,... | collective-permute-start | bytes 153608 | tf_op jit(solution)/shard_map/ppermute | solution.py:219
  19.5 0.7 %collective-permute-start.3 = (bf16[1,100,256]{2,1,0:T(8,128)(2,1)S(1)}, bf16[1,100,256]{2,1,0:T(8,128)(2,1)S(1)}, u32[]{:S(2)}, u32[]{:S(2)}) collective-permute-start(bf16[1,100,256]{2,1,0:T(8,128)(2,1)S(1)} %shard_map.103), channel_id=1, source_target_pairs={{6,2},{2,6},{14,10},{10,14},{22,18},{18,22},{30,26},{26,30},{7,3},... | collective-permute-start | bytes 153608 | tf_op jit(solution)/shard_map/ppermute | solution.py:219
  22.3 1.8 %collective-permute-start.8 = (bf16[8,100,256]{2,1,0:T(8,128)(2,1)S(1)}, bf16[8,100,256]{2,1,0:T(8,128)(2,1)S(1)}, u32[]{:S(2)}, u32[]{:S(2)}) collective-permute-start(bf16[8,100,256]{2,1,0:T(8,128)(2,1)S(1)} %constant_dynamic-update-slice_fusion.stack), channel_id=1, source_target_pairs={{2,0},{0,2},{6,4},{4,6},{10,8},{8,10},{14,12},{12,14},{18,16},{16,... | collective-permute-start | bytes 1228808 | tf_op jit(solution)/shard_map/ppermute | solution.py:219
  25.1 4.4 %collective-permute-start.9 = (s16[144,256]{1,0:T(8,128)(2,1)S(1)}, s16[144,256]{1,0:T(8,128)(2,1)S(1)}, u32[]{:S(2)}, u32[]{:S(2)}) collective-permute-start(s16[144,256]{1,0:T(8,128)(2,1)S(1)} %get-tuple-element.31), channel_id=1, source_target_pairs={{1,0},{0,1},{3,2},{2,3},{5,4},{4,5},{7,6},{6,7},{9,8},{8,9},{11,10... | collective-permute-start | bytes 221192 | tf_op jit(solution)/shard_map/ppermute | solution.py:213
  40.0 1.4 %collective-permute-start.10 = (bf16[8,48,256]{2,1,0:T(8,128)(2,1)S(1)}, bf16[8,48,256]{2,1,0:T(8,128)(2,1)S(1)}, u32[]{:S(2)}, u32[]{:S(2)}) collective-permute-start(bf16[8,48,256]{2,1,0:T(8,128)(2,1)S(1)} %all_to_all.5.near), channel_id=1, source_target_pairs={{2,0},{0,2},{6,4},{4,6},{10,8},{8,10},{14,12},{12,14},{18,16},{16,... | collective-permute-start | bytes 589832 | tf_op jit(solution)/shard_map/ppermute | solution.py:219
  42.0 3.9 %collective-permute-start.11 = (s16[48,256]{1,0:T(8,128)(2,1)S(1)}, s16[48,256]{1,0:T(8,128)(2,1)S(1)}, u32[]{:S(2)}, u32[]{:S(2)}) collective-permute-start(s16[48,256]{1,0:T(8,128)(2,1)S(1)} %get-tuple-element.36), channel_id=1, source_target_pairs={{1,0},{0,1},{3,2},{2,3},{5,4},{4,5},{7,6},{6,7},{9,8},{8,9},{11,10... | collective-permute-start | bytes 73736 | tf_op jit(solution)/shard_map/ppermute | solution.py:213

commit v19 on v16

--- a/solution.py
+++ b/solution.py
@@ -217,22 +217,17 @@
     return lax.ppermute(value, "blk", [(d ^ masks[d % 2], d) for d in range(lax.axis_size("blk"))])
 
 
-def outer_order(outer):
-    rest = list(range(2, outer))
-    return 1, list(zip(rest[0::2], rest[1::2]))
-
-
-def two_ways(pairs):
-    return pairs, [(pair[1], pair[0]) for pair in pairs]
+def outer_steps(outer):
+    steps = list(range(1, outer))
+    return list(zip(steps[1:] + steps[:1], steps))
 
 
 def panel_order(outer, core):
-    first, pairs = outer_order(outer)
     lists = []
     for here in (core, 1 - core):
-        early, late = ([4 * jnp.where(here == 0, *sides) for sides in way] for way in two_ways(pairs))
-        crossed, over = [apart + 2 for apart in late], [apart + 2 for apart in early]
-        lists.append([0, 4 * first, *crossed, *late, *early, 2, 4 * first + 2, *over])
+        first, *rest, last = [4 * jnp.where(here == 0, *sides) for sides in outer_steps(outer)]
+        over = [apart + 2 for apart in [0, first, *rest, last]]
+        lists.append([0, first, last, *rest, *over])
     return lists[0], [apart ^ 1 for apart in lists[1]]
 
 
@@ -247,13 +242,10 @@
 
 def gather_features(value):
     outer = lax.axis_size("blk") // 4
-    first, pairs = outer_order(outer)
-    ahead = swapped(value, (4 * first, 4 * first))
-    early, late = ([swapped(value, (4 * a, 4 * b)) for a, b in way] for way in two_ways(pairs))
-    crossed = [swapped(value, (4 * a + 2, 4 * b + 2)) for a, b in two_ways(pairs)[1]]
-    here, early = packed(value, ahead), packed(*early)
-    over = [swapped(here, (2, 2)), swapped(early, (2, 2))]
-    near = jnp.concatenate([here, packed(*crossed), packed(*late), early, *over])
+    first, *rest, last = [swapped(value, (4 * a, 4 * b)) for a, b in outer_steps(outer)]
+    stacks = packed(value, first), packed(*rest), packed(last)
+    over = [swapped(stack, (2, 2)) for stack in stacks]
+    near = jnp.concatenate([stacks[0], stacks[2], stacks[1], *over])
     return near, swapped(near, (1, 1))
 
 

time: 45.8 us -> 46.9 us (1.024)
  starting transfers between devices: 17.5 us -> 13.5 us
  waiting for transfers between devices: 10.6 us -> 14.6 us
  blocking collectives: 11.2 us -> 12.4 us
    ppermute x8, waiting for transfers between devices: 5.27 us -> 8.35 us  [swapped(): lax.ppermute(value, 'blk', [(d ^ masks[d % 2], d) for d in range(lax.axis...]
    ppermute x8, starting transfers between devices: 11.6 us -> 8.54 us  [swapped(): lax.ppermute(value, 'blk', [(d ^ masks[d % 2], d) for d in range(lax.axis...]
    all_to_all x1, blocking collectives: 11.2 us -> 12.4 us  [gather_classes(): near = lax.all_to_all(copies, 'blk', 0, 0, axis_index_groups=groups)]
    ppermute x3, waiting for transfers between devices: 5.34 us -> 6.25 us  [shifted(): lax.ppermute(value, axis, [((d + step) % size, d) for d in range(size)])]
    ppermute x3, starting transfers between devices: 5.91 us -> 5 us  [shifted(): lax.ppermute(value, axis, [((d + step) % size, d) for d in range(size)])]
    pallas_call x10 -> x11, Pallas kernels: 5.43 us -> 5.44 us  [call(): pl.pallas_call(kernel, out_shape=outs, in_specs=[pl.BlockSpec(memory_spac...]
  transfers between devices with their start and end apart: 11 -> 11, of which waited for: 7 -> 9; matrix products, arithmetic and copies ran while one was open for 0% -> 0% of each run, Pallas kernels for 6% -> 6%
where the time goes in v19:
time: 46.9 us; the launch traced here: 46.7 us
  waiting for transfers between devices  14.6 us (31%)
  starting transfers between devices  13.5 us (29%)
  blocking collectives  12.4 us (26%)
  Pallas kernels  5.44 us (12%)
  between operations  0.74 us (2%)
    all_to_all x1, blocking collectives, gather_classes(): near = lax.all_to_all(copies, 'blk', 0, 0, axis_index_groups=groups)  12.4 us
    ppermute x8, starting transfers between devices, swapped(): lax.ppermute(value, 'blk', [(d ^ masks[d % 2], d) for d in range(lax.axis...  8.54 us
    ppermute x8, waiting for transfers between devices, swapped(): lax.ppermute(value, 'blk', [(d ^ masks[d % 2], d) for d in range(lax.axis...  8.35 us
    ppermute x3, waiting for transfers between devices, shifted(): lax.ppermute(value, axis, [((d + step) % size, d) for d in range(size)])  6.25 us
    pallas_call x11, Pallas kernels, call(): pl.pallas_call(kernel, out_shape=outs, in_specs=[pl.BlockSpec(memory_spac...  5.44 us
    ppermute x3, starting transfers between devices, shifted(): lax.ppermute(value, axis, [((d + step) % size, d) for d in range(size)])  5 us
  transfers between devices with their start and end apart: 11, of which 9 were waited for; matrix products, arithmetic and copies ran while one was open for 0% of the time, Pallas kernels for 6%

profile of v19, /device:TPU:0, one launch (start us, length us, event | category | flops | bytes accessed | tf_op | source)
XLA Modules:
  0.0 46.7 jit_solution(2278881197706859072)
XLA Ops:
  0.0 2.9 %collective-permute-start = (bf16[100,256]{1,0:T(8,128)(2,1)}, bf16[100,256]{1,0:T(8,128)(2,1)S(1)}, u32[]{:S(2)}, u32[]{:S(2)}) collective-permute-start(bf16[100,256]{1,0:T(8,128)(2,1)} %bitcast.7), channel_id=1, source_target_pairs={{1,0},{0,1},{3,2},{2,3},{5,4},{4,5},{7,6},{6,7},{9,8},{8,9},{11,10... | collective-permute-start | bytes 153608 | tf_op jit(solution)/shard_map/ppermute | solution.py:213
  3.6 1.8 %shard_map.100 = (s32[32]{0:T(128)S(4)}, f32[100,256]{1,0:T(8,128)S(1)}, s32[1,256]{1,0:T(1,128)S(1)}, bf16[16,256,256]{2,1,0:T(8,128)(2,1)S(1)}, f32[128,1]{1,0...) custom-call(s32[1]{0:T(128)S(6)} %copy.16.live, s32[1,512]{1,0:T(1,128)} %refs_0_.1, ...), custom_call_target="tpu_custom_call" | custom-call | flops 1048576 | bytes 1048576 | tf_op jit(solution)/shard_map/pallas_call | solution.py:31
  5.4 0.0 collective-permute-done.rest_0_
  5.4 0.2 shard_map.101.refs_0_
  5.6 3.0 %collective-permute-start.1 = (bf16[100,256]{1,0:T(8,128)(2,1)S(1)}, bf16[100,256]{1,0:T(8,128)(2,1)S(1)}, u32[]{:S(2)}, u32[]{:S(2)}) collective-permute-start(bf16[100,256]{1,0:T(8,128)(2,1)S(1)} %shard_map.101.refs_0_), channel_id=1, source_target_pairs={{16,0},{10,2},{20,4},{14,6},{24,8},{2,10},{28,12},{6,14},{0,16},{2... | collective-permute-start | bytes 153608 | tf_op jit(solution)/shard_map/ppermute | solution.py:217
  8.6 1.3 %collective-permute-start.3 = (bf16[100,256]{1,0:T(8,128)(2,1)S(1)}, bf16[100,256]{1,0:T(8,128)(2,1)S(1)}, u32[]{:S(2)}, u32[]{:S(2)}) collective-permute-start(bf16[100,256]{1,0:T(8,128)(2,1)S(1)} %shard_map.101.refs_0_), channel_id=1, source_target_pairs={{24,0},{18,2},{28,4},{22,6},{16,8},{26,10},{20,12},{30,14},{8,16},... | collective-permute-start | bytes 153608 | tf_op jit(solution)/shard_map/ppermute | solution.py:217
  10.0 0.2 collective-permute-start.2
  10.2 2.2 %collective-permute-done.1.refs_1_ = bf16[100,256]{1,0:T(8,128)(2,1)S(1)} collective-permute-done((bf16[100,256]{1,0:T(8,128)(2,1)S(1)}, bf16[100,256]{1,0:T(8,128)(2,1)S(1)}, u32[]{:S(2)}, u32[]{:S(2)}) %collective-permute-start.1) | collective-permute-done | bytes 51232 | tf_op jit(solution)/shard_map/ppermute | solution.py:217
  12.5 1.8 %collective-permute-start.4 = (bf16[2,100,256]{2,1,0:T(8,128)(2,1)S(1)}, bf16[2,100,256]{2,1,0:T(8,128)(2,1)S(1)}, u32[]{:S(2)}, u32[]{:S(2)}) collective-permute-start(bf16[2,100,256]{2,1,0:T(8,128)(2,1)S(1)} %shard_map.102), channel_id=1, source_target_pairs={{4,0},{6,2},{0,4},{2,6},{12,8},{14,10},{8,12},{10,14},{20,16},{22,... | collective-permute-start | bytes 307208 | tf_op jit(solution)/shard_map/ppermute | solution.py:217
  14.3 0.3 collective-permute-done.3.refs_0_
  14.6 1.5 %collective-permute-start.5 = (bf16[1,100,256]{2,1,0:T(8,128)(2,1)S(1)}, bf16[1,100,256]{2,1,0:T(8,128)(2,1)S(1)}, u32[]{:S(2)}, u32[]{:S(2)}) collective-permute-start(bf16[1,100,256]{2,1,0:T(8,128)(2,1)S(1)} %shard_map.104), channel_id=1, source_target_pairs={{4,0},{6,2},{0,4},{2,6},{12,8},{14,10},{8,12},{10,14},{20,16},{22,... | collective-permute-start | bytes 153608 | tf_op jit(solution)/shard_map/ppermute | solution.py:217
  16.1 0.0 collective-permute-done.2.refs_0_
  16.2 0.6 %collective-permute-start.6 = (bf16[1,100,256]{2,1,0:T(8,128)(2,1)S(1)}, bf16[1,100,256]{2,1,0:T(8,128)(2,1)S(1)}, u32[]{:S(2)}, u32[]{:S(2)}) collective-permute-start(bf16[1,100,256]{2,1,0:T(8,128)(2,1)S(1)} %shard_map.103), channel_id=1, source_target_pairs={{4,0},{6,2},{0,4},{2,6},{12,8},{14,10},{8,12},{10,14},{20,16},{22,... | collective-permute-start | bytes 153608 | tf_op jit(solution)/shard_map/ppermute | solution.py:217
  16.7 1.1 %collective-permute-done.4 = bf16[2,100,256]{2,1,0:T(8,128)(2,1)S(1)} collective-permute-done((bf16[2,100,256]{2,1,0:T(8,128)(2,1)S(1)}, bf16[2,100,256]{2,1,0:T(8,128)(2,1)S(1)}, u32[]{:S(2)}, u32[]{:S(2)}) %collective-permute-start.4) | collective-permute-done | bytes 102432 | tf_op jit(solution)/shard_map/ppermute | solution.py:217
  17.8 0.9 %collective-permute-done.5 = bf16[1,100,256]{2,1,0:T(8,128)(2,1)S(1)} collective-permute-done((bf16[1,100,256]{2,1,0:T(8,128)(2,1)S(1)}, bf16[1,100,256]{2,1,0:T(8,128)(2,1)S(1)}, u32[]{:S(2)}, u32[]{:S(2)}) %collective-permute-start.5) | collective-permute-done | bytes 51232 | tf_op jit(solution)/shard_map/ppermute | solution.py:217
  18.8 1.6 %collective-permute-done.6 = bf16[1,100,256]{2,1,0:T(8,128)(2,1)S(1)} collective-permute-done((bf16[1,100,256]{2,1,0:T(8,128)(2,1)S(1)}, bf16[1,100,256]{2,1,0:T(8,128)(2,1)S(1)}, u32[]{:S(2)}, u32[]{:S(2)}) %collective-permute-start.6) | collective-permute-done | bytes 51232 | tf_op jit(solution)/shard_map/ppermute | solution.py:217
  20.4 0.0 collective-permute-start.7
  20.4 0.7 %shard_map.106 = (bf16[16,256,256]{2,1,0:T(8,128)(2,1)S(1)}, f32[2,8,256]{2,1,0:T(8,128)S(1)}) custom-call(bf16[16,256,256]{2,1,0:T(8,128)(2,1)S(1)} %get-tuple-element.26.tiles, s32[32]{0:T(128)S(4)} %get-tuple-element.27.plan), custom_call_target="tpu_custom_call" | custom-call | flops 1048576 | bytes 1048576 | tf_op jit(solution)/shard_map/pallas_call | solution.py:31
  21.1 0.3 shard_map.105.projected.hidden_in
  21.4 0.7 %collective-permute-done.7.far = bf16[8,100,256]{2,1,0:T(8,128)(2,1)S(1)} collective-permute-done((bf16[8,100,256]{2,1,0:T(8,128)(2,1)S(1)}, bf16[8,100,256]{2,1,0:T(8,128)(2,1)S(1)}, u32[]{:S(2)}, u32[]{:S(2)}) %collective-permute-start.7) | collective-permute-done | bytes 409632 | tf_op jit(solution)/shard_map/ppermute | solution.py:217
  22.1 1.0 %shard_map.107 = (f32[128,256]{1,0:T(8,128)S(1)}, s16[144,256]{1,0:T(8,128)(2,1)S(1)}) custom-call(bf16[8,128,256]{2,1,0:T(8,128)(2,1)S(1)} %shard_map.105.projected.hidden_in, bf16[8,100,256]{2,1,0:T(8,128)(2,1)S(1)} %collective-permute-done.7.far, bf16[128,100]{1,0:T(8,128)(2,1)S(1)} %get-tuple-element.21.weight_t, ...), custom_call_target="tpu_custom_call" | custom-call | flops 1048576 | bytes 1048576 | tf_op jit(solution)/shard_map/pallas_call | solution.py:31
  23.2 1.6 %collective-permute-start.8 = (s16[144,256]{1,0:T(8,128)(2,1)S(1)}, s16[144,256]{1,0:T(8,128)(2,1)S(1)}, u32[]{:S(2)}, u32[]{:S(2)}) collective-permute-start(s16[144,256]{1,0:T(8,128)(2,1)S(1)} %get-tuple-element.31), channel_id=1, source_target_pairs={{1,0},{0,1},{3,2},{2,3},{5,4},{4,5},{7,6},{6,7},{9,8},{8,9},{11,10... | collective-permute-start | bytes 221192 | tf_op jit(solution)/shard_map/ppermute | solution.py:213
  24.7 2.8 %collective-permute-done.8.rest_0_ = s16[144,256]{1,0:T(8,128)(2,1)S(1)} collective-permute-done((s16[144,256]{1,0:T(8,128)(2,1)S(1)}, s16[144,256]{1,0:T(8,128)(2,1)S(1)}, u32[]{:S(2)}, u32[]{:S(2)}) %collective-permute-start.8) | collective-permute-done | bytes 73760 | tf_op jit(solution)/shard_map/ppermute | solution.py:213
  27.6 0.2 shard_map.108
  27.8 12.4 %all_to_all.5.near = bf16[8,48,256]{2,1,0:T(8,128)(2,1)S(1)} all-to-all(bf16[8,48,256]{2,1,0:T(8,128)(2,1)S(1)} %broadcast_in_dim.14), channel_id=1, replica_groups={{0,4,8,12,16,20,24,28},{2,6,10,14,18,22,26,30},{1,5,9,13,17,21,25,29},{..., dimensions={0} | all-to-all | bytes 393216 | tf_op jit(solution)/shard_map/all_to_all | solution.py:256
  40.2 0.0 collective-permute-start.9
  40.2 1.4 %collective-permute-done.9.far = bf16[8,48,256]{2,1,0:T(8,128)(2,1)S(1)} collective-permute-done((bf16[8,48,256]{2,1,0:T(8,128)(2,1)S(1)}, bf16[8,48,256]{2,1,0:T(8,128)(2,1)S(1)}, u32[]{:S(2)}, u32[]{:S(2)}) %collective-permute-start.9) | collective-permute-done | bytes 196640 | tf_op jit(solution)/shard_map/ppermute | solution.py:217
  41.6 0.5 %shard_map.109 = (f32[48,256]{1,0:T(8,128)S(1)}, s16[48,256]{1,0:T(8,128)(2,1)S(1)}) custom-call(bf16[8,48,256]{2,1,0:T(8,128)(2,1)S(1)} %all_to_all.5.near, bf16[8,48,256]{2,1,0:T(8,128)(2,1)S(1)} %collective-permute-done.9.far, bf16[16,256,256]{2,1,0:T(8,128)(2,1)S(1)} %get-tuple-element.29.tiles_t, s32[32]{0:T(128)S(4)} %get-tuple-element.27.plan), custom_call_target="tpu_custom_call" | custom-call | flops 1048576 | bytes 1048576 | tf_op jit(solution)/shard_map/pallas_call | solution.py:31
  42.1 0.5 %collective-permute-start.10 = (s16[48,256]{1,0:T(8,128)(2,1)S(1)}, s16[48,256]{1,0:T(8,128)(2,1)S(1)}, u32[]{:S(2)}, u32[]{:S(2)}) collective-permute-start(s16[48,256]{1,0:T(8,128)(2,1)S(1)} %get-tuple-element.36), channel_id=1, source_target_pairs={{1,0},{0,1},{3,2},{2,3},{5,4},{4,5},{7,6},{6,7},{9,8},{8,9},{11,10... | collective-permute-start | bytes 73736 | tf_op jit(solution)/shard_map/ppermute | solution.py:213
  42.6 3.4 %collective-permute-done.10.rest_0_ = s16[48,256]{1,0:T(8,128)(2,1)S(1)} collective-permute-done((s16[48,256]{1,0:T(8,128)(2,1)S(1)}, s16[48,256]{1,0:T(8,128)(2,1)S(1)}, u32[]{:S(2)}, u32[]{:S(2)}) %collective-permute-start.10) | collective-permute-done | bytes 24608 | tf_op jit(solution)/shard_map/ppermute | solution.py:213
  46.0 0.7 %shard_map.110 = f32[47,256]{1,0:T(8,128)} custom-call(bf16[48,256]{1,0:T(8,128)(2,1)S(1)} %get-tuple-element.32.classes_in, f32[1,256]{1,0:T(1,128)S(1)} %get-tuple-element.33.scaling, f32[47,1]{1,0:T(8,128)S(1)} %get-tuple-element.34.bias, f32[48,256]{1,0:T(8,128)S(1)} %get-tuple-element.35.own, s16[48,256]{1,0:T(8,128)(2,1)S(1)} %collective-permute-done.10.rest_0_), custom_call_target="tpu_custom_call" | custom-call | flops 1048576 | bytes 1048576 | tf_op jit(solution)/shard_map/pallas_call | solution.py:31
  (10 shorter events, 0.1 us)
Async XLA Ops:
  0.0 5.4 %collective-permute-start = (bf16[100,256]{1,0:T(8,128)(2,1)}, bf16[100,256]{1,0:T(8,128)(2,1)S(1)}, u32[]{:S(2)}, u32[]{:S(2)}) collective-permute-start(bf16[100,256]{1,0:T(8,128)(2,1)} %bitcast.7), channel_id=1, source_target_pairs={{1,0},{0,1},{3,2},{2,3},{5,4},{4,5},{7,6},{6,7},{9,8},{8,9},{11,10... | collective-permute-start | bytes 153608 | tf_op jit(solution)/shard_map/ppermute | solution.py:213
  5.6 6.9 %collective-permute-start.1 = (bf16[100,256]{1,0:T(8,128)(2,1)S(1)}, bf16[100,256]{1,0:T(8,128)(2,1)S(1)}, u32[]{:S(2)}, u32[]{:S(2)}) collective-permute-start(bf16[100,256]{1,0:T(8,128)(2,1)S(1)} %shard_map.101.refs_0_), channel_id=1, source_target_pairs={{16,0},{10,2},{20,4},{14,6},{24,8},{2,10},{28,12},{6,14},{0,16},{2... | collective-permute-start | bytes 153608 | tf_op jit(solution)/shard_map/ppermute | solution.py:217
  8.6 6.0 %collective-permute-start.3 = (bf16[100,256]{1,0:T(8,128)(2,1)S(1)}, bf16[100,256]{1,0:T(8,128)(2,1)S(1)}, u32[]{:S(2)}, u32[]{:S(2)}) collective-permute-start(bf16[100,256]{1,0:T(8,128)(2,1)S(1)} %shard_map.101.refs_0_), channel_id=1, source_target_pairs={{24,0},{18,2},{28,4},{22,6},{16,8},{26,10},{20,12},{30,14},{8,16},... | collective-permute-start | bytes 153608 | tf_op jit(solution)/shard_map/ppermute | solution.py:217
  10.0 6.2 %collective-permute-start.2 = (bf16[100,256]{1,0:T(8,128)(2,1)S(1)}, bf16[100,256]{1,0:T(8,128)(2,1)S(1)}, u32[]{:S(2)}, u32[]{:S(2)}) collective-permute-start(bf16[100,256]{1,0:T(8,128)(2,1)S(1)} %shard_map.101.refs_0_), channel_id=1, source_target_pairs={{8,0},{26,2},{12,4},{30,6},{0,8},{18,10},{4,12},{22,14},{24,16},{1... | collective-permute-start | bytes 153608 | tf_op jit(solution)/shard_map/ppermute | solution.py:217
  12.5 5.3 %collective-permute-start.4 = (bf16[2,100,256]{2,1,0:T(8,128)(2,1)S(1)}, bf16[2,100,256]{2,1,0:T(8,128)(2,1)S(1)}, u32[]{:S(2)}, u32[]{:S(2)}) collective-permute-start(bf16[2,100,256]{2,1,0:T(8,128)(2,1)S(1)} %shard_map.102), channel_id=1, source_target_pairs={{4,0},{6,2},{0,4},{2,6},{12,8},{14,10},{8,12},{10,14},{20,16},{22,... | collective-permute-start | bytes 307208 | tf_op jit(solution)/shard_map/ppermute | solution.py:217
  14.6 4.1 %collective-permute-start.5 = (bf16[1,100,256]{2,1,0:T(8,128)(2,1)S(1)}, bf16[1,100,256]{2,1,0:T(8,128)(2,1)S(1)}, u32[]{:S(2)}, u32[]{:S(2)}) collective-permute-start(bf16[1,100,256]{2,1,0:T(8,128)(2,1)S(1)} %shard_map.104), channel_id=1, source_target_pairs={{4,0},{6,2},{0,4},{2,6},{12,8},{14,10},{8,12},{10,14},{20,16},{22,... | collective-permute-start | bytes 153608 | tf_op jit(solution)/shard_map/ppermute | solution.py:217
  16.2 4.2 %collective-permute-start.6 = (bf16[1,100,256]{2,1,0:T(8,128)(2,1)S(1)}, bf16[1,100,256]{2,1,0:T(8,128)(2,1)S(1)}, u32[]{:S(2)}, u32[]{:S(2)}) collective-permute-start(bf16[1,100,256]{2,1,0:T(8,128)(2,1)S(1)} %shard_map.103), channel_id=1, source_target_pairs={{4,0},{6,2},{0,4},{2,6},{12,8},{14,10},{8,12},{10,14},{20,16},{22,... | collective-permute-start | bytes 153608 | tf_op jit(solution)/shard_map/ppermute | solution.py:217
  20.4 1.8 %collective-permute-start.7 = (bf16[8,100,256]{2,1,0:T(8,128)(2,1)S(1)}, bf16[8,100,256]{2,1,0:T(8,128)(2,1)S(1)}, u32[]{:S(2)}, u32[]{:S(2)}) collective-permute-start(bf16[8,100,256]{2,1,0:T(8,128)(2,1)S(1)} %constant_dynamic-update-slice_fusion.stack), channel_id=1, source_target_pairs={{2,0},{0,2},{6,4},{4,6},{10,8},{8,10},{14,12},{12,14},{18,16},{16,... | collective-permute-start | bytes 1228808 | tf_op jit(solution)/shard_map/ppermute | solution.py:217
  23.2 4.4 %collective-permute-start.8 = (s16[144,256]{1,0:T(8,128)(2,1)S(1)}, s16[144,256]{1,0:T(8,128)(2,1)S(1)}, u32[]{:S(2)}, u32[]{:S(2)}) collective-permute-start(s16[144,256]{1,0:T(8,128)(2,1)S(1)} %get-tuple-element.31), channel_id=1, source_target_pairs={{1,0},{0,1},{3,2},{2,3},{5,4},{4,5},{7,6},{6,7},{9,8},{8,9},{11,10... | collective-permute-start | bytes 221192 | tf_op jit(solution)/shard_map/ppermute | solution.py:213
  40.2 1.4 %collective-permute-start.9 = (bf16[8,48,256]{2,1,0:T(8,128)(2,1)S(1)}, bf16[8,48,256]{2,1,0:T(8,128)(2,1)S(1)}, u32[]{:S(2)}, u32[]{:S(2)}) collective-permute-start(bf16[8,48,256]{2,1,0:T(8,128)(2,1)S(1)} %all_to_all.5.near), channel_id=1, source_target_pairs={{2,0},{0,2},{6,4},{4,6},{10,8},{8,10},{14,12},{12,14},{18,16},{16,... | collective-permute-start | bytes 589832 | tf_op jit(solution)/shard_map/ppermute | solution.py:217
  42.1 3.9 %collective-permute-start.10 = (s16[48,256]{1,0:T(8,128)(2,1)S(1)}, s16[48,256]{1,0:T(8,128)(2,1)S(1)}, u32[]{:S(2)}, u32[]{:S(2)}) collective-permute-start(s16[48,256]{1,0:T(8,128)(2,1)S(1)} %get-tuple-element.36), channel_id=1, source_target_pairs={{1,0},{0,1},{3,2},{2,3},{5,4},{4,5},{7,6},{6,7},{9,8},{8,9},{11,10... | collective-permute-start | bytes 73736 | tf_op jit(solution)/shard_map/ppermute | solution.py:213

commit v20 on v16

--- a/solution.py
+++ b/solution.py
@@ -232,7 +232,7 @@
     for here in (core, 1 - core):
         early, late = ([4 * jnp.where(here == 0, *sides) for sides in way] for way in two_ways(pairs))
         crossed, over = [apart + 2 for apart in late], [apart + 2 for apart in early]
-        lists.append([0, 4 * first, *crossed, *late, *early, 2, 4 * first + 2, *over])
+        lists.append([0, 4 * first, 2, 4 * first + 2, *early, *over, *late, *crossed])
     return lists[0], [apart ^ 1 for apart in lists[1]]
 
 
@@ -253,7 +253,7 @@
     crossed = [swapped(value, (4 * a + 2, 4 * b + 2)) for a, b in two_ways(pairs)[1]]
     here, early = packed(value, ahead), packed(*early)
     over = [swapped(here, (2, 2)), swapped(early, (2, 2))]
-    near = jnp.concatenate([here, packed(*crossed), packed(*late), early, *over])
+    near = jnp.concatenate([here, over[0], early, over[1], packed(*late), packed(*crossed)])
     return near, swapped(near, (1, 1))
 
 

time: 45.8 us -> 47 us (1.026)
  blocking collectives: 11.2 us -> 12.3 us
    all_to_all x1, blocking collectives: 11.2 us -> 12.3 us  [gather_classes(): near = lax.all_to_all(copies, 'blk', 0, 0, axis_index_groups=groups)]
  transfers between devices with their start and end apart: 11 -> 11, of which waited for: 7 -> 5; matrix products, arithmetic and copies ran while one was open for 0% -> 0% of each run, Pallas kernels for 6% -> 6%
where the time goes in v20:
time: 47 us; the launch traced here: 46.8 us
  starting transfers between devices  17.4 us (37%)
  blocking collectives  12.3 us (26%)
  waiting for transfers between devices  10.8 us (23%)
  Pallas kernels  5.43 us (12%)
  between operations  0.78 us (2%)
    all_to_all x1, blocking collectives, gather_classes(): near = lax.all_to_all(copies, 'blk', 0, 0, axis_index_groups=groups)  12.3 us
    ppermute x8, starting transfers between devices, swapped(): lax.ppermute(value, 'blk', [(d ^ masks[d % 2], d) for d in range(lax.axis...  11.6 us
    ppermute x3, starting transfers between devices, shifted(): lax.ppermute(value, axis, [((d + step) % size, d) for d in range(size)])  5.79 us
    ppermute x3, waiting for transfers between devices, shifted(): lax.ppermute(value, axis, [((d + step) % size, d) for d in range(size)])  5.46 us
    pallas_call x10, Pallas kernels, call(): pl.pallas_call(kernel, out_shape=outs, in_specs=[pl.BlockSpec(memory_spac...  5.43 us
    ppermute x8, waiting for transfers between devices, swapped(): lax.ppermute(value, 'blk', [(d ^ masks[d % 2], d) for d in range(lax.axis...  5.35 us
  transfers between devices with their start and end apart: 11, of which 5 were waited for; matrix products, arithmetic and copies ran while one was open for 0% of the time, Pallas kernels for 6%

profile of v20, /device:TPU:0, one launch (start us, length us, event | category | flops | bytes accessed | tf_op | source)
XLA Modules:
  0.0 46.8 jit_solution(11370653152849061600)
XLA Ops:
  0.0 2.9 %collective-permute-start = (bf16[100,256]{1,0:T(8,128)(2,1)}, bf16[100,256]{1,0:T(8,128)(2,1)S(1)}, u32[]{:S(2)}, u32[]{:S(2)}) collective-permute-start(bf16[100,256]{1,0:T(8,128)(2,1)} %bitcast.7), channel_id=1, source_target_pairs={{1,0},{0,1},{3,2},{2,3},{5,4},{4,5},{7,6},{6,7},{9,8},{8,9},{11,10... | collective-permute-start | bytes 153608 | tf_op jit(solution)/shard_map/ppermute | solution.py:213
  3.6 1.8 %shard_map.100 = (s32[32]{0:T(128)S(4)}, f32[100,256]{1,0:T(8,128)S(1)}, s32[1,256]{1,0:T(1,128)S(1)}, bf16[16,256,256]{2,1,0:T(8,128)(2,1)S(1)}, f32[128,1]{1,0...) custom-call(s32[1]{0:T(128)S(6)} %copy.16.live, s32[1,512]{1,0:T(1,128)} %refs_0_.1, ...), custom_call_target="tpu_custom_call" | custom-call | flops 1048576 | bytes 1048576 | tf_op jit(solution)/shard_map/pallas_call | solution.py:31
  5.4 0.0 collective-permute-done.rest_0_
  5.4 0.2 shard_map.101.refs_0_
  5.6 3.0 %collective-permute-start.3 = (bf16[100,256]{1,0:T(8,128)(2,1)S(1)}, bf16[100,256]{1,0:T(8,128)(2,1)S(1)}, u32[]{:S(2)}, u32[]{:S(2)}) collective-permute-start(bf16[100,256]{1,0:T(8,128)(2,1)S(1)} %shard_map.101.refs_0_), channel_id=1, source_target_pairs={{16,0},{26,2},{20,4},{30,6},{24,8},{18,10},{28,12},{22,14},{0,16},... | collective-permute-start | bytes 153608 | tf_op jit(solution)/shard_map/ppermute | solution.py:217
  8.6 1.6 %collective-permute-start.1 = (bf16[100,256]{1,0:T(8,128)(2,1)S(1)}, bf16[100,256]{1,0:T(8,128)(2,1)S(1)}, u32[]{:S(2)}, u32[]{:S(2)}) collective-permute-start(bf16[100,256]{1,0:T(8,128)(2,1)S(1)} %shard_map.101.refs_0_), channel_id=1, source_target_pairs={{8,0},{10,2},{12,4},{14,6},{0,8},{2,10},{4,12},{6,14},{24,16},{26,... | collective-permute-start | bytes 153608 | tf_op jit(solution)/shard_map/ppermute | solution.py:217
  10.2 1.2 %collective-permute-start.6 = (bf16[100,256]{1,0:T(8,128)(2,1)S(1)}, bf16[100,256]{1,0:T(8,128)(2,1)S(1)}, u32[]{:S(2)}, u32[]{:S(2)}) collective-permute-start(bf16[100,256]{1,0:T(8,128)(2,1)S(1)} %shard_map.101.refs_0_), channel_id=1, source_target_pairs={{28,0},{22,2},{24,4},{18,6},{20,8},{30,10},{16,12},{26,14},{12,16}... | collective-permute-start | bytes 153608 | tf_op jit(solution)/shard_map/ppermute | solution.py:217
  11.4 3.6 %collective-permute-start.5 = (bf16[100,256]{1,0:T(8,128)(2,1)S(1)}, bf16[100,256]{1,0:T(8,128)(2,1)S(1)}, u32[]{:S(2)}, u32[]{:S(2)}) collective-permute-start(bf16[100,256]{1,0:T(8,128)(2,1)S(1)} %shard_map.101.refs_0_), channel_id=1, source_target_pairs={{24,0},{18,2},{28,4},{22,6},{16,8},{26,10},{20,12},{30,14},{8,16},... | collective-permute-start | bytes 153608 | tf_op jit(solution)/shard_map/ppermute | solution.py:217
  15.0 0.0 collective-permute-done.3.refs_0_
  15.0 0.6 %collective-permute-start.4 = (bf16[1,100,256]{2,1,0:T(8,128)(2,1)S(1)}, bf16[1,100,256]{2,1,0:T(8,128)(2,1)S(1)}, u32[]{:S(2)}, u32[]{:S(2)}) collective-permute-start(bf16[1,100,256]{2,1,0:T(8,128)(2,1)S(1)} %shard_map.103), channel_id=1, source_target_pairs={{4,0},{6,2},{0,4},{2,6},{12,8},{14,10},{8,12},{10,14},{20,16},{22,... | collective-permute-start | bytes 153608 | tf_op jit(solution)/shard_map/ppermute | solution.py:217
  15.6 0.0 collective-permute-done.1.refs_1_
  15.6 1.6 %collective-permute-start.2 = (bf16[2,100,256]{2,1,0:T(8,128)(2,1)S(1)}, bf16[2,100,256]{2,1,0:T(8,128)(2,1)S(1)}, u32[]{:S(2)}, u32[]{:S(2)}) collective-permute-start(bf16[2,100,256]{2,1,0:T(8,128)(2,1)S(1)} %shard_map.102), channel_id=1, source_target_pairs={{4,0},{6,2},{0,4},{2,6},{12,8},{14,10},{8,12},{10,14},{20,16},{22,... | collective-permute-start | bytes 307208 | tf_op jit(solution)/shard_map/ppermute | solution.py:217
  17.2 3.2 %collective-permute-done.2 = bf16[2,100,256]{2,1,0:T(8,128)(2,1)S(1)} collective-permute-done((bf16[2,100,256]{2,1,0:T(8,128)(2,1)S(1)}, bf16[2,100,256]{2,1,0:T(8,128)(2,1)S(1)}, u32[]{:S(2)}, u32[]{:S(2)}) %collective-permute-start.2) | collective-permute-done | bytes 102432 | tf_op jit(solution)/shard_map/ppermute | solution.py:217
  20.4 0.0 collective-permute-done.4
  20.4 0.0 collective-permute-done.5
  20.4 0.0 collective-permute-done.6
  20.5 0.1 collective-permute-start.7
  20.5 0.7 %shard_map.105 = (bf16[16,256,256]{2,1,0:T(8,128)(2,1)S(1)}, f32[2,8,256]{2,1,0:T(8,128)S(1)}) custom-call(bf16[16,256,256]{2,1,0:T(8,128)(2,1)S(1)} %get-tuple-element.26.tiles, s32[32]{0:T(128)S(4)} %get-tuple-element.27.plan), custom_call_target="tpu_custom_call" | custom-call | flops 1048576 | bytes 1048576 | tf_op jit(solution)/shard_map/pallas_call | solution.py:31
  21.3 0.3 shard_map.104.projected.hidden_in
  21.6 0.7 %collective-permute-done.7.far = bf16[8,100,256]{2,1,0:T(8,128)(2,1)S(1)} collective-permute-done((bf16[8,100,256]{2,1,0:T(8,128)(2,1)S(1)}, bf16[8,100,256]{2,1,0:T(8,128)(2,1)S(1)}, u32[]{:S(2)}, u32[]{:S(2)}) %collective-permute-start.7) | collective-permute-done | bytes 409632 | tf_op jit(solution)/shard_map/ppermute | solution.py:217
  22.3 1.0 %shard_map.106 = (f32[128,256]{1,0:T(8,128)S(1)}, s16[144,256]{1,0:T(8,128)(2,1)S(1)}) custom-call(bf16[8,128,256]{2,1,0:T(8,128)(2,1)S(1)} %shard_map.104.projected.hidden_in, bf16[8,100,256]{2,1,0:T(8,128)(2,1)S(1)} %collective-permute-done.7.far, bf16[128,100]{1,0:T(8,128)(2,1)S(1)} %get-tuple-element.21.weight_t, ...), custom_call_target="tpu_custom_call" | custom-call | flops 1048576 | bytes 1048576 | tf_op jit(solution)/shard_map/pallas_call | solution.py:31
  23.3 1.6 %collective-permute-start.8 = (s16[144,256]{1,0:T(8,128)(2,1)S(1)}, s16[144,256]{1,0:T(8,128)(2,1)S(1)}, u32[]{:S(2)}, u32[]{:S(2)}) collective-permute-start(s16[144,256]{1,0:T(8,128)(2,1)S(1)} %get-tuple-element.31), channel_id=1, source_target_pairs={{1,0},{0,1},{3,2},{2,3},{5,4},{4,5},{7,6},{6,7},{9,8},{8,9},{11,10... | collective-permute-start | bytes 221192 | tf_op jit(solution)/shard_map/ppermute | solution.py:213
  24.9 2.9 %collective-permute-done.8.rest_0_ = s16[144,256]{1,0:T(8,128)(2,1)S(1)} collective-permute-done((s16[144,256]{1,0:T(8,128)(2,1)S(1)}, s16[144,256]{1,0:T(8,128)(2,1)S(1)}, u32[]{:S(2)}, u32[]{:S(2)}) %collective-permute-start.8) | collective-permute-done | bytes 73760 | tf_op jit(solution)/shard_map/ppermute | solution.py:213
  27.7 0.2 shard_map.107
  28.0 12.3 %all_to_all.5.near = bf16[8,48,256]{2,1,0:T(8,128)(2,1)S(1)} all-to-all(bf16[8,48,256]{2,1,0:T(8,128)(2,1)S(1)} %broadcast_in_dim.14), channel_id=1, replica_groups={{0,4,8,12,16,20,24,28},{2,6,10,14,18,22,26,30},{1,5,9,13,17,21,25,29},{..., dimensions={0} | all-to-all | bytes 393216 | tf_op jit(solution)/shard_map/all_to_all | solution.py:264
  40.2 0.0 collective-permute-start.9
  40.2 1.4 %collective-permute-done.9.far = bf16[8,48,256]{2,1,0:T(8,128)(2,1)S(1)} collective-permute-done((bf16[8,48,256]{2,1,0:T(8,128)(2,1)S(1)}, bf16[8,48,256]{2,1,0:T(8,128)(2,1)S(1)}, u32[]{:S(2)}, u32[]{:S(2)}) %collective-permute-start.9) | collective-permute-done | bytes 196640 | tf_op jit(solution)/shard_map/ppermute | solution.py:217
  41.7 0.5 %shard_map.108 = (f32[48,256]{1,0:T(8,128)S(1)}, s16[48,256]{1,0:T(8,128)(2,1)S(1)}) custom-call(bf16[8,48,256]{2,1,0:T(8,128)(2,1)S(1)} %all_to_all.5.near, bf16[8,48,256]{2,1,0:T(8,128)(2,1)S(1)} %collective-permute-done.9.far, bf16[16,256,256]{2,1,0:T(8,128)(2,1)S(1)} %get-tuple-element.29.tiles_t, s32[32]{0:T(128)S(4)} %get-tuple-element.27.plan), custom_call_target="tpu_custom_call" | custom-call | flops 1048576 | bytes 1048576 | tf_op jit(solution)/shard_map/pallas_call | solution.py:31
  42.2 1.3 %collective-permute-start.10 = (s16[48,256]{1,0:T(8,128)(2,1)S(1)}, s16[48,256]{1,0:T(8,128)(2,1)S(1)}, u32[]{:S(2)}, u32[]{:S(2)}) collective-permute-start(s16[48,256]{1,0:T(8,128)(2,1)S(1)} %get-tuple-element.36), channel_id=1, source_target_pairs={{1,0},{0,1},{3,2},{2,3},{5,4},{4,5},{7,6},{6,7},{9,8},{8,9},{11,10... | collective-permute-start | bytes 73736 | tf_op jit(solution)/shard_map/ppermute | solution.py:213
  43.5 2.6 %collective-permute-done.10.rest_0_ = s16[48,256]{1,0:T(8,128)(2,1)S(1)} collective-permute-done((s16[48,256]{1,0:T(8,128)(2,1)S(1)}, s16[48,256]{1,0:T(8,128)(2,1)S(1)}, u32[]{:S(2)}, u32[]{:S(2)}) %collective-permute-start.10) | collective-permute-done | bytes 24608 | tf_op jit(solution)/shard_map/ppermute | solution.py:213
  46.1 0.7 %shard_map.109 = f32[47,256]{1,0:T(8,128)} custom-call(bf16[48,256]{1,0:T(8,128)(2,1)S(1)} %get-tuple-element.32.classes_in, f32[1,256]{1,0:T(1,128)S(1)} %get-tuple-element.33.scaling, f32[47,1]{1,0:T(8,128)S(1)} %get-tuple-element.34.bias, f32[48,256]{1,0:T(8,128)S(1)} %get-tuple-element.35.own, s16[48,256]{1,0:T(8,128)(2,1)S(1)} %collective-permute-done.10.rest_0_), custom_call_target="tpu_custom_call" | custom-call | flops 1048576 | bytes 1048576 | tf_op jit(solution)/shard_map/pallas_call | solution.py:31
  (9 shorter events, 0.1 us)
Async XLA Ops:
  0.0 5.4 %collective-permute-start = (bf16[100,256]{1,0:T(8,128)(2,1)}, bf16[100,256]{1,0:T(8,128)(2,1)S(1)}, u32[]{:S(2)}, u32[]{:S(2)}) collective-permute-start(bf16[100,256]{1,0:T(8,128)(2,1)} %bitcast.7), channel_id=1, source_target_pairs={{1,0},{0,1},{3,2},{2,3},{5,4},{4,5},{7,6},{6,7},{9,8},{8,9},{11,10... | collective-permute-start | bytes 153608 | tf_op jit(solution)/shard_map/ppermute | solution.py:213
  5.6 9.4 %collective-permute-start.3 = (bf16[100,256]{1,0:T(8,128)(2,1)S(1)}, bf16[100,256]{1,0:T(8,128)(2,1)S(1)}, u32[]{:S(2)}, u32[]{:S(2)}) collective-permute-start(bf16[100,256]{1,0:T(8,128)(2,1)S(1)} %shard_map.101.refs_0_), channel_id=1, source_target_pairs={{16,0},{26,2},{20,4},{30,6},{24,8},{18,10},{28,12},{22,14},{0,16},... | collective-permute-start | bytes 153608 | tf_op jit(solution)/shard_map/ppermute | solution.py:217
  8.6 6.9 %collective-permute-start.1 = (bf16[100,256]{1,0:T(8,128)(2,1)S(1)}, bf16[100,256]{1,0:T(8,128)(2,1)S(1)}, u32[]{:S(2)}, u32[]{:S(2)}) collective-permute-start(bf16[100,256]{1,0:T(8,128)(2,1)S(1)} %shard_map.101.refs_0_), channel_id=1, source_target_pairs={{8,0},{10,2},{12,4},{14,6},{0,8},{2,10},{4,12},{6,14},{24,16},{26,... | collective-permute-start | bytes 153608 | tf_op jit(solution)/shard_map/ppermute | solution.py:217
  10.2 10.2 %collective-permute-start.6 = (bf16[100,256]{1,0:T(8,128)(2,1)S(1)}, bf16[100,256]{1,0:T(8,128)(2,1)S(1)}, u32[]{:S(2)}, u32[]{:S(2)}) collective-permute-start(bf16[100,256]{1,0:T(8,128)(2,1)S(1)} %shard_map.101.refs_0_), channel_id=1, source_target_pairs={{28,0},{22,2},{24,4},{18,6},{20,8},{30,10},{16,12},{26,14},{12,16}... | collective-permute-start | bytes 153608 | tf_op jit(solution)/shard_map/ppermute | solution.py:217
  11.4 9.0 %collective-permute-start.5 = (bf16[100,256]{1,0:T(8,128)(2,1)S(1)}, bf16[100,256]{1,0:T(8,128)(2,1)S(1)}, u32[]{:S(2)}, u32[]{:S(2)}) collective-permute-start(bf16[100,256]{1,0:T(8,128)(2,1)S(1)} %shard_map.101.refs_0_), channel_id=1, source_target_pairs={{24,0},{18,2},{28,4},{22,6},{16,8},{26,10},{20,12},{30,14},{8,16},... | collective-permute-start | bytes 153608 | tf_op jit(solution)/shard_map/ppermute | solution.py:217
  15.0 5.4 %collective-permute-start.4 = (bf16[1,100,256]{2,1,0:T(8,128)(2,1)S(1)}, bf16[1,100,256]{2,1,0:T(8,128)(2,1)S(1)}, u32[]{:S(2)}, u32[]{:S(2)}) collective-permute-start(bf16[1,100,256]{2,1,0:T(8,128)(2,1)S(1)} %shard_map.103), channel_id=1, source_target_pairs={{4,0},{6,2},{0,4},{2,6},{12,8},{14,10},{8,12},{10,14},{20,16},{22,... | collective-permute-start | bytes 153608 | tf_op jit(solution)/shard_map/ppermute | solution.py:217
  15.6 4.8 %collective-permute-start.2 = (bf16[2,100,256]{2,1,0:T(8,128)(2,1)S(1)}, bf16[2,100,256]{2,1,0:T(8,128)(2,1)S(1)}, u32[]{:S(2)}, u32[]{:S(2)}) collective-permute-start(bf16[2,100,256]{2,1,0:T(8,128)(2,1)S(1)} %shard_map.102), channel_id=1, source_target_pairs={{4,0},{6,2},{0,4},{2,6},{12,8},{14,10},{8,12},{10,14},{20,16},{22,... | collective-permute-start | bytes 307208 | tf_op jit(solution)/shard_map/ppermute | solution.py:217
  20.5 1.8 %collective-permute-start.7 = (bf16[8,100,256]{2,1,0:T(8,128)(2,1)S(1)}, bf16[8,100,256]{2,1,0:T(8,128)(2,1)S(1)}, u32[]{:S(2)}, u32[]{:S(2)}) collective-permute-start(bf16[8,100,256]{2,1,0:T(8,128)(2,1)S(1)} %shard_map.110.stack), channel_id=1, source_target_pairs={{2,0},{0,2},{6,4},{4,6},{10,8},{8,10},{14,12},{12,14},{18,16},{16,... | collective-permute-start | bytes 1228808 | tf_op jit(solution)/shard_map/ppermute | solution.py:217
  23.3 4.4 %collective-permute-start.8 = (s16[144,256]{1,0:T(8,128)(2,1)S(1)}, s16[144,256]{1,0:T(8,128)(2,1)S(1)}, u32[]{:S(2)}, u32[]{:S(2)}) collective-permute-start(s16[144,256]{1,0:T(8,128)(2,1)S(1)} %get-tuple-element.31), channel_id=1, source_target_pairs={{1,0},{0,1},{3,2},{2,3},{5,4},{4,5},{7,6},{6,7},{9,8},{8,9},{11,10... | collective-permute-start | bytes 221192 | tf_op jit(solution)/shard_map/ppermute | solution.py:213
  40.2 1.4 %collective-permute-start.9 = (bf16[8,48,256]{2,1,0:T(8,128)(2,1)S(1)}, bf16[8,48,256]{2,1,0:T(8,128)(2,1)S(1)}, u32[]{:S(2)}, u32[]{:S(2)}) collective-permute-start(bf16[8,48,256]{2,1,0:T(8,128)(2,1)S(1)} %all_to_all.5.near), channel_id=1, source_target_pairs={{2,0},{0,2},{6,4},{4,6},{10,8},{8,10},{14,12},{12,14},{18,16},{16,... | collective-permute-start | bytes 589832 | tf_op jit(solution)/shard_map/ppermute | solution.py:217
  42.2 3.9 %collective-permute-start.10 = (s16[48,256]{1,0:T(8,128)(2,1)S(1)}, s16[48,256]{1,0:T(8,128)(2,1)S(1)}, u32[]{:S(2)}, u32[]{:S(2)}) collective-permute-start(s16[48,256]{1,0:T(8,128)(2,1)S(1)} %get-tuple-element.36), channel_id=1, source_target_pairs={{1,0},{0,1},{3,2},{2,3},{5,4},{4,5},{7,6},{6,7},{9,8},{8,9},{11,10... | collective-permute-start | bytes 73736 | tf_op jit(solution)/shard_map/ppermute | solution.py:213

commit v21 on v20

--- a/solution.py
+++ b/solution.py
@@ -231,8 +231,8 @@
     lists = []
     for here in (core, 1 - core):
         early, late = ([4 * jnp.where(here == 0, *sides) for sides in way] for way in two_ways(pairs))
-        crossed, over = [apart + 2 for apart in late], [apart + 2 for apart in early]
-        lists.append([0, 4 * first, 2, 4 * first + 2, *early, *over, *late, *crossed])
+        over = [apart + 2 for apart in [0, 4 * first, *early, *late]]
+        lists.append([0, 4 * first, *late, *early, *over])
     return lists[0], [apart ^ 1 for apart in lists[1]]
 
 
@@ -250,10 +250,9 @@
     first, pairs = outer_order(outer)
     ahead = swapped(value, (4 * first, 4 * first))
     early, late = ([swapped(value, (4 * a, 4 * b)) for a, b in way] for way in two_ways(pairs))
-    crossed = [swapped(value, (4 * a + 2, 4 * b + 2)) for a, b in two_ways(pairs)[1]]
-    here, early = packed(value, ahead), packed(*early)
-    over = [swapped(here, (2, 2)), swapped(early, (2, 2))]
-    near = jnp.concatenate([here, over[0], early, over[1], packed(*late), packed(*crossed)])
+    stacks = packed(value, ahead), packed(*early), packed(*late)
+    over = [swapped(stack, (2, 2)) for stack in stacks]
+    near = jnp.concatenate([stacks[0], stacks[2], stacks[1], *over])
     return near, swapped(near, (1, 1))
 
 

time: 47 us -> 45.6 us (0.970)
  starting transfers between devices: 17.4 us -> 15 us
  waiting for transfers between devices: 10.8 us -> 13.1 us
  blocking collectives: 12.3 us -> 11.1 us
    ppermute x8, starting transfers between devices: 11.6 us -> 9.47 us  [swapped(): lax.ppermute(value, 'blk', [(d ^ masks[d % 2], d) for d in range(lax.axis...]
    ppermute x8, waiting for transfers between devices: 5.35 us -> 7.32 us  [swapped(): lax.ppermute(value, 'blk', [(d ^ masks[d % 2], d) for d in range(lax.axis...]
    all_to_all x1, blocking collectives: 12.3 us -> 11.1 us  [gather_classes(): near = lax.all_to_all(copies, 'blk', 0, 0, axis_index_groups=groups)]
    pallas_call x10 -> x11, Pallas kernels: 5.43 us -> 5.43 us  [call(): pl.pallas_call(kernel, out_shape=outs, in_specs=[pl.BlockSpec(memory_spac...]
  transfers between devices with their start and end apart: 11 -> 11, of which waited for: 5 -> 8; matrix products, arithmetic and copies ran while one was open for 0% -> 0% of each run, Pallas kernels for 6% -> 6%
where the time goes in v21:
time: 45.6 us; the launch traced here: 45.4 us
  starting transfers between devices  15 us (33%)
  waiting for transfers between devices  13.1 us (29%)
  blocking collectives  11.1 us (24%)
  Pallas kernels  5.43 us (12%)
  between operations  0.75 us (2%)
    all_to_all x1, blocking collectives, gather_classes(): near = lax.all_to_all(copies, 'blk', 0, 0, axis_index_groups=groups)  11.1 us
    ppermute x8, starting transfers between devices, swapped(): lax.ppermute(value, 'blk', [(d ^ masks[d % 2], d) for d in range(lax.axis...  9.47 us
    ppermute x8, waiting for transfers between devices, swapped(): lax.ppermute(value, 'blk', [(d ^ masks[d % 2], d) for d in range(lax.axis...  7.32 us
    ppermute x3, waiting for transfers between devices, shifted(): lax.ppermute(value, axis, [((d + step) % size, d) for d in range(size)])  5.76 us
    ppermute x3, starting transfers between devices, shifted(): lax.ppermute(value, axis, [((d + step) % size, d) for d in range(size)])  5.49 us
    pallas_call x11, Pallas kernels, call(): pl.pallas_call(kernel, out_shape=outs, in_specs=[pl.BlockSpec(memory_spac...  5.43 us
  transfers between devices with their start and end apart: 11, of which 8 were waited for; matrix products, arithmetic and copies ran while one was open for 0% of the time, Pallas kernels for 6%

profile of v21, /device:TPU:0, one launch (start us, length us, event | category | flops | bytes accessed | tf_op | source)
XLA Modules:
  0.0 45.4 jit_solution(8255983101029790025)
XLA Ops:
  0.0 2.9 %collective-permute-start = (bf16[100,256]{1,0:T(8,128)(2,1)}, bf16[100,256]{1,0:T(8,128)(2,1)S(1)}, u32[]{:S(2)}, u32[]{:S(2)}) collective-permute-start(bf16[100,256]{1,0:T(8,128)(2,1)} %bitcast.7), channel_id=1, source_target_pairs={{1,0},{0,1},{3,2},{2,3},{5,4},{4,5},{7,6},{6,7},{9,8},{8,9},{11,10... | collective-permute-start | bytes 153608 | tf_op jit(solution)/shard_map/ppermute | solution.py:213
  3.6 1.8 %shard_map.100 = (s32[32]{0:T(128)S(4)}, f32[100,256]{1,0:T(8,128)S(1)}, s32[1,256]{1,0:T(1,128)S(1)}, bf16[16,256,256]{2,1,0:T(8,128)(2,1)S(1)}, f32[128,1]{1,0...) custom-call(s32[1]{0:T(128)S(6)} %copy.16.live, s32[1,512]{1,0:T(1,128)} %refs_0_.1, ...), custom_call_target="tpu_custom_call" | custom-call | flops 1048576 | bytes 1048576 | tf_op jit(solution)/shard_map/pallas_call | solution.py:31
  5.4 0.0 collective-permute-done.rest_0_
  5.4 0.2 shard_map.101.refs_0_
  5.6 2.0 %collective-permute-start.1 = (bf16[100,256]{1,0:T(8,128)(2,1)S(1)}, bf16[100,256]{1,0:T(8,128)(2,1)S(1)}, u32[]{:S(2)}, u32[]{:S(2)}) collective-permute-start(bf16[100,256]{1,0:T(8,128)(2,1)S(1)} %shard_map.101.refs_0_), channel_id=1, source_target_pairs={{8,0},{10,2},{12,4},{14,6},{0,8},{2,10},{4,12},{6,14},{24,16},{26,... | collective-permute-start | bytes 153608 | tf_op jit(solution)/shard_map/ppermute | solution.py:217
  7.6 2.6 %collective-permute-start.3 = (bf16[100,256]{1,0:T(8,128)(2,1)S(1)}, bf16[100,256]{1,0:T(8,128)(2,1)S(1)}, u32[]{:S(2)}, u32[]{:S(2)}) collective-permute-start(bf16[100,256]{1,0:T(8,128)(2,1)S(1)} %shard_map.101.refs_0_), channel_id=1, source_target_pairs={{16,0},{26,2},{20,4},{30,6},{24,8},{18,10},{28,12},{22,14},{0,16},... | collective-permute-start | bytes 153608 | tf_op jit(solution)/shard_map/ppermute | solution.py:217
  10.2 0.0 collective-permute-start.2
  10.2 0.0 collective-permute-done.1.refs_1_
  10.2 1.8 %collective-permute-start.4 = (bf16[2,100,256]{2,1,0:T(8,128)(2,1)S(1)}, bf16[2,100,256]{2,1,0:T(8,128)(2,1)S(1)}, u32[]{:S(2)}, u32[]{:S(2)}) collective-permute-start(bf16[2,100,256]{2,1,0:T(8,128)(2,1)S(1)} %shard_map.102), channel_id=1, source_target_pairs={{4,0},{6,2},{0,4},{2,6},{12,8},{14,10},{8,12},{10,14},{20,16},{22,... | collective-permute-start | bytes 307208 | tf_op jit(solution)/shard_map/ppermute | solution.py:217
  12.0 2.2 %collective-permute-done.3.refs_0_ = bf16[100,256]{1,0:T(8,128)(2,1)S(1)} collective-permute-done((bf16[100,256]{1,0:T(8,128)(2,1)S(1)}, bf16[100,256]{1,0:T(8,128)(2,1)S(1)}, u32[]{:S(2)}, u32[]{:S(2)}) %collective-permute-start.3) | collective-permute-done | bytes 51232 | tf_op jit(solution)/shard_map/ppermute | solution.py:217
  14.2 1.5 %collective-permute-start.5 = (bf16[1,100,256]{2,1,0:T(8,128)(2,1)S(1)}, bf16[1,100,256]{2,1,0:T(8,128)(2,1)S(1)}, u32[]{:S(2)}, u32[]{:S(2)}) collective-permute-start(bf16[1,100,256]{2,1,0:T(8,128)(2,1)S(1)} %shard_map.104), channel_id=1, source_target_pairs={{4,0},{6,2},{0,4},{2,6},{12,8},{14,10},{8,12},{10,14},{20,16},{22,... | collective-permute-start | bytes 153608 | tf_op jit(solution)/shard_map/ppermute | solution.py:217
  15.8 0.4 collective-permute-done.2.refs_0_
  16.1 1.5 %collective-permute-start.6 = (bf16[1,100,256]{2,1,0:T(8,128)(2,1)S(1)}, bf16[1,100,256]{2,1,0:T(8,128)(2,1)S(1)}, u32[]{:S(2)}, u32[]{:S(2)}) collective-permute-start(bf16[1,100,256]{2,1,0:T(8,128)(2,1)S(1)} %shard_map.103), channel_id=1, source_target_pairs={{4,0},{6,2},{0,4},{2,6},{12,8},{14,10},{8,12},{10,14},{20,16},{22,... | collective-permute-start | bytes 153608 | tf_op jit(solution)/shard_map/ppermute | solution.py:217
  17.7 0.0 collective-permute-done.4
  17.7 0.7 %collective-permute-done.5 = bf16[1,100,256]{2,1,0:T(8,128)(2,1)S(1)} collective-permute-done((bf16[1,100,256]{2,1,0:T(8,128)(2,1)S(1)}, bf16[1,100,256]{2,1,0:T(8,128)(2,1)S(1)}, u32[]{:S(2)}, u32[]{:S(2)}) %collective-permute-start.5) | collective-permute-done | bytes 51232 | tf_op jit(solution)/shard_map/ppermute | solution.py:217
  18.4 1.9 %collective-permute-done.6 = bf16[1,100,256]{2,1,0:T(8,128)(2,1)S(1)} collective-permute-done((bf16[1,100,256]{2,1,0:T(8,128)(2,1)S(1)}, bf16[1,100,256]{2,1,0:T(8,128)(2,1)S(1)}, u32[]{:S(2)}, u32[]{:S(2)}) %collective-permute-start.6) | collective-permute-done | bytes 51232 | tf_op jit(solution)/shard_map/ppermute | solution.py:217
  20.3 0.0 collective-permute-start.7
  20.3 0.7 %shard_map.106 = (bf16[16,256,256]{2,1,0:T(8,128)(2,1)S(1)}, f32[2,8,256]{2,1,0:T(8,128)S(1)}) custom-call(bf16[16,256,256]{2,1,0:T(8,128)(2,1)S(1)} %get-tuple-element.26.tiles, s32[32]{0:T(128)S(4)} %get-tuple-element.27.plan), custom_call_target="tpu_custom_call" | custom-call | flops 1048576 | bytes 1048576 | tf_op jit(solution)/shard_map/pallas_call | solution.py:31
  21.0 0.3 shard_map.105.projected.hidden_in
  21.3 0.7 %collective-permute-done.7.far = bf16[8,100,256]{2,1,0:T(8,128)(2,1)S(1)} collective-permute-done((bf16[8,100,256]{2,1,0:T(8,128)(2,1)S(1)}, bf16[8,100,256]{2,1,0:T(8,128)(2,1)S(1)}, u32[]{:S(2)}, u32[]{:S(2)}) %collective-permute-start.7) | collective-permute-done | bytes 409632 | tf_op jit(solution)/shard_map/ppermute | solution.py:217
  22.0 1.0 %shard_map.107 = (f32[128,256]{1,0:T(8,128)S(1)}, s16[144,256]{1,0:T(8,128)(2,1)S(1)}) custom-call(bf16[8,128,256]{2,1,0:T(8,128)(2,1)S(1)} %shard_map.105.projected.hidden_in, bf16[8,100,256]{2,1,0:T(8,128)(2,1)S(1)} %collective-permute-done.7.far, bf16[128,100]{1,0:T(8,128)(2,1)S(1)} %get-tuple-element.21.weight_t, ...), custom_call_target="tpu_custom_call" | custom-call | flops 1048576 | bytes 1048576 | tf_op jit(solution)/shard_map/pallas_call | solution.py:31
  23.1 1.6 %collective-permute-start.8 = (s16[144,256]{1,0:T(8,128)(2,1)S(1)}, s16[144,256]{1,0:T(8,128)(2,1)S(1)}, u32[]{:S(2)}, u32[]{:S(2)}) collective-permute-start(s16[144,256]{1,0:T(8,128)(2,1)S(1)} %get-tuple-element.31), channel_id=1, source_target_pairs={{1,0},{0,1},{3,2},{2,3},{5,4},{4,5},{7,6},{6,7},{9,8},{8,9},{11,10... | collective-permute-start | bytes 221192 | tf_op jit(solution)/shard_map/ppermute | solution.py:213
  24.6 2.9 %collective-permute-done.8.rest_0_ = s16[144,256]{1,0:T(8,128)(2,1)S(1)} collective-permute-done((s16[144,256]{1,0:T(8,128)(2,1)S(1)}, s16[144,256]{1,0:T(8,128)(2,1)S(1)}, u32[]{:S(2)}, u32[]{:S(2)}) %collective-permute-start.8) | collective-permute-done | bytes 73760 | tf_op jit(solution)/shard_map/ppermute | solution.py:213
  27.5 0.2 shard_map.108
  27.7 11.1 %all_to_all.5.near = bf16[8,48,256]{2,1,0:T(8,128)(2,1)S(1)} all-to-all(bf16[8,48,256]{2,1,0:T(8,128)(2,1)S(1)} %broadcast_in_dim.14), channel_id=1, replica_groups={{0,4,8,12,16,20,24,28},{2,6,10,14,18,22,26,30},{1,5,9,13,17,21,25,29},{..., dimensions={0} | all-to-all | bytes 393216 | tf_op jit(solution)/shard_map/all_to_all | solution.py:263
  38.9 0.0 collective-permute-start.9
  38.9 1.4 %collective-permute-done.9.far = bf16[8,48,256]{2,1,0:T(8,128)(2,1)S(1)} collective-permute-done((bf16[8,48,256]{2,1,0:T(8,128)(2,1)S(1)}, bf16[8,48,256]{2,1,0:T(8,128)(2,1)S(1)}, u32[]{:S(2)}, u32[]{:S(2)}) %collective-permute-start.9) | collective-permute-done | bytes 196640 | tf_op jit(solution)/shard_map/ppermute | solution.py:217
  40.3 0.5 %shard_map.109 = (f32[48,256]{1,0:T(8,128)S(1)}, s16[48,256]{1,0:T(8,128)(2,1)S(1)}) custom-call(bf16[8,48,256]{2,1,0:T(8,128)(2,1)S(1)} %all_to_all.5.near, bf16[8,48,256]{2,1,0:T(8,128)(2,1)S(1)} %collective-permute-done.9.far, bf16[16,256,256]{2,1,0:T(8,128)(2,1)S(1)} %get-tuple-element.29.tiles_t, s32[32]{0:T(128)S(4)} %get-tuple-element.27.plan), custom_call_target="tpu_custom_call" | custom-call | flops 1048576 | bytes 1048576 | tf_op jit(solution)/shard_map/pallas_call | solution.py:31
  40.8 1.0 %collective-permute-start.10 = (s16[48,256]{1,0:T(8,128)(2,1)S(1)}, s16[48,256]{1,0:T(8,128)(2,1)S(1)}, u32[]{:S(2)}, u32[]{:S(2)}) collective-permute-start(s16[48,256]{1,0:T(8,128)(2,1)S(1)} %get-tuple-element.36), channel_id=1, source_target_pairs={{1,0},{0,1},{3,2},{2,3},{5,4},{4,5},{7,6},{6,7},{9,8},{8,9},{11,10... | collective-permute-start | bytes 73736 | tf_op jit(solution)/shard_map/ppermute | solution.py:213
  41.8 2.9 %collective-permute-done.10.rest_0_ = s16[48,256]{1,0:T(8,128)(2,1)S(1)} collective-permute-done((s16[48,256]{1,0:T(8,128)(2,1)S(1)}, s16[48,256]{1,0:T(8,128)(2,1)S(1)}, u32[]{:S(2)}, u32[]{:S(2)}) %collective-permute-start.10) | collective-permute-done | bytes 24608 | tf_op jit(solution)/shard_map/ppermute | solution.py:213
  44.7 0.7 %shard_map.110 = f32[47,256]{1,0:T(8,128)} custom-call(bf16[48,256]{1,0:T(8,128)(2,1)S(1)} %get-tuple-element.32.classes_in, f32[1,256]{1,0:T(1,128)S(1)} %get-tuple-element.33.scaling, f32[47,1]{1,0:T(8,128)S(1)} %get-tuple-element.34.bias, f32[48,256]{1,0:T(8,128)S(1)} %get-tuple-element.35.own, s16[48,256]{1,0:T(8,128)(2,1)S(1)} %collective-permute-done.10.rest_0_), custom_call_target="tpu_custom_call" | custom-call | flops 1048576 | bytes 1048576 | tf_op jit(solution)/shard_map/pallas_call | solution.py:31
  (10 shorter events, 0.1 us)
Async XLA Ops:
  0.0 5.4 %collective-permute-start = (bf16[100,256]{1,0:T(8,128)(2,1)}, bf16[100,256]{1,0:T(8,128)(2,1)S(1)}, u32[]{:S(2)}, u32[]{:S(2)}) collective-permute-start(bf16[100,256]{1,0:T(8,128)(2,1)} %bitcast.7), channel_id=1, source_target_pairs={{1,0},{0,1},{3,2},{2,3},{5,4},{4,5},{7,6},{6,7},{9,8},{8,9},{11,10... | collective-permute-start | bytes 153608 | tf_op jit(solution)/shard_map/ppermute | solution.py:213
  5.6 4.6 %collective-permute-start.1 = (bf16[100,256]{1,0:T(8,128)(2,1)S(1)}, bf16[100,256]{1,0:T(8,128)(2,1)S(1)}, u32[]{:S(2)}, u32[]{:S(2)}) collective-permute-start(bf16[100,256]{1,0:T(8,128)(2,1)S(1)} %shard_map.101.refs_0_), channel_id=1, source_target_pairs={{8,0},{10,2},{12,4},{14,6},{0,8},{2,10},{4,12},{6,14},{24,16},{26,... | collective-permute-start | bytes 153608 | tf_op jit(solution)/shard_map/ppermute | solution.py:217
  7.6 6.6 %collective-permute-start.3 = (bf16[100,256]{1,0:T(8,128)(2,1)S(1)}, bf16[100,256]{1,0:T(8,128)(2,1)S(1)}, u32[]{:S(2)}, u32[]{:S(2)}) collective-permute-start(bf16[100,256]{1,0:T(8,128)(2,1)S(1)} %shard_map.101.refs_0_), channel_id=1, source_target_pairs={{16,0},{26,2},{20,4},{30,6},{24,8},{18,10},{28,12},{22,14},{0,16},... | collective-permute-start | bytes 153608 | tf_op jit(solution)/shard_map/ppermute | solution.py:217
  10.2 5.9 %collective-permute-start.2 = (bf16[100,256]{1,0:T(8,128)(2,1)S(1)}, bf16[100,256]{1,0:T(8,128)(2,1)S(1)}, u32[]{:S(2)}, u32[]{:S(2)}) collective-permute-start(bf16[100,256]{1,0:T(8,128)(2,1)S(1)} %shard_map.101.refs_0_), channel_id=1, source_target_pairs={{24,0},{18,2},{28,4},{22,6},{16,8},{26,10},{20,12},{30,14},{8,16},... | collective-permute-start | bytes 153608 | tf_op jit(solution)/shard_map/ppermute | solution.py:217
  10.2 7.5 %collective-permute-start.4 = (bf16[2,100,256]{2,1,0:T(8,128)(2,1)S(1)}, bf16[2,100,256]{2,1,0:T(8,128)(2,1)S(1)}, u32[]{:S(2)}, u32[]{:S(2)}) collective-permute-start(bf16[2,100,256]{2,1,0:T(8,128)(2,1)S(1)} %shard_map.102), channel_id=1, source_target_pairs={{4,0},{6,2},{0,4},{2,6},{12,8},{14,10},{8,12},{10,14},{20,16},{22,... | collective-permute-start | bytes 307208 | tf_op jit(solution)/shard_map/ppermute | solution.py:217
  14.2 4.1 %collective-permute-start.5 = (bf16[1,100,256]{2,1,0:T(8,128)(2,1)S(1)}, bf16[1,100,256]{2,1,0:T(8,128)(2,1)S(1)}, u32[]{:S(2)}, u32[]{:S(2)}) collective-permute-start(bf16[1,100,256]{2,1,0:T(8,128)(2,1)S(1)} %shard_map.104), channel_id=1, source_target_pairs={{4,0},{6,2},{0,4},{2,6},{12,8},{14,10},{8,12},{10,14},{20,16},{22,... | collective-permute-start | bytes 153608 | tf_op jit(solution)/shard_map/ppermute | solution.py:217
  16.1 4.1 %collective-permute-start.6 = (bf16[1,100,256]{2,1,0:T(8,128)(2,1)S(1)}, bf16[1,100,256]{2,1,0:T(8,128)(2,1)S(1)}, u32[]{:S(2)}, u32[]{:S(2)}) collective-permute-start(bf16[1,100,256]{2,1,0:T(8,128)(2,1)S(1)} %shard_map.103), channel_id=1, source_target_pairs={{4,0},{6,2},{0,4},{2,6},{12,8},{14,10},{8,12},{10,14},{20,16},{22,... | collective-permute-start | bytes 153608 | tf_op jit(solution)/shard_map/ppermute | solution.py:217
  20.3 1.8 %collective-permute-start.7 = (bf16[8,100,256]{2,1,0:T(8,128)(2,1)S(1)}, bf16[8,100,256]{2,1,0:T(8,128)(2,1)S(1)}, u32[]{:S(2)}, u32[]{:S(2)}) collective-permute-start(bf16[8,100,256]{2,1,0:T(8,128)(2,1)S(1)} %constant_dynamic-update-slice_fusion.stack), channel_id=1, source_target_pairs={{2,0},{0,2},{6,4},{4,6},{10,8},{8,10},{14,12},{12,14},{18,16},{16,... | collective-permute-start | bytes 1228808 | tf_op jit(solution)/shard_map/ppermute | solution.py:217
  23.1 4.4 %collective-permute-start.8 = (s16[144,256]{1,0:T(8,128)(2,1)S(1)}, s16[144,256]{1,0:T(8,128)(2,1)S(1)}, u32[]{:S(2)}, u32[]{:S(2)}) collective-permute-start(s16[144,256]{1,0:T(8,128)(2,1)S(1)} %get-tuple-element.31), channel_id=1, source_target_pairs={{1,0},{0,1},{3,2},{2,3},{5,4},{4,5},{7,6},{6,7},{9,8},{8,9},{11,10... | collective-permute-start | bytes 221192 | tf_op jit(solution)/shard_map/ppermute | solution.py:213
  38.9 1.4 %collective-permute-start.9 = (bf16[8,48,256]{2,1,0:T(8,128)(2,1)S(1)}, bf16[8,48,256]{2,1,0:T(8,128)(2,1)S(1)}, u32[]{:S(2)}, u32[]{:S(2)}) collective-permute-start(bf16[8,48,256]{2,1,0:T(8,128)(2,1)S(1)} %all_to_all.5.near), channel_id=1, source_target_pairs={{2,0},{0,2},{6,4},{4,6},{10,8},{8,10},{14,12},{12,14},{18,16},{16,... | collective-permute-start | bytes 589832 | tf_op jit(solution)/shard_map/ppermute | solution.py:217
  40.8 3.9 %collective-permute-start.10 = (s16[48,256]{1,0:T(8,128)(2,1)S(1)}, s16[48,256]{1,0:T(8,128)(2,1)S(1)}, u32[]{:S(2)}, u32[]{:S(2)}) collective-permute-start(s16[48,256]{1,0:T(8,128)(2,1)S(1)} %get-tuple-element.36), channel_id=1, source_target_pairs={{1,0},{0,1},{3,2},{2,3},{5,4},{4,5},{7,6},{6,7},{9,8},{8,9},{11,10... | collective-permute-start | bytes 73736 | tf_op jit(solution)/shard_map/ppermute | solution.py:213

commit v22 on v21

--- a/solution.py
+++ b/solution.py
@@ -55,16 +55,16 @@
     return nn(features[...], jnp.where(source == wanted, 1.0, 0.0).astype(BF16))
 
 
-def prepare(reps, live, *refs):
-    order, features, tiles, rows, columns, *sources = refs[:9]
-    plan, part, wanted_out, tiles_out, bias_1, bias_2, weight_1, weight_2 = refs[9:17]
-    order_in, features_in, rows_in, columns_in, row_1, row_2, weight_in, sems = refs[17:]
+def prepare(reps, features, live, *refs):
+    order, tiles, rows, columns, *sources = refs[:6]
+    plan, part, wanted_out, tiles_out, bias_1, bias_2 = refs[6:12]
+    order_in, rows_in, columns_in, row_1, row_2, sems = refs[12:]
     copies = fetched(
-        (order, features, rows, columns, *sources, tiles),
-        (order_in, features_in, rows_in, columns_in, row_1, row_2, weight_in, weight_2, tiles_out),
+        (order, rows, columns, *sources, tiles),
+        (order_in, rows_in, columns_in, row_1, row_2, tiles_out),
         sems,
     )
-    for copy in copies[:7]:
+    for copy in copies[:5]:
         copy.wait()
     tile = features.shape[1]
     slots = rows_in.shape[1]
@@ -72,17 +72,15 @@
     block, member = lax.axis_index("blk"), lax.axis_index("rep")
     wanted = order_in[:, pl.ds(pl.multiple_of(member * tile, tile), tile)]
     wanted_out[...] = wanted
-    part[...] = picked(features_in, wanted, member)
+    part[...] = picked(features, wanted, member)
     bias_1[...] = jnp.broadcast_to(row_1[...], (8, row_1.shape[1])).T[:, :1]
     bias_2[...] = jnp.broadcast_to(row_2[...], (8, row_2.shape[1])).T[:, :1]
-    weight_1[...] = weight_in[...].astype(F32).T.astype(BF16)
     for slot in range(slots):
         plan[slot] = lax.clamp(0, columns_in[0, slot] // reps, blocks - 1) ^ block
         local = rows_in[0, slot] - block * reps
         step = lax.rem(local - member + reps, reps)
         plan[slots + slot] = jnp.where((slot < live[0]) & (local >= 0) & (local < reps), step, -1)
-    for copy in copies[7:]:
-        copy.wait()
+    copies[5].wait()
 
 
 def arrange(part, wanted, *rest):
@@ -101,7 +99,8 @@
         out[index] = nn(weight_t[...], stack[index]).astype(BF16)
 
 
-def turn(tiles, plan, tiles_t, degrees):
+def turn(tiles, weight, plan, tiles_t, degrees, weight_t):
+    weight_t[...] = weight[...].astype(F32).T.astype(BF16)
     slots, tile = tiles.shape[0], tiles.shape[1]
     count = degrees.shape[0]
     total = jnp.zeros((count * ONES_ROWS, tile), F32)
@@ -289,7 +288,7 @@
 
     own_t = features.T
     others = [shifted(own_t, "rep", step) for step in range(1, reps)]
-    plan, part, wanted, tiles, bias_1, bias_2, weight_1, weight_2 = call(
+    plan, part, wanted, tiles, bias_1, bias_2 = call(
         functools.partial(prepare, reps),
         [
             pltpu.SMEM((2 * slots,), jnp.int32),
@@ -298,39 +297,33 @@
             shape(tile_values.shape[1:], BF16),
             shape((hidden, 1), F32),
             shape((classes, 1), F32),
-            shape((hidden, width), BF16),
-            shape((classes, hidden), BF16),
         ],
+        vmem=(own_t,),
         smem=(tile_live,),
         hbm=(
             node_order,
-            own_t,
             tile_values[0],
             tile_rows,
             tile_columns,
             first_bias[None],
             second_bias[None],
-            first_weight,
-            second_weight.T,
         ),
         scratch=[
             pltpu.VMEM(node_order.shape, jnp.int32),
-            pltpu.VMEM(own_t.shape, BF16),
             pltpu.SMEM((1, slots), jnp.int32),
             pltpu.SMEM((1, slots), jnp.int32),
             pltpu.VMEM((1, hidden), F32),
             pltpu.VMEM((1, classes), F32),
-            pltpu.VMEM(first_weight.shape, BF16),
-            pltpu.SemaphoreType.DMA((9,)),
+            pltpu.SemaphoreType.DMA((6,)),
         ],
         smem_outs=1,
     )
     (ordered,) = call(arrange, [shape((width, tile), BF16)], vmem=(part, wanted, *others))
     near, far = gather_features(ordered)
-    tiles_t, degrees = call(
+    tiles_t, degrees, weight_1 = call(
         turn,
-        [shape(tiles.shape, BF16), shape((reps, 8, tile), F32)],
-        vmem=(tiles,),
+        [shape(tiles.shape, BF16), shape((reps, 8, tile), F32), shape((hidden, width), BF16)],
+        vmem=(tiles, first_weight),
         smem=(plan,),
     )
     (projected,) = call(
@@ -348,7 +341,7 @@
     classes_in, scaling = call(
         combine,
         [shape((padded, tile), BF16), shape((1, tile), F32)],
-        vmem=(projected, bias_1, weight_2, degrees, own, *exchanged(sums)),
+        vmem=(projected, bias_1, second_weight.T, degrees, own, *exchanged(sums)),
     )
     own, *sums = call(
         aggregate_classes,

time: 45.6 us -> 46.4 us (1.018)
  starting transfers between devices: 15 us -> 13.7 us
  waiting for transfers between devices: 13.1 us -> 14 us
  local copies, waits for them, and re-layouts: 0.05 us -> 0.86 us
    ppermute x3, starting transfers between devices: 5.49 us -> 4.58 us  [shifted(): lax.ppermute(value, axis, [((d + step) % size, d) for d in range(size)])]
    ppermute x3, waiting for transfers between devices: 5.76 us -> 6.67 us  [shifted(): lax.ppermute(value, axis, [((d + step) % size, d) for d in range(size)])]
    unnamed x5 -> x11, local copies, waits for them, and re-layouts: 0.03 us -> 0.84 us
where the time goes in v22:
time: 46.4 us; the launch traced here: 46.1 us
  waiting for transfers between devices  14 us (30%)
  starting transfers between devices  13.7 us (30%)
  blocking collectives  11.5 us (25%)
  Pallas kernels  5.35 us (12%)
  local copies, waits for them, and re-layouts  0.86 us (2%)
  between operations  0.78 us (2%)
    all_to_all x1, blocking collectives, gather_classes(): near = lax.all_to_all(copies, 'blk', 0, 0, axis_index_groups=groups)  11.5 us
    ppermute x8, starting transfers between devices, swapped(): lax.ppermute(value, 'blk', [(d ^ masks[d % 2], d) for d in range(lax.axis...  9.08 us
    ppermute x8, waiting for transfers between devices, swapped(): lax.ppermute(value, 'blk', [(d ^ masks[d % 2], d) for d in range(lax.axis...  7.3 us
    ppermute x3, waiting for transfers between devices, shifted(): lax.ppermute(value, axis, [((d + step) % size, d) for d in range(size)])  6.67 us
    pallas_call x11, Pallas kernels, call(): pl.pallas_call(kernel, out_shape=outs, in_specs=[pl.BlockSpec(memory_spac...  5.35 us
    ppermute x3, starting transfers between devices, shifted(): lax.ppermute(value, axis, [((d + step) % size, d) for d in range(size)])  4.58 us
  transfers between devices with their start and end apart: 11, of which 8 were waited for; matrix products, arithmetic and copies ran while one was open for 0% of the time, Pallas kernels for 6%

profile of v22, /device:TPU:0, one launch (start us, length us, event | category | flops | bytes accessed | tf_op | source)
XLA Modules:
  0.0 46.1 jit_solution(4965032323780789382)
XLA Ops:
  0.0 2.9 %collective-permute-start = (bf16[100,256]{1,0:T(8,128)(2,1)}, bf16[100,256]{1,0:T(8,128)(2,1)S(1)}, u32[]{:S(2)}, u32[]{:S(2)}) collective-permute-start(bf16[100,256]{1,0:T(8,128)(2,1)} %bitcast.6), channel_id=1, source_target_pairs={{1,0},{0,1},{3,2},{2,3},{5,4},{4,5},{7,6},{6,7},{9,8},{8,9},{11,10... | collective-permute-start | bytes 153608 | tf_op jit(solution)/shard_map/ppermute | solution.py:212
  3.6 0.0 copy-start
  3.6 0.8 %copy-done = bf16[256,100]{0,1:T(8,128)(2,1)S(1)} copy-done((bf16[256,100]{0,1:T(8,128)(2,1)S(1)}, bf16[256,100]{0,1:T(8,128)(2,1)}, u32[]{:S(2)}) %copy-start) | copy-done | bytes 51224
  4.4 0.0 copy-start.1
  4.4 1.7 %shard_map.100 = (s32[32]{0:T(128)S(4)}, f32[100,256]{1,0:T(8,128)S(1)}, s32[1,256]{1,0:T(1,128)S(1)}, bf16[16,256,256]{2,1,0:T(8,128)(2,1)S(1)}, f32[128,1]{1,0:T(8,128)S(1)}, /*index=5*/f32[47,1]{1,0:T(8,128)S(1)}) custom-call(bf16[100,256]{1,0:T(8,128)(2,1)S(1)} %bitcast.7, s32[1]{0:T(128)S(6)} %copy.16.live, s32[1,512]{1,0:T(1,128)} %refs_0_.1, ...), custom_call_target="tpu_custom_call" | custom-call | flops 1048576 | bytes 1048576 | tf_op jit(solution)/shard_map/pallas_call | solution.py:31
  6.1 0.0 collective-permute-done.rest_0_
  6.1 0.2 shard_map.102.refs_0_
  6.3 1.6 %collective-permute-start.1 = (bf16[100,256]{1,0:T(8,128)(2,1)S(1)}, bf16[100,256]{1,0:T(8,128)(2,1)S(1)}, u32[]{:S(2)}, u32[]{:S(2)}) collective-permute-start(bf16[100,256]{1,0:T(8,128)(2,1)S(1)} %shard_map.102.refs_0_), channel_id=1, source_target_pairs={{8,0},{10,2},{12,4},{14,6},{0,8},{2,10},{4,12},{6,14},{24,16},{26,... | collective-permute-start | bytes 153608 | tf_op jit(solution)/shard_map/ppermute | solution.py:216
  7.9 2.6 %collective-permute-start.3 = (bf16[100,256]{1,0:T(8,128)(2,1)S(1)}, bf16[100,256]{1,0:T(8,128)(2,1)S(1)}, u32[]{:S(2)}, u32[]{:S(2)}) collective-permute-start(bf16[100,256]{1,0:T(8,128)(2,1)S(1)} %shard_map.102.refs_0_), channel_id=1, source_target_pairs={{16,0},{26,2},{20,4},{30,6},{24,8},{18,10},{28,12},{22,14},{0,16},... | collective-permute-start | bytes 153608 | tf_op jit(solution)/shard_map/ppermute | solution.py:216
  10.5 0.2 collective-permute-start.2
  10.8 0.0 collective-permute-done.1.refs_1_
  10.8 1.6 %collective-permute-start.4 = (bf16[2,100,256]{2,1,0:T(8,128)(2,1)S(1)}, bf16[2,100,256]{2,1,0:T(8,128)(2,1)S(1)}, u32[]{:S(2)}, u32[]{:S(2)}) collective-permute-start(bf16[2,100,256]{2,1,0:T(8,128)(2,1)S(1)} %shard_map.103), channel_id=1, source_target_pairs={{4,0},{6,2},{0,4},{2,6},{12,8},{14,10},{8,12},{10,14},{20,16},{22,... | collective-permute-start | bytes 307208 | tf_op jit(solution)/shard_map/ppermute | solution.py:216
  12.4 2.0 %collective-permute-done.3.refs_0_ = bf16[100,256]{1,0:T(8,128)(2,1)S(1)} collective-permute-done((bf16[100,256]{1,0:T(8,128)(2,1)S(1)}, bf16[100,256]{1,0:T(8,128)(2,1)S(1)}, u32[]{:S(2)}, u32[]{:S(2)}) %collective-permute-start.3) | collective-permute-done | bytes 51232 | tf_op jit(solution)/shard_map/ppermute | solution.py:216
  14.4 1.5 %collective-permute-start.5 = (bf16[1,100,256]{2,1,0:T(8,128)(2,1)S(1)}, bf16[1,100,256]{2,1,0:T(8,128)(2,1)S(1)}, u32[]{:S(2)}, u32[]{:S(2)}) collective-permute-start(bf16[1,100,256]{2,1,0:T(8,128)(2,1)S(1)} %shard_map.105), channel_id=1, source_target_pairs={{4,0},{6,2},{0,4},{2,6},{12,8},{14,10},{8,12},{10,14},{20,16},{22,... | collective-permute-start | bytes 153608 | tf_op jit(solution)/shard_map/ppermute | solution.py:216
  15.9 0.5 %collective-permute-done.2.refs_0_ = bf16[100,256]{1,0:T(8,128)(2,1)S(1)} collective-permute-done((bf16[100,256]{1,0:T(8,128)(2,1)S(1)}, bf16[100,256]{1,0:T(8,128)(2,1)S(1)}, u32[]{:S(2)}, u32[]{:S(2)}) %collective-permute-start.2) | collective-permute-done | bytes 51232 | tf_op jit(solution)/shard_map/ppermute | solution.py:216
  16.5 1.5 %collective-permute-start.6 = (bf16[1,100,256]{2,1,0:T(8,128)(2,1)S(1)}, bf16[1,100,256]{2,1,0:T(8,128)(2,1)S(1)}, u32[]{:S(2)}, u32[]{:S(2)}) collective-permute-start(bf16[1,100,256]{2,1,0:T(8,128)(2,1)S(1)} %shard_map.104), channel_id=1, source_target_pairs={{4,0},{6,2},{0,4},{2,6},{12,8},{14,10},{8,12},{10,14},{20,16},{22,... | collective-permute-start | bytes 153608 | tf_op jit(solution)/shard_map/ppermute | solution.py:216
  18.0 0.0 collective-permute-done.4
  18.0 0.6 %collective-permute-done.5 = bf16[1,100,256]{2,1,0:T(8,128)(2,1)S(1)} collective-permute-done((bf16[1,100,256]{2,1,0:T(8,128)(2,1)S(1)}, bf16[1,100,256]{2,1,0:T(8,128)(2,1)S(1)}, u32[]{:S(2)}, u32[]{:S(2)}) %collective-permute-start.5) | collective-permute-done | bytes 51232 | tf_op jit(solution)/shard_map/ppermute | solution.py:216
  18.6 2.0 %collective-permute-done.6 = bf16[1,100,256]{2,1,0:T(8,128)(2,1)S(1)} collective-permute-done((bf16[1,100,256]{2,1,0:T(8,128)(2,1)S(1)}, bf16[1,100,256]{2,1,0:T(8,128)(2,1)S(1)}, u32[]{:S(2)}, u32[]{:S(2)}) %collective-permute-start.6) | collective-permute-done | bytes 51232 | tf_op jit(solution)/shard_map/ppermute | solution.py:216
  20.6 0.0 collective-permute-start.7
  20.6 0.0 copy-done.1
  20.6 0.7 %shard_map.101 = (bf16[16,256,256]{2,1,0:T(8,128)(2,1)S(1)}, f32[2,8,256]{2,1,0:T(8,128)S(1)}, bf16[128,100]{1,0:T(8,128)(2,1)S(1)}) custom-call(bf16[16,256,256]{2,1,0:T(8,128)(2,1)S(1)} %get-tuple-element.20.tiles, bf16[100,128]{1,0:T(8,128)(2,1)S(1)} %copy-done.1, s32[32]{0:T(128)S(4)} %get-tuple-element.21.plan), custom_call_target="tpu_custom_call" | custom-call | flops 1048576 | bytes 1048576 | tf_op jit(solution)/shard_map/pallas_call | solution.py:31
  21.4 0.0 copy-start.2
  21.4 0.3 shard_map.106.projected.hidden_in
  21.7 0.7 %collective-permute-done.7.far = bf16[8,100,256]{2,1,0:T(8,128)(2,1)S(1)} collective-permute-done((bf16[8,100,256]{2,1,0:T(8,128)(2,1)S(1)}, bf16[8,100,256]{2,1,0:T(8,128)(2,1)S(1)}, u32[]{:S(2)}, u32[]{:S(2)}) %collective-permute-start.7) | collective-permute-done | bytes 409632 | tf_op jit(solution)/shard_map/ppermute | solution.py:216
  22.4 1.0 %shard_map.107 = (f32[128,256]{1,0:T(8,128)S(1)}, s16[144,256]{1,0:T(8,128)(2,1)S(1)}) custom-call(bf16[8,128,256]{2,1,0:T(8,128)(2,1)S(1)} %shard_map.106.projected.hidden_in, bf16[8,100,256]{2,1,0:T(8,128)(2,1)S(1)} %collective-permute-done.7.far, bf16[128,100]{1,0:T(8,128)(2,1)S(1)} %get-tuple-element.22.weight_t, ...), custom_call_target="tpu_custom_call" | custom-call | flops 1048576 | bytes 1048576 | tf_op jit(solution)/shard_map/pallas_call | solution.py:31
  23.4 1.2 %collective-permute-start.8 = (s16[144,256]{1,0:T(8,128)(2,1)S(1)}, s16[144,256]{1,0:T(8,128)(2,1)S(1)}, u32[]{:S(2)}, u32[]{:S(2)}) collective-permute-start(s16[144,256]{1,0:T(8,128)(2,1)S(1)} %get-tuple-element.29), channel_id=1, source_target_pairs={{1,0},{0,1},{3,2},{2,3},{5,4},{4,5},{7,6},{6,7},{9,8},{8,9},{11,10... | collective-permute-start | bytes 221192 | tf_op jit(solution)/shard_map/ppermute | solution.py:212
  24.6 3.2 %collective-permute-done.8.rest_0_ = s16[144,256]{1,0:T(8,128)(2,1)S(1)} collective-permute-done((s16[144,256]{1,0:T(8,128)(2,1)S(1)}, s16[144,256]{1,0:T(8,128)(2,1)S(1)}, u32[]{:S(2)}, u32[]{:S(2)}) %collective-permute-start.8) | collective-permute-done | bytes 73760 | tf_op jit(solution)/shard_map/ppermute | solution.py:212
  27.8 0.0 copy-done.2
  27.8 0.2 shard_map.108
  28.1 11.5 %all_to_all.5.near = bf16[8,48,256]{2,1,0:T(8,128)(2,1)S(1)} all-to-all(bf16[8,48,256]{2,1,0:T(8,128)(2,1)S(1)} %broadcast_in_dim.14), channel_id=1, replica_groups={{0,4,8,12,16,20,24,28},{2,6,10,14,18,22,26,30},{1,5,9,13,17,21,25,29},{..., dimensions={0} | all-to-all | bytes 393216 | tf_op jit(solution)/shard_map/all_to_all | solution.py:262
  39.6 0.0 collective-permute-start.9
  39.6 1.4 %collective-permute-done.9.far = bf16[8,48,256]{2,1,0:T(8,128)(2,1)S(1)} collective-permute-done((bf16[8,48,256]{2,1,0:T(8,128)(2,1)S(1)}, bf16[8,48,256]{2,1,0:T(8,128)(2,1)S(1)}, u32[]{:S(2)}, u32[]{:S(2)}) %collective-permute-start.9) | collective-permute-done | bytes 196640 | tf_op jit(solution)/shard_map/ppermute | solution.py:216
  41.0 0.5 %shard_map.109 = (f32[48,256]{1,0:T(8,128)S(1)}, s16[48,256]{1,0:T(8,128)(2,1)S(1)}) custom-call(bf16[8,48,256]{2,1,0:T(8,128)(2,1)S(1)} %all_to_all.5.near, bf16[8,48,256]{2,1,0:T(8,128)(2,1)S(1)} %collective-permute-done.9.far, bf16[16,256,256]{2,1,0:T(8,128)(2,1)S(1)} %get-tuple-element.27.tiles_t, s32[32]{0:T(128)S(4)} %get-tuple-element.21.plan), custom_call_target="tpu_custom_call" | custom-call | flops 1048576 | bytes 1048576 | tf_op jit(solution)/shard_map/pallas_call | solution.py:31
  41.5 0.4 collective-permute-start.10
  42.0 3.5 %collective-permute-done.10.rest_0_ = s16[48,256]{1,0:T(8,128)(2,1)S(1)} collective-permute-done((s16[48,256]{1,0:T(8,128)(2,1)S(1)}, s16[48,256]{1,0:T(8,128)(2,1)S(1)}, u32[]{:S(2)}, u32[]{:S(2)}) %collective-permute-start.10) | collective-permute-done | bytes 24608 | tf_op jit(solution)/shard_map/ppermute | solution.py:212
  45.4 0.7 %shard_map.110 = f32[47,256]{1,0:T(8,128)} custom-call(bf16[48,256]{1,0:T(8,128)(2,1)S(1)} %get-tuple-element.30.classes_in, f32[1,256]{1,0:T(1,128)S(1)} %get-tuple-element.31.scaling, f32[47,1]{1,0:T(8,128)S(1)} %get-tuple-element.32.bias, f32[48,256]{1,0:T(8,128)S(1)} %get-tuple-element.33.own, s16[48,256]{1,0:T(8,128)(2,1)S(1)} %collective-permute-done.10.rest_0_), custom_call_target="tpu_custom_call" | custom-call | flops 1048576 | bytes 1048576 | tf_op jit(solution)/shard_map/pallas_call | solution.py:31
  (10 shorter events, 0.1 us)
Async XLA Ops:
  0.0 6.1 %collective-permute-start = (bf16[100,256]{1,0:T(8,128)(2,1)}, bf16[100,256]{1,0:T(8,128)(2,1)S(1)}, u32[]{:S(2)}, u32[]{:S(2)}) collective-permute-start(bf16[100,256]{1,0:T(8,128)(2,1)} %bitcast.6), channel_id=1, source_target_pairs={{1,0},{0,1},{3,2},{2,3},{5,4},{4,5},{7,6},{6,7},{9,8},{8,9},{11,10... | collective-permute-start | bytes 153608 | tf_op jit(solution)/shard_map/ppermute | solution.py:212
  3.6 0.8 %copy-start = (bf16[256,100]{0,1:T(8,128)(2,1)S(1)}, bf16[256,100]{0,1:T(8,128)(2,1)}, u32[]{:S(2)}) copy-start(bf16[256,100]{0,1:T(8,128)(2,1)} %param.10) | copy-start | bytes 153604
  4.4 16.2 %copy-start.1 = (bf16[100,128]{1,0:T(8,128)(2,1)S(1)}, bf16[100,128]{1,0:T(8,128)(2,1)}, u32[]{:S(2)}) copy-start(bf16[100,128]{1,0:T(8,128)(2,1)} %weight.1) | copy-start | bytes 76804
  6.3 4.5 %collective-permute-start.1 = (bf16[100,256]{1,0:T(8,128)(2,1)S(1)}, bf16[100,256]{1,0:T(8,128)(2,1)S(1)}, u32[]{:S(2)}, u32[]{:S(2)}) collective-permute-start(bf16[100,256]{1,0:T(8,128)(2,1)S(1)} %shard_map.102.refs_0_), channel_id=1, source_target_pairs={{8,0},{10,2},{12,4},{14,6},{0,8},{2,10},{4,12},{6,14},{24,16},{26,... | collective-permute-start | bytes 153608 | tf_op jit(solution)/shard_map/ppermute | solution.py:216
  7.9 6.5 %collective-permute-start.3 = (bf16[100,256]{1,0:T(8,128)(2,1)S(1)}, bf16[100,256]{1,0:T(8,128)(2,1)S(1)}, u32[]{:S(2)}, u32[]{:S(2)}) collective-permute-start(bf16[100,256]{1,0:T(8,128)(2,1)S(1)} %shard_map.102.refs_0_), channel_id=1, source_target_pairs={{16,0},{26,2},{20,4},{30,6},{24,8},{18,10},{28,12},{22,14},{0,16},... | collective-permute-start | bytes 153608 | tf_op jit(solution)/shard_map/ppermute | solution.py:216
  10.5 5.9 %collective-permute-start.2 = (bf16[100,256]{1,0:T(8,128)(2,1)S(1)}, bf16[100,256]{1,0:T(8,128)(2,1)S(1)}, u32[]{:S(2)}, u32[]{:S(2)}) collective-permute-start(bf16[100,256]{1,0:T(8,128)(2,1)S(1)} %shard_map.102.refs_0_), channel_id=1, source_target_pairs={{24,0},{18,2},{28,4},{22,6},{16,8},{26,10},{20,12},{30,14},{8,16},... | collective-permute-start | bytes 153608 | tf_op jit(solution)/shard_map/ppermute | solution.py:216
  10.8 7.2 %collective-permute-start.4 = (bf16[2,100,256]{2,1,0:T(8,128)(2,1)S(1)}, bf16[2,100,256]{2,1,0:T(8,128)(2,1)S(1)}, u32[]{:S(2)}, u32[]{:S(2)}) collective-permute-start(bf16[2,100,256]{2,1,0:T(8,128)(2,1)S(1)} %shard_map.103), channel_id=1, source_target_pairs={{4,0},{6,2},{0,4},{2,6},{12,8},{14,10},{8,12},{10,14},{20,16},{22,... | collective-permute-start | bytes 307208 | tf_op jit(solution)/shard_map/ppermute | solution.py:216
  14.4 4.2 %collective-permute-start.5 = (bf16[1,100,256]{2,1,0:T(8,128)(2,1)S(1)}, bf16[1,100,256]{2,1,0:T(8,128)(2,1)S(1)}, u32[]{:S(2)}, u32[]{:S(2)}) collective-permute-start(bf16[1,100,256]{2,1,0:T(8,128)(2,1)S(1)} %shard_map.105), channel_id=1, source_target_pairs={{4,0},{6,2},{0,4},{2,6},{12,8},{14,10},{8,12},{10,14},{20,16},{22,... | collective-permute-start | bytes 153608 | tf_op jit(solution)/shard_map/ppermute | solution.py:216
  16.5 4.1 %collective-permute-start.6 = (bf16[1,100,256]{2,1,0:T(8,128)(2,1)S(1)}, bf16[1,100,256]{2,1,0:T(8,128)(2,1)S(1)}, u32[]{:S(2)}, u32[]{:S(2)}) collective-permute-start(bf16[1,100,256]{2,1,0:T(8,128)(2,1)S(1)} %shard_map.104), channel_id=1, source_target_pairs={{4,0},{6,2},{0,4},{2,6},{12,8},{14,10},{8,12},{10,14},{20,16},{22,... | collective-permute-start | bytes 153608 | tf_op jit(solution)/shard_map/ppermute | solution.py:216
  20.6 1.8 %collective-permute-start.7 = (bf16[8,100,256]{2,1,0:T(8,128)(2,1)S(1)}, bf16[8,100,256]{2,1,0:T(8,128)(2,1)S(1)}, u32[]{:S(2)}, u32[]{:S(2)}) collective-permute-start(bf16[8,100,256]{2,1,0:T(8,128)(2,1)S(1)} %constant_dynamic-update-slice_fusion.stack), channel_id=1, source_target_pairs={{2,0},{0,2},{6,4},{4,6},{10,8},{8,10},{14,12},{12,14},{18,16},{16,... | collective-permute-start | bytes 1228808 | tf_op jit(solution)/shard_map/ppermute | solution.py:216
  21.4 6.5 %copy-start.2 = (bf16[128,47]{0,1:T(8,128)(2,1)S(1)}, bf16[128,47]{0,1:T(8,128)(2,1)}, u32[]{:S(2)}) copy-start(bf16[128,47]{0,1:T(8,128)(2,1)} %param.18) | copy-start | bytes 36100
  23.4 4.4 %collective-permute-start.8 = (s16[144,256]{1,0:T(8,128)(2,1)S(1)}, s16[144,256]{1,0:T(8,128)(2,1)S(1)}, u32[]{:S(2)}, u32[]{:S(2)}) collective-permute-start(s16[144,256]{1,0:T(8,128)(2,1)S(1)} %get-tuple-element.29), channel_id=1, source_target_pairs={{1,0},{0,1},{3,2},{2,3},{5,4},{4,5},{7,6},{6,7},{9,8},{8,9},{11,10... | collective-permute-start | bytes 221192 | tf_op jit(solution)/shard_map/ppermute | solution.py:212
  39.6 1.4 %collective-permute-start.9 = (bf16[8,48,256]{2,1,0:T(8,128)(2,1)S(1)}, bf16[8,48,256]{2,1,0:T(8,128)(2,1)S(1)}, u32[]{:S(2)}, u32[]{:S(2)}) collective-permute-start(bf16[8,48,256]{2,1,0:T(8,128)(2,1)S(1)} %all_to_all.5.near), channel_id=1, source_target_pairs={{2,0},{0,2},{6,4},{4,6},{10,8},{8,10},{14,12},{12,14},{18,16},{16,... | collective-permute-start | bytes 589832 | tf_op jit(solution)/shard_map/ppermute | solution.py:216
  41.5 3.9 %collective-permute-start.10 = (s16[48,256]{1,0:T(8,128)(2,1)S(1)}, s16[48,256]{1,0:T(8,128)(2,1)S(1)}, u32[]{:S(2)}, u32[]{:S(2)}) collective-permute-start(s16[48,256]{1,0:T(8,128)(2,1)S(1)} %get-tuple-element.34), channel_id=1, source_target_pairs={{1,0},{0,1},{3,2},{2,3},{5,4},{4,5},{7,6},{6,7},{9,8},{8,9},{11,10... | collective-permute-start | bytes 73736 | tf_op jit(solution)/shard_map/ppermute | solution.py:212

commit v23 on v21

--- a/solution.py
+++ b/solution.py
@@ -232,7 +232,7 @@
     for here in (core, 1 - core):
         early, late = ([4 * jnp.where(here == 0, *sides) for sides in way] for way in two_ways(pairs))
         over = [apart + 2 for apart in [0, 4 * first, *early, *late]]
-        lists.append([0, 4 * first, *late, *early, *over])
+        lists.append([0, 4 * first, *early, *late, *over])
     return lists[0], [apart ^ 1 for apart in lists[1]]
 
 
@@ -252,7 +252,7 @@
     early, late = ([swapped(value, (4 * a, 4 * b)) for a, b in way] for way in two_ways(pairs))
     stacks = packed(value, ahead), packed(*early), packed(*late)
     over = [swapped(stack, (2, 2)) for stack in stacks]
-    near = jnp.concatenate([stacks[0], stacks[2], stacks[1], *over])
+    near = jnp.concatenate([*stacks, *over])
     return near, swapped(near, (1, 1))
 
 

time: 45.6 us -> 45.4 us (level)
  waiting for transfers between devices: 13.1 us -> 11.8 us
  starting transfers between devices: 15 us -> 15.8 us
    ppermute x8, waiting for transfers between devices: 7.32 us -> 6.63 us  [swapped(): lax.ppermute(value, 'blk', [(d ^ masks[d % 2], d) for d in range(lax.axis...]
    ppermute x3, starting transfers between devices: 5.49 us -> 6.05 us  [shifted(): lax.ppermute(value, axis, [((d + step) % size, d) for d in range(size)])]
    ppermute x3, waiting for transfers between devices: 5.76 us -> 5.2 us  [shifted(): lax.ppermute(value, axis, [((d + step) % size, d) for d in range(size)])]
  transfers between devices with their start and end apart: 11 -> 11, of which waited for: 8 -> 7; matrix products, arithmetic and copies ran while one was open for 0% -> 0% of each run, Pallas kernels for 6% -> 6%
where the time goes in v23:
time: 45.4 us; the launch traced here: 45.2 us
  starting transfers between devices  15.8 us (35%)
  waiting for transfers between devices  11.8 us (26%)
  blocking collectives  11.3 us (25%)
  Pallas kernels  5.43 us (12%)
  between operations  0.77 us (2%)
    all_to_all x1, blocking collectives, gather_classes(): near = lax.all_to_all(copies, 'blk', 0, 0, axis_index_groups=groups)  11.3 us
    ppermute x8, starting transfers between devices, swapped(): lax.ppermute(value, 'blk', [(d ^ masks[d % 2], d) for d in range(lax.axis...  9.78 us
    ppermute x8, waiting for transfers between devices, swapped(): lax.ppermute(value, 'blk', [(d ^ masks[d % 2], d) for d in range(lax.axis...  6.63 us
    ppermute x3, starting transfers between devices, shifted(): lax.ppermute(value, axis, [((d + step) % size, d) for d in range(size)])  6.05 us
    pallas_call x11, Pallas kernels, call(): pl.pallas_call(kernel, out_shape=outs, in_specs=[pl.BlockSpec(memory_spac...  5.43 us
    ppermute x3, waiting for transfers between devices, shifted(): lax.ppermute(value, axis, [((d + step) % size, d) for d in range(size)])  5.2 us
  transfers between devices with their start and end apart: 11, of which 7 were waited for; matrix products, arithmetic and copies ran while one was open for 0% of the time, Pallas kernels for 6%

profile of v23, /device:TPU:0, one launch (start us, length us, event | category | flops | bytes accessed | tf_op | source)
XLA Modules:
  0.0 45.2 jit_solution(8018096979451458684)
XLA Ops:
  0.0 2.9 %collective-permute-start = (bf16[100,256]{1,0:T(8,128)(2,1)}, bf16[100,256]{1,0:T(8,128)(2,1)S(1)}, u32[]{:S(2)}, u32[]{:S(2)}) collective-permute-start(bf16[100,256]{1,0:T(8,128)(2,1)} %bitcast.7), channel_id=1, source_target_pairs={{1,0},{0,1},{3,2},{2,3},{5,4},{4,5},{7,6},{6,7},{9,8},{8,9},{11,10... | collective-permute-start | bytes 153608 | tf_op jit(solution)/shard_map/ppermute | solution.py:213
  3.6 1.8 %shard_map.100 = (s32[32]{0:T(128)S(4)}, f32[100,256]{1,0:T(8,128)S(1)}, s32[1,256]{1,0:T(1,128)S(1)}, bf16[16,256,256]{2,1,0:T(8,128)(2,1)S(1)}, f32[128,1]{1,0...) custom-call(s32[1]{0:T(128)S(6)} %copy.16.live, s32[1,512]{1,0:T(1,128)} %refs_0_.1, ...), custom_call_target="tpu_custom_call" | custom-call | flops 1048576 | bytes 1048576 | tf_op jit(solution)/shard_map/pallas_call | solution.py:31
  5.4 0.0 collective-permute-done.rest_0_
  5.4 0.2 shard_map.101.refs_0_
  5.6 2.0 %collective-permute-start.1 = (bf16[100,256]{1,0:T(8,128)(2,1)S(1)}, bf16[100,256]{1,0:T(8,128)(2,1)S(1)}, u32[]{:S(2)}, u32[]{:S(2)}) collective-permute-start(bf16[100,256]{1,0:T(8,128)(2,1)S(1)} %shard_map.101.refs_0_), channel_id=1, source_target_pairs={{8,0},{10,2},{12,4},{14,6},{0,8},{2,10},{4,12},{6,14},{24,16},{26,... | collective-permute-start | bytes 153608 | tf_op jit(solution)/shard_map/ppermute | solution.py:217
  7.6 2.5 %collective-permute-start.3 = (bf16[100,256]{1,0:T(8,128)(2,1)S(1)}, bf16[100,256]{1,0:T(8,128)(2,1)S(1)}, u32[]{:S(2)}, u32[]{:S(2)}) collective-permute-start(bf16[100,256]{1,0:T(8,128)(2,1)S(1)} %shard_map.101.refs_0_), channel_id=1, source_target_pairs={{24,0},{18,2},{28,4},{22,6},{16,8},{26,10},{20,12},{30,14},{8,16},... | collective-permute-start | bytes 153608 | tf_op jit(solution)/shard_map/ppermute | solution.py:217
  10.1 0.1 collective-permute-start.2
  10.2 0.0 collective-permute-done.1.refs_1_
  10.2 2.0 %collective-permute-start.4 = (bf16[2,100,256]{2,1,0:T(8,128)(2,1)S(1)}, bf16[2,100,256]{2,1,0:T(8,128)(2,1)S(1)}, u32[]{:S(2)}, u32[]{:S(2)}) collective-permute-start(bf16[2,100,256]{2,1,0:T(8,128)(2,1)S(1)} %shard_map.102), channel_id=1, source_target_pairs={{4,0},{6,2},{0,4},{2,6},{12,8},{14,10},{8,12},{10,14},{20,16},{22,... | collective-permute-start | bytes 307208 | tf_op jit(solution)/shard_map/ppermute | solution.py:217
  12.3 1.6 %collective-permute-done.3.refs_0_ = bf16[100,256]{1,0:T(8,128)(2,1)S(1)} collective-permute-done((bf16[100,256]{1,0:T(8,128)(2,1)S(1)}, bf16[100,256]{1,0:T(8,128)(2,1)S(1)}, u32[]{:S(2)}, u32[]{:S(2)}) %collective-permute-start.3) | collective-permute-done | bytes 51232 | tf_op jit(solution)/shard_map/ppermute | solution.py:217
  13.9 1.5 %collective-permute-start.6 = (bf16[1,100,256]{2,1,0:T(8,128)(2,1)S(1)}, bf16[1,100,256]{2,1,0:T(8,128)(2,1)S(1)}, u32[]{:S(2)}, u32[]{:S(2)}) collective-permute-start(bf16[1,100,256]{2,1,0:T(8,128)(2,1)S(1)} %shard_map.104), channel_id=1, source_target_pairs={{4,0},{6,2},{0,4},{2,6},{12,8},{14,10},{8,12},{10,14},{20,16},{22,... | collective-permute-start | bytes 153608 | tf_op jit(solution)/shard_map/ppermute | solution.py:217
  15.4 0.3 collective-permute-done.2.refs_0_
  15.7 1.5 %collective-permute-start.5 = (bf16[1,100,256]{2,1,0:T(8,128)(2,1)S(1)}, bf16[1,100,256]{2,1,0:T(8,128)(2,1)S(1)}, u32[]{:S(2)}, u32[]{:S(2)}) collective-permute-start(bf16[1,100,256]{2,1,0:T(8,128)(2,1)S(1)} %shard_map.103), channel_id=1, source_target_pairs={{4,0},{6,2},{0,4},{2,6},{12,8},{14,10},{8,12},{10,14},{20,16},{22,... | collective-permute-start | bytes 153608 | tf_op jit(solution)/shard_map/ppermute | solution.py:217
  17.2 0.0 collective-permute-done.4
  17.3 2.6 %collective-permute-done.5 = bf16[1,100,256]{2,1,0:T(8,128)(2,1)S(1)} collective-permute-done((bf16[1,100,256]{2,1,0:T(8,128)(2,1)S(1)}, bf16[1,100,256]{2,1,0:T(8,128)(2,1)S(1)}, u32[]{:S(2)}, u32[]{:S(2)}) %collective-permute-start.5) | collective-permute-done | bytes 51232 | tf_op jit(solution)/shard_map/ppermute | solution.py:217
  19.8 0.0 collective-permute-done.6
  19.9 0.1 collective-permute-start.7
  19.9 0.7 %shard_map.106 = (bf16[16,256,256]{2,1,0:T(8,128)(2,1)S(1)}, f32[2,8,256]{2,1,0:T(8,128)S(1)}) custom-call(bf16[16,256,256]{2,1,0:T(8,128)(2,1)S(1)} %get-tuple-element.26.tiles, s32[32]{0:T(128)S(4)} %get-tuple-element.27.plan), custom_call_target="tpu_custom_call" | custom-call | flops 1048576 | bytes 1048576 | tf_op jit(solution)/shard_map/pallas_call | solution.py:31
  20.7 0.3 shard_map.105.projected.hidden_in
  21.0 0.7 %collective-permute-done.7.far = bf16[8,100,256]{2,1,0:T(8,128)(2,1)S(1)} collective-permute-done((bf16[8,100,256]{2,1,0:T(8,128)(2,1)S(1)}, bf16[8,100,256]{2,1,0:T(8,128)(2,1)S(1)}, u32[]{:S(2)}, u32[]{:S(2)}) %collective-permute-start.7) | collective-permute-done | bytes 409632 | tf_op jit(solution)/shard_map/ppermute | solution.py:217
  21.7 1.0 %shard_map.107 = (f32[128,256]{1,0:T(8,128)S(1)}, s16[144,256]{1,0:T(8,128)(2,1)S(1)}) custom-call(bf16[8,128,256]{2,1,0:T(8,128)(2,1)S(1)} %shard_map.105.projected.hidden_in, bf16[8,100,256]{2,1,0:T(8,128)(2,1)S(1)} %collective-permute-done.7.far, bf16[128,100]{1,0:T(8,128)(2,1)S(1)} %get-tuple-element.21.weight_t, ...), custom_call_target="tpu_custom_call" | custom-call | flops 1048576 | bytes 1048576 | tf_op jit(solution)/shard_map/pallas_call | solution.py:31
  22.7 1.6 %collective-permute-start.8 = (s16[144,256]{1,0:T(8,128)(2,1)S(1)}, s16[144,256]{1,0:T(8,128)(2,1)S(1)}, u32[]{:S(2)}, u32[]{:S(2)}) collective-permute-start(s16[144,256]{1,0:T(8,128)(2,1)S(1)} %get-tuple-element.31), channel_id=1, source_target_pairs={{1,0},{0,1},{3,2},{2,3},{5,4},{4,5},{7,6},{6,7},{9,8},{8,9},{11,10... | collective-permute-start | bytes 221192 | tf_op jit(solution)/shard_map/ppermute | solution.py:213
  24.3 2.9 %collective-permute-done.8.rest_0_ = s16[144,256]{1,0:T(8,128)(2,1)S(1)} collective-permute-done((s16[144,256]{1,0:T(8,128)(2,1)S(1)}, s16[144,256]{1,0:T(8,128)(2,1)S(1)}, u32[]{:S(2)}, u32[]{:S(2)}) %collective-permute-start.8) | collective-permute-done | bytes 73760 | tf_op jit(solution)/shard_map/ppermute | solution.py:213
  27.1 0.2 shard_map.108
  27.4 11.3 %all_to_all.5.near = bf16[8,48,256]{2,1,0:T(8,128)(2,1)S(1)} all-to-all(bf16[8,48,256]{2,1,0:T(8,128)(2,1)S(1)} %broadcast_in_dim.14), channel_id=1, replica_groups={{0,4,8,12,16,20,24,28},{2,6,10,14,18,22,26,30},{1,5,9,13,17,21,25,29},{..., dimensions={0} | all-to-all | bytes 393216 | tf_op jit(solution)/shard_map/all_to_all | solution.py:263
  38.6 0.0 collective-permute-start.9
  38.6 1.4 %collective-permute-done.9.far = bf16[8,48,256]{2,1,0:T(8,128)(2,1)S(1)} collective-permute-done((bf16[8,48,256]{2,1,0:T(8,128)(2,1)S(1)}, bf16[8,48,256]{2,1,0:T(8,128)(2,1)S(1)}, u32[]{:S(2)}, u32[]{:S(2)}) %collective-permute-start.9) | collective-permute-done | bytes 196640 | tf_op jit(solution)/shard_map/ppermute | solution.py:217
  40.1 0.5 %shard_map.109 = (f32[48,256]{1,0:T(8,128)S(1)}, s16[48,256]{1,0:T(8,128)(2,1)S(1)}) custom-call(bf16[8,48,256]{2,1,0:T(8,128)(2,1)S(1)} %all_to_all.5.near, bf16[8,48,256]{2,1,0:T(8,128)(2,1)S(1)} %collective-permute-done.9.far, bf16[16,256,256]{2,1,0:T(8,128)(2,1)S(1)} %get-tuple-element.29.tiles_t, s32[32]{0:T(128)S(4)} %get-tuple-element.27.plan), custom_call_target="tpu_custom_call" | custom-call | flops 1048576 | bytes 1048576 | tf_op jit(solution)/shard_map/pallas_call | solution.py:31
  40.6 1.6 %collective-permute-start.10 = (s16[48,256]{1,0:T(8,128)(2,1)S(1)}, s16[48,256]{1,0:T(8,128)(2,1)S(1)}, u32[]{:S(2)}, u32[]{:S(2)}) collective-permute-start(s16[48,256]{1,0:T(8,128)(2,1)S(1)} %get-tuple-element.36), channel_id=1, source_target_pairs={{1,0},{0,1},{3,2},{2,3},{5,4},{4,5},{7,6},{6,7},{9,8},{8,9},{11,10... | collective-permute-start | bytes 73736 | tf_op jit(solution)/shard_map/ppermute | solution.py:213
  42.2 2.3 %collective-permute-done.10.rest_0_ = s16[48,256]{1,0:T(8,128)(2,1)S(1)} collective-permute-done((s16[48,256]{1,0:T(8,128)(2,1)S(1)}, s16[48,256]{1,0:T(8,128)(2,1)S(1)}, u32[]{:S(2)}, u32[]{:S(2)}) %collective-permute-start.10) | collective-permute-done | bytes 24608 | tf_op jit(solution)/shard_map/ppermute | solution.py:213
  44.5 0.7 %shard_map.110 = f32[47,256]{1,0:T(8,128)} custom-call(bf16[48,256]{1,0:T(8,128)(2,1)S(1)} %get-tuple-element.32.classes_in, f32[1,256]{1,0:T(1,128)S(1)} %get-tuple-element.33.scaling, f32[47,1]{1,0:T(8,128)S(1)} %get-tuple-element.34.bias, f32[48,256]{1,0:T(8,128)S(1)} %get-tuple-element.35.own, s16[48,256]{1,0:T(8,128)(2,1)S(1)} %collective-permute-done.10.rest_0_), custom_call_target="tpu_custom_call" | custom-call | flops 1048576 | bytes 1048576 | tf_op jit(solution)/shard_map/pallas_call | solution.py:31
  (10 shorter events, 0.1 us)
Async XLA Ops:
  0.0 5.4 %collective-permute-start = (bf16[100,256]{1,0:T(8,128)(2,1)}, bf16[100,256]{1,0:T(8,128)(2,1)S(1)}, u32[]{:S(2)}, u32[]{:S(2)}) collective-permute-start(bf16[100,256]{1,0:T(8,128)(2,1)} %bitcast.7), channel_id=1, source_target_pairs={{1,0},{0,1},{3,2},{2,3},{5,4},{4,5},{7,6},{6,7},{9,8},{8,9},{11,10... | collective-permute-start | bytes 153608 | tf_op jit(solution)/shard_map/ppermute | solution.py:213
  5.6 4.6 %collective-permute-start.1 = (bf16[100,256]{1,0:T(8,128)(2,1)S(1)}, bf16[100,256]{1,0:T(8,128)(2,1)S(1)}, u32[]{:S(2)}, u32[]{:S(2)}) collective-permute-start(bf16[100,256]{1,0:T(8,128)(2,1)S(1)} %shard_map.101.refs_0_), channel_id=1, source_target_pairs={{8,0},{10,2},{12,4},{14,6},{0,8},{2,10},{4,12},{6,14},{24,16},{26,... | collective-permute-start | bytes 153608 | tf_op jit(solution)/shard_map/ppermute | solution.py:217
  7.6 6.3 %collective-permute-start.3 = (bf16[100,256]{1,0:T(8,128)(2,1)S(1)}, bf16[100,256]{1,0:T(8,128)(2,1)S(1)}, u32[]{:S(2)}, u32[]{:S(2)}) collective-permute-start(bf16[100,256]{1,0:T(8,128)(2,1)S(1)} %shard_map.101.refs_0_), channel_id=1, source_target_pairs={{24,0},{18,2},{28,4},{22,6},{16,8},{26,10},{20,12},{30,14},{8,16},... | collective-permute-start | bytes 153608 | tf_op jit(solution)/shard_map/ppermute | solution.py:217
  10.1 5.6 %collective-permute-start.2 = (bf16[100,256]{1,0:T(8,128)(2,1)S(1)}, bf16[100,256]{1,0:T(8,128)(2,1)S(1)}, u32[]{:S(2)}, u32[]{:S(2)}) collective-permute-start(bf16[100,256]{1,0:T(8,128)(2,1)S(1)} %shard_map.101.refs_0_), channel_id=1, source_target_pairs={{16,0},{26,2},{20,4},{30,6},{24,8},{18,10},{28,12},{22,14},{0,16},... | collective-permute-start | bytes 153608 | tf_op jit(solution)/shard_map/ppermute | solution.py:217
  10.2 7.0 %collective-permute-start.4 = (bf16[2,100,256]{2,1,0:T(8,128)(2,1)S(1)}, bf16[2,100,256]{2,1,0:T(8,128)(2,1)S(1)}, u32[]{:S(2)}, u32[]{:S(2)}) collective-permute-start(bf16[2,100,256]{2,1,0:T(8,128)(2,1)S(1)} %shard_map.102), channel_id=1, source_target_pairs={{4,0},{6,2},{0,4},{2,6},{12,8},{14,10},{8,12},{10,14},{20,16},{22,... | collective-permute-start | bytes 307208 | tf_op jit(solution)/shard_map/ppermute | solution.py:217
  13.9 5.9 %collective-permute-start.6 = (bf16[1,100,256]{2,1,0:T(8,128)(2,1)S(1)}, bf16[1,100,256]{2,1,0:T(8,128)(2,1)S(1)}, u32[]{:S(2)}, u32[]{:S(2)}) collective-permute-start(bf16[1,100,256]{2,1,0:T(8,128)(2,1)S(1)} %shard_map.104), channel_id=1, source_target_pairs={{4,0},{6,2},{0,4},{2,6},{12,8},{14,10},{8,12},{10,14},{20,16},{22,... | collective-permute-start | bytes 153608 | tf_op jit(solution)/shard_map/ppermute | solution.py:217
  15.7 4.1 %collective-permute-start.5 = (bf16[1,100,256]{2,1,0:T(8,128)(2,1)S(1)}, bf16[1,100,256]{2,1,0:T(8,128)(2,1)S(1)}, u32[]{:S(2)}, u32[]{:S(2)}) collective-permute-start(bf16[1,100,256]{2,1,0:T(8,128)(2,1)S(1)} %shard_map.103), channel_id=1, source_target_pairs={{4,0},{6,2},{0,4},{2,6},{12,8},{14,10},{8,12},{10,14},{20,16},{22,... | collective-permute-start | bytes 153608 | tf_op jit(solution)/shard_map/ppermute | solution.py:217
  19.9 1.8 %collective-permute-start.7 = (bf16[8,100,256]{2,1,0:T(8,128)(2,1)S(1)}, bf16[8,100,256]{2,1,0:T(8,128)(2,1)S(1)}, u32[]{:S(2)}, u32[]{:S(2)}) collective-permute-start(bf16[8,100,256]{2,1,0:T(8,128)(2,1)S(1)} %constant_dynamic-update-slice_fusion.stack), channel_id=1, source_target_pairs={{2,0},{0,2},{6,4},{4,6},{10,8},{8,10},{14,12},{12,14},{18,16},{16,... | collective-permute-start | bytes 1228808 | tf_op jit(solution)/shard_map/ppermute | solution.py:217
  22.7 4.4 %collective-permute-start.8 = (s16[144,256]{1,0:T(8,128)(2,1)S(1)}, s16[144,256]{1,0:T(8,128)(2,1)S(1)}, u32[]{:S(2)}, u32[]{:S(2)}) collective-permute-start(s16[144,256]{1,0:T(8,128)(2,1)S(1)} %get-tuple-element.31), channel_id=1, source_target_pairs={{1,0},{0,1},{3,2},{2,3},{5,4},{4,5},{7,6},{6,7},{9,8},{8,9},{11,10... | collective-permute-start | bytes 221192 | tf_op jit(solution)/shard_map/ppermute | solution.py:213
  38.6 1.4 %collective-permute-start.9 = (bf16[8,48,256]{2,1,0:T(8,128)(2,1)S(1)}, bf16[8,48,256]{2,1,0:T(8,128)(2,1)S(1)}, u32[]{:S(2)}, u32[]{:S(2)}) collective-permute-start(bf16[8,48,256]{2,1,0:T(8,128)(2,1)S(1)} %all_to_all.5.near), channel_id=1, source_target_pairs={{2,0},{0,2},{6,4},{4,6},{10,8},{8,10},{14,12},{12,14},{18,16},{16,... | collective-permute-start | bytes 589832 | tf_op jit(solution)/shard_map/ppermute | solution.py:217
  40.6 3.9 %collective-permute-start.10 = (s16[48,256]{1,0:T(8,128)(2,1)S(1)}, s16[48,256]{1,0:T(8,128)(2,1)S(1)}, u32[]{:S(2)}, u32[]{:S(2)}) collective-permute-start(s16[48,256]{1,0:T(8,128)(2,1)S(1)} %get-tuple-element.36), channel_id=1, source_target_pairs={{1,0},{0,1},{3,2},{2,3},{5,4},{4,5},{7,6},{6,7},{9,8},{8,9},{11,10... | collective-permute-start | bytes 73736 | tf_op jit(solution)/shard_map/ppermute | solution.py:213
